TPU v7x, 256 devices: a whole 4x4x8 slice. The times are simulated.
256 devices in a mesh: event: 32 (over x, z), feat: 8 (over y, core).
Axes of the slice: x: 4, y: 4, z: 8, core: 2. Of those that a mesh axis runs over, the one named last changes fastest.
Arguments:
- events: bfloat16 [40960, 32768], P('event', 'feat')
- labels: int32 [40960], P('event'), may hold values 0 or 1
- weights: float32 [32768], P('feat'), may hold values from -6 to 6
- contexts: int32 [63], replicated, may hold values from 0 to 40959
Outputs:
- new_weights: float32 [32768], P('feat')
- widths: float32 [63], replicated
All inputs are finite; a program needn't handle non-finite values. No bound on the sum of `labels` on one device may be relied on, other than what follows from the above.
Results may differ from a plain program's by a relative error of at most 0.0022.
Values may be sent and summed in bfloat16 or wider, within the bound.
No kernel may reach another device: no remote copies, remote signals or barrier semaphores. Data moves between devices by JAX's collectives and lax.ppermute only.
A program may use at most 64 MiB of HBM per device.

v0:
```python
import jax
import jax.numpy as jnp
from jax import lax
from jax.sharding import PartitionSpec as P

ITERS = 2


LAMBDA = 0.5


def split_pair(values):
    leading = values.astype(jnp.bfloat16)
    rest = values - lax.optimization_barrier(leading).astype(jnp.float32)
    return (leading, rest.astype(jnp.bfloat16))


def feature_total(partials):
    return lax.psum(partials, "feat")


def on_device(events, labels, weights, contexts):
    row_count = events.shape[0]
    weight_half = weights.astype(jnp.bfloat16)
    margin = lax.psum(jnp.dot(events, weight_half, preferred_element_type=jnp.float32), "feat")
    chance = jax.nn.sigmoid(margin)
    curvature_rate = chance * (1.0 - chance)
    errors = chance - labels.astype(jnp.float32)
    err_lead, err_rest = split_pair(errors)
    row_start = lax.axis_index("event") * row_count
    positions = row_start + jnp.arange(row_count, dtype=jnp.int32)
    selector = (contexts[:, None] == positions[None, :]).astype(jnp.bfloat16)
    stacked = jnp.concatenate([err_lead[None, :], err_rest[None, :], selector], axis=0)
    product_rows = jnp.dot(stacked, events, preferred_element_type=jnp.float32)
    partial_rhs = jnp.concatenate([product_rows[0:1] + product_rows[1:2], product_rows[2:]], axis=0)
    rhs_rows = partial_rhs.shape[0]
    lead_mask = (jnp.arange(rhs_rows) == 0).astype(jnp.float32)
    right_side = lax.psum(partial_rhs, "event")
    right_side = right_side + LAMBDA * lead_mask[:, None] * weights[None, :]
    solution = jnp.zeros_like(right_side)
    residual = right_side
    direction = right_side
    norm_now = feature_total(jnp.sum(residual * residual, axis=1))
    for iteration in range(ITERS):
        dir_lead, dir_rest = split_pair(direction)
        dir_pair = jnp.concatenate([dir_lead, dir_rest], axis=0)
        both_scores = lax.dot_general(
            dir_pair, events, (((1,), (1,)), ((), ())), preferred_element_type=jnp.float32
        )
        partial_scores = both_scores[:rhs_rows] + both_scores[rhs_rows:]
        squares = jnp.sum(direction * direction, axis=1)
        scores = lax.psum(partial_scores, "feat")
        weighted = curvature_rate[None, :] * scores
        q_lead, q_rest = split_pair(weighted)
        q_pair = jnp.concatenate([q_lead, q_rest], axis=0)
        hess_both = jnp.dot(q_pair, events, preferred_element_type=jnp.float32)
        hess_part = hess_both[:rhs_rows] + hess_both[rhs_rows:]
        hess_sum = lax.psum(hess_part, "event")
        curvature = feature_total(jnp.sum(direction * hess_sum, axis=1) + LAMBDA * squares)
        step_size = norm_now / curvature
        solution = solution + step_size[:, None] * direction
        if iteration + 1 < ITERS:
            hess_vec = hess_sum + LAMBDA * direction
            residual = residual - step_size[:, None] * hess_vec
            norm_next = feature_total(jnp.sum(residual * residual, axis=1))
            direction = residual + (norm_next / norm_now)[:, None] * direction
            norm_now = norm_next
    widths = feature_total(jnp.sum(right_side[1:] * solution[1:], axis=1))
    step_full = solution[0]
    return (weights - step_full, widths)


def solution(mesh):
    in_specs = (P("event", "feat"), P("event"), P("feat"), P())
    out_specs = (P("feat"), P())
    return jax.shard_map(
        on_device, mesh=mesh, in_specs=in_specs, out_specs=out_specs, check_vma=False
    )
```

profile of v0, /device:TPU:1, one launch (start us, length us, event | category | flops | bytes accessed | tf_op | source)
XLA Modules:
  0.0 708.6 jit_solution(1363269900664141204)
XLA Ops:
  7.2 0.0 copy-start.1
  7.2 0.0 copy-start.2
  7.2 0.0 all-reduce.7.cloned.1.call-start
  7.2 0.7 convert_element_type.56
  8.0 6.8 convolution_reduce_fusion
  14.8 15.2 %psum.77 = f32[1280]{0:T(1024)S(1)} all-reduce(f32[1280]{0:T(1024)S(1)} %convolution_reduce_fusion), channel_id=1, replica_groups=mesh['event'=32,'feat'=8] {'feat'}, use_global_device_ids=true, to_apply=%region_0.0 | all-reduce | flops 1280 | bytes 10240 | tf_op jit(solution)/shard_map/psum | solution.py:25
  30.0 0.0 copy-done.1
  30.1 0.0 copy-done.2
  30.1 0.1 compare_convert_fusion
  30.2 0.0 copy-start
  30.2 5.9 fusion.17
  36.2 0.1 slice.58
  36.3 1.1 pad_maximum_fusion
  37.4 0.0 all-reduce.7.cloned.1.call-update
  37.4 0.0 all-reduce.9.cloned.1.call-start
  37.5 145.9 %all-reduce.7.cloned.1.call-done = f32[64,4096]{1,0:T(8,128)} async-done(((f32[64,4096]{1,0:T(8,128)}), f32[64,4096]{1,0:T(8,128)}) %all-reduce.7.cloned.1.call-update) | async-done | bytes 1048592 | tf_op jit(solution)/shard_map/psum | solution.py:38
  183.4 0.0 copy-done
  183.4 1.4 fusion.30
  184.9 0.1 subtract_convert_fusion.1
  185.0 7.6 %fusion.1 = f32[128,1280]{1,0:T(8,128)S(1)} fusion(bf16[1280,4096]{1,0:T(8,128)(2,1)} %param.4, bf16[64,4096]{1,0:T(8,128)(2,1)S(1)} %subtract_convert_fusion.1, bf16[64,4096]{1,0:T(8,128)(2,1)S(1)} %get-tuple-element.10), kind=kOutput, calls=%fused_computation.6 | convolution fusion | flops 1344274432 | bytes 12189696 | tf_op jit(solution)/shard_map/dot_general | solution.py:47
  192.6 0.8 slice_add_fusion.3
  193.3 0.0 all-reduce.9.cloned.1.call-update
  193.3 0.0 all-reduce.11.cloned.1.call-start
  193.4 65.3 %all-reduce.9.cloned.1.call-done = f32[64,1280]{1,0:T(8,128)} async-done(((f32[64,1280]{1,0:T(8,128)}), f32[64,1280]{1,0:T(8,128)}) %all-reduce.9.cloned.1.call-update) | async-done | bytes 327696 | tf_op jit(solution)/shard_map/psum | solution.py:52
  258.7 1.0 multiply_convert_fusion.1
  259.7 1.0 subtract_convert_fusion.3
  260.8 5.5 fusion.9
  266.3 1.1 slice_add_fusion.1
  267.4 0.0 all-reduce.11.cloned.1.call-update
  267.4 0.0 all-reduce.13.cloned.1.call-start
  267.5 146.1 %all-reduce.11.cloned.1.call-done = f32[64,4096]{1,0:T(8,128)} async-done(((f32[64,4096]{1,0:T(8,128)}), f32[64,4096]{1,0:T(8,128)}) %all-reduce.11.cloned.1.call-update) | async-done | bytes 1048592 | tf_op jit(solution)/shard_map/psum | solution.py:58
  413.6 1.5 multiply_reduce_fusion.3
  415.1 17.0 %all-reduce = (f32[64]{0:T(128)S(1)}, f32[64]{0:T(128)S(1)}) all-reduce(f32[64]{0:T(128)S(1)} %get-tuple-element.5, f32[64]{0:T(128)S(1)} %multiply_add_fusion.4), channel_id=1, replica_groups=mesh['event'=32,'feat'=8] {'feat'}, use_global_device_ids=true, to_apply=%region_3.0 | all-reduce | flops 128 | bytes 1024 | tf_op jit(solution)/shard_map/psum | solution.py:19
  432.1 1.6 multiply_reduce_fusion.2
  433.7 12.6 %psum.83 = f32[64]{0:T(128)S(1)} all-reduce(f32[64]{0:T(128)S(1)} %multiply_reduce_fusion.2), channel_id=1, replica_groups=mesh['event'=32,'feat'=8] {'feat'}, use_global_device_ids=true, to_apply=%region_9.0 | all-reduce | flops 64 | bytes 512 | tf_op jit(solution)/shard_map/psum | solution.py:19
  446.3 1.5 fusion.29
  447.8 0.1 subtract_convert_fusion
  448.0 7.6 %fusion.5 = f32[128,1280]{1,0:T(8,128)S(1)} fusion(bf16[1280,4096]{1,0:T(8,128)(2,1)} %param.4, bf16[64,4096]{1,0:T(8,128)(2,1)S(1)} %subtract_convert_fusion, bf16[64,4096]{1,0:T(8,128)(2,1)S(1)} %get-tuple-element.8), kind=kOutput, calls=%fused_computation.10 | convolution fusion | flops 1344274432 | bytes 12189696 | tf_op jit(solution)/shard_map/dot_general | solution.py:47
  455.5 0.8 slice_add_fusion.2
  456.3 0.0 all-reduce.13.cloned.1.call-update
  456.3 0.0 all-reduce.15.cloned.1.call-start
  456.4 58.2 %all-reduce.13.cloned.1.call-done = f32[64,1280]{1,0:T(8,128)} async-done(((f32[64,1280]{1,0:T(8,128)}), f32[64,1280]{1,0:T(8,128)}) %all-reduce.13.cloned.1.call-update) | async-done | bytes 327696 | tf_op jit(solution)/shard_map/psum | solution.py:52
  514.6 1.0 multiply_convert_fusion
  515.6 1.0 subtract_convert_fusion.2
  516.6 5.5 fusion.13
  522.1 1.1 slice_add_fusion
  523.3 0.0 all-reduce.15.cloned.1.call-update
  523.3 146.2 %all-reduce.15.cloned.1.call-done = f32[64,4096]{1,0:T(8,128)} async-done(((f32[64,4096]{1,0:T(8,128)}), f32[64,4096]{1,0:T(8,128)}) %all-reduce.15.cloned.1.call-update) | async-done | bytes 1048592 | tf_op jit(solution)/shard_map/psum | solution.py:58
  669.5 1.5 multiply_reduce_fusion
  671.0 17.0 %psum.86 = f32[64]{0:T(128)S(1)} all-reduce(f32[64]{0:T(128)S(1)} %multiply_add_fusion.3), channel_id=1, replica_groups=mesh['event'=32,'feat'=8] {'feat'}, use_global_device_ids=true, to_apply=%region_14.0 | all-reduce | flops 64 | bytes 512 | tf_op jit(solution)/shard_map/psum | solution.py:19
  688.0 0.2 multiply_add_fusion
  688.2 0.3 fusion
  688.6 0.6 sub.35
  689.2 12.9 %psum.87 = f32[63]{0:T(128)} all-reduce(f32[63]{0:T(128)S(1)} %fusion), channel_id=1, replica_groups=mesh['event'=32,'feat'=8] {'feat'}, use_global_device_ids=true, to_apply=%region_16.0 | all-reduce | flops 63 | bytes 504 | tf_op jit(solution)/shard_map/psum | solution.py:19
  (14 shorter events, 0.1 us)
Async XLA Ops:
  7.2 22.8 %copy-start.1 = (s32[1280]{0:T(1024)S(1)}, s32[1280]{0:T(1024)}, u32[]{:S(2)}) copy-start(s32[1280]{0:T(1024)} %param.5) | copy-start | bytes 15364
  7.2 22.9 %copy-start.2 = (s32[63]{0:T(128)S(1)}, s32[63]{0:T(128)}, u32[]{:S(2)}) copy-start(s32[63]{0:T(128)} %param.7) | copy-start | bytes 760
  7.2 176.2 %all-reduce.7.cloned.1.call-start = ((), (), s32[]{:S(2)}) async-start(), calls=%async_computation | async-start | bytes 2097152 | tf_op jit(solution)/shard_map/psum | solution.py:38
  30.2 153.2 %copy-start = (f32[4096]{0:T(1024)S(1)}, f32[4096]{0:T(1024)}, u32[]{:S(2)}) copy-start(f32[4096]{0:T(1024)} %param.6) | copy-start | bytes 49156
  37.4 221.3 %all-reduce.9.cloned.1.call-start = ((), (), s32[]{:S(2)}) async-start(), calls=%async_computation.1 | async-start | bytes 655360 | tf_op jit(solution)/shard_map/psum | solution.py:52
  193.3 220.3 %all-reduce.11.cloned.1.call-start = ((), (), s32[]{:S(2)}) async-start(), calls=%async_computation.2 | async-start | bytes 2097152 | tf_op jit(solution)/shard_map/psum | solution.py:58
  267.4 247.2 %all-reduce.13.cloned.1.call-start = ((), (), s32[]{:S(2)}) async-start(), calls=%async_computation.3 | async-start | bytes 655360 | tf_op jit(solution)/shard_map/psum | solution.py:52
  456.3 213.2 %all-reduce.15.cloned.1.call-start = ((), (), s32[]{:S(2)}) async-start(), calls=%async_computation.4 | async-start | bytes 2097152 | tf_op jit(solution)/shard_map/psum | solution.py:58
Sparse Core Ops, SparseCore 0:
  37.5 145.8 all-reduce.6
  193.5 65.2 all-reduce.8
  267.6 146.0 all-reduce.10
  456.4 58.1 all-reduce.12
  523.4 146.0 all-reduce.14
where the time goes:
time: 709 us
  waiting for transfers between devices  562 us (79%)
  blocking collectives  74.8 us (11%)
  matrix products  38.9 us (5%)
  other arithmetic  18.6 us (3%)
  between operations  14 us (2%)
    psum x2, waiting for transfers between devices, on_device(): hess_sum = lax.psum(hess_part, 'event')  292 us
    psum x1, waiting for transfers between devices, on_device(): right_side = lax.psum(partial_rhs, 'event')  146 us
    psum x2, waiting for transfers between devices, on_device(): scores = lax.psum(partial_scores, 'feat')  124 us
    psum x4, blocking collectives, feature_total(): return lax.psum(partials, 'feat')  59.6 us
    psum x1, blocking collectives, on_device(): lax.psum(jnp.dot(events, weight_half, preferred_element_type=jnp.float32)...  15.2 us
    dot_general x2, matrix products, on_device(): lax.dot_general(dir_pair, events, (((1,), (1,)), ((), ())), preferred_ele...  15.1 us
  transfers between devices with their start and end apart: 5, of which 5 were waited for; matrix products, arithmetic and copies ran while one was open for 0% of the time, Pallas kernels for 0%

commit v1 on v0

v1 whole, which is shorter than its diff:
```python
import jax
import jax.numpy as jnp
from jax import lax
from jax.experimental import pallas as pl
from jax.experimental.pallas import tpu as pltpu
from jax.sharding import PartitionSpec as P

LAMBDA = 0.5
XN, ZN, YN, CN = 4, 8, 4, 2
EN = XN * ZN
ROWS = 64
TILES = 32
QUARTER = TILES // XN
COUNT = 1280
HALF = COUNT // 2
F32, BF16 = jnp.float32, jnp.bfloat16
VMEM = pl.BlockSpec(memory_space=pltpu.VMEM)
SMEM = pl.BlockSpec(memory_space=pltpu.SMEM)
HBM = pl.BlockSpec(memory_space=pltpu.HBM)
ACROSS = (((1,), (1,)), ((), ()))


def shaped(*shape, dtype=F32):
    return jax.ShapeDtypeStruct(shape, dtype)


def kernel_call(body, ins, outs, args, scratch=(), micros=0.5):
    return pl.pallas_call(
        body,
        out_shape=outs,
        in_specs=ins,
        out_specs=[VMEM] * len(outs),
        scratch_shapes=list(scratch),
        compiler_params=pltpu.CompilerParams(vmem_limit_bytes=28 << 20),
        cost_estimate=pl.CostEstimate(flops=0, bytes_accessed=int(micros * 3.6e6), transcendentals=0),
    )(*args)


def x_moves(v):
    n = XN * ZN
    return [lax.ppermute(v, "event", [(i, (i + k * ZN) % n) for i in range(n)]) for k in (1, 2, 3)]


def y_moves(v):
    n = YN * CN
    return [lax.ppermute(v, "feat", [(i, (i + k * CN) % n) for i in range(n)]) for k in (1, 2, 3)]


def core_move(v):
    return lax.ppermute(v, "feat", [(i, i ^ 1) for i in range(YN * CN)])


def z_exchange(v):
    groups = [[x * ZN + z for z in range(ZN)] for x in range(XN)]
    return lax.all_to_all(v, "event", 0, 0, axis_index_groups=groups)


def four(own, one, two, three):
    return (own + two) + (one + three)


def pair_of(v):
    lead = v.astype(BF16)
    return lead, (v - lead.astype(F32)).astype(BF16)


def triple_of(v):
    lead, rest = v.astype(BF16), v
    rest = v - lead.astype(F32)
    mid = rest.astype(BF16)
    return lead, mid, (rest - mid.astype(F32)).astype(BF16)


def row_is(shape, i):
    return lax.broadcasted_iota(jnp.int32, shape, 0) == i


def stacked(lines, rows):
    out = jnp.zeros((rows, lines[0].shape[1]), F32)
    for i, line in enumerate(lines):
        out = jnp.where(row_is(out.shape, i), line.astype(F32), out)
    return out


def joined(v):
    top = v[:ROWS]
    return top + jnp.where(row_is(top.shape, ROWS - 1), v[ROWS : ROWS + 1], 0.0)


def line_sums(top, bottom):
    return jnp.sum(jnp.transpose(jnp.concatenate([top, bottom], axis=0)), axis=0, keepdims=True)


def tile_sums(v):
    total = v[:, :128]
    for t in range(1, v.shape[1] // 128):
        total = total + v[:, t * 128 : (t + 1) * 128]
    return total


def first_kernel(local_ref, w_ref, events_ref, held_ref, margin_ref, out_ref, rows, sems):
    piece = COUNT // 5
    copies = [
        pltpu.make_async_copy(
            events_ref.at[pl.ds(c * piece, piece), :], held_ref.at[pl.ds(c * piece, piece), :], sems.at[c]
        )
        for c in range(5)
    ]
    for copy in copies:
        copy.start()
    rows[...] = jnp.zeros_like(rows)
    w = jnp.broadcast_to(w_ref[...], (16, TILES * 128)).astype(BF16)
    for c, copy in enumerate(copies):
        copy.wait()
        part = lax.dot_general(w, held_ref[c * piece : (c + 1) * piece, :], ACROSS, preferred_element_type=F32)
        margin_ref[2 * c : 2 * c + 1, :] = part[:1, :128]
        margin_ref[2 * c + 1 : 2 * c + 2, :] = part[:1, 128:]

    @pl.loop(0, ROWS - 1)
    def _(j):
        r = local_ref[j]

        @pl.when(jnp.logical_and(r >= 0, r < COUNT))
        def _():
            start = pl.multiple_of(lax.div(r, 16) * 16, 16)
            block = held_ref[pl.ds(start, 16), :].astype(F32)
            found = jnp.where(row_is(block.shape, lax.rem(r, 16)), block, 0.0)
            rows[pl.ds(j, 1), :] = jnp.sum(found, axis=0, keepdims=True)

    for t in range(TILES):
        out_ref[t] = rows[:, t * 128 : (t + 1) * 128].astype(BF16)


def gradient_kernel(held_ref, own, one, two, three, labels_ref, rate_ref, grad_ref, errs):
    margin = four(own[...], one[...], two[...], three[...])
    chance = jax.nn.sigmoid(margin)
    rate = chance * (1.0 - chance)
    errors = chance - labels_ref[...].astype(F32)
    lead, rest = pair_of(errors)
    lead, rest = lead.astype(F32), rest.astype(F32)
    for i in range(COUNT // 128):
        at = slice(i * 128, (i + 1) * 128)
        rate_ref[:, at] = rate[i : i + 1]
        errs[:, at] = stacked([lead[i : i + 1], rest[i : i + 1]], 16).astype(BF16)
    for n in range(0, TILES, 4):
        part = jnp.dot(errs[...], held_ref[:, n * 128 : (n + 4) * 128], preferred_element_type=F32)
        line = part[:1] + part[1:2]
        for u in range(4):
            grad_ref[n + u : n + u + 1, :] = line[:, u * 128 : (u + 1) * 128]


def spread_kernel(chunks_ref, grad_ref, out_ref):
    total = chunks_ref[0].astype(F32)
    for e in range(1, EN):
        total = total + chunks_ref[e].astype(F32)
    lead, rest = pair_of(grad_ref[...])
    for z in range(ZN):
        out_ref[z, :ROWS, :] = total.astype(BF16)
        out_ref[z, ROWS : ROWS + TILES, :] = lead
        out_ref[z, ROWS + TILES :, :] = rest


def collect_kernel(in_ref, out_ref):
    grad = jnp.zeros((TILES, 128), F32)
    for z in range(ZN):
        out_ref[z * ROWS : (z + 1) * ROWS, :] = in_ref[z, :ROWS, :]
        grad = grad + (in_ref[z, ROWS : ROWS + TILES, :].astype(F32) + in_ref[z, ROWS + TILES :, :].astype(F32))
    lead, rest = pair_of(grad)
    out_ref[QUARTER * ROWS : QUARTER * ROWS + TILES, :] = lead
    out_ref[QUARTER * ROWS + TILES :, :] = rest


def put_scores(held_ref, rhs, core, other_ref, own_ref, lines):
    for half, out_ref in ((1 - core, other_ref), (core, own_ref)):
        start = pl.multiple_of(half * HALF, HALF)
        part = lax.dot_general(held_ref[pl.ds(start, HALF), :], rhs[...], ACROSS, preferred_element_type=F32)
        for t in range(HALF // 128):
            out_ref[:ROWS, t * 128 : (t + 1) * 128] = joined(jnp.transpose(part[t * 128 : (t + 1) * 128]))
            out_ref[ROWS:, t * 128 : (t + 1) * 128] = lines if t == 0 else jnp.zeros_like(lines)


def scores_kernel(idx_ref, held_ref, w_ref, own, one, two, three, rhs_ref, grad_ref, other_ref, mine_ref):
    x, core = idx_ref[0], idx_ref[2]
    top = QUARTER * ROWS
    grads = [p[top : top + TILES, :].astype(F32) + p[top + TILES :, :].astype(F32) for p in (own, one, two, three)]
    grad_ref[...] = four(*grads) + LAMBDA * w_ref[...]
    norm = jnp.zeros((ROWS, 128), F32)
    rhs_ref[ROWS:, :] = jnp.zeros((128 - ROWS, TILES * 128), BF16)
    for k, part in enumerate((own, one, two, three)):
        quarter = lax.rem(x + XN - k, XN)
        for t in range(QUARTER):
            tile = quarter * QUARTER + t
            grad = grad_ref[pl.ds(tile, 1), :]
            lead, rest = pair_of(grad)
            values = part[t * ROWS : (t + 1) * ROWS, :].astype(F32)
            last = row_is(values.shape, ROWS - 1)
            exact = jnp.where(last, grad, values)
            norm = norm + exact * exact
            at = pl.ds(pl.multiple_of(tile * 128, 128), 128)
            rhs_ref[:ROWS, at] = jnp.where(last, lead.astype(F32), values).astype(BF16)
            rhs_ref[ROWS : ROWS + 16, at] = stacked([rest], 16).astype(BF16)
    line = line_sums(norm, jnp.zeros_like(norm))
    put_scores(held_ref, rhs_ref, core, other_ref, mine_ref, stacked([line], 8))


def pack_kernel(own, other, out_ref):
    total = own[...] + other[...]
    scores, lines = total[:ROWS], total[ROWS:]
    lead = scores.astype(BF16)
    rest = scores[ROWS - 1 :] - lead[ROWS - 1 :].astype(F32)
    out_ref[:ROWS, :] = lead
    out_ref[ROWS:, :] = stacked([rest, *triple_of(lines[:1]), *triple_of(lines[1:2])], 16).astype(BF16)


def unpacked(own, one, two, three):
    total = four(*(p[...].astype(F32) for p in (own, one, two, three)))
    first = total[65:66] + total[66:67] + total[67:68]
    second = total[68:69] + total[69:70] + total[70:71]
    return joined(total), first[:, :128], second[:, :128]


def unpack_kernel(own, one, two, three, scores_ref, norm_ref):
    scores, norm, _ = unpacked(own, one, two, three)
    scores_ref[...] = scores
    norm_ref[...] = stacked([norm], 8)


def hessian_kernel(idx_ref, held_ref, mine_ref, theirs_ref, rate_ref, own_ref, curv_ref, one_ref, two_ref, three_ref, q):
    x, core = idx_ref[0], idx_ref[2]
    curv = jnp.zeros((ROWS, 128), F32)
    for half in range(2):
        scores = jnp.where(core == half, mine_ref[...], theirs_ref[...])
        at = slice(half * HALF, (half + 1) * HALF)
        weighted = rate_ref[:, at] * scores
        curv = curv + tile_sums(weighted * scores)
        lead = weighted.astype(BF16)
        q[:ROWS, at] = lead
        q[ROWS:, at] = stacked([weighted[ROWS - 1 :] - lead[ROWS - 1 :].astype(F32)], 16).astype(BF16)
    triple = [v.astype(F32) for v in triple_of(line_sums(curv, jnp.zeros_like(curv)))]
    curv_ref[...] = stacked(triple, 8)
    for k, out_ref in ((2, two_ref), (1, one_ref), (3, three_ref), (0, own_ref)):
        quarter = lax.rem(x + k, XN)
        columns = pl.ds(pl.multiple_of(quarter * QUARTER * 128, 128), QUARTER * 128)
        total = joined(jnp.dot(q[...], held_ref[:, columns], preferred_element_type=F32))
        rests = []
        for t in range(QUARTER):
            values = total[:, t * 128 : (t + 1) * 128]
            out_ref[t * ROWS : (t + 1) * ROWS, :] = values.astype(out_ref.dtype)
            rests.append(values[ROWS - 1 :] - values[ROWS - 1 :].astype(BF16).astype(F32))
        if k:
            out_ref[QUARTER * ROWS :, :] = stacked(rests + triple, 16).astype(BF16)


def cut_kernel(own, curv_ref, one, two, three, out_ref):
    top = QUARTER * ROWS
    tails = [p[top:, :].astype(F32) for p in (one, two, three)]
    curvs = [curv_ref[0:1] + curv_ref[1:2] + curv_ref[2:3]]
    curvs += [v[QUARTER : QUARTER + 1] + v[QUARTER + 1 : QUARTER + 2] + v[QUARTER + 2 : QUARTER + 3] for v in tails]
    curv = triple_of(four(*curvs))
    for t in range(QUARTER):
        at = slice(t * ROWS, (t + 1) * ROWS)
        total = four(own[at, :], one[at, :].astype(F32), two[at, :].astype(F32), three[at, :].astype(F32))
        rest = tails[0][t : t + 1] + tails[1][t : t + 1] + tails[2][t : t + 1]
        total = total + jnp.where(row_is(total.shape, ROWS - 1), rest, 0.0)
        lead = total.astype(BF16)
        rest = total[ROWS - 1 :] - lead[ROWS - 1 :].astype(F32)
        out_ref[t, :ROWS, :] = lead
        out_ref[t, ROWS:, :] = stacked([rest, *curv], 8).astype(BF16)


def residual_kernel(idx_ref, in_ref, norm_ref, rhs_ref, grad_ref, out_ref, scalars_ref):
    tile = idx_ref[0] * QUARTER + idx_ref[1]
    total = in_ref[0].astype(F32)
    for z in range(1, ZN):
        total = total + in_ref[z].astype(F32)
    curv = total[65:66] + total[66:67] + total[67:68]
    norm = norm_ref[:1]
    step = norm / (curv + LAMBDA * norm)
    square = (ROWS, 128)
    eye = lax.broadcasted_iota(jnp.int32, square, 0) == lax.broadcasted_iota(jnp.int32, square, 1)
    column = jnp.sum(jnp.where(eye, step, 0.0), axis=1, keepdims=True)
    right = rhs_ref[:ROWS, pl.ds(pl.multiple_of(tile * 128, 128), 128)].astype(F32)
    right = jnp.where(row_is(square, ROWS - 1), grad_ref[pl.ds(tile, 1), :], right)
    residual = right - column * (joined(total) + LAMBDA * right)
    lead = residual.astype(BF16)
    rest = stacked([residual[ROWS - 1 :] - lead[ROWS - 1 :].astype(F32)], 8).astype(BF16)
    for z in range(ZN):
        out_ref[z, :ROWS, :] = lead
        out_ref[z, ROWS:, :] = rest
    scalars_ref[...] = stacked([step, curv, norm], 8)


def second_kernel(idx_ref, held_ref, rhs_ref, grad_ref, own, one, two, three, other_ref, mine_ref, first_ref, res):
    x, core = idx_ref[0], idx_ref[2]
    norm = jnp.zeros((ROWS, 128), F32)
    cross = jnp.zeros((ROWS, 128), F32)
    res[ROWS:, :] = jnp.zeros((128 - ROWS, TILES * 128), BF16)
    for k, part in enumerate((own, one, two, three)):
        quarter = lax.rem(x + XN - k, XN)
        for t in range(QUARTER):
            tile = quarter * QUARTER + t
            at = pl.ds(pl.multiple_of(tile * 128, 128), 128)
            rows = part[t]
            values = joined(rows.astype(F32))
            right = rhs_ref[:ROWS, at].astype(F32)
            right = jnp.where(row_is(right.shape, ROWS - 1), grad_ref[pl.ds(tile, 1), :], right)
            norm = norm + values * values
            cross = cross + values * right
            first_ref[pl.ds(tile, 1), :] = values[ROWS - 1 :]
            res[:ROWS, at] = rows[:ROWS]
            res[ROWS : ROWS + 16, at] = stacked([rows[ROWS:].astype(F32)[:1]], 16).astype(BF16)
    line = line_sums(norm, cross)
    lines = stacked([line, pltpu.roll(line, ROWS, 1)], 8)
    put_scores(held_ref, res, core, other_ref, mine_ref, lines)


def tail_kernel(idx_ref, own, one, two, three, scores_ref, rate_ref, tail_ref, lines_ref):
    scores, norm, cross = unpacked(own, one, two, three)
    rate = jnp.where(idx_ref[2] == 0, rate_ref[:, :HALF], rate_ref[:, HALF:])
    weighted = rate * scores
    tail_ref[...] = line_sums(tile_sums(weighted * scores_ref[...]), tile_sums(weighted * scores))
    lines_ref[...] = stacked([norm, cross], 8)


def end_kernel(tails_ref, scalars_ref, lines_ref, w_ref, grad_ref, first_ref, weights_ref, widths_ref):
    tail = tails_ref[0]
    for e in range(1, EN):
        tail = tail + tails_ref[e]
    mixed, square = tail, pltpu.roll(tail, ROWS, 1)
    step_one, curv, norm = scalars_ref[0:1], scalars_ref[1:2], scalars_ref[2:3]
    norm_next, cross = lines_ref[0:1], lines_ref[1:2]
    ratio = norm_next / norm
    curvature = square + 2.0 * ratio * mixed + ratio * ratio * curv
    curvature = curvature + LAMBDA * (norm_next + 2.0 * ratio * cross + ratio * ratio * norm)
    step_two = norm_next / curvature
    widths_ref[...] = step_one * norm + step_two * (cross + ratio * norm)
    at = slice(ROWS - 1, ROWS)
    grad = grad_ref[...]
    step = step_one[:, at] * grad + step_two[:, at] * (first_ref[...] + ratio[:, at] * grad)
    weights_ref[...] = w_ref[...] - step


def on_device(events, labels, weights, contexts):
    place = lax.axis_index("event")
    core = lax.rem(lax.axis_index("feat"), CN)
    idx = jnp.stack([place // ZN, lax.rem(place, ZN), core]).astype(jnp.int32)
    features = TILES * 128
    tiled = weights.reshape(TILES, 128)

    held, margin, picked = kernel_call(
        first_kernel,
        [SMEM, VMEM, HBM],
        [shaped(COUNT, features, dtype=BF16), shaped(COUNT // 128, 128), shaped(TILES, ROWS, 128, dtype=BF16)],
        (contexts - place * COUNT, weights.reshape(1, features), events),
        [pltpu.VMEM((ROWS, features), F32), pltpu.SemaphoreType.DMA((5,))],
        micros=4,
    )
    chunks = lax.all_to_all(picked, "event", 0, 0)

    margin = margin + core_move(margin)
    rate, grad = kernel_call(
        gradient_kernel,
        [VMEM] * 6,
        [shaped(1, COUNT), shaped(TILES, 128)],
        (held, margin, *y_moves(margin), labels.reshape(COUNT // 128, 128)),
        [pltpu.VMEM((16, COUNT), BF16)],
        micros=3,
    )
    (message,) = kernel_call(
        spread_kernel, [VMEM] * 2, [shaped(ZN, ROWS + 2 * TILES, 128, dtype=BF16)], (chunks, grad)
    )
    message = z_exchange(message)
    (message,) = kernel_call(
        collect_kernel, [VMEM], [shaped(QUARTER * ROWS + 2 * TILES, 128, dtype=BF16)], (message,)
    )

    half = [shaped(ROWS + 8, HALF), shaped(ROWS + 8, HALF)]
    rhs, grad, other, mine = kernel_call(
        scores_kernel,
        [SMEM] + [VMEM] * 6,
        [shaped(128, features, dtype=BF16), shaped(TILES, 128)] + half,
        (idx, held, tiled, message, *x_moves(message)),
        micros=3,
    )
    packed = [shaped(ROWS + 16, HALF, dtype=BF16)]
    (message,) = kernel_call(pack_kernel, [VMEM] * 2, packed, (mine, core_move(other)))
    scores, norm = kernel_call(
        unpack_kernel, [VMEM] * 4, [shaped(ROWS, HALF), shaped(8, 128)], (message, *y_moves(message))
    )

    part = shaped(QUARTER * ROWS + 16, 128, dtype=BF16)
    own, curv, one, two, three = kernel_call(
        hessian_kernel,
        [SMEM] + [VMEM] * 4,
        [shaped(QUARTER * ROWS, 128), shaped(8, 128), part, part, part],
        (idx, held, scores, core_move(scores), rate),
        [pltpu.VMEM((ROWS + 16, COUNT), BF16)],
        micros=3,
    )
    moved = [
        lax.ppermute(v, "event", [(i, (i + k * ZN) % EN) for i in range(EN)])
        for k, v in ((1, one), (2, two), (3, three))
    ]
    shard = [shaped(ZN, ROWS + 8, 128, dtype=BF16)]
    (message,) = kernel_call(cut_kernel, [VMEM] * 5, shard, (own, curv, *moved))
    message, scalars = kernel_call(
        residual_kernel,
        [SMEM] + [VMEM] * 4,
        shard + [shaped(8, 128)],
        (idx, z_exchange(message), norm, rhs, grad),
    )
    message = z_exchange(message)

    other, mine, first = kernel_call(
        second_kernel,
        [SMEM] + [VMEM] * 7,
        half + [shaped(TILES, 128)],
        (idx, held, rhs, grad, message, *x_moves(message)),
        [pltpu.VMEM((128, features), BF16)],
        micros=3,
    )
    (message,) = kernel_call(pack_kernel, [VMEM] * 2, packed, (mine, core_move(other)))
    tail, lines = kernel_call(
        tail_kernel,
        [SMEM] + [VMEM] * 6,
        [shaped(1, 128), shaped(8, 128)],
        (idx, message, *y_moves(message), scores, rate),
    )
    tail = tail + core_move(tail)
    tails = lax.all_to_all(jnp.broadcast_to(tail[None], (EN, 1, 128)), "event", 0, 0)
    updated, widths = kernel_call(
        end_kernel, [VMEM] * 6, [shaped(TILES, 128), shaped(1, 128)], (tails, scalars, lines, tiled, grad, first)
    )
    return updated.reshape(features), widths[0, : ROWS - 1]


def solution(mesh):
    in_specs = (P("event", "feat"), P("event"), P("feat"), P())
    out_specs = (P("feat"), P())
    return jax.shard_map(on_device, mesh=mesh, in_specs=in_specs, out_specs=out_specs, check_vma=False)
```

time: 709 us -> 177 us (0.25)
  waiting for transfers between devices: 562 us -> 40.2 us
  starting transfers between devices: 0.21 us -> 42.9 us
  matrix products: 38.9 us -> 0 us
  blocking collectives: 74.8 us -> 48.5 us
  Pallas kernels: 0 us -> 22.4 us
  local copies, waits for them, and re-layouts: 0.13 us -> 21.2 us
  other arithmetic: 18.6 us -> 0.74 us
  between operations: 14 us -> 0.77 us
    psum x5 -> x0, waiting for transfers between devices: 562 us -> none  [the longest x2 292 us: on_device(): hess_sum = lax.psum(hess_part, 'event')]
    psum x5 -> x0, blocking collectives: 74.8 us -> none  [the longest x4 59.6 us: feature_total(): return lax.psum(partials, 'feat')]
    all_to_all x0 -> x4, blocking collectives: none -> 48.5 us  [the longest x3 36.9 us: z_exchange(): return lax.all_to_all(v, 'event', 0, 0, axis_index_groups=groups)]
    ppermute x0 -> x23, waiting for transfers between devices: none -> 40.2 us  [the longest x9 17.3 us: y_moves(): lax.ppermute(v, 'feat', [(i, (i + k * CN) % n) for i in range(n)])]
    dot_general x6 -> x0, matrix products: 38.9 us -> none  [the longest x2 15.1 us: on_device(): lax.dot_general(dir_pair, events, (((1,), (1,)), ((), ())), preferred_ele...]
    ppermute x0 -> x23, starting transfers between devices: none -> 31 us  [the longest x5 12 us: core_move(): return lax.ppermute(v, 'feat', [(i, i ^ 1) for i in range(YN * CN)])]
    pallas_call x0 -> x14, Pallas kernels: none -> 22.4 us  [kernel_call(): pl.pallas_call(body, out_shape=outs, in_specs=ins, out_specs=[VMEM] * len...]
    unnamed x6 -> x22, local copies, waits for them, and re-layouts: 0.01 us -> 20.7 us
  transfers between devices with their start and end apart: 5 -> 24, of which waited for: 5 -> 21; matrix products, arithmetic and copies ran while one was open for 0% -> 0% of each run, Pallas kernels for 0% -> 1%
where the time goes in v1:
time: 177 us
  blocking collectives  48.5 us (27%)
  starting transfers between devices  42.9 us (24%)
  waiting for transfers between devices  40.2 us (23%)
  Pallas kernels  22.4 us (13%)
  local copies, waits for them, and re-layouts  21.2 us (12%)
    all_to_all x3, blocking collectives, z_exchange(): return lax.all_to_all(v, 'event', 0, 0, axis_index_groups=groups)  36.9 us
    pallas_call x14, Pallas kernels, kernel_call(): pl.pallas_call(body, out_shape=outs, in_specs=ins, out_specs=[VMEM] * len...  22.4 us
    unnamed x22, local copies, waits for them, and re-layouts  20.7 us
    ppermute x9, waiting for transfers between devices, y_moves(): lax.ppermute(v, 'feat', [(i, (i + k * CN) % n) for i in range(n)])  17.3 us
    ppermute x6, waiting for transfers between devices, x_moves(): lax.ppermute(v, 'event', [(i, (i + k * ZN) % n) for i in range(n)])  12.1 us
    ppermute x5, starting transfers between devices, core_move(): return lax.ppermute(v, 'feat', [(i, i ^ 1) for i in range(YN * CN)])  12 us
    all_to_all x1, starting transfers between devices, on_device(): chunks = lax.all_to_all(picked, 'event', 0, 0)  11.9 us
    all_to_all x1, blocking collectives, on_device(): lax.all_to_all(jnp.broadcast_to(tail[None], (EN, 1, 128)), 'event', 0, 0)  11.6 us
  transfers between devices with their start and end apart: 24, of which 21 were waited for; matrix products, arithmetic and copies ran while one was open for 0% of the time, Pallas kernels for 1%

profile of v1, /device:TPU:1, one launch (start us, length us, event | category | flops | bytes accessed | tf_op | source)
XLA Modules:
  0.0 176.7 jit_solution(6985920987911303099)
XLA Ops:
  0.6 0.7 broadcast_subtract_fusion.local_ref
  1.3 4.0 %copy-done.4 = bf16[1280,4096]{1,0:T(8,128)(2,1)S(1)} copy-done((bf16[1280,4096]{1,0:T(8,128)(2,1)S(1)}, bf16[1280,4096]{1,0:T(8,128)(2,1)}, u32[]{:S(2)}) %copy-start.4) | copy-done | bytes 10485784
  5.3 0.7 copy-done.5
  6.0 8.6 %shard_map.59 = (bf16[1280,4096]{1,0:T(8,128)(2,1)S(1)}, f32[10,128]{1,0:T(8,128)S(1)}, bf16[32,64,128]{2,1,0:T(8,128)(2,1)}) custom-call(s32[63]{0:T(128)S(1)} %broadcast_subtract_fusion.local_ref, f32[1,4096]{1,0:T(1,128)S(1)} %bitcast.13, bf16[1280,4096]{1,0:T(8,128)(2,1)S(1)} %copy-done.4), custom_call_target="tpu_custom_call" | custom-call | bytes 14400000 | tf_op jit(solution)/shard_map/pallas_call | solution.py:28
  14.6 4.0 %copy-done = bf16[1280,4096]{1,0:T(8,128)(2,1)} copy-done((bf16[1280,4096]{1,0:T(8,128)(2,1)}, bf16[1280,4096]{1,0:T(8,128)(2,1)S(1)}, u32[]{:S(2)}) %copy-start) | copy-done | bytes 10485784
  18.6 11.9 %all-to-all-start = ((bf16[32,64,128]{2,1,0:T(8,128)(2,1)}), bf16[32,64,128]{2,1,0:T(8,128)(2,1)S(1)}, u32[]{:S(2)}, u32[]{:S(2)}) async-start(bf16[32,64,128]{2,1,0:T(8,128)(2,1)} %get-tuple-element.28), calls=%async_computation | async-start | bytes 1048576 | tf_op jit(solution)/shard_map/all_to_all | solution.py:358
  30.5 1.0 collective-permute-start
  31.6 0.8 collective-permute-done
  32.4 2.7 %collective-permute-start.3 = (f32[10,128]{1,0:T(8,128)S(1)}, f32[10,128]{1,0:T(8,128)S(1)}, u32[]{:S(2)}, u32[]{:S(2)}) collective-permute-start(f32[10,128]{1,0:T(8,128)S(1)} %add.7.own), channel_id=1, source_target_pairs={{0,6},{1,7},{2,0},{3,1},{4,2},{5,3},{6,4},{7,5},{8,14},{9,15},{10,... | collective-permute-start | bytes 15368 | tf_op jit(solution)/shard_map/ppermute | solution.py:46
  35.1 0.3 collective-permute-start.2
  35.5 0.7 collective-permute-start.1
  36.2 3.3 %collective-permute-done.2.two = f32[10,128]{1,0:T(8,128)S(1)} collective-permute-done((f32[10,128]{1,0:T(8,128)S(1)}, f32[10,128]{1,0:T(8,128)S(1)}, u32[]{:S(2)}, u32[]{:S(2)}) %collective-permute-start.2) | collective-permute-done | bytes 5152 | tf_op jit(solution)/shard_map/ppermute | solution.py:46
  39.5 4.0 %copy-done.1 = bf16[1280,4096]{1,0:T(8,128)(2,1)S(1)} copy-done((bf16[1280,4096]{1,0:T(8,128)(2,1)S(1)}, bf16[1280,4096]{1,0:T(8,128)(2,1)}, u32[]{:S(2)}) %copy-start.1) | copy-done | bytes 10485784
  43.5 1.5 shard_map.60
  45.0 0.1 shard_map.61
  45.1 15.7 %all_to_all.25.in_ref = bf16[8,128,128]{2,1,0:T(8,128)(2,1)S(1)} all-to-all(bf16[8,128,128]{2,1,0:T(8,128)(2,1)S(1)} %shard_map.61), channel_id=1, replica_groups={{0,8,16,24,32,40,48,56},{64,72,80,88,96,104,112,120},{128,136,144,152,1..., dimensions={0} | all-to-all | bytes 524288 | tf_op jit(solution)/shard_map/all_to_all | solution.py:55
  60.8 2.5 %collective-permute-start.6 = (bf16[576,128]{1,0:T(8,128)(2,1)S(1)}, bf16[576,128]{1,0:T(8,128)(2,1)S(1)}, u32[]{:S(2)}, u32[]{:S(2)}) collective-permute-start(bf16[576,128]{1,0:T(8,128)(2,1)S(1)} %shard_map.62.own), channel_id=1, source_target_pairs={{0,192},{8,200},{16,208},{24,216},{32,224},{40,232},{48,240},{56,2... | collective-permute-start | bytes 442376 | tf_op jit(solution)/shard_map/ppermute | solution.py:41
  63.3 0.5 collective-permute-start.5
  63.8 0.6 collective-permute-start.4
  64.5 2.5 %collective-permute-done.6.three = bf16[576,128]{1,0:T(8,128)(2,1)S(1)} collective-permute-done((bf16[576,128]{1,0:T(8,128)(2,1)S(1)}, bf16[576,128]{1,0:T(8,128)(2,1)S(1)}, u32[]{:S(2)}, u32[]{:S(2)}) %collective-permute-start.6) | collective-permute-done | bytes 147488 | tf_op jit(solution)/shard_map/ppermute | solution.py:41
  67.0 1.9 %collective-permute-done.5.two = bf16[576,128]{1,0:T(8,128)(2,1)S(1)} collective-permute-done((bf16[576,128]{1,0:T(8,128)(2,1)S(1)}, bf16[576,128]{1,0:T(8,128)(2,1)S(1)}, u32[]{:S(2)}, u32[]{:S(2)}) %collective-permute-start.5) | collective-permute-done | bytes 147488 | tf_op jit(solution)/shard_map/ppermute | solution.py:41
  68.9 1.5 collective-permute-done.4.one
  70.4 4.0 %copy-done.2 = bf16[1280,4096]{1,0:T(8,128)(2,1)S(1)} copy-done((bf16[1280,4096]{1,0:T(8,128)(2,1)S(1)}, bf16[1280,4096]{1,0:T(8,128)(2,1)}, u32[]{:S(2)}) %copy-start.2) | copy-done | bytes 10485784
  74.4 3.6 %shard_map.63 = (bf16[128,4096]{1,0:T(8,128)(2,1)S(1)}, f32[32,128]{1,0:T(8,128)S(1)}, f32[72,640]{1,0:T(8,128)S(1)}, f32[72,640]{1,0:T(8,128)S(1)}) custom-call(s32[3]{0:T(128)S(1)} %pad_add_fusion.idx_ref, bf16[1280,4096]{1,0:T(8,128)(2,1)S(1)} %copy-done.2, f32[32,128]{1,0:T(8,128)S(1)} %bitcast.14, bf16[576,128]{1,0:T(8,128)(2,1)S(1)} %shard_map.62.own, ...), custom_call_target="tpu_custom_call" | custom-call | bytes 10800000 | tf_op jit(solution)/shard_map/pallas_call | solution.py:28
  78.0 5.2 %collective-permute-start.7 = (f32[72,640]{1,0:T(8,128)S(1)}, f32[72,640]{1,0:T(8,128)S(1)}, u32[]{:S(2)}, u32[]{:S(2)}) collective-permute-start(f32[72,640]{1,0:T(8,128)S(1)} %get-tuple-element.34), channel_id=1, source_target_pairs={{0,1},{1,0},{2,3},{3,2},{4,5},{5,4},{6,7},{7,6},{8,9},{9,8},{10,11... | collective-permute-start | bytes 552968 | tf_op jit(solution)/shard_map/ppermute | solution.py:50
  83.2 1.1 collective-permute-done.7.other
  84.3 0.7 collective-permute-start.10
  85.0 1.1 collective-permute-start.9
  86.1 0.8 collective-permute-start.8
  86.8 1.8 %collective-permute-done.10.three = bf16[80,640]{1,0:T(8,128)(2,1)S(1)} collective-permute-done((bf16[80,640]{1,0:T(8,128)(2,1)S(1)}, bf16[80,640]{1,0:T(8,128)(2,1)S(1)}, u32[]{:S(2)}, u32[]{:S(2)}) %collective-permute-start.10) | collective-permute-done | bytes 102432 | tf_op jit(solution)/shard_map/ppermute | solution.py:46
  88.6 1.4 collective-permute-done.9.two
  90.0 3.4 %collective-permute-done.8.one = bf16[80,640]{1,0:T(8,128)(2,1)S(1)} collective-permute-done((bf16[80,640]{1,0:T(8,128)(2,1)S(1)}, bf16[80,640]{1,0:T(8,128)(2,1)S(1)}, u32[]{:S(2)}, u32[]{:S(2)}) %collective-permute-start.8) | collective-permute-done | bytes 102432 | tf_op jit(solution)/shard_map/ppermute | solution.py:46
  93.4 0.7 collective-permute-start.11
  94.1 1.0 collective-permute-done.11.theirs_ref
  95.2 4.0 %copy-done.3 = bf16[1280,4096]{1,0:T(8,128)(2,1)S(1)} copy-done((bf16[1280,4096]{1,0:T(8,128)(2,1)S(1)}, bf16[1280,4096]{1,0:T(8,128)(2,1)}, u32[]{:S(2)}) %copy-start.3) | copy-done | bytes 10485784
  99.1 2.5 %shard_map.66 = (f32[512,128]{1,0:T(8,128)S(1)}, f32[8,128]{1,0:T(8,128)S(1)}, bf16[528,128]{1,0:T(8,128)(2,1)S(1)}, bf16[528,128]{1,0:T(8,128)(2,1)S(1)}, bf16[528,128]{1,0:T(8,128)(2,1)S(1)}) custom-call(s32[3]{0:T(128)S(1)} %pad_add_fusion.idx_ref, bf16[1280,4096]{1,0:T(8,128)(2,1)S(1)} %copy-done.3, f32[64,640]{1,0:T(8,128)S(1)} %get-tuple-element.35.mine_ref.scores_ref, ...), custom_call_target="tpu_custom_call" | custom-call | bytes 10800000 | tf_op jit(solution)/shard_map/pallas_call | solution.py:28
  101.7 1.5 collective-permute-start.13
  103.2 1.7 collective-permute-start.14
  104.9 5.7 %collective-permute-done.12.one = bf16[528,128]{1,0:T(8,128)(2,1)S(1)} collective-permute-done((bf16[528,128]{1,0:T(8,128)(2,1)S(1)}, bf16[528,128]{1,0:T(8,128)(2,1)S(1)}, u32[]{:S(2)}, u32[]{:S(2)}) %collective-permute-start.12) | collective-permute-done | bytes 135200 | tf_op jit(solution)/shard_map/ppermute | solution.py:401
  110.6 0.3 collective-permute-done.14.three
  110.9 0.1 shard_map.67
  111.0 10.6 %all_to_all.26.in_ref = bf16[8,72,128]{2,1,0:T(8,128)(2,1)S(1)} all-to-all(bf16[8,72,128]{2,1,0:T(8,128)(2,1)S(1)} %shard_map.67), channel_id=1, replica_groups={{0,8,16,24,32,40,48,56},{64,72,80,88,96,104,112,120},{128,136,144,152,1..., dimensions={0} | all-to-all | bytes 294912 | tf_op jit(solution)/shard_map/all_to_all | solution.py:55
  121.6 0.7 shard_map.68
  122.2 10.6 %all_to_all.27.own = bf16[8,72,128]{2,1,0:T(8,128)(2,1)S(1)} all-to-all(bf16[8,72,128]{2,1,0:T(8,128)(2,1)S(1)} %get-tuple-element.43), channel_id=1, replica_groups={{0,8,16,24,32,40,48,56},{64,72,80,88,96,104,112,120},{128,136,144,152,1..., dimensions={0} | all-to-all | bytes 294912 | tf_op jit(solution)/shard_map/all_to_all | solution.py:55
  132.8 3.6 %collective-permute-start.17 = (bf16[8,72,128]{2,1,0:T(8,128)(2,1)S(1)}, bf16[8,72,128]{2,1,0:T(8,128)(2,1)S(1)}, u32[]{:S(2)}, u32[]{:S(2)}) collective-permute-start(bf16[8,72,128]{2,1,0:T(8,128)(2,1)S(1)} %all_to_all.27.own), channel_id=1, source_target_pairs={{0,192},{8,200},{16,208},{24,216},{32,224},{40,232},{48,240},{56,2... | collective-permute-start | bytes 442376 | tf_op jit(solution)/shard_map/ppermute | solution.py:41
  136.5 0.6 collective-permute-start.15
  137.0 3.1 %collective-permute-done.17.three = bf16[8,72,128]{2,1,0:T(8,128)(2,1)S(1)} collective-permute-done((bf16[8,72,128]{2,1,0:T(8,128)(2,1)S(1)}, bf16[8,72,128]{2,1,0:T(8,128)(2,1)S(1)}, u32[]{:S(2)}, u32[]{:S(2)}) %collective-permute-start.17) | collective-permute-done | bytes 147488 | tf_op jit(solution)/shard_map/ppermute | solution.py:41
  140.1 1.9 %collective-permute-done.16.two = bf16[8,72,128]{2,1,0:T(8,128)(2,1)S(1)} collective-permute-done((bf16[8,72,128]{2,1,0:T(8,128)(2,1)S(1)}, bf16[8,72,128]{2,1,0:T(8,128)(2,1)S(1)}, u32[]{:S(2)}, u32[]{:S(2)}) %collective-permute-start.16) | collective-permute-done | bytes 147488 | tf_op jit(solution)/shard_map/ppermute | solution.py:41
  142.1 1.2 collective-permute-done.15.one
  143.3 3.8 %shard_map.69 = (f32[72,640]{1,0:T(8,128)S(1)}, f32[72,640]{1,0:T(8,128)S(1)}, f32[32,128]{1,0:T(8,128)S(1)}) custom-call(s32[3]{0:T(128)S(1)} %pad_add_fusion.idx_ref, bf16[1280,4096]{1,0:T(8,128)(2,1)S(1)} %bitcast.12, bf16[128,4096]{1,0:T(8,128)(2,1)S(1)} %get-tuple-element.31.rhs_ref, f32[32,128]{1,0:T(8,128)S(1)} %get-tuple-element.32.grad_ref, ...), custom_call_target="tpu_custom_call" | custom-call | bytes 10800000 | tf_op jit(solution)/shard_map/pallas_call | solution.py:28
  147.0 4.5 %collective-permute-start.18 = (f32[72,640]{1,0:T(8,128)S(1)}, f32[72,640]{1,0:T(8,128)S(1)}, u32[]{:S(2)}, u32[]{:S(2)}) collective-permute-start(f32[72,640]{1,0:T(8,128)S(1)} %get-tuple-element.45), channel_id=1, source_target_pairs={{0,1},{1,0},{2,3},{3,2},{4,5},{5,4},{6,7},{7,6},{8,9},{9,8},{10,11... | collective-permute-start | bytes 552968 | tf_op jit(solution)/shard_map/ppermute | solution.py:50
  151.6 1.1 collective-permute-done.18.other
  152.7 0.5 collective-permute-start.21
  153.1 0.3 collective-permute-start.20
  153.4 0.8 collective-permute-start.19
  154.2 2.6 %collective-permute-done.21.three = bf16[80,640]{1,0:T(8,128)(2,1)S(1)} collective-permute-done((bf16[80,640]{1,0:T(8,128)(2,1)S(1)}, bf16[80,640]{1,0:T(8,128)(2,1)S(1)}, u32[]{:S(2)}, u32[]{:S(2)}) %collective-permute-start.21) | collective-permute-done | bytes 102432 | tf_op jit(solution)/shard_map/ppermute | solution.py:46
  156.8 1.4 collective-permute-done.20.two
  158.2 3.4 %collective-permute-done.19.one = bf16[80,640]{1,0:T(8,128)(2,1)S(1)} collective-permute-done((bf16[80,640]{1,0:T(8,128)(2,1)S(1)}, bf16[80,640]{1,0:T(8,128)(2,1)S(1)}, u32[]{:S(2)}, u32[]{:S(2)}) %collective-permute-start.19) | collective-permute-done | bytes 102432 | tf_op jit(solution)/shard_map/ppermute | solution.py:46
  161.7 0.7 shard_map.71
  162.4 0.6 collective-permute-start.22
  162.9 0.8 collective-permute-done.22
  163.8 11.6 %all_to_all.28.tails_ref = f32[32,1,128]{2,1,0:T(1,128)S(1)} all-to-all(f32[32,1,128]{2,1,0:T(1,128)S(1)} %broadcast_in_dim.9), channel_id=1, replica_groups=mesh['event'=32,'feat'=8] {'event'}, dimensions={0} | all-to-all | bytes 32768 | tf_op jit(solution)/shard_map/all_to_all | solution.py:430
  175.4 0.8 shard_map.72
  176.2 0.5 slice_bitcast_fusion
  (31 shorter events, 0.5 us)
Async XLA Ops:
  0.6 38.9 %copy-start.7 = (s32[1280]{0:T(1024)S(1)}, s32[1280]{0:T(1024)}, u32[]{:S(2)}) copy-start(s32[1280]{0:T(1024)} %param.5) | copy-start | bytes 15364
  1.3 4.0 %copy-start.4 = (bf16[1280,4096]{1,0:T(8,128)(2,1)S(1)}, bf16[1280,4096]{1,0:T(8,128)(2,1)}, u32[]{:S(2)}) copy-start(bf16[1280,4096]{1,0:T(8,128)(2,1)} %events_ref.1) | copy-start | bytes 31457284
  5.3 0.7 copy-start.5
  6.0 64.4 %copy-start.6 = (f32[4096]{0:T(1024)S(1)}, f32[4096]{0:T(1024)}, u32[]{:S(2)}) copy-start(f32[4096]{0:T(1024)} %param.6) | copy-start | bytes 49156
  14.6 4.0 %copy-start = (bf16[1280,4096]{1,0:T(8,128)(2,1)}, bf16[1280,4096]{1,0:T(8,128)(2,1)S(1)}, u32[]{:S(2)}) copy-start(bf16[1280,4096]{1,0:T(8,128)(2,1)S(1)} %get-tuple-element.27.held_ref) | copy-start | bytes 31457284
  18.6 26.4 %all-to-all-start = ((bf16[32,64,128]{2,1,0:T(8,128)(2,1)}), bf16[32,64,128]{2,1,0:T(8,128)(2,1)S(1)}, u32[]{:S(2)}, u32[]{:S(2)}) async-start(bf16[32,64,128]{2,1,0:T(8,128)(2,1)} %get-tuple-element.28), calls=%async_computation | async-start | bytes 1048576 | tf_op jit(solution)/shard_map/all_to_all | solution.py:358
  30.5 1.9 %collective-permute-start = (f32[10,128]{1,0:T(8,128)S(1)}, f32[10,128]{1,0:T(8,128)S(1)}, u32[]{:S(2)}, u32[]{:S(2)}) collective-permute-start(f32[10,128]{1,0:T(8,128)S(1)} %get-tuple-element.29), channel_id=1, source_target_pairs={{0,1},{1,0},{2,3},{3,2},{4,5},{5,4},{6,7},{7,6},{8,9},{9,8},{10,11... | collective-permute-start | bytes 15368 | tf_op jit(solution)/shard_map/ppermute | solution.py:50
  32.4 3.8 %collective-permute-start.3 = (f32[10,128]{1,0:T(8,128)S(1)}, f32[10,128]{1,0:T(8,128)S(1)}, u32[]{:S(2)}, u32[]{:S(2)}) collective-permute-start(f32[10,128]{1,0:T(8,128)S(1)} %add.7.own), channel_id=1, source_target_pairs={{0,6},{1,7},{2,0},{3,1},{4,2},{5,3},{6,4},{7,5},{8,14},{9,15},{10,... | collective-permute-start | bytes 15368 | tf_op jit(solution)/shard_map/ppermute | solution.py:46
  35.1 4.3 %collective-permute-start.2 = (f32[10,128]{1,0:T(8,128)S(1)}, f32[10,128]{1,0:T(8,128)S(1)}, u32[]{:S(2)}, u32[]{:S(2)}) collective-permute-start(f32[10,128]{1,0:T(8,128)S(1)} %add.7.own), channel_id=1, source_target_pairs={{0,4},{1,5},{2,6},{3,7},{4,0},{5,1},{6,2},{7,3},{8,12},{9,13},{10,... | collective-permute-start | bytes 15368 | tf_op jit(solution)/shard_map/ppermute | solution.py:46
  35.5 4.0 %collective-permute-start.1 = (f32[10,128]{1,0:T(8,128)S(1)}, f32[10,128]{1,0:T(8,128)S(1)}, u32[]{:S(2)}, u32[]{:S(2)}) collective-permute-start(f32[10,128]{1,0:T(8,128)S(1)} %add.7.own), channel_id=1, source_target_pairs={{0,2},{1,3},{2,4},{3,5},{4,6},{5,7},{6,0},{7,1},{8,10},{9,11},{10,... | collective-permute-start | bytes 15368 | tf_op jit(solution)/shard_map/ppermute | solution.py:46
  39.5 4.0 %copy-start.1 = (bf16[1280,4096]{1,0:T(8,128)(2,1)S(1)}, bf16[1280,4096]{1,0:T(8,128)(2,1)}, u32[]{:S(2)}) copy-start(bf16[1280,4096]{1,0:T(8,128)(2,1)} %copy-done) | copy-start | bytes 31457284
  43.5 99.7 %slice-start = ((s8[10485760]{0:T(1024)(128)(4,1)}), s8[2097152]{0:T(1024)(128)(4,1)S(1)}, s32[]{:S(2)}) async-start(s8[10485760]{0:T(1024)(128)(4,1)} %bitcast.11), calls=%async_computation.5 | async-start | bytes 4194304
  60.8 6.2 %collective-permute-start.6 = (bf16[576,128]{1,0:T(8,128)(2,1)S(1)}, bf16[576,128]{1,0:T(8,128)(2,1)S(1)}, u32[]{:S(2)}, u32[]{:S(2)}) collective-permute-start(bf16[576,128]{1,0:T(8,128)(2,1)S(1)} %shard_map.62.own), channel_id=1, source_target_pairs={{0,192},{8,200},{16,208},{24,216},{32,224},{40,232},{48,240},{56,2... | collective-permute-start | bytes 442376 | tf_op jit(solution)/shard_map/ppermute | solution.py:41
  63.3 5.6 %collective-permute-start.5 = (bf16[576,128]{1,0:T(8,128)(2,1)S(1)}, bf16[576,128]{1,0:T(8,128)(2,1)S(1)}, u32[]{:S(2)}, u32[]{:S(2)}) collective-permute-start(bf16[576,128]{1,0:T(8,128)(2,1)S(1)} %shard_map.62.own), channel_id=1, source_target_pairs={{0,128},{8,136},{16,144},{24,152},{32,160},{40,168},{48,176},{56,1... | collective-permute-start | bytes 442376 | tf_op jit(solution)/shard_map/ppermute | solution.py:41
  63.8 6.6 %collective-permute-start.4 = (bf16[576,128]{1,0:T(8,128)(2,1)S(1)}, bf16[576,128]{1,0:T(8,128)(2,1)S(1)}, u32[]{:S(2)}, u32[]{:S(2)}) collective-permute-start(bf16[576,128]{1,0:T(8,128)(2,1)S(1)} %shard_map.62.own), channel_id=1, source_target_pairs={{0,64},{8,72},{16,80},{24,88},{32,96},{40,104},{48,112},{56,120},{... | collective-permute-start | bytes 442376 | tf_op jit(solution)/shard_map/ppermute | solution.py:41
  70.4 4.0 %copy-start.2 = (bf16[1280,4096]{1,0:T(8,128)(2,1)S(1)}, bf16[1280,4096]{1,0:T(8,128)(2,1)}, u32[]{:S(2)}) copy-start(bf16[1280,4096]{1,0:T(8,128)(2,1)} %copy-done) | copy-start | bytes 31457284
  74.4 68.8 %slice-start.1 = ((s8[10485760]{0:T(1024)(128)(4,1)}), s8[4194304]{0:T(1024)(128)(4,1)S(1)}, s32[]{:S(2)}) async-start(s8[10485760]{0:T(1024)(128)(4,1)} %bitcast.11), calls=%async_computation.6 | async-start | bytes 8388608
  78.0 6.2 %collective-permute-start.7 = (f32[72,640]{1,0:T(8,128)S(1)}, f32[72,640]{1,0:T(8,128)S(1)}, u32[]{:S(2)}, u32[]{:S(2)}) collective-permute-start(f32[72,640]{1,0:T(8,128)S(1)} %get-tuple-element.34), channel_id=1, source_target_pairs={{0,1},{1,0},{2,3},{3,2},{4,5},{5,4},{6,7},{7,6},{8,9},{9,8},{10,11... | collective-permute-start | bytes 552968 | tf_op jit(solution)/shard_map/ppermute | solution.py:50
  84.3 4.4 %collective-permute-start.10 = (bf16[80,640]{1,0:T(8,128)(2,1)S(1)}, bf16[80,640]{1,0:T(8,128)(2,1)S(1)}, u32[]{:S(2)}, u32[]{:S(2)}) collective-permute-start(bf16[80,640]{1,0:T(8,128)(2,1)S(1)} %shard_map.64.own), channel_id=1, source_target_pairs={{0,6},{1,7},{2,0},{3,1},{4,2},{5,3},{6,4},{7,5},{8,14},{9,15},{10,... | collective-permute-start | bytes 307208 | tf_op jit(solution)/shard_map/ppermute | solution.py:46
  85.0 5.0 %collective-permute-start.9 = (bf16[80,640]{1,0:T(8,128)(2,1)S(1)}, bf16[80,640]{1,0:T(8,128)(2,1)S(1)}, u32[]{:S(2)}, u32[]{:S(2)}) collective-permute-start(bf16[80,640]{1,0:T(8,128)(2,1)S(1)} %shard_map.64.own), channel_id=1, source_target_pairs={{0,4},{1,5},{2,6},{3,7},{4,0},{5,1},{6,2},{7,3},{8,12},{9,13},{10,... | collective-permute-start | bytes 307208 | tf_op jit(solution)/shard_map/ppermute | solution.py:46
  86.1 7.3 %collective-permute-start.8 = (bf16[80,640]{1,0:T(8,128)(2,1)S(1)}, bf16[80,640]{1,0:T(8,128)(2,1)S(1)}, u32[]{:S(2)}, u32[]{:S(2)}) collective-permute-start(bf16[80,640]{1,0:T(8,128)(2,1)S(1)} %shard_map.64.own), channel_id=1, source_target_pairs={{0,2},{1,3},{2,4},{3,5},{4,6},{5,7},{6,0},{7,1},{8,10},{9,11},{10,... | collective-permute-start | bytes 307208 | tf_op jit(solution)/shard_map/ppermute | solution.py:46
  93.4 1.7 collective-permute-start.11
  95.1 4.0 %copy-start.3 = (bf16[1280,4096]{1,0:T(8,128)(2,1)S(1)}, bf16[1280,4096]{1,0:T(8,128)(2,1)}, u32[]{:S(2)}) copy-start(bf16[1280,4096]{1,0:T(8,128)(2,1)} %copy-done) | copy-start | bytes 31457284
  99.1 44.1 %slice-start.2 = ((s8[10485760]{0:T(1024)(128)(4,1)}), s8[4194304]{0:T(1024)(128)(4,1)S(1)}, s32[]{:S(2)}) async-start(s8[10485760]{0:T(1024)(128)(4,1)} %bitcast.11), calls=%async_computation.7 | async-start | bytes 8388608
  101.6 9.0 %collective-permute-start.12 = (bf16[528,128]{1,0:T(8,128)(2,1)S(1)}, bf16[528,128]{1,0:T(8,128)(2,1)S(1)}, u32[]{:S(2)}, u32[]{:S(2)}) collective-permute-start(bf16[528,128]{1,0:T(8,128)(2,1)S(1)} %get-tuple-element.39), channel_id=1, source_target_pairs={{0,64},{8,72},{16,80},{24,88},{32,96},{40,104},{48,112},{56,120},{... | collective-permute-start | bytes 405512 | tf_op jit(solution)/shard_map/ppermute | solution.py:401
  101.7 8.9 %collective-permute-start.13 = (bf16[528,128]{1,0:T(8,128)(2,1)S(1)}, bf16[528,128]{1,0:T(8,128)(2,1)S(1)}, u32[]{:S(2)}, u32[]{:S(2)}) collective-permute-start(bf16[528,128]{1,0:T(8,128)(2,1)S(1)} %get-tuple-element.40), channel_id=1, source_target_pairs={{0,128},{8,136},{16,144},{24,152},{32,160},{40,168},{48,176},{56,1... | collective-permute-start | bytes 405512 | tf_op jit(solution)/shard_map/ppermute | solution.py:401
  103.2 7.7 %collective-permute-start.14 = (bf16[528,128]{1,0:T(8,128)(2,1)S(1)}, bf16[528,128]{1,0:T(8,128)(2,1)S(1)}, u32[]{:S(2)}, u32[]{:S(2)}) collective-permute-start(bf16[528,128]{1,0:T(8,128)(2,1)S(1)} %get-tuple-element.41), channel_id=1, source_target_pairs={{0,192},{8,200},{16,208},{24,216},{32,224},{40,232},{48,240},{56,2... | collective-permute-start | bytes 405512 | tf_op jit(solution)/shard_map/ppermute | solution.py:401
  132.8 7.3 %collective-permute-start.17 = (bf16[8,72,128]{2,1,0:T(8,128)(2,1)S(1)}, bf16[8,72,128]{2,1,0:T(8,128)(2,1)S(1)}, u32[]{:S(2)}, u32[]{:S(2)}) collective-permute-start(bf16[8,72,128]{2,1,0:T(8,128)(2,1)S(1)} %all_to_all.27.own), channel_id=1, source_target_pairs={{0,192},{8,200},{16,208},{24,216},{32,224},{40,232},{48,240},{56,2... | collective-permute-start | bytes 442376 | tf_op jit(solution)/shard_map/ppermute | solution.py:41
  136.5 5.6 %collective-permute-start.16 = (bf16[8,72,128]{2,1,0:T(8,128)(2,1)S(1)}, bf16[8,72,128]{2,1,0:T(8,128)(2,1)S(1)}, u32[]{:S(2)}, u32[]{:S(2)}) collective-permute-start(bf16[8,72,128]{2,1,0:T(8,128)(2,1)S(1)} %all_to_all.27.own), channel_id=1, source_target_pairs={{0,128},{8,136},{16,144},{24,152},{32,160},{40,168},{48,176},{56,1... | collective-permute-start | bytes 442376 | tf_op jit(solution)/shard_map/ppermute | solution.py:41
  136.5 6.8 %collective-permute-start.15 = (bf16[8,72,128]{2,1,0:T(8,128)(2,1)S(1)}, bf16[8,72,128]{2,1,0:T(8,128)(2,1)S(1)}, u32[]{:S(2)}, u32[]{:S(2)}) collective-permute-start(bf16[8,72,128]{2,1,0:T(8,128)(2,1)S(1)} %all_to_all.27.own), channel_id=1, source_target_pairs={{0,64},{8,72},{16,80},{24,88},{32,96},{40,104},{48,112},{56,120},{... | collective-permute-start | bytes 442376 | tf_op jit(solution)/shard_map/ppermute | solution.py:41
  147.0 5.6 %collective-permute-start.18 = (f32[72,640]{1,0:T(8,128)S(1)}, f32[72,640]{1,0:T(8,128)S(1)}, u32[]{:S(2)}, u32[]{:S(2)}) collective-permute-start(f32[72,640]{1,0:T(8,128)S(1)} %get-tuple-element.45), channel_id=1, source_target_pairs={{0,1},{1,0},{2,3},{3,2},{4,5},{5,4},{6,7},{7,6},{8,9},{9,8},{10,11... | collective-permute-start | bytes 552968 | tf_op jit(solution)/shard_map/ppermute | solution.py:50
  152.7 4.2 %collective-permute-start.21 = (bf16[80,640]{1,0:T(8,128)(2,1)S(1)}, bf16[80,640]{1,0:T(8,128)(2,1)S(1)}, u32[]{:S(2)}, u32[]{:S(2)}) collective-permute-start(bf16[80,640]{1,0:T(8,128)(2,1)S(1)} %shard_map.70.own), channel_id=1, source_target_pairs={{0,6},{1,7},{2,0},{3,1},{4,2},{5,3},{6,4},{7,5},{8,14},{9,15},{10,... | collective-permute-start | bytes 307208 | tf_op jit(solution)/shard_map/ppermute | solution.py:46
  153.1 5.1 %collective-permute-start.20 = (bf16[80,640]{1,0:T(8,128)(2,1)S(1)}, bf16[80,640]{1,0:T(8,128)(2,1)S(1)}, u32[]{:S(2)}, u32[]{:S(2)}) collective-permute-start(bf16[80,640]{1,0:T(8,128)(2,1)S(1)} %shard_map.70.own), channel_id=1, source_target_pairs={{0,4},{1,5},{2,6},{3,7},{4,0},{5,1},{6,2},{7,3},{8,12},{9,13},{10,... | collective-permute-start | bytes 307208 | tf_op jit(solution)/shard_map/ppermute | solution.py:46
  153.4 8.2 %collective-permute-start.19 = (bf16[80,640]{1,0:T(8,128)(2,1)S(1)}, bf16[80,640]{1,0:T(8,128)(2,1)S(1)}, u32[]{:S(2)}, u32[]{:S(2)}) collective-permute-start(bf16[80,640]{1,0:T(8,128)(2,1)S(1)} %shard_map.70.own), channel_id=1, source_target_pairs={{0,2},{1,3},{2,4},{3,5},{4,6},{5,7},{6,0},{7,1},{8,10},{9,11},{10,... | collective-permute-start | bytes 307208 | tf_op jit(solution)/shard_map/ppermute | solution.py:46
  162.4 1.4 collective-permute-start.22

commit v2 on v1

--- a/solution.py
+++ b/solution.py
@@ -13,6 +13,7 @@
 QUARTER = TILES // XN
 COUNT = 1280
 HALF = COUNT // 2
+ROOM = 48
 F32, BF16 = jnp.float32, jnp.bfloat16
 VMEM = pl.BlockSpec(memory_space=pltpu.VMEM)
 SMEM = pl.BlockSpec(memory_space=pltpu.SMEM)
@@ -24,14 +25,14 @@
     return jax.ShapeDtypeStruct(shape, dtype)
 
 
-def kernel_call(body, ins, outs, args, scratch=(), micros=0.5):
+def kernel_call(body, ins, outs, args, scratch=(), micros=0.5, room=8):
     return pl.pallas_call(
         body,
         out_shape=outs,
         in_specs=ins,
         out_specs=[VMEM] * len(outs),
         scratch_shapes=list(scratch),
-        compiler_params=pltpu.CompilerParams(vmem_limit_bytes=28 << 20),
+        compiler_params=pltpu.CompilerParams(vmem_limit_bytes=room << 20),
         cost_estimate=pl.CostEstimate(flops=0, bytes_accessed=int(micros * 3.6e6), transcendentals=0),
     )(*args)
 
@@ -98,40 +99,58 @@
     return total
 
 
-def first_kernel(local_ref, w_ref, events_ref, held_ref, margin_ref, out_ref, rows, sems):
-    piece = COUNT // 5
-    copies = [
-        pltpu.make_async_copy(
-            events_ref.at[pl.ds(c * piece, piece), :], held_ref.at[pl.ds(c * piece, piece), :], sems.at[c]
-        )
-        for c in range(5)
-    ]
-    for copy in copies:
+def stream(events_ref, held, sems, starts, size, axis):
+    copies = []
+    for i, start in enumerate(starts):
+        start = pl.multiple_of(start, 128)
+        at = (pl.ds(start, size), slice(None)) if axis == 0 else (slice(None), pl.ds(start, size))
+        copies.append((pltpu.make_async_copy(events_ref.at[at], held.at[i], sems.at[i]), i))
+    for copy, _ in copies:
         copy.start()
+    return copies
+
+
+def pick_kernel(local_ref, events_ref, out_ref, blocks, rows, sems):
+    def owned(j):
+        return jnp.logical_and(local_ref[j] >= 0, local_ref[j] < COUNT)
+
+    def fetch(j):
+        start = pl.multiple_of(lax.div(local_ref[j], 16) * 16, 16)
+        return pltpu.make_async_copy(events_ref.at[pl.ds(start, 16), :], blocks.at[j], sems.at[j])
+
+    @pl.loop(0, ROWS - 1)
+    def _(j):
+        @pl.when(owned(j))
+        def _():
+            fetch(j).start()
+
     rows[...] = jnp.zeros_like(rows)
+
+    @pl.loop(0, ROWS - 1)
+    def _(j):
+        @pl.when(owned(j))
+        def _():
+            fetch(j).wait()
+            block = blocks[j].astype(F32)
+            found = jnp.where(row_is(block.shape, lax.rem(local_ref[j], 16)), block, 0.0)
+            rows[pl.ds(j, 1), :] = jnp.sum(found, axis=0, keepdims=True)
+
+    for t in range(TILES):
+        out_ref[t] = rows[:, t * 128 : (t + 1) * 128].astype(BF16)
+
+
+def margin_kernel(w_ref, events_ref, _after, margin_ref, held, sems):
+    copies = stream(events_ref, held, sems, [c * 256 for c in range(5)], 256, 0)
     w = jnp.broadcast_to(w_ref[...], (16, TILES * 128)).astype(BF16)
-    for c, copy in enumerate(copies):
+    for copy, c in copies:
         copy.wait()
-        part = lax.dot_general(w, held_ref[c * piece : (c + 1) * piece, :], ACROSS, preferred_element_type=F32)
+        part = lax.dot_general(w, held[c], ACROSS, preferred_element_type=F32)
         margin_ref[2 * c : 2 * c + 1, :] = part[:1, :128]
         margin_ref[2 * c + 1 : 2 * c + 2, :] = part[:1, 128:]
 
-    @pl.loop(0, ROWS - 1)
-    def _(j):
-        r = local_ref[j]
-
-        @pl.when(jnp.logical_and(r >= 0, r < COUNT))
-        def _():
-            start = pl.multiple_of(lax.div(r, 16) * 16, 16)
-            block = held_ref[pl.ds(start, 16), :].astype(F32)
-            found = jnp.where(row_is(block.shape, lax.rem(r, 16)), block, 0.0)
-            rows[pl.ds(j, 1), :] = jnp.sum(found, axis=0, keepdims=True)
-
-    for t in range(TILES):
-        out_ref[t] = rows[:, t * 128 : (t + 1) * 128].astype(BF16)
-
-
-def gradient_kernel(held_ref, own, one, two, three, labels_ref, rate_ref, grad_ref, errs):
+
+def gradient_kernel(events_ref, own, one, two, three, labels_ref, rate_ref, grad_ref, errs, held, sems):
+    copies = stream(events_ref, held, sems, [c * 1024 for c in range(4)], 1024, 1)
     margin = four(own[...], one[...], two[...], three[...])
     chance = jax.nn.sigmoid(margin)
     rate = chance * (1.0 - chance)
@@ -142,11 +161,13 @@
         at = slice(i * 128, (i + 1) * 128)
         rate_ref[:, at] = rate[i : i + 1]
         errs[:, at] = stacked([lead[i : i + 1], rest[i : i + 1]], 16).astype(BF16)
-    for n in range(0, TILES, 4):
-        part = jnp.dot(errs[...], held_ref[:, n * 128 : (n + 4) * 128], preferred_element_type=F32)
+    for copy, c in copies:
+        copy.wait()
+        part = jnp.dot(errs[...], held[c], preferred_element_type=F32)
         line = part[:1] + part[1:2]
-        for u in range(4):
-            grad_ref[n + u : n + u + 1, :] = line[:, u * 128 : (u + 1) * 128]
+        for u in range(QUARTER):
+            at = c * QUARTER + u
+            grad_ref[at : at + 1, :] = line[:, u * 128 : (u + 1) * 128]
 
 
 def spread_kernel(chunks_ref, grad_ref, out_ref):
@@ -170,17 +191,38 @@
     out_ref[QUARTER * ROWS + TILES :, :] = rest
 
 
-def put_scores(held_ref, rhs, core, other_ref, own_ref, lines):
-    for half, out_ref in ((1 - core, other_ref), (core, own_ref)):
-        start = pl.multiple_of(half * HALF, HALF)
-        part = lax.dot_general(held_ref[pl.ds(start, HALF), :], rhs[...], ACROSS, preferred_element_type=F32)
-        for t in range(HALF // 128):
-            out_ref[:ROWS, t * 128 : (t + 1) * 128] = joined(jnp.transpose(part[t * 128 : (t + 1) * 128]))
-            out_ref[ROWS:, t * 128 : (t + 1) * 128] = lines if t == 0 else jnp.zeros_like(lines)
-
-
-def scores_kernel(idx_ref, held_ref, w_ref, own, one, two, three, rhs_ref, grad_ref, other_ref, mine_ref):
+def half_starts(core):
+    return [(half * HALF + first, size) for half in (1 - core, core) for first, size in ((0, 256), (256, 384))]
+
+
+def stream_halves(events_ref, held, sems, core):
+    copies = []
+    at = 0
+    for i, (start, size) in enumerate(half_starts(core)):
+        source = events_ref.at[pl.ds(pl.multiple_of(start, 128), size), :]
+        copies.append((pltpu.make_async_copy(source, held.at[pl.ds(at, size), :], sems.at[i]), at, size))
+        at += size
+    for copy, _, _ in copies:
+        copy.start()
+    return copies
+
+
+def put_scores(copies, held, rhs, other_ref, own_ref, lines):
+    for copy, at, size in copies:
+        copy.wait()
+        part = lax.dot_general(held[at : at + size, :], rhs[...], ACROSS, preferred_element_type=F32)
+        out_ref = other_ref if at < HALF else own_ref
+        for t in range(size // 128):
+            columns = slice(at % HALF + t * 128, at % HALF + (t + 1) * 128)
+            out_ref[:ROWS, columns] = joined(jnp.transpose(part[t * 128 : (t + 1) * 128]))
+            out_ref[ROWS:, columns] = lines if at % HALF + t == 0 else jnp.zeros_like(lines)
+
+
+def scores_kernel(
+    idx_ref, events_ref, w_ref, own, one, two, three, rhs_ref, grad_ref, other_ref, mine_ref, held, sems
+):
     x, core = idx_ref[0], idx_ref[2]
+    copies = stream_halves(events_ref, held, sems, core)
     top = QUARTER * ROWS
     grads = [p[top : top + TILES, :].astype(F32) + p[top + TILES :, :].astype(F32) for p in (own, one, two, three)]
     grad_ref[...] = four(*grads) + LAMBDA * w_ref[...]
@@ -200,7 +242,7 @@
             rhs_ref[:ROWS, at] = jnp.where(last, lead.astype(F32), values).astype(BF16)
             rhs_ref[ROWS : ROWS + 16, at] = stacked([rest], 16).astype(BF16)
     line = line_sums(norm, jnp.zeros_like(norm))
-    put_scores(held_ref, rhs_ref, core, other_ref, mine_ref, stacked([line], 8))
+    put_scores(copies, held, rhs_ref, other_ref, mine_ref, stacked([line], 8))
 
 
 def pack_kernel(own, other, out_ref):
@@ -225,8 +267,13 @@
     norm_ref[...] = stacked([norm], 8)
 
 
-def hessian_kernel(idx_ref, held_ref, mine_ref, theirs_ref, rate_ref, own_ref, curv_ref, one_ref, two_ref, three_ref, q):
+def hessian_kernel(
+    idx_ref, events_ref, mine_ref, theirs_ref, rate_ref, own_ref, curv_ref, one_ref, two_ref, three_ref, q, held, sems
+):
     x, core = idx_ref[0], idx_ref[2]
+    outs = ((2, two_ref), (1, one_ref), (3, three_ref), (0, own_ref))
+    width = QUARTER * 128
+    copies = stream(events_ref, held, sems, [lax.rem(x + k, XN) * width for k, _ in outs], width, 1)
     curv = jnp.zeros((ROWS, 128), F32)
     for half in range(2):
         scores = jnp.where(core == half, mine_ref[...], theirs_ref[...])
@@ -238,10 +285,9 @@
         q[ROWS:, at] = stacked([weighted[ROWS - 1 :] - lead[ROWS - 1 :].astype(F32)], 16).astype(BF16)
     triple = [v.astype(F32) for v in triple_of(line_sums(curv, jnp.zeros_like(curv)))]
     curv_ref[...] = stacked(triple, 8)
-    for k, out_ref in ((2, two_ref), (1, one_ref), (3, three_ref), (0, own_ref)):
-        quarter = lax.rem(x + k, XN)
-        columns = pl.ds(pl.multiple_of(quarter * QUARTER * 128, 128), QUARTER * 128)
-        total = joined(jnp.dot(q[...], held_ref[:, columns], preferred_element_type=F32))
+    for (copy, c), (k, out_ref) in zip(copies, outs, strict=True):
+        copy.wait()
+        total = joined(jnp.dot(q[...], held[c], preferred_element_type=F32))
         rests = []
         for t in range(QUARTER):
             values = total[:, t * 128 : (t + 1) * 128]
@@ -290,8 +336,11 @@
     scalars_ref[...] = stacked([step, curv, norm], 8)
 
 
-def second_kernel(idx_ref, held_ref, rhs_ref, grad_ref, own, one, two, three, other_ref, mine_ref, first_ref, res):
+def second_kernel(
+    idx_ref, events_ref, rhs_ref, grad_ref, own, one, two, three, other_ref, mine_ref, first_ref, res, held, sems
+):
     x, core = idx_ref[0], idx_ref[2]
+    copies = stream_halves(events_ref, held, sems, core)
     norm = jnp.zeros((ROWS, 128), F32)
     cross = jnp.zeros((ROWS, 128), F32)
     res[ROWS:, :] = jnp.zeros((128 - ROWS, TILES * 128), BF16)
@@ -311,7 +360,7 @@
             res[ROWS : ROWS + 16, at] = stacked([rows[ROWS:].astype(F32)[:1]], 16).astype(BF16)
     line = line_sums(norm, cross)
     lines = stacked([line, pltpu.roll(line, ROWS, 1)], 8)
-    put_scores(held_ref, res, core, other_ref, mine_ref, lines)
+    put_scores(copies, held, res, other_ref, mine_ref, lines)
 
 
 def tail_kernel(idx_ref, own, one, two, three, scores_ref, rate_ref, tail_ref, lines_ref):
@@ -347,24 +396,39 @@
     features = TILES * 128
     tiled = weights.reshape(TILES, 128)
 
-    held, margin, picked = kernel_call(
-        first_kernel,
-        [SMEM, VMEM, HBM],
-        [shaped(COUNT, features, dtype=BF16), shaped(COUNT // 128, 128), shaped(TILES, ROWS, 128, dtype=BF16)],
-        (contexts - place * COUNT, weights.reshape(1, features), events),
-        [pltpu.VMEM((ROWS, features), F32), pltpu.SemaphoreType.DMA((5,))],
+    (picked,) = kernel_call(
+        pick_kernel,
+        [SMEM, HBM],
+        [shaped(TILES, ROWS, 128, dtype=BF16)],
+        (contexts - place * COUNT, events),
+        [
+            pltpu.VMEM((ROWS - 1, 16, features), BF16),
+            pltpu.VMEM((ROWS, features), F32),
+            pltpu.SemaphoreType.DMA((ROWS - 1,)),
+        ],
+        micros=2,
+        room=ROOM,
+    )
+    chunks = lax.all_to_all(picked, "event", 0, 0)
+    (margin,) = kernel_call(
+        margin_kernel,
+        [VMEM, HBM, HBM],
+        [shaped(COUNT // 128, 128)],
+        (weights.reshape(1, features), events, picked),
+        [pltpu.VMEM((5, 256, features), BF16), pltpu.SemaphoreType.DMA((5,))],
         micros=4,
-    )
-    chunks = lax.all_to_all(picked, "event", 0, 0)
+        room=ROOM,
+    )
 
     margin = margin + core_move(margin)
     rate, grad = kernel_call(
         gradient_kernel,
-        [VMEM] * 6,
+        [HBM] + [VMEM] * 5,
         [shaped(1, COUNT), shaped(TILES, 128)],
-        (held, margin, *y_moves(margin), labels.reshape(COUNT // 128, 128)),
-        [pltpu.VMEM((16, COUNT), BF16)],
-        micros=3,
+        (events, margin, *y_moves(margin), labels.reshape(COUNT // 128, 128)),
+        [pltpu.VMEM((16, COUNT), BF16), pltpu.VMEM((4, COUNT, 1024), BF16), pltpu.SemaphoreType.DMA((4,))],
+        micros=4,
+        room=ROOM,
     )
     (message,) = kernel_call(
         spread_kernel, [VMEM] * 2, [shaped(ZN, ROWS + 2 * TILES, 128, dtype=BF16)], (chunks, grad)
@@ -377,10 +441,12 @@
     half = [shaped(ROWS + 8, HALF), shaped(ROWS + 8, HALF)]
     rhs, grad, other, mine = kernel_call(
         scores_kernel,
-        [SMEM] + [VMEM] * 6,
+        [SMEM, HBM] + [VMEM] * 5,
         [shaped(128, features, dtype=BF16), shaped(TILES, 128)] + half,
-        (idx, held, tiled, message, *x_moves(message)),
-        micros=3,
+        (idx, events, tiled, message, *x_moves(message)),
+        [pltpu.VMEM((COUNT, features), BF16), pltpu.SemaphoreType.DMA((4,))],
+        micros=4,
+        room=ROOM,
     )
     packed = [shaped(ROWS + 16, HALF, dtype=BF16)]
     (message,) = kernel_call(pack_kernel, [VMEM] * 2, packed, (mine, core_move(other)))
@@ -391,11 +457,12 @@
     part = shaped(QUARTER * ROWS + 16, 128, dtype=BF16)
     own, curv, one, two, three = kernel_call(
         hessian_kernel,
-        [SMEM] + [VMEM] * 4,
+        [SMEM, HBM] + [VMEM] * 3,
         [shaped(QUARTER * ROWS, 128), shaped(8, 128), part, part, part],
-        (idx, held, scores, core_move(scores), rate),
-        [pltpu.VMEM((ROWS + 16, COUNT), BF16)],
-        micros=3,
+        (idx, events, scores, core_move(scores), rate),
+        [pltpu.VMEM((ROWS + 16, COUNT), BF16), pltpu.VMEM((4, COUNT, 1024), BF16), pltpu.SemaphoreType.DMA((4,))],
+        micros=4,
+        room=ROOM,
     )
     moved = [
         lax.ppermute(v, "event", [(i, (i + k * ZN) % EN) for i in range(EN)])
@@ -413,11 +480,12 @@
 
     other, mine, first = kernel_call(
         second_kernel,
-        [SMEM] + [VMEM] * 7,
+        [SMEM, HBM] + [VMEM] * 6,
         half + [shaped(TILES, 128)],
-        (idx, held, rhs, grad, message, *x_moves(message)),
-        [pltpu.VMEM((128, features), BF16)],
-        micros=3,
+        (idx, events, rhs, grad, message, *x_moves(message)),
+        [pltpu.VMEM((128, features), BF16), pltpu.VMEM((COUNT, features), BF16), pltpu.SemaphoreType.DMA((4,))],
+        micros=4,
+        room=ROOM,
     )
     (message,) = kernel_call(pack_kernel, [VMEM] * 2, packed, (mine, core_move(other)))
     tail, lines = kernel_call(

time: 177 us -> 173 us (0.977)
  local copies, waits for them, and re-layouts: 21.2 us -> 0.53 us
  Pallas kernels: 22.4 us -> 39.9 us
    unnamed x22 -> x4, local copies, waits for them, and re-layouts: 20.7 us -> 0.01 us
    pallas_call x14 -> x15, Pallas kernels: 22.4 us -> 39.9 us  [kernel_call(): pl.pallas_call(body, out_shape=outs, in_specs=ins, out_specs=[VMEM] * len...]
  transfers between devices with their start and end apart: 24 -> 24, of which waited for: 21 -> 21; matrix products, arithmetic and copies ran while one was open for 0% -> 0% of each run, Pallas kernels for 1% -> 7%
where the time goes in v2:
time: 173 us
  blocking collectives  48.5 us (28%)
  starting transfers between devices  42.4 us (25%)
  Pallas kernels  39.9 us (23%)
  waiting for transfers between devices  39.7 us (23%)
    pallas_call x15, Pallas kernels, kernel_call(): pl.pallas_call(body, out_shape=outs, in_specs=ins, out_specs=[VMEM] * len...  39.9 us
    all_to_all x3, blocking collectives, z_exchange(): return lax.all_to_all(v, 'event', 0, 0, axis_index_groups=groups)  36.9 us
    ppermute x9, waiting for transfers between devices, y_moves(): lax.ppermute(v, 'feat', [(i, (i + k * CN) % n) for i in range(n)])  16.3 us
    ppermute x5, starting transfers between devices, core_move(): return lax.ppermute(v, 'feat', [(i, i ^ 1) for i in range(YN * CN)])  12.9 us
    ppermute x6, waiting for transfers between devices, x_moves(): lax.ppermute(v, 'event', [(i, (i + k * ZN) % n) for i in range(n)])  12.1 us
    all_to_all x1, blocking collectives, on_device(): lax.all_to_all(jnp.broadcast_to(tail[None], (EN, 1, 128)), 'event', 0, 0)  11.6 us
    all_to_all x1, starting transfers between devices, on_device(): chunks = lax.all_to_all(picked, 'event', 0, 0)  11.6 us
    ppermute x9, starting transfers between devices, y_moves(): lax.ppermute(v, 'feat', [(i, (i + k * CN) % n) for i in range(n)])  8.45 us
  transfers between devices with their start and end apart: 24, of which 21 were waited for; matrix products, arithmetic and copies ran while one was open for 0% of the time, Pallas kernels for 7%

profile of v2, /device:TPU:1, one launch (start us, length us, event | category | flops | bytes accessed | tf_op | source)
XLA Modules:
  0.0 172.5 jit_solution(1688431308248824020)
XLA Ops:
  0.6 0.7 broadcast_subtract_fusion.local_ref
  1.3 4.2 %shard_map.59._after = bf16[32,64,128]{2,1,0:T(8,128)(2,1)} custom-call(s32[63]{0:T(128)S(1)} %broadcast_subtract_fusion.local_ref, bf16[1280,4096]{1,0:T(8,128)(2,1)} %events_ref.11), custom_call_target="tpu_custom_call" | custom-call | bytes 7200000 | tf_op jit(solution)/shard_map/pallas_call | solution.py:29
  5.5 11.6 %all-to-all-start = ((bf16[32,64,128]{2,1,0:T(8,128)(2,1)}), bf16[32,64,128]{2,1,0:T(8,128)(2,1)S(1)}, u32[]{:S(2)}, u32[]{:S(2)}) async-start(bf16[32,64,128]{2,1,0:T(8,128)(2,1)} %shard_map.59._after), calls=%async_computation | async-start | bytes 1048576 | tf_op jit(solution)/shard_map/all_to_all | solution.py:412
  17.1 7.1 %shard_map.60 = f32[10,128]{1,0:T(8,128)S(1)} custom-call(f32[1,4096]{1,0:T(1,128)S(1)} %bitcast.11, bf16[1280,4096]{1,0:T(8,128)(2,1)} %events_ref.11, bf16[32,64,128]{2,1,0:T(8,128)(2,1)} %shard_map.59._after), custom_call_target="tpu_custom_call" | custom-call | bytes 14400000 | tf_op jit(solution)/shard_map/pallas_call | solution.py:29
  24.2 1.0 collective-permute-start
  25.3 0.8 collective-permute-done
  26.1 2.7 %collective-permute-start.3 = (f32[10,128]{1,0:T(8,128)S(1)}, f32[10,128]{1,0:T(8,128)S(1)}, u32[]{:S(2)}, u32[]{:S(2)}) collective-permute-start(f32[10,128]{1,0:T(8,128)S(1)} %add.7.own), channel_id=1, source_target_pairs={{0,6},{1,7},{2,0},{3,1},{4,2},{5,3},{6,4},{7,5},{8,14},{9,15},{10,... | collective-permute-start | bytes 15368 | tf_op jit(solution)/shard_map/ppermute | solution.py:47
  28.8 0.3 collective-permute-start.2
  29.2 0.7 collective-permute-start.1
  29.9 3.3 %collective-permute-done.2.two = f32[10,128]{1,0:T(8,128)S(1)} collective-permute-done((f32[10,128]{1,0:T(8,128)S(1)}, f32[10,128]{1,0:T(8,128)S(1)}, u32[]{:S(2)}, u32[]{:S(2)}) %collective-permute-start.2) | collective-permute-done | bytes 5152 | tf_op jit(solution)/shard_map/ppermute | solution.py:47
  33.1 0.1 collective-permute-done.1.one
  33.2 4.6 %shard_map.61 = (f32[1,1280]{1,0:T(1,128)S(1)}, f32[32,128]{1,0:T(8,128)S(1)}) custom-call(bf16[1280,4096]{1,0:T(8,128)(2,1)} %events_ref.11, f32[10,128]{1,0:T(8,128)S(1)} %add.7.own, f32[10,128]{1,0:T(8,128)S(1)} %collective-permute-done.1.one, f32[10,128]{1,0:T(8,128)S(1)} %collective-permute-done.2.two, f32[10,128]{1,0:T(8,128)S(1)} %collective-permute-done.3.three, ...), custom_call_target="tpu_custom_call" | custom-call | bytes 14400000 | tf_op jit(solution)/shard_map/pallas_call | solution.py:29
  37.8 0.1 shard_map.62
  37.9 15.7 %all_to_all.25.in_ref = bf16[8,128,128]{2,1,0:T(8,128)(2,1)S(1)} all-to-all(bf16[8,128,128]{2,1,0:T(8,128)(2,1)S(1)} %shard_map.62), channel_id=1, replica_groups={{0,8,16,24,32,40,48,56},{64,72,80,88,96,104,112,120},{128,136,144,152,1..., dimensions={0} | all-to-all | bytes 524288 | tf_op jit(solution)/shard_map/all_to_all | solution.py:56
  53.6 2.5 %collective-permute-start.6 = (bf16[576,128]{1,0:T(8,128)(2,1)S(1)}, bf16[576,128]{1,0:T(8,128)(2,1)S(1)}, u32[]{:S(2)}, u32[]{:S(2)}) collective-permute-start(bf16[576,128]{1,0:T(8,128)(2,1)S(1)} %shard_map.63.own), channel_id=1, source_target_pairs={{0,192},{8,200},{16,208},{24,216},{32,224},{40,232},{48,240},{56,2... | collective-permute-start | bytes 442376 | tf_op jit(solution)/shard_map/ppermute | solution.py:42
  56.2 0.5 collective-permute-start.5
  56.7 0.6 collective-permute-start.4
  57.3 0.1 pad_add_fusion.idx_ref
  57.4 2.5 %collective-permute-done.6.three = bf16[576,128]{1,0:T(8,128)(2,1)S(1)} collective-permute-done((bf16[576,128]{1,0:T(8,128)(2,1)S(1)}, bf16[576,128]{1,0:T(8,128)(2,1)S(1)}, u32[]{:S(2)}, u32[]{:S(2)}) %collective-permute-start.6) | collective-permute-done | bytes 147488 | tf_op jit(solution)/shard_map/ppermute | solution.py:42
  59.8 1.9 %collective-permute-done.5.two = bf16[576,128]{1,0:T(8,128)(2,1)S(1)} collective-permute-done((bf16[576,128]{1,0:T(8,128)(2,1)S(1)}, bf16[576,128]{1,0:T(8,128)(2,1)S(1)}, u32[]{:S(2)}, u32[]{:S(2)}) %collective-permute-start.5) | collective-permute-done | bytes 147488 | tf_op jit(solution)/shard_map/ppermute | solution.py:42
  61.8 1.5 collective-permute-done.4.one
  63.3 8.0 %shard_map.64 = (bf16[128,4096]{1,0:T(8,128)(2,1)S(1)}, f32[32,128]{1,0:T(8,128)S(1)}, f32[72,640]{1,0:T(8,128)S(1)}, f32[72,640]{1,0:T(8,128)S(1)}) custom-call(s32[3]{0:T(128)S(1)} %pad_add_fusion.idx_ref, bf16[1280,4096]{1,0:T(8,128)(2,1)} %events_ref.11, f32[32,128]{1,0:T(8,128)S(1)} %bitcast.12, bf16[576,128]{1,0:T(8,128)(2,1)S(1)} %shard_map.63.own, ...), custom_call_target="tpu_custom_call" | custom-call | bytes 14400000 | tf_op jit(solution)/shard_map/pallas_call | solution.py:29
  71.3 5.0 %collective-permute-start.7 = (f32[72,640]{1,0:T(8,128)S(1)}, f32[72,640]{1,0:T(8,128)S(1)}, u32[]{:S(2)}, u32[]{:S(2)}) collective-permute-start(f32[72,640]{1,0:T(8,128)S(1)} %get-tuple-element.28), channel_id=1, source_target_pairs={{0,1},{1,0},{2,3},{3,2},{4,5},{5,4},{6,7},{7,6},{8,9},{9,8},{10,11... | collective-permute-start | bytes 552968 | tf_op jit(solution)/shard_map/ppermute | solution.py:51
  76.3 1.1 collective-permute-done.7.other
  77.4 0.1 shard_map.65.own
  77.4 0.7 collective-permute-start.10
  78.1 1.2 collective-permute-start.9
  79.2 0.8 collective-permute-start.8
  80.0 1.6 collective-permute-done.10.three
  81.6 1.5 collective-permute-done.9.two
  83.1 3.2 %collective-permute-done.8.one = bf16[80,640]{1,0:T(8,128)(2,1)S(1)} collective-permute-done((bf16[80,640]{1,0:T(8,128)(2,1)S(1)}, bf16[80,640]{1,0:T(8,128)(2,1)S(1)}, u32[]{:S(2)}, u32[]{:S(2)}) %collective-permute-start.8) | collective-permute-done | bytes 102432 | tf_op jit(solution)/shard_map/ppermute | solution.py:47
  86.3 0.1 shard_map.66
  86.4 0.9 collective-permute-start.11
  87.2 1.0 collective-permute-done.11.theirs_ref
  88.3 5.3 %shard_map.67 = (f32[512,128]{1,0:T(8,128)S(1)}, f32[8,128]{1,0:T(8,128)S(1)}, bf16[528,128]{1,0:T(8,128)(2,1)S(1)}, bf16[528,128]{1,0:T(8,128)(2,1)S(1)}, bf16[528,128]{1,0:T(8,128)(2,1)S(1)}) custom-call(s32[3]{0:T(128)S(1)} %pad_add_fusion.idx_ref, bf16[1280,4096]{1,0:T(8,128)(2,1)} %events_ref.11, f32[64,640]{1,0:T(8,128)S(1)} %get-tuple-element.29.mine_ref.scores_ref, ...), custom_call_target="tpu_custom_call" | custom-call | bytes 14400000 | tf_op jit(solution)/shard_map/pallas_call | solution.py:29
  93.6 0.1 collective-permute-start.12
  93.7 1.5 collective-permute-start.13
  95.1 1.2 collective-permute-start.14
  96.3 6.2 %collective-permute-done.12.one = bf16[528,128]{1,0:T(8,128)(2,1)S(1)} collective-permute-done((bf16[528,128]{1,0:T(8,128)(2,1)S(1)}, bf16[528,128]{1,0:T(8,128)(2,1)S(1)}, u32[]{:S(2)}, u32[]{:S(2)}) %collective-permute-start.12) | collective-permute-done | bytes 135200 | tf_op jit(solution)/shard_map/ppermute | solution.py:468
  102.6 0.3 collective-permute-done.14.three
  102.9 0.1 shard_map.68
  103.0 10.6 %all_to_all.26.in_ref = bf16[8,72,128]{2,1,0:T(8,128)(2,1)S(1)} all-to-all(bf16[8,72,128]{2,1,0:T(8,128)(2,1)S(1)} %shard_map.68), channel_id=1, replica_groups={{0,8,16,24,32,40,48,56},{64,72,80,88,96,104,112,120},{128,136,144,152,1..., dimensions={0} | all-to-all | bytes 294912 | tf_op jit(solution)/shard_map/all_to_all | solution.py:56
  113.6 0.7 shard_map.69
  114.2 10.6 %all_to_all.27.own = bf16[8,72,128]{2,1,0:T(8,128)(2,1)S(1)} all-to-all(bf16[8,72,128]{2,1,0:T(8,128)(2,1)S(1)} %get-tuple-element.37), channel_id=1, replica_groups={{0,8,16,24,32,40,48,56},{64,72,80,88,96,104,112,120},{128,136,144,152,1..., dimensions={0} | all-to-all | bytes 294912 | tf_op jit(solution)/shard_map/all_to_all | solution.py:56
  124.8 2.5 %collective-permute-start.17 = (bf16[8,72,128]{2,1,0:T(8,128)(2,1)S(1)}, bf16[8,72,128]{2,1,0:T(8,128)(2,1)S(1)}, u32[]{:S(2)}, u32[]{:S(2)}) collective-permute-start(bf16[8,72,128]{2,1,0:T(8,128)(2,1)S(1)} %all_to_all.27.own), channel_id=1, source_target_pairs={{0,192},{8,200},{16,208},{24,216},{32,224},{40,232},{48,240},{56,2... | collective-permute-start | bytes 442376 | tf_op jit(solution)/shard_map/ppermute | solution.py:42
  127.3 0.6 collective-permute-start.15
  127.9 3.1 %collective-permute-done.17.three = bf16[8,72,128]{2,1,0:T(8,128)(2,1)S(1)} collective-permute-done((bf16[8,72,128]{2,1,0:T(8,128)(2,1)S(1)}, bf16[8,72,128]{2,1,0:T(8,128)(2,1)S(1)}, u32[]{:S(2)}, u32[]{:S(2)}) %collective-permute-start.17) | collective-permute-done | bytes 147488 | tf_op jit(solution)/shard_map/ppermute | solution.py:42
  131.0 1.9 %collective-permute-done.16.two = bf16[8,72,128]{2,1,0:T(8,128)(2,1)S(1)} collective-permute-done((bf16[8,72,128]{2,1,0:T(8,128)(2,1)S(1)}, bf16[8,72,128]{2,1,0:T(8,128)(2,1)S(1)}, u32[]{:S(2)}, u32[]{:S(2)}) %collective-permute-start.16) | collective-permute-done | bytes 147488 | tf_op jit(solution)/shard_map/ppermute | solution.py:42
  132.9 1.2 collective-permute-done.15.one
  134.1 8.2 %shard_map.70 = (f32[72,640]{1,0:T(8,128)S(1)}, f32[72,640]{1,0:T(8,128)S(1)}, f32[32,128]{1,0:T(8,128)S(1)}) custom-call(s32[3]{0:T(128)S(1)} %pad_add_fusion.idx_ref, bf16[1280,4096]{1,0:T(8,128)(2,1)} %events_ref.11, bf16[128,4096]{1,0:T(8,128)(2,1)S(1)} %get-tuple-element.25.rhs_ref, f32[32,128]{1,0:T(8,128)S(1)} %get-tuple-element.26.grad_ref, ...), custom_call_target="tpu_custom_call" | custom-call | bytes 14400000 | tf_op jit(solution)/shard_map/pallas_call | solution.py:29
  142.3 5.2 %collective-permute-start.18 = (f32[72,640]{1,0:T(8,128)S(1)}, f32[72,640]{1,0:T(8,128)S(1)}, u32[]{:S(2)}, u32[]{:S(2)}) collective-permute-start(f32[72,640]{1,0:T(8,128)S(1)} %get-tuple-element.39), channel_id=1, source_target_pairs={{0,1},{1,0},{2,3},{3,2},{4,5},{5,4},{6,7},{7,6},{8,9},{9,8},{10,11... | collective-permute-start | bytes 552968 | tf_op jit(solution)/shard_map/ppermute | solution.py:51
  147.5 1.1 collective-permute-done.18.other
  148.6 0.4 collective-permute-start.21
  149.0 1.1 collective-permute-start.20
  150.1 0.6 collective-permute-start.19
  150.7 2.1 %collective-permute-done.21.three = bf16[80,640]{1,0:T(8,128)(2,1)S(1)} collective-permute-done((bf16[80,640]{1,0:T(8,128)(2,1)S(1)}, bf16[80,640]{1,0:T(8,128)(2,1)S(1)}, u32[]{:S(2)}, u32[]{:S(2)}) %collective-permute-start.21) | collective-permute-done | bytes 102432 | tf_op jit(solution)/shard_map/ppermute | solution.py:47
  152.8 1.3 collective-permute-done.20.two
  154.0 3.3 %collective-permute-done.19.one = bf16[80,640]{1,0:T(8,128)(2,1)S(1)} collective-permute-done((bf16[80,640]{1,0:T(8,128)(2,1)S(1)}, bf16[80,640]{1,0:T(8,128)(2,1)S(1)}, u32[]{:S(2)}, u32[]{:S(2)}) %collective-permute-start.19) | collective-permute-done | bytes 102432 | tf_op jit(solution)/shard_map/ppermute | solution.py:47
  157.3 0.7 shard_map.72
  158.0 0.8 collective-permute-start.22
  158.8 0.8 collective-permute-done.22
  159.6 11.6 %all_to_all.28.tails_ref = f32[32,1,128]{2,1,0:T(1,128)S(1)} all-to-all(f32[32,1,128]{2,1,0:T(1,128)S(1)} %broadcast_in_dim.9), channel_id=1, replica_groups=mesh['event'=32,'feat'=8] {'event'}, dimensions={0} | all-to-all | bytes 32768 | tf_op jit(solution)/shard_map/all_to_all | solution.py:498
  171.2 0.8 shard_map.73
  172.0 0.5 slice_bitcast_fusion
  (13 shorter events, 0.1 us)
Async XLA Ops:
  0.6 16.5 %copy-start = (f32[4096]{0:T(1024)S(1)}, f32[4096]{0:T(1024)}, u32[]{:S(2)}) copy-start(f32[4096]{0:T(1024)} %param.6) | copy-start | bytes 49156
  1.3 31.9 %copy-start.1 = (s32[1280]{0:T(1024)S(1)}, s32[1280]{0:T(1024)}, u32[]{:S(2)}) copy-start(s32[1280]{0:T(1024)} %param.5) | copy-start | bytes 15364
  5.5 32.3 %all-to-all-start = ((bf16[32,64,128]{2,1,0:T(8,128)(2,1)}), bf16[32,64,128]{2,1,0:T(8,128)(2,1)S(1)}, u32[]{:S(2)}, u32[]{:S(2)}) async-start(bf16[32,64,128]{2,1,0:T(8,128)(2,1)} %shard_map.59._after), calls=%async_computation | async-start | bytes 1048576 | tf_op jit(solution)/shard_map/all_to_all | solution.py:412
  24.2 1.9 %collective-permute-start = (f32[10,128]{1,0:T(8,128)S(1)}, f32[10,128]{1,0:T(8,128)S(1)}, u32[]{:S(2)}, u32[]{:S(2)}) collective-permute-start(f32[10,128]{1,0:T(8,128)S(1)} %shard_map.60), channel_id=1, source_target_pairs={{0,1},{1,0},{2,3},{3,2},{4,5},{5,4},{6,7},{7,6},{8,9},{9,8},{10,11... | collective-permute-start | bytes 15368 | tf_op jit(solution)/shard_map/ppermute | solution.py:51
  26.1 3.8 %collective-permute-start.3 = (f32[10,128]{1,0:T(8,128)S(1)}, f32[10,128]{1,0:T(8,128)S(1)}, u32[]{:S(2)}, u32[]{:S(2)}) collective-permute-start(f32[10,128]{1,0:T(8,128)S(1)} %add.7.own), channel_id=1, source_target_pairs={{0,6},{1,7},{2,0},{3,1},{4,2},{5,3},{6,4},{7,5},{8,14},{9,15},{10,... | collective-permute-start | bytes 15368 | tf_op jit(solution)/shard_map/ppermute | solution.py:47
  28.8 4.3 %collective-permute-start.2 = (f32[10,128]{1,0:T(8,128)S(1)}, f32[10,128]{1,0:T(8,128)S(1)}, u32[]{:S(2)}, u32[]{:S(2)}) collective-permute-start(f32[10,128]{1,0:T(8,128)S(1)} %add.7.own), channel_id=1, source_target_pairs={{0,4},{1,5},{2,6},{3,7},{4,0},{5,1},{6,2},{7,3},{8,12},{9,13},{10,... | collective-permute-start | bytes 15368 | tf_op jit(solution)/shard_map/ppermute | solution.py:47
  29.2 4.0 %collective-permute-start.1 = (f32[10,128]{1,0:T(8,128)S(1)}, f32[10,128]{1,0:T(8,128)S(1)}, u32[]{:S(2)}, u32[]{:S(2)}) collective-permute-start(f32[10,128]{1,0:T(8,128)S(1)} %add.7.own), channel_id=1, source_target_pairs={{0,2},{1,3},{2,4},{3,5},{4,6},{5,7},{6,0},{7,1},{8,10},{9,11},{10,... | collective-permute-start | bytes 15368 | tf_op jit(solution)/shard_map/ppermute | solution.py:47
  53.6 6.2 %collective-permute-start.6 = (bf16[576,128]{1,0:T(8,128)(2,1)S(1)}, bf16[576,128]{1,0:T(8,128)(2,1)S(1)}, u32[]{:S(2)}, u32[]{:S(2)}) collective-permute-start(bf16[576,128]{1,0:T(8,128)(2,1)S(1)} %shard_map.63.own), channel_id=1, source_target_pairs={{0,192},{8,200},{16,208},{24,216},{32,224},{40,232},{48,240},{56,2... | collective-permute-start | bytes 442376 | tf_op jit(solution)/shard_map/ppermute | solution.py:42
  56.2 5.6 %collective-permute-start.5 = (bf16[576,128]{1,0:T(8,128)(2,1)S(1)}, bf16[576,128]{1,0:T(8,128)(2,1)S(1)}, u32[]{:S(2)}, u32[]{:S(2)}) collective-permute-start(bf16[576,128]{1,0:T(8,128)(2,1)S(1)} %shard_map.63.own), channel_id=1, source_target_pairs={{0,128},{8,136},{16,144},{24,152},{32,160},{40,168},{48,176},{56,1... | collective-permute-start | bytes 442376 | tf_op jit(solution)/shard_map/ppermute | solution.py:42
  56.7 6.6 %collective-permute-start.4 = (bf16[576,128]{1,0:T(8,128)(2,1)S(1)}, bf16[576,128]{1,0:T(8,128)(2,1)S(1)}, u32[]{:S(2)}, u32[]{:S(2)}) collective-permute-start(bf16[576,128]{1,0:T(8,128)(2,1)S(1)} %shard_map.63.own), channel_id=1, source_target_pairs={{0,64},{8,72},{16,80},{24,88},{32,96},{40,104},{48,112},{56,120},{... | collective-permute-start | bytes 442376 | tf_op jit(solution)/shard_map/ppermute | solution.py:42
  71.3 6.1 %collective-permute-start.7 = (f32[72,640]{1,0:T(8,128)S(1)}, f32[72,640]{1,0:T(8,128)S(1)}, u32[]{:S(2)}, u32[]{:S(2)}) collective-permute-start(f32[72,640]{1,0:T(8,128)S(1)} %get-tuple-element.28), channel_id=1, source_target_pairs={{0,1},{1,0},{2,3},{3,2},{4,5},{5,4},{6,7},{7,6},{8,9},{9,8},{10,11... | collective-permute-start | bytes 552968 | tf_op jit(solution)/shard_map/ppermute | solution.py:51
  77.4 4.2 %collective-permute-start.10 = (bf16[80,640]{1,0:T(8,128)(2,1)S(1)}, bf16[80,640]{1,0:T(8,128)(2,1)S(1)}, u32[]{:S(2)}, u32[]{:S(2)}) collective-permute-start(bf16[80,640]{1,0:T(8,128)(2,1)S(1)} %shard_map.65.own), channel_id=1, source_target_pairs={{0,6},{1,7},{2,0},{3,1},{4,2},{5,3},{6,4},{7,5},{8,14},{9,15},{10,... | collective-permute-start | bytes 307208 | tf_op jit(solution)/shard_map/ppermute | solution.py:47
  78.1 5.0 %collective-permute-start.9 = (bf16[80,640]{1,0:T(8,128)(2,1)S(1)}, bf16[80,640]{1,0:T(8,128)(2,1)S(1)}, u32[]{:S(2)}, u32[]{:S(2)}) collective-permute-start(bf16[80,640]{1,0:T(8,128)(2,1)S(1)} %shard_map.65.own), channel_id=1, source_target_pairs={{0,4},{1,5},{2,6},{3,7},{4,0},{5,1},{6,2},{7,3},{8,12},{9,13},{10,... | collective-permute-start | bytes 307208 | tf_op jit(solution)/shard_map/ppermute | solution.py:47
  79.2 7.1 %collective-permute-start.8 = (bf16[80,640]{1,0:T(8,128)(2,1)S(1)}, bf16[80,640]{1,0:T(8,128)(2,1)S(1)}, u32[]{:S(2)}, u32[]{:S(2)}) collective-permute-start(bf16[80,640]{1,0:T(8,128)(2,1)S(1)} %shard_map.65.own), channel_id=1, source_target_pairs={{0,2},{1,3},{2,4},{3,5},{4,6},{5,7},{6,0},{7,1},{8,10},{9,11},{10,... | collective-permute-start | bytes 307208 | tf_op jit(solution)/shard_map/ppermute | solution.py:47
  86.4 1.9 %collective-permute-start.11 = (f32[64,640]{1,0:T(8,128)S(1)}, f32[64,640]{1,0:T(8,128)S(1)}, u32[]{:S(2)}, u32[]{:S(2)}) collective-permute-start(f32[64,640]{1,0:T(8,128)S(1)} %get-tuple-element.29.mine_ref.scores_ref), channel_id=1, source_target_pairs={{0,1},{1,0},{2,3},{3,2},{4,5},{5,4},{6,7},{7,6},{8,9},{9,8},{10,11... | collective-permute-start | bytes 491528 | tf_op jit(solution)/shard_map/ppermute | solution.py:51
  93.6 9.0 %collective-permute-start.12 = (bf16[528,128]{1,0:T(8,128)(2,1)S(1)}, bf16[528,128]{1,0:T(8,128)(2,1)S(1)}, u32[]{:S(2)}, u32[]{:S(2)}) collective-permute-start(bf16[528,128]{1,0:T(8,128)(2,1)S(1)} %get-tuple-element.33), channel_id=1, source_target_pairs={{0,64},{8,72},{16,80},{24,88},{32,96},{40,104},{48,112},{56,120},{... | collective-permute-start | bytes 405512 | tf_op jit(solution)/shard_map/ppermute | solution.py:468
  93.7 8.9 %collective-permute-start.13 = (bf16[528,128]{1,0:T(8,128)(2,1)S(1)}, bf16[528,128]{1,0:T(8,128)(2,1)S(1)}, u32[]{:S(2)}, u32[]{:S(2)}) collective-permute-start(bf16[528,128]{1,0:T(8,128)(2,1)S(1)} %get-tuple-element.34), channel_id=1, source_target_pairs={{0,128},{8,136},{16,144},{24,152},{32,160},{40,168},{48,176},{56,1... | collective-permute-start | bytes 405512 | tf_op jit(solution)/shard_map/ppermute | solution.py:468
  95.1 7.8 %collective-permute-start.14 = (bf16[528,128]{1,0:T(8,128)(2,1)S(1)}, bf16[528,128]{1,0:T(8,128)(2,1)S(1)}, u32[]{:S(2)}, u32[]{:S(2)}) collective-permute-start(bf16[528,128]{1,0:T(8,128)(2,1)S(1)} %get-tuple-element.35), channel_id=1, source_target_pairs={{0,192},{8,200},{16,208},{24,216},{32,224},{40,232},{48,240},{56,2... | collective-permute-start | bytes 405512 | tf_op jit(solution)/shard_map/ppermute | solution.py:468
  124.8 6.2 %collective-permute-start.17 = (bf16[8,72,128]{2,1,0:T(8,128)(2,1)S(1)}, bf16[8,72,128]{2,1,0:T(8,128)(2,1)S(1)}, u32[]{:S(2)}, u32[]{:S(2)}) collective-permute-start(bf16[8,72,128]{2,1,0:T(8,128)(2,1)S(1)} %all_to_all.27.own), channel_id=1, source_target_pairs={{0,192},{8,200},{16,208},{24,216},{32,224},{40,232},{48,240},{56,2... | collective-permute-start | bytes 442376 | tf_op jit(solution)/shard_map/ppermute | solution.py:42
  127.3 5.6 %collective-permute-start.16 = (bf16[8,72,128]{2,1,0:T(8,128)(2,1)S(1)}, bf16[8,72,128]{2,1,0:T(8,128)(2,1)S(1)}, u32[]{:S(2)}, u32[]{:S(2)}) collective-permute-start(bf16[8,72,128]{2,1,0:T(8,128)(2,1)S(1)} %all_to_all.27.own), channel_id=1, source_target_pairs={{0,128},{8,136},{16,144},{24,152},{32,160},{40,168},{48,176},{56,1... | collective-permute-start | bytes 442376 | tf_op jit(solution)/shard_map/ppermute | solution.py:42
  127.3 6.8 %collective-permute-start.15 = (bf16[8,72,128]{2,1,0:T(8,128)(2,1)S(1)}, bf16[8,72,128]{2,1,0:T(8,128)(2,1)S(1)}, u32[]{:S(2)}, u32[]{:S(2)}) collective-permute-start(bf16[8,72,128]{2,1,0:T(8,128)(2,1)S(1)} %all_to_all.27.own), channel_id=1, source_target_pairs={{0,64},{8,72},{16,80},{24,88},{32,96},{40,104},{48,112},{56,120},{... | collective-permute-start | bytes 442376 | tf_op jit(solution)/shard_map/ppermute | solution.py:42
  142.3 6.2 %collective-permute-start.18 = (f32[72,640]{1,0:T(8,128)S(1)}, f32[72,640]{1,0:T(8,128)S(1)}, u32[]{:S(2)}, u32[]{:S(2)}) collective-permute-start(f32[72,640]{1,0:T(8,128)S(1)} %get-tuple-element.39), channel_id=1, source_target_pairs={{0,1},{1,0},{2,3},{3,2},{4,5},{5,4},{6,7},{7,6},{8,9},{9,8},{10,11... | collective-permute-start | bytes 552968 | tf_op jit(solution)/shard_map/ppermute | solution.py:51
  148.6 4.2 %collective-permute-start.21 = (bf16[80,640]{1,0:T(8,128)(2,1)S(1)}, bf16[80,640]{1,0:T(8,128)(2,1)S(1)}, u32[]{:S(2)}, u32[]{:S(2)}) collective-permute-start(bf16[80,640]{1,0:T(8,128)(2,1)S(1)} %shard_map.71.own), channel_id=1, source_target_pairs={{0,6},{1,7},{2,0},{3,1},{4,2},{5,3},{6,4},{7,5},{8,14},{9,15},{10,... | collective-permute-start | bytes 307208 | tf_op jit(solution)/shard_map/ppermute | solution.py:47
  149.0 5.0 %collective-permute-start.20 = (bf16[80,640]{1,0:T(8,128)(2,1)S(1)}, bf16[80,640]{1,0:T(8,128)(2,1)S(1)}, u32[]{:S(2)}, u32[]{:S(2)}) collective-permute-start(bf16[80,640]{1,0:T(8,128)(2,1)S(1)} %shard_map.71.own), channel_id=1, source_target_pairs={{0,4},{1,5},{2,6},{3,7},{4,0},{5,1},{6,2},{7,3},{8,12},{9,13},{10,... | collective-permute-start | bytes 307208 | tf_op jit(solution)/shard_map/ppermute | solution.py:47
  150.1 7.2 %collective-permute-start.19 = (bf16[80,640]{1,0:T(8,128)(2,1)S(1)}, bf16[80,640]{1,0:T(8,128)(2,1)S(1)}, u32[]{:S(2)}, u32[]{:S(2)}) collective-permute-start(bf16[80,640]{1,0:T(8,128)(2,1)S(1)} %shard_map.71.own), channel_id=1, source_target_pairs={{0,2},{1,3},{2,4},{3,5},{4,6},{5,7},{6,0},{7,1},{8,10},{9,11},{10,... | collective-permute-start | bytes 307208 | tf_op jit(solution)/shard_map/ppermute | solution.py:47
  158.0 1.6 collective-permute-start.22

commit v3 on v1

--- a/solution.py
+++ b/solution.py
@@ -13,6 +13,8 @@
 QUARTER = TILES // XN
 COUNT = 1280
 HALF = COUNT // 2
+WINDOW = 4
+ROOM = 48
 F32, BF16 = jnp.float32, jnp.bfloat16
 VMEM = pl.BlockSpec(memory_space=pltpu.VMEM)
 SMEM = pl.BlockSpec(memory_space=pltpu.SMEM)
@@ -24,14 +26,14 @@
     return jax.ShapeDtypeStruct(shape, dtype)
 
 
-def kernel_call(body, ins, outs, args, scratch=(), micros=0.5):
+def kernel_call(body, ins, outs, args, scratch=(), micros=0.5, room=8):
     return pl.pallas_call(
         body,
         out_shape=outs,
         in_specs=ins,
         out_specs=[VMEM] * len(outs),
         scratch_shapes=list(scratch),
-        compiler_params=pltpu.CompilerParams(vmem_limit_bytes=28 << 20),
+        compiler_params=pltpu.CompilerParams(vmem_limit_bytes=room << 20),
         cost_estimate=pl.CostEstimate(flops=0, bytes_accessed=int(micros * 3.6e6), transcendentals=0),
     )(*args)
 
@@ -98,32 +100,62 @@
     return total
 
 
-def first_kernel(local_ref, w_ref, events_ref, held_ref, margin_ref, out_ref, rows, sems):
-    piece = COUNT // 5
-    copies = [
-        pltpu.make_async_copy(
-            events_ref.at[pl.ds(c * piece, piece), :], held_ref.at[pl.ds(c * piece, piece), :], sems.at[c]
+class Stream:
+    def __init__(self, pieces, sems):
+        self.copies = [pltpu.make_async_copy(source, target, sems.at[i]) for i, (source, target) in enumerate(pieces)]
+        for copy in self.copies[:WINDOW]:
+            copy.start()
+
+    def take(self, i):
+        self.copies[i].wait()
+        if i + WINDOW < len(self.copies):
+            self.copies[i + WINDOW].start()
+
+
+def row_stream(events_ref, held, sems, starts):
+    pieces = [
+        (events_ref.at[pl.ds(pl.multiple_of(start, 128), 128), :], held.at[pl.ds(i * 128, 128), :])
+        for i, start in enumerate(starts)
+    ]
+    return Stream(pieces, sems)
+
+
+def column_stream(events_ref, held, sems, starts):
+    pieces = [
+        (events_ref.at[:, pl.ds(pl.multiple_of(start, 512), 512)], held.at[i]) for i, start in enumerate(starts)
+    ]
+    return Stream(pieces, sems)
+
+
+def place():
+    event = lax.axis_index("event")
+    return lax.div(event, ZN), lax.rem(event, ZN), lax.rem(lax.axis_index("feat"), CN)
+
+
+def first_kernel(contexts_ref, w_ref, events_ref, margin_ref, out_ref, rhs, rows, held, sems):
+    pieces = row_stream(events_ref, held, sems, [i * 128 for i in range(COUNT // 128)])
+    rhs[:16, :] = jnp.broadcast_to(w_ref[...], (16, TILES * 128)).astype(BF16)
+    rhs[16:, :] = jnp.zeros((112, TILES * 128), BF16)
+    rows[...] = jnp.zeros_like(rows)
+    for c in range(0, COUNT // 128, 2):
+        pieces.take(c)
+        pieces.take(c + 1)
+        part = lax.dot_general(
+            held[c * 128 : (c + 2) * 128, :], rhs[...], ACROSS, preferred_element_type=F32
         )
-        for c in range(5)
-    ]
-    for copy in copies:
-        copy.start()
-    rows[...] = jnp.zeros_like(rows)
-    w = jnp.broadcast_to(w_ref[...], (16, TILES * 128)).astype(BF16)
-    for c, copy in enumerate(copies):
-        copy.wait()
-        part = lax.dot_general(w, held_ref[c * piece : (c + 1) * piece, :], ACROSS, preferred_element_type=F32)
-        margin_ref[2 * c : 2 * c + 1, :] = part[:1, :128]
-        margin_ref[2 * c + 1 : 2 * c + 2, :] = part[:1, 128:]
+        for u in range(2):
+            margin_ref[c + u : c + u + 1, :] = jnp.transpose(part[u * 128 : (u + 1) * 128])[:1]
+
+    base = lax.axis_index("event") * COUNT
 
     @pl.loop(0, ROWS - 1)
     def _(j):
-        r = local_ref[j]
+        r = contexts_ref[j] - base
 
         @pl.when(jnp.logical_and(r >= 0, r < COUNT))
         def _():
             start = pl.multiple_of(lax.div(r, 16) * 16, 16)
-            block = held_ref[pl.ds(start, 16), :].astype(F32)
+            block = held[pl.ds(start, 16), :].astype(F32)
             found = jnp.where(row_is(block.shape, lax.rem(r, 16)), block, 0.0)
             rows[pl.ds(j, 1), :] = jnp.sum(found, axis=0, keepdims=True)
 
@@ -131,7 +163,8 @@
         out_ref[t] = rows[:, t * 128 : (t + 1) * 128].astype(BF16)
 
 
-def gradient_kernel(held_ref, own, one, two, three, labels_ref, rate_ref, grad_ref, errs):
+def gradient_kernel(events_ref, own, one, two, three, labels_ref, rate_ref, grad_ref, errs, held, sems):
+    pieces = column_stream(events_ref, held, sems, [c * 512 for c in range(8)])
     margin = four(own[...], one[...], two[...], three[...])
     chance = jax.nn.sigmoid(margin)
     rate = chance * (1.0 - chance)
@@ -142,11 +175,12 @@
         at = slice(i * 128, (i + 1) * 128)
         rate_ref[:, at] = rate[i : i + 1]
         errs[:, at] = stacked([lead[i : i + 1], rest[i : i + 1]], 16).astype(BF16)
-    for n in range(0, TILES, 4):
-        part = jnp.dot(errs[...], held_ref[:, n * 128 : (n + 4) * 128], preferred_element_type=F32)
+    for c in range(8):
+        pieces.take(c)
+        part = jnp.dot(errs[...], held[c], preferred_element_type=F32)
         line = part[:1] + part[1:2]
         for u in range(4):
-            grad_ref[n + u : n + u + 1, :] = line[:, u * 128 : (u + 1) * 128]
+            grad_ref[c * 4 + u : c * 4 + u + 1, :] = line[:, u * 128 : (u + 1) * 128]
 
 
 def spread_kernel(chunks_ref, grad_ref, out_ref):
@@ -170,17 +204,29 @@
     out_ref[QUARTER * ROWS + TILES :, :] = rest
 
 
-def put_scores(held_ref, rhs, core, other_ref, own_ref, lines):
-    for half, out_ref in ((1 - core, other_ref), (core, own_ref)):
-        start = pl.multiple_of(half * HALF, HALF)
-        part = lax.dot_general(held_ref[pl.ds(start, HALF), :], rhs[...], ACROSS, preferred_element_type=F32)
-        for t in range(HALF // 128):
-            out_ref[:ROWS, t * 128 : (t + 1) * 128] = joined(jnp.transpose(part[t * 128 : (t + 1) * 128]))
-            out_ref[ROWS:, t * 128 : (t + 1) * 128] = lines if t == 0 else jnp.zeros_like(lines)
-
-
-def scores_kernel(idx_ref, held_ref, w_ref, own, one, two, three, rhs_ref, grad_ref, other_ref, mine_ref):
-    x, core = idx_ref[0], idx_ref[2]
+def half_stream(events_ref, held, sems, core):
+    starts = [half * HALF + i * 128 for half in (1 - core, core) for i in range(HALF // 128)]
+    return row_stream(events_ref, held, sems, starts)
+
+
+def put_scores(pieces, held, rhs, other_ref, own_ref, lines):
+    for first, out_ref in ((0, other_ref), (HALF // 128, own_ref)):
+        for at, size in ((0, 2), (2, 3)):
+            for i in range(size):
+                pieces.take(first + at + i)
+            events = held[(first + at) * 128 : (first + at + size) * 128, :]
+            part = lax.dot_general(events, rhs[...], ACROSS, preferred_element_type=F32)
+            for t in range(size):
+                columns = slice((at + t) * 128, (at + t + 1) * 128)
+                out_ref[:ROWS, columns] = joined(jnp.transpose(part[t * 128 : (t + 1) * 128]))
+                out_ref[ROWS:, columns] = lines if at + t == 0 else jnp.zeros_like(lines)
+
+
+def scores_kernel(
+    events_ref, w_ref, own, one, two, three, rhs_ref, grad_ref, other_ref, mine_ref, held, sems
+):
+    x, _, core = place()
+    pieces = half_stream(events_ref, held, sems, core)
     top = QUARTER * ROWS
     grads = [p[top : top + TILES, :].astype(F32) + p[top + TILES :, :].astype(F32) for p in (own, one, two, three)]
     grad_ref[...] = four(*grads) + LAMBDA * w_ref[...]
@@ -200,7 +246,7 @@
             rhs_ref[:ROWS, at] = jnp.where(last, lead.astype(F32), values).astype(BF16)
             rhs_ref[ROWS : ROWS + 16, at] = stacked([rest], 16).astype(BF16)
     line = line_sums(norm, jnp.zeros_like(norm))
-    put_scores(held_ref, rhs_ref, core, other_ref, mine_ref, stacked([line], 8))
+    put_scores(pieces, held, rhs_ref, other_ref, mine_ref, stacked([line], 8))
 
 
 def pack_kernel(own, other, out_ref):
@@ -225,8 +271,13 @@
     norm_ref[...] = stacked([norm], 8)
 
 
-def hessian_kernel(idx_ref, held_ref, mine_ref, theirs_ref, rate_ref, own_ref, curv_ref, one_ref, two_ref, three_ref, q):
-    x, core = idx_ref[0], idx_ref[2]
+def hessian_kernel(
+    events_ref, mine_ref, theirs_ref, rate_ref, own_ref, curv_ref, one_ref, two_ref, three_ref, q, held, sems
+):
+    x, _, core = place()
+    outs = ((2, two_ref), (1, one_ref), (3, three_ref), (0, own_ref))
+    starts = [lax.rem(x + k, XN) * QUARTER * 128 + part * 512 for k, _ in outs for part in range(2)]
+    pieces = column_stream(events_ref, held, sems, starts)
     curv = jnp.zeros((ROWS, 128), F32)
     for half in range(2):
         scores = jnp.where(core == half, mine_ref[...], theirs_ref[...])
@@ -238,15 +289,16 @@
         q[ROWS:, at] = stacked([weighted[ROWS - 1 :] - lead[ROWS - 1 :].astype(F32)], 16).astype(BF16)
     triple = [v.astype(F32) for v in triple_of(line_sums(curv, jnp.zeros_like(curv)))]
     curv_ref[...] = stacked(triple, 8)
-    for k, out_ref in ((2, two_ref), (1, one_ref), (3, three_ref), (0, own_ref)):
-        quarter = lax.rem(x + k, XN)
-        columns = pl.ds(pl.multiple_of(quarter * QUARTER * 128, 128), QUARTER * 128)
-        total = joined(jnp.dot(q[...], held_ref[:, columns], preferred_element_type=F32))
+    for i, (k, out_ref) in enumerate(outs):
         rests = []
-        for t in range(QUARTER):
-            values = total[:, t * 128 : (t + 1) * 128]
-            out_ref[t * ROWS : (t + 1) * ROWS, :] = values.astype(out_ref.dtype)
-            rests.append(values[ROWS - 1 :] - values[ROWS - 1 :].astype(BF16).astype(F32))
+        for part in range(2):
+            pieces.take(2 * i + part)
+            total = joined(jnp.dot(q[...], held[2 * i + part], preferred_element_type=F32))
+            for u in range(4):
+                t = part * 4 + u
+                values = total[:, u * 128 : (u + 1) * 128]
+                out_ref[t * ROWS : (t + 1) * ROWS, :] = values.astype(out_ref.dtype)
+                rests.append(values[ROWS - 1 :] - values[ROWS - 1 :].astype(BF16).astype(F32))
         if k:
             out_ref[QUARTER * ROWS :, :] = stacked(rests + triple, 16).astype(BF16)
 
@@ -268,8 +320,9 @@
         out_ref[t, ROWS:, :] = stacked([rest, *curv], 8).astype(BF16)
 
 
-def residual_kernel(idx_ref, in_ref, norm_ref, rhs_ref, grad_ref, out_ref, scalars_ref):
-    tile = idx_ref[0] * QUARTER + idx_ref[1]
+def residual_kernel(in_ref, norm_ref, rhs_ref, grad_ref, out_ref, scalars_ref):
+    x, z, _ = place()
+    tile = x * QUARTER + z
     total = in_ref[0].astype(F32)
     for z in range(1, ZN):
         total = total + in_ref[z].astype(F32)
@@ -290,8 +343,11 @@
     scalars_ref[...] = stacked([step, curv, norm], 8)
 
 
-def second_kernel(idx_ref, held_ref, rhs_ref, grad_ref, own, one, two, three, other_ref, mine_ref, first_ref, res):
-    x, core = idx_ref[0], idx_ref[2]
+def second_kernel(
+    events_ref, rhs_ref, grad_ref, own, one, two, three, other_ref, mine_ref, first_ref, res, held, sems
+):
+    x, _, core = place()
+    pieces = half_stream(events_ref, held, sems, core)
     norm = jnp.zeros((ROWS, 128), F32)
     cross = jnp.zeros((ROWS, 128), F32)
     res[ROWS:, :] = jnp.zeros((128 - ROWS, TILES * 128), BF16)
@@ -311,12 +367,12 @@
             res[ROWS : ROWS + 16, at] = stacked([rows[ROWS:].astype(F32)[:1]], 16).astype(BF16)
     line = line_sums(norm, cross)
     lines = stacked([line, pltpu.roll(line, ROWS, 1)], 8)
-    put_scores(held_ref, res, core, other_ref, mine_ref, lines)
-
-
-def tail_kernel(idx_ref, own, one, two, three, scores_ref, rate_ref, tail_ref, lines_ref):
+    put_scores(pieces, held, res, other_ref, mine_ref, lines)
+
+
+def tail_kernel(own, one, two, three, scores_ref, rate_ref, tail_ref, lines_ref):
     scores, norm, cross = unpacked(own, one, two, three)
-    rate = jnp.where(idx_ref[2] == 0, rate_ref[:, :HALF], rate_ref[:, HALF:])
+    rate = jnp.where(place()[2] == 0, rate_ref[:, :HALF], rate_ref[:, HALF:])
     weighted = rate * scores
     tail_ref[...] = line_sums(tile_sums(weighted * scores_ref[...]), tile_sums(weighted * scores))
     lines_ref[...] = stacked([norm, cross], 8)
@@ -341,30 +397,32 @@
 
 
 def on_device(events, labels, weights, contexts):
-    place = lax.axis_index("event")
-    core = lax.rem(lax.axis_index("feat"), CN)
-    idx = jnp.stack([place // ZN, lax.rem(place, ZN), core]).astype(jnp.int32)
     features = TILES * 128
     tiled = weights.reshape(TILES, 128)
 
-    held, margin, picked = kernel_call(
+    rows = [pltpu.VMEM((COUNT, features), BF16), pltpu.SemaphoreType.DMA((10,))]
+    columns = [pltpu.VMEM((8, COUNT, 512), BF16), pltpu.SemaphoreType.DMA((8,))]
+
+    margin, picked = kernel_call(
         first_kernel,
         [SMEM, VMEM, HBM],
-        [shaped(COUNT, features, dtype=BF16), shaped(COUNT // 128, 128), shaped(TILES, ROWS, 128, dtype=BF16)],
-        (contexts - place * COUNT, weights.reshape(1, features), events),
-        [pltpu.VMEM((ROWS, features), F32), pltpu.SemaphoreType.DMA((5,))],
-        micros=4,
+        [shaped(COUNT // 128, 128), shaped(TILES, ROWS, 128, dtype=BF16)],
+        (contexts, weights.reshape(1, features), events),
+        [pltpu.VMEM((128, features), BF16), pltpu.VMEM((ROWS, features), F32), *rows],
+        micros=6,
+        room=ROOM,
     )
     chunks = lax.all_to_all(picked, "event", 0, 0)
 
     margin = margin + core_move(margin)
     rate, grad = kernel_call(
         gradient_kernel,
-        [VMEM] * 6,
+        [HBM] + [VMEM] * 5,
         [shaped(1, COUNT), shaped(TILES, 128)],
-        (held, margin, *y_moves(margin), labels.reshape(COUNT // 128, 128)),
-        [pltpu.VMEM((16, COUNT), BF16)],
-        micros=3,
+        (events, margin, *y_moves(margin), labels.reshape(COUNT // 128, 128)),
+        [pltpu.VMEM((16, COUNT), BF16), *columns],
+        micros=4,
+        room=ROOM,
     )
     (message,) = kernel_call(
         spread_kernel, [VMEM] * 2, [shaped(ZN, ROWS + 2 * TILES, 128, dtype=BF16)], (chunks, grad)
@@ -377,10 +435,12 @@
     half = [shaped(ROWS + 8, HALF), shaped(ROWS + 8, HALF)]
     rhs, grad, other, mine = kernel_call(
         scores_kernel,
-        [SMEM] + [VMEM] * 6,
+        [HBM] + [VMEM] * 5,
         [shaped(128, features, dtype=BF16), shaped(TILES, 128)] + half,
-        (idx, held, tiled, message, *x_moves(message)),
-        micros=3,
+        (events, tiled, message, *x_moves(message)),
+        rows,
+        micros=4,
+        room=ROOM,
     )
     packed = [shaped(ROWS + 16, HALF, dtype=BF16)]
     (message,) = kernel_call(pack_kernel, [VMEM] * 2, packed, (mine, core_move(other)))
@@ -391,11 +451,12 @@
     part = shaped(QUARTER * ROWS + 16, 128, dtype=BF16)
     own, curv, one, two, three = kernel_call(
         hessian_kernel,
-        [SMEM] + [VMEM] * 4,
+        [HBM] + [VMEM] * 3,
         [shaped(QUARTER * ROWS, 128), shaped(8, 128), part, part, part],
-        (idx, held, scores, core_move(scores), rate),
-        [pltpu.VMEM((ROWS + 16, COUNT), BF16)],
-        micros=3,
+        (events, scores, core_move(scores), rate),
+        [pltpu.VMEM((ROWS + 16, COUNT), BF16), *columns],
+        micros=4,
+        room=ROOM,
     )
     moved = [
         lax.ppermute(v, "event", [(i, (i + k * ZN) % EN) for i in range(EN)])
@@ -405,26 +466,27 @@
     (message,) = kernel_call(cut_kernel, [VMEM] * 5, shard, (own, curv, *moved))
     message, scalars = kernel_call(
         residual_kernel,
-        [SMEM] + [VMEM] * 4,
+        [VMEM] * 4,
         shard + [shaped(8, 128)],
-        (idx, z_exchange(message), norm, rhs, grad),
+        (z_exchange(message), norm, rhs, grad),
     )
     message = z_exchange(message)
 
     other, mine, first = kernel_call(
         second_kernel,
-        [SMEM] + [VMEM] * 7,
+        [HBM] + [VMEM] * 6,
         half + [shaped(TILES, 128)],
-        (idx, held, rhs, grad, message, *x_moves(message)),
-        [pltpu.VMEM((128, features), BF16)],
-        micros=3,
+        (events, rhs, grad, message, *x_moves(message)),
+        [pltpu.VMEM((128, features), BF16), *rows],
+        micros=4,
+        room=ROOM,
     )
     (message,) = kernel_call(pack_kernel, [VMEM] * 2, packed, (mine, core_move(other)))
     tail, lines = kernel_call(
         tail_kernel,
-        [SMEM] + [VMEM] * 6,
+        [VMEM] * 6,
         [shaped(1, 128), shaped(8, 128)],
-        (idx, message, *y_moves(message), scores, rate),
+        (message, *y_moves(message), scores, rate),
     )
     tail = tail + core_move(tail)
     tails = lax.all_to_all(jnp.broadcast_to(tail[None], (EN, 1, 128)), "event", 0, 0)

time: 177 us -> 172 us (0.972)
  local copies, waits for them, and re-layouts: 21.2 us -> 1.9 us
  Pallas kernels: 22.4 us -> 36 us
    unnamed x22 -> x8, local copies, waits for them, and re-layouts: 20.7 us -> 1.37 us
    pallas_call x14, Pallas kernels: 22.4 us -> 36 us  [kernel_call(): pl.pallas_call(body, out_shape=outs, in_specs=ins, out_specs=[VMEM] * len...]
  transfers between devices with their start and end apart: 24 -> 24, of which waited for: 21 -> 22; matrix products, arithmetic and copies ran while one was open for 0% -> 0% of each run, Pallas kernels for 1% -> 3%
where the time goes in v3:
time: 172 us; the launch traced here: 171 us
  blocking collectives  47.8 us (28%)
  starting transfers between devices  43.2 us (25%)
  waiting for transfers between devices  41.6 us (24%)
  Pallas kernels  36 us (21%)
  local copies, waits for them, and re-layouts  1.9 us (1%)
    all_to_all x3, blocking collectives, z_exchange(): return lax.all_to_all(v, 'event', 0, 0, axis_index_groups=groups)  36.2 us
    pallas_call x14, Pallas kernels, kernel_call(): pl.pallas_call(body, out_shape=outs, in_specs=ins, out_specs=[VMEM] * len...  36 us
    ppermute x9, waiting for transfers between devices, y_moves(): lax.ppermute(v, 'feat', [(i, (i + k * CN) % n) for i in range(n)])  18 us
    ppermute x5, starting transfers between devices, core_move(): return lax.ppermute(v, 'feat', [(i, i ^ 1) for i in range(YN * CN)])  12.4 us
    ppermute x6, waiting for transfers between devices, x_moves(): lax.ppermute(v, 'event', [(i, (i + k * ZN) % n) for i in range(n)])  12.2 us
    all_to_all x1, starting transfers between devices, on_device(): chunks = lax.all_to_all(picked, 'event', 0, 0)  12 us
    all_to_all x1, blocking collectives, on_device(): lax.all_to_all(jnp.broadcast_to(tail[None], (EN, 1, 128)), 'event', 0, 0)  11.6 us
    ppermute x6, starting transfers between devices, x_moves(): lax.ppermute(v, 'event', [(i, (i + k * ZN) % n) for i in range(n)])  7.88 us
  transfers between devices with their start and end apart: 24, of which 22 were waited for; matrix products, arithmetic and copies ran while one was open for 0% of the time, Pallas kernels for 3%

profile of v3, /device:TPU:1, one launch (start us, length us, event | category | flops | bytes accessed | tf_op | source)
XLA Modules:
  0.0 171.3 jit_solution(904717150232923651)
XLA Ops:
  0.6 0.7 copy-done
  1.4 0.7 copy-done.3
  2.0 9.8 %shard_map.59 = (f32[10,128]{1,0:T(8,128)S(1)}, bf16[32,64,128]{2,1,0:T(8,128)(2,1)}) custom-call(s32[63]{0:T(128)S(1)} %copy-done.3, f32[1,4096]{1,0:T(1,128)S(1)} %bitcast.8, bf16[1280,4096]{1,0:T(8,128)(2,1)} %events_ref.9), custom_call_target="tpu_custom_call" | custom-call | bytes 21600000 | tf_op jit(solution)/shard_map/pallas_call | solution.py:30
  11.9 12.0 %all-to-all-start = ((bf16[32,64,128]{2,1,0:T(8,128)(2,1)}), bf16[32,64,128]{2,1,0:T(8,128)(2,1)S(1)}, u32[]{:S(2)}, u32[]{:S(2)}) async-start(bf16[32,64,128]{2,1,0:T(8,128)(2,1)} %get-tuple-element.26), calls=%async_computation | async-start | bytes 1048576 | tf_op jit(solution)/shard_map/all_to_all | solution.py:415
  23.9 1.0 collective-permute-start
  24.9 0.8 collective-permute-done
  25.7 2.7 %collective-permute-start.3 = (f32[10,128]{1,0:T(8,128)S(1)}, f32[10,128]{1,0:T(8,128)S(1)}, u32[]{:S(2)}, u32[]{:S(2)}) collective-permute-start(f32[10,128]{1,0:T(8,128)S(1)} %add.6.own), channel_id=1, source_target_pairs={{0,6},{1,7},{2,0},{3,1},{4,2},{5,3},{6,4},{7,5},{8,14},{9,15},{10,... | collective-permute-start | bytes 15368 | tf_op jit(solution)/shard_map/ppermute | solution.py:48
  28.5 0.3 collective-permute-start.2
  28.8 0.7 collective-permute-start.1
  29.5 0.0 collective-permute-done.3.three
  29.5 3.3 %collective-permute-done.2.two = f32[10,128]{1,0:T(8,128)S(1)} collective-permute-done((f32[10,128]{1,0:T(8,128)S(1)}, f32[10,128]{1,0:T(8,128)S(1)}, u32[]{:S(2)}, u32[]{:S(2)}) %collective-permute-start.2) | collective-permute-done | bytes 5152 | tf_op jit(solution)/shard_map/ppermute | solution.py:48
  32.8 0.1 collective-permute-done.1.one
  32.9 4.7 %shard_map.60 = (f32[1,1280]{1,0:T(1,128)S(1)}, f32[32,128]{1,0:T(8,128)S(1)}) custom-call(bf16[1280,4096]{1,0:T(8,128)(2,1)} %events_ref.9, f32[10,128]{1,0:T(8,128)S(1)} %add.6.own, f32[10,128]{1,0:T(8,128)S(1)} %collective-permute-done.1.one, f32[10,128]{1,0:T(8,128)S(1)} %collective-permute-done.2.two, f32[10,128]{1,0:T(8,128)S(1)} %collective-permute-done.3.three, ...), custom_call_target="tpu_custom_call" | custom-call | bytes 14400000 | tf_op jit(solution)/shard_map/pallas_call | solution.py:30
  37.5 0.6 all-to-all-done.chunks_ref
  38.2 0.1 shard_map.61
  38.3 15.1 %all_to_all.25.in_ref = bf16[8,128,128]{2,1,0:T(8,128)(2,1)S(1)} all-to-all(bf16[8,128,128]{2,1,0:T(8,128)(2,1)S(1)} %shard_map.61), channel_id=1, replica_groups={{0,8,16,24,32,40,48,56},{64,72,80,88,96,104,112,120},{128,136,144,152,1..., dimensions={0} | all-to-all | bytes 524288 | tf_op jit(solution)/shard_map/all_to_all | solution.py:57
  53.4 2.5 %collective-permute-start.6 = (bf16[576,128]{1,0:T(8,128)(2,1)S(1)}, bf16[576,128]{1,0:T(8,128)(2,1)S(1)}, u32[]{:S(2)}, u32[]{:S(2)}) collective-permute-start(bf16[576,128]{1,0:T(8,128)(2,1)S(1)} %shard_map.62.own), channel_id=1, source_target_pairs={{0,192},{8,200},{16,208},{24,216},{32,224},{40,232},{48,240},{56,2... | collective-permute-start | bytes 442376 | tf_op jit(solution)/shard_map/ppermute | solution.py:43
  55.9 0.5 collective-permute-start.5
  56.4 0.6 collective-permute-start.4
  57.0 2.6 %collective-permute-done.6.three = bf16[576,128]{1,0:T(8,128)(2,1)S(1)} collective-permute-done((bf16[576,128]{1,0:T(8,128)(2,1)S(1)}, bf16[576,128]{1,0:T(8,128)(2,1)S(1)}, u32[]{:S(2)}, u32[]{:S(2)}) %collective-permute-start.6) | collective-permute-done | bytes 147488 | tf_op jit(solution)/shard_map/ppermute | solution.py:43
  59.6 1.9 %collective-permute-done.5.two = bf16[576,128]{1,0:T(8,128)(2,1)S(1)} collective-permute-done((bf16[576,128]{1,0:T(8,128)(2,1)S(1)}, bf16[576,128]{1,0:T(8,128)(2,1)S(1)}, u32[]{:S(2)}, u32[]{:S(2)}) %collective-permute-start.5) | collective-permute-done | bytes 147488 | tf_op jit(solution)/shard_map/ppermute | solution.py:43
  61.5 1.5 collective-permute-done.4.one
  63.0 7.6 %shard_map.63 = (bf16[128,4096]{1,0:T(8,128)(2,1)S(1)}, f32[32,128]{1,0:T(8,128)S(1)}, f32[72,640]{1,0:T(8,128)S(1)}, f32[72,640]{1,0:T(8,128)S(1)}) custom-call(bf16[1280,4096]{1,0:T(8,128)(2,1)} %events_ref.9, f32[32,128]{1,0:T(8,128)S(1)} %bitcast.9, bf16[576,128]{1,0:T(8,128)(2,1)S(1)} %shard_map.62.own, ...), custom_call_target="tpu_custom_call" | custom-call | bytes 14400000 | tf_op jit(solution)/shard_map/pallas_call | solution.py:30
  70.5 5.3 %collective-permute-start.7 = (f32[72,640]{1,0:T(8,128)S(1)}, f32[72,640]{1,0:T(8,128)S(1)}, u32[]{:S(2)}, u32[]{:S(2)}) collective-permute-start(f32[72,640]{1,0:T(8,128)S(1)} %get-tuple-element.32), channel_id=1, source_target_pairs={{0,1},{1,0},{2,3},{3,2},{4,5},{5,4},{6,7},{7,6},{8,9},{9,8},{10,11... | collective-permute-start | bytes 552968 | tf_op jit(solution)/shard_map/ppermute | solution.py:52
  75.9 1.1 collective-permute-done.7.other
  77.0 1.3 collective-permute-start.10
  78.3 0.3 collective-permute-start.9
  78.6 0.7 collective-permute-start.8
  79.3 1.8 %collective-permute-done.10.three = bf16[80,640]{1,0:T(8,128)(2,1)S(1)} collective-permute-done((bf16[80,640]{1,0:T(8,128)(2,1)S(1)}, bf16[80,640]{1,0:T(8,128)(2,1)S(1)}, u32[]{:S(2)}, u32[]{:S(2)}) %collective-permute-start.10) | collective-permute-done | bytes 102432 | tf_op jit(solution)/shard_map/ppermute | solution.py:48
  81.2 2.2 %collective-permute-done.9.two = bf16[80,640]{1,0:T(8,128)(2,1)S(1)} collective-permute-done((bf16[80,640]{1,0:T(8,128)(2,1)S(1)}, bf16[80,640]{1,0:T(8,128)(2,1)S(1)}, u32[]{:S(2)}, u32[]{:S(2)}) %collective-permute-start.9) | collective-permute-done | bytes 102432 | tf_op jit(solution)/shard_map/ppermute | solution.py:48
  83.4 3.3 %collective-permute-done.8.one = bf16[80,640]{1,0:T(8,128)(2,1)S(1)} collective-permute-done((bf16[80,640]{1,0:T(8,128)(2,1)S(1)}, bf16[80,640]{1,0:T(8,128)(2,1)S(1)}, u32[]{:S(2)}, u32[]{:S(2)}) %collective-permute-start.8) | collective-permute-done | bytes 102432 | tf_op jit(solution)/shard_map/ppermute | solution.py:48
  86.7 0.1 shard_map.65
  86.8 0.7 collective-permute-start.11
  87.4 1.0 collective-permute-done.11.theirs_ref
  88.5 4.8 %shard_map.66 = (f32[512,128]{1,0:T(8,128)S(1)}, f32[8,128]{1,0:T(8,128)S(1)}, bf16[528,128]{1,0:T(8,128)(2,1)S(1)}, bf16[528,128]{1,0:T(8,128)(2,1)S(1)}, bf16[528,128]{1,0:T(8,128)(2,1)S(1)}) custom-call(bf16[1280,4096]{1,0:T(8,128)(2,1)} %events_ref.9, f32[64,640]{1,0:T(8,128)S(1)} %get-tuple-element.33.mine_ref.scores_ref, ...), custom_call_target="tpu_custom_call" | custom-call | bytes 14400000 | tf_op jit(solution)/shard_map/pallas_call | solution.py:30
  93.3 0.1 collective-permute-start.12
  93.3 1.5 collective-permute-start.13
  94.8 1.7 %collective-permute-start.14 = (bf16[528,128]{1,0:T(8,128)(2,1)S(1)}, bf16[528,128]{1,0:T(8,128)(2,1)S(1)}, u32[]{:S(2)}, u32[]{:S(2)}) collective-permute-start(bf16[528,128]{1,0:T(8,128)(2,1)S(1)} %get-tuple-element.39), channel_id=1, source_target_pairs={{0,192},{8,200},{16,208},{24,216},{32,224},{40,232},{48,240},{56,2... | collective-permute-start | bytes 405512 | tf_op jit(solution)/shard_map/ppermute | solution.py:462
  96.5 5.7 %collective-permute-done.12.one = bf16[528,128]{1,0:T(8,128)(2,1)S(1)} collective-permute-done((bf16[528,128]{1,0:T(8,128)(2,1)S(1)}, bf16[528,128]{1,0:T(8,128)(2,1)S(1)}, u32[]{:S(2)}, u32[]{:S(2)}) %collective-permute-start.12) | collective-permute-done | bytes 135200 | tf_op jit(solution)/shard_map/ppermute | solution.py:462
  102.2 0.3 collective-permute-done.14.three
  102.5 0.1 shard_map.67
  102.6 10.6 %all_to_all.26.in_ref = bf16[8,72,128]{2,1,0:T(8,128)(2,1)S(1)} all-to-all(bf16[8,72,128]{2,1,0:T(8,128)(2,1)S(1)} %shard_map.67), channel_id=1, replica_groups={{0,8,16,24,32,40,48,56},{64,72,80,88,96,104,112,120},{128,136,144,152,1..., dimensions={0} | all-to-all | bytes 294912 | tf_op jit(solution)/shard_map/all_to_all | solution.py:57
  113.2 0.1 shard_map.68
  113.3 10.6 %all_to_all.27.own = bf16[8,72,128]{2,1,0:T(8,128)(2,1)S(1)} all-to-all(bf16[8,72,128]{2,1,0:T(8,128)(2,1)S(1)} %get-tuple-element.41), channel_id=1, replica_groups={{0,8,16,24,32,40,48,56},{64,72,80,88,96,104,112,120},{128,136,144,152,1..., dimensions={0} | all-to-all | bytes 294912 | tf_op jit(solution)/shard_map/all_to_all | solution.py:57
  123.9 3.7 %collective-permute-start.17 = (bf16[8,72,128]{2,1,0:T(8,128)(2,1)S(1)}, bf16[8,72,128]{2,1,0:T(8,128)(2,1)S(1)}, u32[]{:S(2)}, u32[]{:S(2)}) collective-permute-start(bf16[8,72,128]{2,1,0:T(8,128)(2,1)S(1)} %all_to_all.27.own), channel_id=1, source_target_pairs={{0,192},{8,200},{16,208},{24,216},{32,224},{40,232},{48,240},{56,2... | collective-permute-start | bytes 442376 | tf_op jit(solution)/shard_map/ppermute | solution.py:43
  127.5 0.6 collective-permute-start.15
  128.1 3.1 %collective-permute-done.17.three = bf16[8,72,128]{2,1,0:T(8,128)(2,1)S(1)} collective-permute-done((bf16[8,72,128]{2,1,0:T(8,128)(2,1)S(1)}, bf16[8,72,128]{2,1,0:T(8,128)(2,1)S(1)}, u32[]{:S(2)}, u32[]{:S(2)}) %collective-permute-start.17) | collective-permute-done | bytes 147488 | tf_op jit(solution)/shard_map/ppermute | solution.py:43
  131.2 1.9 %collective-permute-done.16.two = bf16[8,72,128]{2,1,0:T(8,128)(2,1)S(1)} collective-permute-done((bf16[8,72,128]{2,1,0:T(8,128)(2,1)S(1)}, bf16[8,72,128]{2,1,0:T(8,128)(2,1)S(1)}, u32[]{:S(2)}, u32[]{:S(2)}) %collective-permute-start.16) | collective-permute-done | bytes 147488 | tf_op jit(solution)/shard_map/ppermute | solution.py:43
  133.1 1.2 collective-permute-done.15.one
  134.3 7.8 %shard_map.69 = (f32[72,640]{1,0:T(8,128)S(1)}, f32[72,640]{1,0:T(8,128)S(1)}, f32[32,128]{1,0:T(8,128)S(1)}) custom-call(bf16[1280,4096]{1,0:T(8,128)(2,1)} %events_ref.9, bf16[128,4096]{1,0:T(8,128)(2,1)S(1)} %get-tuple-element.29.rhs_ref, f32[32,128]{1,0:T(8,128)S(1)} %get-tuple-element.30.grad_ref, bf16[8,72,128]{2,1,0:T(8,128)(2,1)S(1)} %all_to_all.27.own, ...), custom_call_target="tpu_custom_call" | custom-call | bytes 14400000 | tf_op jit(solution)/shard_map/pallas_call | solution.py:30
  142.1 4.7 %collective-permute-start.18 = (f32[72,640]{1,0:T(8,128)S(1)}, f32[72,640]{1,0:T(8,128)S(1)}, u32[]{:S(2)}, u32[]{:S(2)}) collective-permute-start(f32[72,640]{1,0:T(8,128)S(1)} %get-tuple-element.43), channel_id=1, source_target_pairs={{0,1},{1,0},{2,3},{3,2},{4,5},{5,4},{6,7},{7,6},{8,9},{9,8},{10,11... | collective-permute-start | bytes 552968 | tf_op jit(solution)/shard_map/ppermute | solution.py:52
  146.8 1.1 collective-permute-done.18.other
  147.9 0.4 collective-permute-start.21
  148.3 0.4 collective-permute-start.20
  148.7 0.8 collective-permute-start.19
  149.5 2.6 %collective-permute-done.21.three = bf16[80,640]{1,0:T(8,128)(2,1)S(1)} collective-permute-done((bf16[80,640]{1,0:T(8,128)(2,1)S(1)}, bf16[80,640]{1,0:T(8,128)(2,1)S(1)}, u32[]{:S(2)}, u32[]{:S(2)}) %collective-permute-start.21) | collective-permute-done | bytes 102432 | tf_op jit(solution)/shard_map/ppermute | solution.py:48
  152.1 1.3 collective-permute-done.20.two
  153.4 3.4 %collective-permute-done.19.one = bf16[80,640]{1,0:T(8,128)(2,1)S(1)} collective-permute-done((bf16[80,640]{1,0:T(8,128)(2,1)S(1)}, bf16[80,640]{1,0:T(8,128)(2,1)S(1)}, u32[]{:S(2)}, u32[]{:S(2)}) %collective-permute-start.19) | collective-permute-done | bytes 102432 | tf_op jit(solution)/shard_map/ppermute | solution.py:48
  156.8 0.2 shard_map.71
  157.0 0.6 collective-permute-start.22
  157.6 0.8 collective-permute-done.22
  158.4 11.6 %all_to_all.28.tails_ref = f32[32,1,128]{2,1,0:T(1,128)S(1)} all-to-all(f32[32,1,128]{2,1,0:T(1,128)S(1)} %broadcast_in_dim.9), channel_id=1, replica_groups=mesh['event'=32,'feat'=8] {'event'}, dimensions={0} | all-to-all | bytes 32768 | tf_op jit(solution)/shard_map/all_to_all | solution.py:492
  170.0 0.8 shard_map.72
  170.8 0.5 slice_bitcast_fusion
  (14 shorter events, 0.1 us)
Async XLA Ops:
  0.6 0.7 copy-start
  1.3 0.7 copy-start.3
  2.0 30.9 %copy-start.2 = (s32[1280]{0:T(1024)S(1)}, s32[1280]{0:T(1024)}, u32[]{:S(2)}) copy-start(s32[1280]{0:T(1024)} %param.5) | copy-start | bytes 15364
  2.0 61.0 %copy-start.1 = (f32[4096]{0:T(1024)S(1)}, f32[4096]{0:T(1024)}, u32[]{:S(2)}) copy-start(f32[4096]{0:T(1024)} %param.6) | copy-start | bytes 49156
  11.9 26.3 %all-to-all-start = ((bf16[32,64,128]{2,1,0:T(8,128)(2,1)}), bf16[32,64,128]{2,1,0:T(8,128)(2,1)S(1)}, u32[]{:S(2)}, u32[]{:S(2)}) async-start(bf16[32,64,128]{2,1,0:T(8,128)(2,1)} %get-tuple-element.26), calls=%async_computation | async-start | bytes 1048576 | tf_op jit(solution)/shard_map/all_to_all | solution.py:415
  23.9 1.9 %collective-permute-start = (f32[10,128]{1,0:T(8,128)S(1)}, f32[10,128]{1,0:T(8,128)S(1)}, u32[]{:S(2)}, u32[]{:S(2)}) collective-permute-start(f32[10,128]{1,0:T(8,128)S(1)} %get-tuple-element.27), channel_id=1, source_target_pairs={{0,1},{1,0},{2,3},{3,2},{4,5},{5,4},{6,7},{7,6},{8,9},{9,8},{10,11... | collective-permute-start | bytes 15368 | tf_op jit(solution)/shard_map/ppermute | solution.py:52
  25.7 3.8 %collective-permute-start.3 = (f32[10,128]{1,0:T(8,128)S(1)}, f32[10,128]{1,0:T(8,128)S(1)}, u32[]{:S(2)}, u32[]{:S(2)}) collective-permute-start(f32[10,128]{1,0:T(8,128)S(1)} %add.6.own), channel_id=1, source_target_pairs={{0,6},{1,7},{2,0},{3,1},{4,2},{5,3},{6,4},{7,5},{8,14},{9,15},{10,... | collective-permute-start | bytes 15368 | tf_op jit(solution)/shard_map/ppermute | solution.py:48
  28.5 4.3 %collective-permute-start.2 = (f32[10,128]{1,0:T(8,128)S(1)}, f32[10,128]{1,0:T(8,128)S(1)}, u32[]{:S(2)}, u32[]{:S(2)}) collective-permute-start(f32[10,128]{1,0:T(8,128)S(1)} %add.6.own), channel_id=1, source_target_pairs={{0,4},{1,5},{2,6},{3,7},{4,0},{5,1},{6,2},{7,3},{8,12},{9,13},{10,... | collective-permute-start | bytes 15368 | tf_op jit(solution)/shard_map/ppermute | solution.py:48
  28.8 4.0 %collective-permute-start.1 = (f32[10,128]{1,0:T(8,128)S(1)}, f32[10,128]{1,0:T(8,128)S(1)}, u32[]{:S(2)}, u32[]{:S(2)}) collective-permute-start(f32[10,128]{1,0:T(8,128)S(1)} %add.6.own), channel_id=1, source_target_pairs={{0,2},{1,3},{2,4},{3,5},{4,6},{5,7},{6,0},{7,1},{8,10},{9,11},{10,... | collective-permute-start | bytes 15368 | tf_op jit(solution)/shard_map/ppermute | solution.py:48
  53.4 6.2 %collective-permute-start.6 = (bf16[576,128]{1,0:T(8,128)(2,1)S(1)}, bf16[576,128]{1,0:T(8,128)(2,1)S(1)}, u32[]{:S(2)}, u32[]{:S(2)}) collective-permute-start(bf16[576,128]{1,0:T(8,128)(2,1)S(1)} %shard_map.62.own), channel_id=1, source_target_pairs={{0,192},{8,200},{16,208},{24,216},{32,224},{40,232},{48,240},{56,2... | collective-permute-start | bytes 442376 | tf_op jit(solution)/shard_map/ppermute | solution.py:43
  55.9 5.6 %collective-permute-start.5 = (bf16[576,128]{1,0:T(8,128)(2,1)S(1)}, bf16[576,128]{1,0:T(8,128)(2,1)S(1)}, u32[]{:S(2)}, u32[]{:S(2)}) collective-permute-start(bf16[576,128]{1,0:T(8,128)(2,1)S(1)} %shard_map.62.own), channel_id=1, source_target_pairs={{0,128},{8,136},{16,144},{24,152},{32,160},{40,168},{48,176},{56,1... | collective-permute-start | bytes 442376 | tf_op jit(solution)/shard_map/ppermute | solution.py:43
  56.4 6.6 %collective-permute-start.4 = (bf16[576,128]{1,0:T(8,128)(2,1)S(1)}, bf16[576,128]{1,0:T(8,128)(2,1)S(1)}, u32[]{:S(2)}, u32[]{:S(2)}) collective-permute-start(bf16[576,128]{1,0:T(8,128)(2,1)S(1)} %shard_map.62.own), channel_id=1, source_target_pairs={{0,64},{8,72},{16,80},{24,88},{32,96},{40,104},{48,112},{56,120},{... | collective-permute-start | bytes 442376 | tf_op jit(solution)/shard_map/ppermute | solution.py:43
  70.5 6.4 %collective-permute-start.7 = (f32[72,640]{1,0:T(8,128)S(1)}, f32[72,640]{1,0:T(8,128)S(1)}, u32[]{:S(2)}, u32[]{:S(2)}) collective-permute-start(f32[72,640]{1,0:T(8,128)S(1)} %get-tuple-element.32), channel_id=1, source_target_pairs={{0,1},{1,0},{2,3},{3,2},{4,5},{5,4},{6,7},{7,6},{8,9},{9,8},{10,11... | collective-permute-start | bytes 552968 | tf_op jit(solution)/shard_map/ppermute | solution.py:52
  77.0 4.2 %collective-permute-start.10 = (bf16[80,640]{1,0:T(8,128)(2,1)S(1)}, bf16[80,640]{1,0:T(8,128)(2,1)S(1)}, u32[]{:S(2)}, u32[]{:S(2)}) collective-permute-start(bf16[80,640]{1,0:T(8,128)(2,1)S(1)} %shard_map.64.own), channel_id=1, source_target_pairs={{0,6},{1,7},{2,0},{3,1},{4,2},{5,3},{6,4},{7,5},{8,14},{9,15},{10,... | collective-permute-start | bytes 307208 | tf_op jit(solution)/shard_map/ppermute | solution.py:48
  78.3 5.1 %collective-permute-start.9 = (bf16[80,640]{1,0:T(8,128)(2,1)S(1)}, bf16[80,640]{1,0:T(8,128)(2,1)S(1)}, u32[]{:S(2)}, u32[]{:S(2)}) collective-permute-start(bf16[80,640]{1,0:T(8,128)(2,1)S(1)} %shard_map.64.own), channel_id=1, source_target_pairs={{0,4},{1,5},{2,6},{3,7},{4,0},{5,1},{6,2},{7,3},{8,12},{9,13},{10,... | collective-permute-start | bytes 307208 | tf_op jit(solution)/shard_map/ppermute | solution.py:48
  78.6 8.1 %collective-permute-start.8 = (bf16[80,640]{1,0:T(8,128)(2,1)S(1)}, bf16[80,640]{1,0:T(8,128)(2,1)S(1)}, u32[]{:S(2)}, u32[]{:S(2)}) collective-permute-start(bf16[80,640]{1,0:T(8,128)(2,1)S(1)} %shard_map.64.own), channel_id=1, source_target_pairs={{0,2},{1,3},{2,4},{3,5},{4,6},{5,7},{6,0},{7,1},{8,10},{9,11},{10,... | collective-permute-start | bytes 307208 | tf_op jit(solution)/shard_map/ppermute | solution.py:48
  86.8 1.7 collective-permute-start.11
  93.3 9.0 %collective-permute-start.12 = (bf16[528,128]{1,0:T(8,128)(2,1)S(1)}, bf16[528,128]{1,0:T(8,128)(2,1)S(1)}, u32[]{:S(2)}, u32[]{:S(2)}) collective-permute-start(bf16[528,128]{1,0:T(8,128)(2,1)S(1)} %get-tuple-element.37), channel_id=1, source_target_pairs={{0,64},{8,72},{16,80},{24,88},{32,96},{40,104},{48,112},{56,120},{... | collective-permute-start | bytes 405512 | tf_op jit(solution)/shard_map/ppermute | solution.py:462
  93.3 8.9 %collective-permute-start.13 = (bf16[528,128]{1,0:T(8,128)(2,1)S(1)}, bf16[528,128]{1,0:T(8,128)(2,1)S(1)}, u32[]{:S(2)}, u32[]{:S(2)}) collective-permute-start(bf16[528,128]{1,0:T(8,128)(2,1)S(1)} %get-tuple-element.38), channel_id=1, source_target_pairs={{0,128},{8,136},{16,144},{24,152},{32,160},{40,168},{48,176},{56,1... | collective-permute-start | bytes 405512 | tf_op jit(solution)/shard_map/ppermute | solution.py:462
  94.8 7.7 %collective-permute-start.14 = (bf16[528,128]{1,0:T(8,128)(2,1)S(1)}, bf16[528,128]{1,0:T(8,128)(2,1)S(1)}, u32[]{:S(2)}, u32[]{:S(2)}) collective-permute-start(bf16[528,128]{1,0:T(8,128)(2,1)S(1)} %get-tuple-element.39), channel_id=1, source_target_pairs={{0,192},{8,200},{16,208},{24,216},{32,224},{40,232},{48,240},{56,2... | collective-permute-start | bytes 405512 | tf_op jit(solution)/shard_map/ppermute | solution.py:462
  123.9 7.3 %collective-permute-start.17 = (bf16[8,72,128]{2,1,0:T(8,128)(2,1)S(1)}, bf16[8,72,128]{2,1,0:T(8,128)(2,1)S(1)}, u32[]{:S(2)}, u32[]{:S(2)}) collective-permute-start(bf16[8,72,128]{2,1,0:T(8,128)(2,1)S(1)} %all_to_all.27.own), channel_id=1, source_target_pairs={{0,192},{8,200},{16,208},{24,216},{32,224},{40,232},{48,240},{56,2... | collective-permute-start | bytes 442376 | tf_op jit(solution)/shard_map/ppermute | solution.py:43
  127.5 5.6 %collective-permute-start.16 = (bf16[8,72,128]{2,1,0:T(8,128)(2,1)S(1)}, bf16[8,72,128]{2,1,0:T(8,128)(2,1)S(1)}, u32[]{:S(2)}, u32[]{:S(2)}) collective-permute-start(bf16[8,72,128]{2,1,0:T(8,128)(2,1)S(1)} %all_to_all.27.own), channel_id=1, source_target_pairs={{0,128},{8,136},{16,144},{24,152},{32,160},{40,168},{48,176},{56,1... | collective-permute-start | bytes 442376 | tf_op jit(solution)/shard_map/ppermute | solution.py:43
  127.5 6.8 %collective-permute-start.15 = (bf16[8,72,128]{2,1,0:T(8,128)(2,1)S(1)}, bf16[8,72,128]{2,1,0:T(8,128)(2,1)S(1)}, u32[]{:S(2)}, u32[]{:S(2)}) collective-permute-start(bf16[8,72,128]{2,1,0:T(8,128)(2,1)S(1)} %all_to_all.27.own), channel_id=1, source_target_pairs={{0,64},{8,72},{16,80},{24,88},{32,96},{40,104},{48,112},{56,120},{... | collective-permute-start | bytes 442376 | tf_op jit(solution)/shard_map/ppermute | solution.py:43
  142.1 5.8 %collective-permute-start.18 = (f32[72,640]{1,0:T(8,128)S(1)}, f32[72,640]{1,0:T(8,128)S(1)}, u32[]{:S(2)}, u32[]{:S(2)}) collective-permute-start(f32[72,640]{1,0:T(8,128)S(1)} %get-tuple-element.43), channel_id=1, source_target_pairs={{0,1},{1,0},{2,3},{3,2},{4,5},{5,4},{6,7},{7,6},{8,9},{9,8},{10,11... | collective-permute-start | bytes 552968 | tf_op jit(solution)/shard_map/ppermute | solution.py:52
  147.9 4.2 %collective-permute-start.21 = (bf16[80,640]{1,0:T(8,128)(2,1)S(1)}, bf16[80,640]{1,0:T(8,128)(2,1)S(1)}, u32[]{:S(2)}, u32[]{:S(2)}) collective-permute-start(bf16[80,640]{1,0:T(8,128)(2,1)S(1)} %shard_map.70.own), channel_id=1, source_target_pairs={{0,6},{1,7},{2,0},{3,1},{4,2},{5,3},{6,4},{7,5},{8,14},{9,15},{10,... | collective-permute-start | bytes 307208 | tf_op jit(solution)/shard_map/ppermute | solution.py:48
  148.3 5.1 %collective-permute-start.20 = (bf16[80,640]{1,0:T(8,128)(2,1)S(1)}, bf16[80,640]{1,0:T(8,128)(2,1)S(1)}, u32[]{:S(2)}, u32[]{:S(2)}) collective-permute-start(bf16[80,640]{1,0:T(8,128)(2,1)S(1)} %shard_map.70.own), channel_id=1, source_target_pairs={{0,4},{1,5},{2,6},{3,7},{4,0},{5,1},{6,2},{7,3},{8,12},{9,13},{10,... | collective-permute-start | bytes 307208 | tf_op jit(solution)/shard_map/ppermute | solution.py:48
  148.7 8.1 %collective-permute-start.19 = (bf16[80,640]{1,0:T(8,128)(2,1)S(1)}, bf16[80,640]{1,0:T(8,128)(2,1)S(1)}, u32[]{:S(2)}, u32[]{:S(2)}) collective-permute-start(bf16[80,640]{1,0:T(8,128)(2,1)S(1)} %shard_map.70.own), channel_id=1, source_target_pairs={{0,2},{1,3},{2,4},{3,5},{4,6},{5,7},{6,0},{7,1},{8,10},{9,11},{10,... | collective-permute-start | bytes 307208 | tf_op jit(solution)/shard_map/ppermute | solution.py:48
  157.0 1.4 collective-permute-start.22

commit v4 on v3

--- a/solution.py
+++ b/solution.py
@@ -112,19 +112,38 @@
             self.copies[i + WINDOW].start()
 
 
-def row_stream(events_ref, held, sems, starts):
-    pieces = [
-        (events_ref.at[pl.ds(pl.multiple_of(start, 128), 128), :], held.at[pl.ds(i * 128, 128), :])
-        for i, start in enumerate(starts)
-    ]
-    return Stream(pieces, sems)
-
-
-def column_stream(events_ref, held, sems, starts):
-    pieces = [
-        (events_ref.at[:, pl.ds(pl.multiple_of(start, 512), 512)], held.at[i]) for i, start in enumerate(starts)
-    ]
-    return Stream(pieces, sems)
+class Rows:
+    def __init__(self, events_ref, held, sems, starts):
+        self.events, self.held = events_ref, held
+        self.starts = [pl.multiple_of(start, 128) for start in starts]
+        if held is not None:
+            pieces = [
+                (events_ref.at[pl.ds(start, 128), :], held.at[pl.ds(i * 128, 128), :])
+                for i, start in enumerate(self.starts)
+            ]
+            self.stream = Stream(pieces, sems)
+
+    def take(self, first, count):
+        if self.held is None:
+            return self.events[pl.ds(self.starts[first], count * 128), :]
+        for i in range(count):
+            self.stream.take(first + i)
+        return self.held[first * 128 : (first + count) * 128, :]
+
+
+class Columns:
+    def __init__(self, events_ref, held, sems, starts):
+        self.events, self.held = events_ref, held
+        self.starts = [pl.multiple_of(start, 512) for start in starts]
+        if held is not None:
+            pieces = [(events_ref.at[:, pl.ds(start, 512)], held.at[i]) for i, start in enumerate(self.starts)]
+            self.stream = Stream(pieces, sems)
+
+    def take(self, i):
+        if self.held is None:
+            return self.events[:, pl.ds(self.starts[i], 512)]
+        self.stream.take(i)
+        return self.held[i]
 
 
 def place():
@@ -132,19 +151,24 @@
     return lax.div(event, ZN), lax.rem(event, ZN), lax.rem(lax.axis_index("feat"), CN)
 
 
-def first_kernel(contexts_ref, w_ref, events_ref, margin_ref, out_ref, rhs, rows, held, sems):
-    pieces = row_stream(events_ref, held, sems, [i * 128 for i in range(COUNT // 128)])
-    rhs[:16, :] = jnp.broadcast_to(w_ref[...], (16, TILES * 128)).astype(BF16)
-    rhs[16:, :] = jnp.zeros((112, TILES * 128), BF16)
+def first_kernel(contexts_ref, w_ref, events_ref, margin_ref, out_ref, w, rows, held, sems, w_sem):
+    pieces = Rows(events_ref, held, sems, [i * 128 for i in range(COUNT // 128)])
+    w_copy = pltpu.make_async_copy(w_ref, w, w_sem)
+    w_copy.start()
     rows[...] = jnp.zeros_like(rows)
-    for c in range(0, COUNT // 128, 2):
-        pieces.take(c)
-        pieces.take(c + 1)
-        part = lax.dot_general(
-            held[c * 128 : (c + 2) * 128, :], rhs[...], ACROSS, preferred_element_type=F32
-        )
-        for u in range(2):
-            margin_ref[c + u : c + u + 1, :] = jnp.transpose(part[u * 128 : (u + 1) * 128])[:1]
+    w_copy.wait()
+    w[...] = w[...].astype(BF16).astype(F32)
+    for c in range(COUNT // 128):
+        pieces.take(c, 1)
+        sums = []
+        for r in range(c * 128, (c + 1) * 128, 16):
+            total = jnp.zeros((16, 128), F32)
+            for t in range(TILES):
+                at = slice(t * 128, (t + 1) * 128)
+                total = total + held[r : r + 16, at].astype(F32) * w[:, at]
+            sums.append(total)
+        turned = jnp.transpose(jnp.concatenate(sums, axis=0))
+        margin_ref[c : c + 1, :] = jnp.sum(turned, axis=0, keepdims=True)
 
     base = lax.axis_index("event") * COUNT
 
@@ -163,8 +187,8 @@
         out_ref[t] = rows[:, t * 128 : (t + 1) * 128].astype(BF16)
 
 
-def gradient_kernel(events_ref, own, one, two, three, labels_ref, rate_ref, grad_ref, errs, held, sems):
-    pieces = column_stream(events_ref, held, sems, [c * 512 for c in range(8)])
+def gradient_kernel(events_ref, own, one, two, three, labels_ref, rate_ref, grad_ref, errs, held=None, sems=None):
+    pieces = Columns(events_ref, held, sems, [c * 512 for c in range(8)])
     margin = four(own[...], one[...], two[...], three[...])
     chance = jax.nn.sigmoid(margin)
     rate = chance * (1.0 - chance)
@@ -176,8 +200,7 @@
         rate_ref[:, at] = rate[i : i + 1]
         errs[:, at] = stacked([lead[i : i + 1], rest[i : i + 1]], 16).astype(BF16)
     for c in range(8):
-        pieces.take(c)
-        part = jnp.dot(errs[...], held[c], preferred_element_type=F32)
+        part = jnp.dot(errs[...], pieces.take(c), preferred_element_type=F32)
         line = part[:1] + part[1:2]
         for u in range(4):
             grad_ref[c * 4 + u : c * 4 + u + 1, :] = line[:, u * 128 : (u + 1) * 128]
@@ -206,32 +229,33 @@
 
 def half_stream(events_ref, held, sems, core):
     starts = [half * HALF + i * 128 for half in (1 - core, core) for i in range(HALF // 128)]
-    return row_stream(events_ref, held, sems, starts)
-
-
-def put_scores(pieces, held, rhs, other_ref, own_ref, lines):
+    return Rows(events_ref, held, sems, starts)
+
+
+def put_scores(pieces, rhs, other_ref, own_ref, lines):
     for first, out_ref in ((0, other_ref), (HALF // 128, own_ref)):
         for at, size in ((0, 2), (2, 3)):
-            for i in range(size):
-                pieces.take(first + at + i)
-            events = held[(first + at) * 128 : (first + at + size) * 128, :]
-            part = lax.dot_general(events, rhs[...], ACROSS, preferred_element_type=F32)
+            part = jnp.dot(pieces.take(first + at, size), rhs[...], preferred_element_type=F32)
             for t in range(size):
                 columns = slice((at + t) * 128, (at + t + 1) * 128)
                 out_ref[:ROWS, columns] = joined(jnp.transpose(part[t * 128 : (t + 1) * 128]))
                 out_ref[ROWS:, columns] = lines if at + t == 0 else jnp.zeros_like(lines)
 
 
+def turned(top, rest):
+    below = jnp.where(row_is(top.shape, 0), rest.astype(F32), 0.0)
+    return jnp.transpose(jnp.concatenate([top, below], axis=0)).astype(BF16)
+
+
 def scores_kernel(
-    events_ref, w_ref, own, one, two, three, rhs_ref, grad_ref, other_ref, mine_ref, held, sems
+    events_ref, w_ref, own, one, two, three, rhs_ref, grad_ref, other_ref, mine_ref, rhs, held=None, sems=None
 ):
     x, _, core = place()
     pieces = half_stream(events_ref, held, sems, core)
-    top = QUARTER * ROWS
-    grads = [p[top : top + TILES, :].astype(F32) + p[top + TILES :, :].astype(F32) for p in (own, one, two, three)]
+    tail = QUARTER * ROWS
+    grads = [p[tail : tail + TILES, :].astype(F32) + p[tail + TILES :, :].astype(F32) for p in (own, one, two, three)]
     grad_ref[...] = four(*grads) + LAMBDA * w_ref[...]
     norm = jnp.zeros((ROWS, 128), F32)
-    rhs_ref[ROWS:, :] = jnp.zeros((128 - ROWS, TILES * 128), BF16)
     for k, part in enumerate((own, one, two, three)):
         quarter = lax.rem(x + XN - k, XN)
         for t in range(QUARTER):
@@ -243,10 +267,11 @@
             exact = jnp.where(last, grad, values)
             norm = norm + exact * exact
             at = pl.ds(pl.multiple_of(tile * 128, 128), 128)
-            rhs_ref[:ROWS, at] = jnp.where(last, lead.astype(F32), values).astype(BF16)
-            rhs_ref[ROWS : ROWS + 16, at] = stacked([rest], 16).astype(BF16)
+            top = jnp.where(last, lead.astype(F32), values)
+            rhs_ref[:, at] = top.astype(BF16)
+            rhs[at, :] = turned(top, rest)
     line = line_sums(norm, jnp.zeros_like(norm))
-    put_scores(pieces, held, rhs_ref, other_ref, mine_ref, stacked([line], 8))
+    put_scores(pieces, rhs, other_ref, mine_ref, stacked([line], 8))
 
 
 def pack_kernel(own, other, out_ref):
@@ -272,12 +297,12 @@
 
 
 def hessian_kernel(
-    events_ref, mine_ref, theirs_ref, rate_ref, own_ref, curv_ref, one_ref, two_ref, three_ref, q, held, sems
+    events_ref, mine_ref, theirs_ref, rate_ref, own_ref, curv_ref, one_ref, two_ref, three_ref, q, held=None, sems=None
 ):
     x, _, core = place()
     outs = ((2, two_ref), (1, one_ref), (3, three_ref), (0, own_ref))
     starts = [lax.rem(x + k, XN) * QUARTER * 128 + part * 512 for k, _ in outs for part in range(2)]
-    pieces = column_stream(events_ref, held, sems, starts)
+    pieces = Columns(events_ref, held, sems, starts)
     curv = jnp.zeros((ROWS, 128), F32)
     for half in range(2):
         scores = jnp.where(core == half, mine_ref[...], theirs_ref[...])
@@ -292,8 +317,7 @@
     for i, (k, out_ref) in enumerate(outs):
         rests = []
         for part in range(2):
-            pieces.take(2 * i + part)
-            total = joined(jnp.dot(q[...], held[2 * i + part], preferred_element_type=F32))
+            total = joined(jnp.dot(q[...], pieces.take(2 * i + part), preferred_element_type=F32))
             for u in range(4):
                 t = part * 4 + u
                 values = total[:, u * 128 : (u + 1) * 128]
@@ -332,7 +356,7 @@
     square = (ROWS, 128)
     eye = lax.broadcasted_iota(jnp.int32, square, 0) == lax.broadcasted_iota(jnp.int32, square, 1)
     column = jnp.sum(jnp.where(eye, step, 0.0), axis=1, keepdims=True)
-    right = rhs_ref[:ROWS, pl.ds(pl.multiple_of(tile * 128, 128), 128)].astype(F32)
+    right = rhs_ref[:, pl.ds(pl.multiple_of(tile * 128, 128), 128)].astype(F32)
     right = jnp.where(row_is(square, ROWS - 1), grad_ref[pl.ds(tile, 1), :], right)
     residual = right - column * (joined(total) + LAMBDA * right)
     lead = residual.astype(BF16)
@@ -344,13 +368,12 @@
 
 
 def second_kernel(
-    events_ref, rhs_ref, grad_ref, own, one, two, three, other_ref, mine_ref, first_ref, res, held, sems
+    events_ref, rhs_ref, grad_ref, own, one, two, three, other_ref, mine_ref, first_ref, res, held=None, sems=None
 ):
     x, _, core = place()
     pieces = half_stream(events_ref, held, sems, core)
     norm = jnp.zeros((ROWS, 128), F32)
     cross = jnp.zeros((ROWS, 128), F32)
-    res[ROWS:, :] = jnp.zeros((128 - ROWS, TILES * 128), BF16)
     for k, part in enumerate((own, one, two, three)):
         quarter = lax.rem(x + XN - k, XN)
         for t in range(QUARTER):
@@ -358,16 +381,16 @@
             at = pl.ds(pl.multiple_of(tile * 128, 128), 128)
             rows = part[t]
             values = joined(rows.astype(F32))
-            right = rhs_ref[:ROWS, at].astype(F32)
+            right = rhs_ref[:, at].astype(F32)
             right = jnp.where(row_is(right.shape, ROWS - 1), grad_ref[pl.ds(tile, 1), :], right)
             norm = norm + values * values
             cross = cross + values * right
             first_ref[pl.ds(tile, 1), :] = values[ROWS - 1 :]
-            res[:ROWS, at] = rows[:ROWS]
-            res[ROWS : ROWS + 16, at] = stacked([rows[ROWS:].astype(F32)[:1]], 16).astype(BF16)
+            exact = rows.astype(F32)
+            res[at, :] = turned(exact[:ROWS], exact[ROWS : ROWS + 1])
     line = line_sums(norm, cross)
     lines = stacked([line, pltpu.roll(line, ROWS, 1)], 8)
-    put_scores(pieces, held, res, other_ref, mine_ref, lines)
+    put_scores(pieces, res, other_ref, mine_ref, lines)
 
 
 def tail_kernel(own, one, two, three, scores_ref, rate_ref, tail_ref, lines_ref):
@@ -389,7 +412,8 @@
     curvature = square + 2.0 * ratio * mixed + ratio * ratio * curv
     curvature = curvature + LAMBDA * (norm_next + 2.0 * ratio * cross + ratio * ratio * norm)
     step_two = norm_next / curvature
-    widths_ref[...] = step_one * norm + step_two * (cross + ratio * norm)
+    widths = step_one * norm + step_two * (cross + ratio * norm)
+    widths_ref[...] = widths[:, : ROWS - 1]
     at = slice(ROWS - 1, ROWS)
     grad = grad_ref[...]
     step = step_one[:, at] * grad + step_two[:, at] * (first_ref[...] + ratio[:, at] * grad)
@@ -405,10 +429,10 @@
 
     margin, picked = kernel_call(
         first_kernel,
-        [SMEM, VMEM, HBM],
+        [SMEM, HBM, HBM],
         [shaped(COUNT // 128, 128), shaped(TILES, ROWS, 128, dtype=BF16)],
         (contexts, weights.reshape(1, features), events),
-        [pltpu.VMEM((128, features), BF16), pltpu.VMEM((ROWS, features), F32), *rows],
+        [pltpu.VMEM((1, features), F32), pltpu.VMEM((ROWS, features), F32), *rows, pltpu.SemaphoreType.DMA],
         micros=6,
         room=ROOM,
     )
@@ -436,9 +460,9 @@
     rhs, grad, other, mine = kernel_call(
         scores_kernel,
         [HBM] + [VMEM] * 5,
-        [shaped(128, features, dtype=BF16), shaped(TILES, 128)] + half,
+        [shaped(ROWS, features, dtype=BF16), shaped(TILES, 128)] + half,
         (events, tiled, message, *x_moves(message)),
-        rows,
+        [pltpu.VMEM((features, 128), BF16), *rows],
         micros=4,
         room=ROOM,
     )
@@ -474,12 +498,12 @@
 
     other, mine, first = kernel_call(
         second_kernel,
-        [HBM] + [VMEM] * 6,
+        [VMEM] + [VMEM] * 6,
         half + [shaped(TILES, 128)],
         (events, rhs, grad, message, *x_moves(message)),
-        [pltpu.VMEM((128, features), BF16), *rows],
+        [pltpu.VMEM((features, 128), BF16)],
         micros=4,
-        room=ROOM,
+        room=8,
     )
     (message,) = kernel_call(pack_kernel, [VMEM] * 2, packed, (mine, core_move(other)))
     tail, lines = kernel_call(
@@ -491,9 +515,9 @@
     tail = tail + core_move(tail)
     tails = lax.all_to_all(jnp.broadcast_to(tail[None], (EN, 1, 128)), "event", 0, 0)
     updated, widths = kernel_call(
-        end_kernel, [VMEM] * 6, [shaped(TILES, 128), shaped(1, 128)], (tails, scalars, lines, tiled, grad, first)
-    )
-    return updated.reshape(features), widths[0, : ROWS - 1]
+        end_kernel, [VMEM] * 6, [shaped(TILES, 128), shaped(1, ROWS - 1)], (tails, scalars, lines, tiled, grad, first)
+    )
+    return updated.reshape(features), widths.reshape(ROWS - 1)
 
 
 def solution(mesh):

time: 172 us -> 165 us (0.959)
  Pallas kernels: 36 us -> 30.4 us
    pallas_call x14, Pallas kernels: 36 us -> 30.4 us  [kernel_call(): pl.pallas_call(body, out_shape=outs, in_specs=ins, out_specs=[VMEM] * len...]
where the time goes in v4:
time: 165 us
  blocking collectives  47.8 us (29%)
  starting transfers between devices  42.8 us (26%)
  waiting for transfers between devices  41.6 us (25%)
  Pallas kernels  30.4 us (18%)
    all_to_all x3, blocking collectives, z_exchange(): return lax.all_to_all(v, 'event', 0, 0, axis_index_groups=groups)  36.2 us
    pallas_call x14, Pallas kernels, kernel_call(): pl.pallas_call(body, out_shape=outs, in_specs=ins, out_specs=[VMEM] * len...  30.4 us
    ppermute x9, waiting for transfers between devices, y_moves(): lax.ppermute(v, 'feat', [(i, (i + k * CN) % n) for i in range(n)])  18 us
    ppermute x6, waiting for transfers between devices, x_moves(): lax.ppermute(v, 'event', [(i, (i + k * ZN) % n) for i in range(n)])  12.2 us
    all_to_all x1, starting transfers between devices, on_device(): chunks = lax.all_to_all(picked, 'event', 0, 0)  12 us
    ppermute x5, starting transfers between devices, core_move(): return lax.ppermute(v, 'feat', [(i, i ^ 1) for i in range(YN * CN)])  12 us
    all_to_all x1, blocking collectives, on_device(): lax.all_to_all(jnp.broadcast_to(tail[None], (EN, 1, 128)), 'event', 0, 0)  11.6 us
    ppermute x6, starting transfers between devices, x_moves(): lax.ppermute(v, 'event', [(i, (i + k * ZN) % n) for i in range(n)])  7.86 us
  transfers between devices with their start and end apart: 24, of which 22 were waited for; matrix products, arithmetic and copies ran while one was open for 0% of the time, Pallas kernels for 3%

profile of v4, /device:TPU:1, one launch (start us, length us, event | category | flops | bytes accessed | tf_op | source)
XLA Modules:
  0.0 164.8 jit_solution(18317384331480292620)
XLA Ops:
  0.6 0.7 copy-done
  1.4 0.7 copy-done.3
  2.0 7.2 %shard_map.59 = (f32[10,128]{1,0:T(8,128)S(1)}, bf16[32,64,128]{2,1,0:T(8,128)(2,1)}) custom-call(s32[63]{0:T(128)S(1)} %copy-done.3, f32[1,4096]{1,0:T(1,128)S(1)} %bitcast.9, bf16[1280,4096]{1,0:T(8,128)(2,1)} %events_ref.9), custom_call_target="tpu_custom_call" | custom-call | bytes 21600000 | tf_op jit(solution)/shard_map/pallas_call | solution.py:30
  9.2 12.0 %all-to-all-start = ((bf16[32,64,128]{2,1,0:T(8,128)(2,1)}), bf16[32,64,128]{2,1,0:T(8,128)(2,1)S(1)}, u32[]{:S(2)}, u32[]{:S(2)}) async-start(bf16[32,64,128]{2,1,0:T(8,128)(2,1)} %get-tuple-element.26), calls=%async_computation | async-start | bytes 1048576 | tf_op jit(solution)/shard_map/all_to_all | solution.py:439
  21.2 1.0 collective-permute-start
  22.3 0.8 collective-permute-done
  23.1 2.7 %collective-permute-start.3 = (f32[10,128]{1,0:T(8,128)S(1)}, f32[10,128]{1,0:T(8,128)S(1)}, u32[]{:S(2)}, u32[]{:S(2)}) collective-permute-start(f32[10,128]{1,0:T(8,128)S(1)} %add.6.own), channel_id=1, source_target_pairs={{0,6},{1,7},{2,0},{3,1},{4,2},{5,3},{6,4},{7,5},{8,14},{9,15},{10,... | collective-permute-start | bytes 15368 | tf_op jit(solution)/shard_map/ppermute | solution.py:48
  25.9 0.3 collective-permute-start.2
  26.2 0.7 collective-permute-start.1
  26.9 3.3 %collective-permute-done.2.two = f32[10,128]{1,0:T(8,128)S(1)} collective-permute-done((f32[10,128]{1,0:T(8,128)S(1)}, f32[10,128]{1,0:T(8,128)S(1)}, u32[]{:S(2)}, u32[]{:S(2)}) %collective-permute-start.2) | collective-permute-done | bytes 5152 | tf_op jit(solution)/shard_map/ppermute | solution.py:48
  30.2 0.1 collective-permute-done.1.one
  30.2 4.7 %shard_map.60 = (f32[1,1280]{1,0:T(1,128)S(1)}, f32[32,128]{1,0:T(8,128)S(1)}) custom-call(bf16[1280,4096]{1,0:T(8,128)(2,1)} %events_ref.9, f32[10,128]{1,0:T(8,128)S(1)} %add.6.own, f32[10,128]{1,0:T(8,128)S(1)} %collective-permute-done.1.one, f32[10,128]{1,0:T(8,128)S(1)} %collective-permute-done.2.two, f32[10,128]{1,0:T(8,128)S(1)} %collective-permute-done.3.three, ...), custom_call_target="tpu_custom_call" | custom-call | bytes 14400000 | tf_op jit(solution)/shard_map/pallas_call | solution.py:30
  34.9 0.6 all-to-all-done.chunks_ref
  35.6 0.1 shard_map.61
  35.6 15.1 %all_to_all.25.in_ref = bf16[8,128,128]{2,1,0:T(8,128)(2,1)S(1)} all-to-all(bf16[8,128,128]{2,1,0:T(8,128)(2,1)S(1)} %shard_map.61), channel_id=1, replica_groups={{0,8,16,24,32,40,48,56},{64,72,80,88,96,104,112,120},{128,136,144,152,1..., dimensions={0} | all-to-all | bytes 524288 | tf_op jit(solution)/shard_map/all_to_all | solution.py:57
  50.7 2.5 %collective-permute-start.6 = (bf16[576,128]{1,0:T(8,128)(2,1)S(1)}, bf16[576,128]{1,0:T(8,128)(2,1)S(1)}, u32[]{:S(2)}, u32[]{:S(2)}) collective-permute-start(bf16[576,128]{1,0:T(8,128)(2,1)S(1)} %shard_map.62.own), channel_id=1, source_target_pairs={{0,192},{8,200},{16,208},{24,216},{32,224},{40,232},{48,240},{56,2... | collective-permute-start | bytes 442376 | tf_op jit(solution)/shard_map/ppermute | solution.py:43
  53.3 0.5 collective-permute-start.5
  53.8 0.6 collective-permute-start.4
  54.4 2.6 %collective-permute-done.6.three = bf16[576,128]{1,0:T(8,128)(2,1)S(1)} collective-permute-done((bf16[576,128]{1,0:T(8,128)(2,1)S(1)}, bf16[576,128]{1,0:T(8,128)(2,1)S(1)}, u32[]{:S(2)}, u32[]{:S(2)}) %collective-permute-start.6) | collective-permute-done | bytes 147488 | tf_op jit(solution)/shard_map/ppermute | solution.py:43
  56.9 1.9 %collective-permute-done.5.two = bf16[576,128]{1,0:T(8,128)(2,1)S(1)} collective-permute-done((bf16[576,128]{1,0:T(8,128)(2,1)S(1)}, bf16[576,128]{1,0:T(8,128)(2,1)S(1)}, u32[]{:S(2)}, u32[]{:S(2)}) %collective-permute-start.5) | collective-permute-done | bytes 147488 | tf_op jit(solution)/shard_map/ppermute | solution.py:43
  58.9 1.5 collective-permute-done.4.one
  60.4 8.8 %shard_map.63 = (bf16[64,4096]{1,0:T(8,128)(2,1)S(1)}, f32[32,128]{1,0:T(8,128)S(1)}, f32[72,640]{1,0:T(8,128)S(1)}, f32[72,640]{1,0:T(8,128)S(1)}) custom-call(bf16[1280,4096]{1,0:T(8,128)(2,1)} %events_ref.9, f32[32,128]{1,0:T(8,128)S(1)} %bitcast.10, bf16[576,128]{1,0:T(8,128)(2,1)S(1)} %shard_map.62.own, ...), custom_call_target="tpu_custom_call" | custom-call | bytes 14400000 | tf_op jit(solution)/shard_map/pallas_call | solution.py:30
  69.2 5.2 %collective-permute-start.7 = (f32[72,640]{1,0:T(8,128)S(1)}, f32[72,640]{1,0:T(8,128)S(1)}, u32[]{:S(2)}, u32[]{:S(2)}) collective-permute-start(f32[72,640]{1,0:T(8,128)S(1)} %get-tuple-element.32), channel_id=1, source_target_pairs={{0,1},{1,0},{2,3},{3,2},{4,5},{5,4},{6,7},{7,6},{8,9},{9,8},{10,11... | collective-permute-start | bytes 552968 | tf_op jit(solution)/shard_map/ppermute | solution.py:52
  74.3 1.1 collective-permute-done.7.other
  75.4 1.3 collective-permute-start.10
  76.7 0.3 collective-permute-start.9
  77.1 0.7 collective-permute-start.8
  77.8 1.8 %collective-permute-done.10.three = bf16[80,640]{1,0:T(8,128)(2,1)S(1)} collective-permute-done((bf16[80,640]{1,0:T(8,128)(2,1)S(1)}, bf16[80,640]{1,0:T(8,128)(2,1)S(1)}, u32[]{:S(2)}, u32[]{:S(2)}) %collective-permute-start.10) | collective-permute-done | bytes 102432 | tf_op jit(solution)/shard_map/ppermute | solution.py:48
  79.6 2.2 %collective-permute-done.9.two = bf16[80,640]{1,0:T(8,128)(2,1)S(1)} collective-permute-done((bf16[80,640]{1,0:T(8,128)(2,1)S(1)}, bf16[80,640]{1,0:T(8,128)(2,1)S(1)}, u32[]{:S(2)}, u32[]{:S(2)}) %collective-permute-start.9) | collective-permute-done | bytes 102432 | tf_op jit(solution)/shard_map/ppermute | solution.py:48
  81.8 3.3 %collective-permute-done.8.one = bf16[80,640]{1,0:T(8,128)(2,1)S(1)} collective-permute-done((bf16[80,640]{1,0:T(8,128)(2,1)S(1)}, bf16[80,640]{1,0:T(8,128)(2,1)S(1)}, u32[]{:S(2)}, u32[]{:S(2)}) %collective-permute-start.8) | collective-permute-done | bytes 102432 | tf_op jit(solution)/shard_map/ppermute | solution.py:48
  85.1 0.1 shard_map.65
  85.2 0.7 collective-permute-start.11
  85.9 1.0 collective-permute-done.11.theirs_ref
  86.9 5.0 %shard_map.66 = (f32[512,128]{1,0:T(8,128)S(1)}, f32[8,128]{1,0:T(8,128)S(1)}, bf16[528,128]{1,0:T(8,128)(2,1)S(1)}, bf16[528,128]{1,0:T(8,128)(2,1)S(1)}, bf16[528,128]{1,0:T(8,128)(2,1)S(1)}) custom-call(bf16[1280,4096]{1,0:T(8,128)(2,1)} %events_ref.9, f32[64,640]{1,0:T(8,128)S(1)} %get-tuple-element.33.mine_ref.scores_ref, ...), custom_call_target="tpu_custom_call" | custom-call | bytes 14400000 | tf_op jit(solution)/shard_map/pallas_call | solution.py:30
  91.9 0.1 collective-permute-start.12
  92.0 1.5 collective-permute-start.13
  93.4 1.7 %collective-permute-start.14 = (bf16[528,128]{1,0:T(8,128)(2,1)S(1)}, bf16[528,128]{1,0:T(8,128)(2,1)S(1)}, u32[]{:S(2)}, u32[]{:S(2)}) collective-permute-start(bf16[528,128]{1,0:T(8,128)(2,1)S(1)} %get-tuple-element.39), channel_id=1, source_target_pairs={{0,192},{8,200},{16,208},{24,216},{32,224},{40,232},{48,240},{56,2... | collective-permute-start | bytes 405512 | tf_op jit(solution)/shard_map/ppermute | solution.py:486
  95.1 5.7 %collective-permute-done.12.one = bf16[528,128]{1,0:T(8,128)(2,1)S(1)} collective-permute-done((bf16[528,128]{1,0:T(8,128)(2,1)S(1)}, bf16[528,128]{1,0:T(8,128)(2,1)S(1)}, u32[]{:S(2)}, u32[]{:S(2)}) %collective-permute-start.12) | collective-permute-done | bytes 135200 | tf_op jit(solution)/shard_map/ppermute | solution.py:486
  100.9 0.0 collective-permute-done.13.two
  100.9 0.3 collective-permute-done.14.three
  101.1 0.1 shard_map.67
  101.2 10.6 %all_to_all.26.in_ref = bf16[8,72,128]{2,1,0:T(8,128)(2,1)S(1)} all-to-all(bf16[8,72,128]{2,1,0:T(8,128)(2,1)S(1)} %shard_map.67), channel_id=1, replica_groups={{0,8,16,24,32,40,48,56},{64,72,80,88,96,104,112,120},{128,136,144,152,1..., dimensions={0} | all-to-all | bytes 294912 | tf_op jit(solution)/shard_map/all_to_all | solution.py:57
  111.8 0.1 shard_map.68
  111.9 10.6 %all_to_all.27.own = bf16[8,72,128]{2,1,0:T(8,128)(2,1)S(1)} all-to-all(bf16[8,72,128]{2,1,0:T(8,128)(2,1)S(1)} %get-tuple-element.41), channel_id=1, replica_groups={{0,8,16,24,32,40,48,56},{64,72,80,88,96,104,112,120},{128,136,144,152,1..., dimensions={0} | all-to-all | bytes 294912 | tf_op jit(solution)/shard_map/all_to_all | solution.py:57
  122.5 3.6 %collective-permute-start.17 = (bf16[8,72,128]{2,1,0:T(8,128)(2,1)S(1)}, bf16[8,72,128]{2,1,0:T(8,128)(2,1)S(1)}, u32[]{:S(2)}, u32[]{:S(2)}) collective-permute-start(bf16[8,72,128]{2,1,0:T(8,128)(2,1)S(1)} %all_to_all.27.own), channel_id=1, source_target_pairs={{0,192},{8,200},{16,208},{24,216},{32,224},{40,232},{48,240},{56,2... | collective-permute-start | bytes 442376 | tf_op jit(solution)/shard_map/ppermute | solution.py:43
  126.2 0.0 collective-permute-start.16
  126.2 0.6 collective-permute-start.15
  126.7 3.1 %collective-permute-done.17.three = bf16[8,72,128]{2,1,0:T(8,128)(2,1)S(1)} collective-permute-done((bf16[8,72,128]{2,1,0:T(8,128)(2,1)S(1)}, bf16[8,72,128]{2,1,0:T(8,128)(2,1)S(1)}, u32[]{:S(2)}, u32[]{:S(2)}) %collective-permute-start.17) | collective-permute-done | bytes 147488 | tf_op jit(solution)/shard_map/ppermute | solution.py:43
  129.8 1.9 %collective-permute-done.16.two = bf16[8,72,128]{2,1,0:T(8,128)(2,1)S(1)} collective-permute-done((bf16[8,72,128]{2,1,0:T(8,128)(2,1)S(1)}, bf16[8,72,128]{2,1,0:T(8,128)(2,1)S(1)}, u32[]{:S(2)}, u32[]{:S(2)}) %collective-permute-start.16) | collective-permute-done | bytes 147488 | tf_op jit(solution)/shard_map/ppermute | solution.py:43
  131.8 1.2 collective-permute-done.15.one
  133.0 3.4 %shard_map.69 = (f32[72,640]{1,0:T(8,128)S(1)}, f32[72,640]{1,0:T(8,128)S(1)}, f32[32,128]{1,0:T(8,128)S(1)}) custom-call(bf16[1280,4096]{1,0:T(8,128)(2,1)S(1)} %bitcast.8, bf16[64,4096]{1,0:T(8,128)(2,1)S(1)} %get-tuple-element.29.rhs_ref, f32[32,128]{1,0:T(8,128)S(1)} %get-tuple-element.30.grad_ref, bf16[8,72,128]{2,1,0:T(8,128)(2,1)S(1)} %all_to_all.27.own, ...), custom_call_target="tpu_custom_call" | custom-call | bytes 14400000 | tf_op jit(solution)/shard_map/pallas_call | solution.py:30
  136.3 4.5 %collective-permute-start.18 = (f32[72,640]{1,0:T(8,128)S(1)}, f32[72,640]{1,0:T(8,128)S(1)}, u32[]{:S(2)}, u32[]{:S(2)}) collective-permute-start(f32[72,640]{1,0:T(8,128)S(1)} %get-tuple-element.43), channel_id=1, source_target_pairs={{0,1},{1,0},{2,3},{3,2},{4,5},{5,4},{6,7},{7,6},{8,9},{9,8},{10,11... | collective-permute-start | bytes 552968 | tf_op jit(solution)/shard_map/ppermute | solution.py:52
  140.8 1.1 collective-permute-done.18.other
  141.9 0.4 collective-permute-start.21
  142.3 0.3 collective-permute-start.20
  142.7 0.8 collective-permute-start.19
  143.5 2.6 %collective-permute-done.21.three = bf16[80,640]{1,0:T(8,128)(2,1)S(1)} collective-permute-done((bf16[80,640]{1,0:T(8,128)(2,1)S(1)}, bf16[80,640]{1,0:T(8,128)(2,1)S(1)}, u32[]{:S(2)}, u32[]{:S(2)}) %collective-permute-start.21) | collective-permute-done | bytes 102432 | tf_op jit(solution)/shard_map/ppermute | solution.py:48
  146.1 1.3 collective-permute-done.20.two
  147.4 3.4 %collective-permute-done.19.one = bf16[80,640]{1,0:T(8,128)(2,1)S(1)} collective-permute-done((bf16[80,640]{1,0:T(8,128)(2,1)S(1)}, bf16[80,640]{1,0:T(8,128)(2,1)S(1)}, u32[]{:S(2)}, u32[]{:S(2)}) %collective-permute-start.19) | collective-permute-done | bytes 102432 | tf_op jit(solution)/shard_map/ppermute | solution.py:48
  150.8 0.2 shard_map.71
  151.0 0.6 collective-permute-start.22
  151.5 0.8 collective-permute-done.22
  152.4 11.6 %all_to_all.28.tails_ref = f32[32,1,128]{2,1,0:T(1,128)S(1)} all-to-all(f32[32,1,128]{2,1,0:T(1,128)S(1)} %broadcast_in_dim.9), channel_id=1, replica_groups=mesh['event'=32,'feat'=8] {'event'}, dimensions={0} | all-to-all | bytes 32768 | tf_op jit(solution)/shard_map/all_to_all | solution.py:516
  164.0 0.8 shard_map.72
  (20 shorter events, 0.2 us)
Async XLA Ops:
  0.6 0.7 copy-start
  1.3 0.7 copy-start.3
  2.0 28.2 %copy-start.2 = (s32[1280]{0:T(1024)S(1)}, s32[1280]{0:T(1024)}, u32[]{:S(2)}) copy-start(s32[1280]{0:T(1024)} %param.5) | copy-start | bytes 15364
  2.0 58.3 %copy-start.1 = (f32[4096]{0:T(1024)S(1)}, f32[4096]{0:T(1024)}, u32[]{:S(2)}) copy-start(f32[4096]{0:T(1024)} %param.6) | copy-start | bytes 49156
  9.2 26.3 %all-to-all-start = ((bf16[32,64,128]{2,1,0:T(8,128)(2,1)}), bf16[32,64,128]{2,1,0:T(8,128)(2,1)S(1)}, u32[]{:S(2)}, u32[]{:S(2)}) async-start(bf16[32,64,128]{2,1,0:T(8,128)(2,1)} %get-tuple-element.26), calls=%async_computation | async-start | bytes 1048576 | tf_op jit(solution)/shard_map/all_to_all | solution.py:439
  21.2 1.9 %collective-permute-start = (f32[10,128]{1,0:T(8,128)S(1)}, f32[10,128]{1,0:T(8,128)S(1)}, u32[]{:S(2)}, u32[]{:S(2)}) collective-permute-start(f32[10,128]{1,0:T(8,128)S(1)} %get-tuple-element.27), channel_id=1, source_target_pairs={{0,1},{1,0},{2,3},{3,2},{4,5},{5,4},{6,7},{7,6},{8,9},{9,8},{10,11... | collective-permute-start | bytes 15368 | tf_op jit(solution)/shard_map/ppermute | solution.py:52
  23.1 3.8 %collective-permute-start.3 = (f32[10,128]{1,0:T(8,128)S(1)}, f32[10,128]{1,0:T(8,128)S(1)}, u32[]{:S(2)}, u32[]{:S(2)}) collective-permute-start(f32[10,128]{1,0:T(8,128)S(1)} %add.6.own), channel_id=1, source_target_pairs={{0,6},{1,7},{2,0},{3,1},{4,2},{5,3},{6,4},{7,5},{8,14},{9,15},{10,... | collective-permute-start | bytes 15368 | tf_op jit(solution)/shard_map/ppermute | solution.py:48
  25.9 4.3 %collective-permute-start.2 = (f32[10,128]{1,0:T(8,128)S(1)}, f32[10,128]{1,0:T(8,128)S(1)}, u32[]{:S(2)}, u32[]{:S(2)}) collective-permute-start(f32[10,128]{1,0:T(8,128)S(1)} %add.6.own), channel_id=1, source_target_pairs={{0,4},{1,5},{2,6},{3,7},{4,0},{5,1},{6,2},{7,3},{8,12},{9,13},{10,... | collective-permute-start | bytes 15368 | tf_op jit(solution)/shard_map/ppermute | solution.py:48
  26.2 4.0 %collective-permute-start.1 = (f32[10,128]{1,0:T(8,128)S(1)}, f32[10,128]{1,0:T(8,128)S(1)}, u32[]{:S(2)}, u32[]{:S(2)}) collective-permute-start(f32[10,128]{1,0:T(8,128)S(1)} %add.6.own), channel_id=1, source_target_pairs={{0,2},{1,3},{2,4},{3,5},{4,6},{5,7},{6,0},{7,1},{8,10},{9,11},{10,... | collective-permute-start | bytes 15368 | tf_op jit(solution)/shard_map/ppermute | solution.py:48
  50.7 6.2 %collective-permute-start.6 = (bf16[576,128]{1,0:T(8,128)(2,1)S(1)}, bf16[576,128]{1,0:T(8,128)(2,1)S(1)}, u32[]{:S(2)}, u32[]{:S(2)}) collective-permute-start(bf16[576,128]{1,0:T(8,128)(2,1)S(1)} %shard_map.62.own), channel_id=1, source_target_pairs={{0,192},{8,200},{16,208},{24,216},{32,224},{40,232},{48,240},{56,2... | collective-permute-start | bytes 442376 | tf_op jit(solution)/shard_map/ppermute | solution.py:43
  53.3 5.6 %collective-permute-start.5 = (bf16[576,128]{1,0:T(8,128)(2,1)S(1)}, bf16[576,128]{1,0:T(8,128)(2,1)S(1)}, u32[]{:S(2)}, u32[]{:S(2)}) collective-permute-start(bf16[576,128]{1,0:T(8,128)(2,1)S(1)} %shard_map.62.own), channel_id=1, source_target_pairs={{0,128},{8,136},{16,144},{24,152},{32,160},{40,168},{48,176},{56,1... | collective-permute-start | bytes 442376 | tf_op jit(solution)/shard_map/ppermute | solution.py:43
  53.8 6.6 %collective-permute-start.4 = (bf16[576,128]{1,0:T(8,128)(2,1)S(1)}, bf16[576,128]{1,0:T(8,128)(2,1)S(1)}, u32[]{:S(2)}, u32[]{:S(2)}) collective-permute-start(bf16[576,128]{1,0:T(8,128)(2,1)S(1)} %shard_map.62.own), channel_id=1, source_target_pairs={{0,64},{8,72},{16,80},{24,88},{32,96},{40,104},{48,112},{56,120},{... | collective-permute-start | bytes 442376 | tf_op jit(solution)/shard_map/ppermute | solution.py:43
  60.4 72.6 %slice-start = ((s8[10485760]{0:T(1024)(128)(4,1)}), s8[2097152]{0:T(1024)(128)(4,1)S(1)}, s32[]{:S(2)}) async-start(s8[10485760]{0:T(1024)(128)(4,1)} %bitcast.7), calls=%async_computation.5 | async-start | bytes 4194304
  60.4 72.6 %slice-start.1 = ((s8[10485760]{0:T(1024)(128)(4,1)}), s8[4194304]{0:T(1024)(128)(4,1)S(1)}, s32[]{:S(2)}) async-start(s8[10485760]{0:T(1024)(128)(4,1)} %bitcast.7), calls=%async_computation.6 | async-start | bytes 8388608
  69.2 6.2 %collective-permute-start.7 = (f32[72,640]{1,0:T(8,128)S(1)}, f32[72,640]{1,0:T(8,128)S(1)}, u32[]{:S(2)}, u32[]{:S(2)}) collective-permute-start(f32[72,640]{1,0:T(8,128)S(1)} %get-tuple-element.32), channel_id=1, source_target_pairs={{0,1},{1,0},{2,3},{3,2},{4,5},{5,4},{6,7},{7,6},{8,9},{9,8},{10,11... | collective-permute-start | bytes 552968 | tf_op jit(solution)/shard_map/ppermute | solution.py:52
  75.4 4.2 %collective-permute-start.10 = (bf16[80,640]{1,0:T(8,128)(2,1)S(1)}, bf16[80,640]{1,0:T(8,128)(2,1)S(1)}, u32[]{:S(2)}, u32[]{:S(2)}) collective-permute-start(bf16[80,640]{1,0:T(8,128)(2,1)S(1)} %shard_map.64.own), channel_id=1, source_target_pairs={{0,6},{1,7},{2,0},{3,1},{4,2},{5,3},{6,4},{7,5},{8,14},{9,15},{10,... | collective-permute-start | bytes 307208 | tf_op jit(solution)/shard_map/ppermute | solution.py:48
  76.7 5.1 %collective-permute-start.9 = (bf16[80,640]{1,0:T(8,128)(2,1)S(1)}, bf16[80,640]{1,0:T(8,128)(2,1)S(1)}, u32[]{:S(2)}, u32[]{:S(2)}) collective-permute-start(bf16[80,640]{1,0:T(8,128)(2,1)S(1)} %shard_map.64.own), channel_id=1, source_target_pairs={{0,4},{1,5},{2,6},{3,7},{4,0},{5,1},{6,2},{7,3},{8,12},{9,13},{10,... | collective-permute-start | bytes 307208 | tf_op jit(solution)/shard_map/ppermute | solution.py:48
  77.1 8.1 %collective-permute-start.8 = (bf16[80,640]{1,0:T(8,128)(2,1)S(1)}, bf16[80,640]{1,0:T(8,128)(2,1)S(1)}, u32[]{:S(2)}, u32[]{:S(2)}) collective-permute-start(bf16[80,640]{1,0:T(8,128)(2,1)S(1)} %shard_map.64.own), channel_id=1, source_target_pairs={{0,2},{1,3},{2,4},{3,5},{4,6},{5,7},{6,0},{7,1},{8,10},{9,11},{10,... | collective-permute-start | bytes 307208 | tf_op jit(solution)/shard_map/ppermute | solution.py:48
  85.2 1.7 %collective-permute-start.11 = (f32[64,640]{1,0:T(8,128)S(1)}, f32[64,640]{1,0:T(8,128)S(1)}, u32[]{:S(2)}, u32[]{:S(2)}) collective-permute-start(f32[64,640]{1,0:T(8,128)S(1)} %get-tuple-element.33.mine_ref.scores_ref), channel_id=1, source_target_pairs={{0,1},{1,0},{2,3},{3,2},{4,5},{5,4},{6,7},{7,6},{8,9},{9,8},{10,11... | collective-permute-start | bytes 491528 | tf_op jit(solution)/shard_map/ppermute | solution.py:52
  86.9 46.0 %slice-start.2 = ((s8[10485760]{0:T(1024)(128)(4,1)}), s8[4194304]{0:T(1024)(128)(4,1)S(1)}, s32[]{:S(2)}) async-start(s8[10485760]{0:T(1024)(128)(4,1)} %bitcast.7), calls=%async_computation.7 | async-start | bytes 8388608
  91.9 9.0 %collective-permute-start.12 = (bf16[528,128]{1,0:T(8,128)(2,1)S(1)}, bf16[528,128]{1,0:T(8,128)(2,1)S(1)}, u32[]{:S(2)}, u32[]{:S(2)}) collective-permute-start(bf16[528,128]{1,0:T(8,128)(2,1)S(1)} %get-tuple-element.37), channel_id=1, source_target_pairs={{0,64},{8,72},{16,80},{24,88},{32,96},{40,104},{48,112},{56,120},{... | collective-permute-start | bytes 405512 | tf_op jit(solution)/shard_map/ppermute | solution.py:486
  92.0 8.9 %collective-permute-start.13 = (bf16[528,128]{1,0:T(8,128)(2,1)S(1)}, bf16[528,128]{1,0:T(8,128)(2,1)S(1)}, u32[]{:S(2)}, u32[]{:S(2)}) collective-permute-start(bf16[528,128]{1,0:T(8,128)(2,1)S(1)} %get-tuple-element.38), channel_id=1, source_target_pairs={{0,128},{8,136},{16,144},{24,152},{32,160},{40,168},{48,176},{56,1... | collective-permute-start | bytes 405512 | tf_op jit(solution)/shard_map/ppermute | solution.py:486
  93.4 7.7 %collective-permute-start.14 = (bf16[528,128]{1,0:T(8,128)(2,1)S(1)}, bf16[528,128]{1,0:T(8,128)(2,1)S(1)}, u32[]{:S(2)}, u32[]{:S(2)}) collective-permute-start(bf16[528,128]{1,0:T(8,128)(2,1)S(1)} %get-tuple-element.39), channel_id=1, source_target_pairs={{0,192},{8,200},{16,208},{24,216},{32,224},{40,232},{48,240},{56,2... | collective-permute-start | bytes 405512 | tf_op jit(solution)/shard_map/ppermute | solution.py:486
  122.5 7.3 %collective-permute-start.17 = (bf16[8,72,128]{2,1,0:T(8,128)(2,1)S(1)}, bf16[8,72,128]{2,1,0:T(8,128)(2,1)S(1)}, u32[]{:S(2)}, u32[]{:S(2)}) collective-permute-start(bf16[8,72,128]{2,1,0:T(8,128)(2,1)S(1)} %all_to_all.27.own), channel_id=1, source_target_pairs={{0,192},{8,200},{16,208},{24,216},{32,224},{40,232},{48,240},{56,2... | collective-permute-start | bytes 442376 | tf_op jit(solution)/shard_map/ppermute | solution.py:43
  126.2 5.6 %collective-permute-start.16 = (bf16[8,72,128]{2,1,0:T(8,128)(2,1)S(1)}, bf16[8,72,128]{2,1,0:T(8,128)(2,1)S(1)}, u32[]{:S(2)}, u32[]{:S(2)}) collective-permute-start(bf16[8,72,128]{2,1,0:T(8,128)(2,1)S(1)} %all_to_all.27.own), channel_id=1, source_target_pairs={{0,128},{8,136},{16,144},{24,152},{32,160},{40,168},{48,176},{56,1... | collective-permute-start | bytes 442376 | tf_op jit(solution)/shard_map/ppermute | solution.py:43
  126.2 6.8 %collective-permute-start.15 = (bf16[8,72,128]{2,1,0:T(8,128)(2,1)S(1)}, bf16[8,72,128]{2,1,0:T(8,128)(2,1)S(1)}, u32[]{:S(2)}, u32[]{:S(2)}) collective-permute-start(bf16[8,72,128]{2,1,0:T(8,128)(2,1)S(1)} %all_to_all.27.own), channel_id=1, source_target_pairs={{0,64},{8,72},{16,80},{24,88},{32,96},{40,104},{48,112},{56,120},{... | collective-permute-start | bytes 442376 | tf_op jit(solution)/shard_map/ppermute | solution.py:43
  136.3 5.6 %collective-permute-start.18 = (f32[72,640]{1,0:T(8,128)S(1)}, f32[72,640]{1,0:T(8,128)S(1)}, u32[]{:S(2)}, u32[]{:S(2)}) collective-permute-start(f32[72,640]{1,0:T(8,128)S(1)} %get-tuple-element.43), channel_id=1, source_target_pairs={{0,1},{1,0},{2,3},{3,2},{4,5},{5,4},{6,7},{7,6},{8,9},{9,8},{10,11... | collective-permute-start | bytes 552968 | tf_op jit(solution)/shard_map/ppermute | solution.py:52
  141.9 4.2 %collective-permute-start.21 = (bf16[80,640]{1,0:T(8,128)(2,1)S(1)}, bf16[80,640]{1,0:T(8,128)(2,1)S(1)}, u32[]{:S(2)}, u32[]{:S(2)}) collective-permute-start(bf16[80,640]{1,0:T(8,128)(2,1)S(1)} %shard_map.70.own), channel_id=1, source_target_pairs={{0,6},{1,7},{2,0},{3,1},{4,2},{5,3},{6,4},{7,5},{8,14},{9,15},{10,... | collective-permute-start | bytes 307208 | tf_op jit(solution)/shard_map/ppermute | solution.py:48
  142.3 5.1 %collective-permute-start.20 = (bf16[80,640]{1,0:T(8,128)(2,1)S(1)}, bf16[80,640]{1,0:T(8,128)(2,1)S(1)}, u32[]{:S(2)}, u32[]{:S(2)}) collective-permute-start(bf16[80,640]{1,0:T(8,128)(2,1)S(1)} %shard_map.70.own), channel_id=1, source_target_pairs={{0,4},{1,5},{2,6},{3,7},{4,0},{5,1},{6,2},{7,3},{8,12},{9,13},{10,... | collective-permute-start | bytes 307208 | tf_op jit(solution)/shard_map/ppermute | solution.py:48
  142.7 8.2 %collective-permute-start.19 = (bf16[80,640]{1,0:T(8,128)(2,1)S(1)}, bf16[80,640]{1,0:T(8,128)(2,1)S(1)}, u32[]{:S(2)}, u32[]{:S(2)}) collective-permute-start(bf16[80,640]{1,0:T(8,128)(2,1)S(1)} %shard_map.70.own), channel_id=1, source_target_pairs={{0,2},{1,3},{2,4},{3,5},{4,6},{5,7},{6,0},{7,1},{8,10},{9,11},{10,... | collective-permute-start | bytes 307208 | tf_op jit(solution)/shard_map/ppermute | solution.py:48
  151.0 1.4 collective-permute-start.22

commit v5 on v4

--- a/solution.py
+++ b/solution.py
@@ -131,33 +131,45 @@
         return self.held[first * 128 : (first + count) * 128, :]
 
 
-class Columns:
-    def __init__(self, events_ref, held, sems, starts):
-        self.events, self.held = events_ref, held
-        self.starts = [pl.multiple_of(start, 512) for start in starts]
-        if held is not None:
-            pieces = [(events_ref.at[:, pl.ds(start, 512)], held.at[i]) for i, start in enumerate(self.starts)]
-            self.stream = Stream(pieces, sems)
-
-    def take(self, i):
-        if self.held is None:
-            return self.events[:, pl.ds(self.starts[i], 512)]
-        self.stream.take(i)
-        return self.held[i]
-
-
 def place():
     event = lax.axis_index("event")
     return lax.div(event, ZN), lax.rem(event, ZN), lax.rem(lax.axis_index("feat"), CN)
 
 
-def first_kernel(contexts_ref, w_ref, events_ref, margin_ref, out_ref, w, rows, held, sems, w_sem):
+def pick_kernel(contexts_ref, events_ref, out_ref, blocks, rows, sems):
+    base = lax.axis_index("event") * COUNT
+
+    def owned(j):
+        return jnp.logical_and(contexts_ref[j] >= base, contexts_ref[j] < base + COUNT)
+
+    def fetch(j):
+        start = pl.multiple_of(lax.div(contexts_ref[j] - base, 16) * 16, 16)
+        return pltpu.make_async_copy(events_ref.at[pl.ds(start, 16), :], blocks.at[j], sems.at[j])
+
+    @pl.loop(0, ROWS - 1, unroll=9)
+    def _(j):
+        @pl.when(owned(j))
+        def _():
+            fetch(j).start()
+
+    rows[...] = jnp.zeros_like(rows)
+
+    @pl.loop(0, ROWS - 1, unroll=9)
+    def _(j):
+        @pl.when(owned(j))
+        def _():
+            fetch(j).wait()
+            block = blocks[j].astype(F32)
+            found = jnp.where(row_is(block.shape, lax.rem(contexts_ref[j] - base, 16)), block, 0.0)
+            rows[pl.ds(j, 1), :] = jnp.sum(found, axis=0, keepdims=True)
+
+    for t in range(TILES):
+        out_ref[t] = rows[:, t * 128 : (t + 1) * 128].astype(BF16)
+
+
+def margin_kernel(w_ref, events_ref, _after, margin_ref, held, w, sems):
     pieces = Rows(events_ref, held, sems, [i * 128 for i in range(COUNT // 128)])
-    w_copy = pltpu.make_async_copy(w_ref, w, w_sem)
-    w_copy.start()
-    rows[...] = jnp.zeros_like(rows)
-    w_copy.wait()
-    w[...] = w[...].astype(BF16).astype(F32)
+    w[...] = w_ref[...].astype(BF16).astype(F32)
     for c in range(COUNT // 128):
         pieces.take(c, 1)
         sums = []
@@ -170,25 +182,8 @@
         turned = jnp.transpose(jnp.concatenate(sums, axis=0))
         margin_ref[c : c + 1, :] = jnp.sum(turned, axis=0, keepdims=True)
 
-    base = lax.axis_index("event") * COUNT
-
-    @pl.loop(0, ROWS - 1)
-    def _(j):
-        r = contexts_ref[j] - base
-
-        @pl.when(jnp.logical_and(r >= 0, r < COUNT))
-        def _():
-            start = pl.multiple_of(lax.div(r, 16) * 16, 16)
-            block = held[pl.ds(start, 16), :].astype(F32)
-            found = jnp.where(row_is(block.shape, lax.rem(r, 16)), block, 0.0)
-            rows[pl.ds(j, 1), :] = jnp.sum(found, axis=0, keepdims=True)
-
-    for t in range(TILES):
-        out_ref[t] = rows[:, t * 128 : (t + 1) * 128].astype(BF16)
-
-
-def gradient_kernel(events_ref, own, one, two, three, labels_ref, rate_ref, grad_ref, errs, held=None, sems=None):
-    pieces = Columns(events_ref, held, sems, [c * 512 for c in range(8)])
+
+def gradient_kernel(events_ref, own, one, two, three, labels_ref, rate_ref, grad_ref, errs):
     margin = four(own[...], one[...], two[...], three[...])
     chance = jax.nn.sigmoid(margin)
     rate = chance * (1.0 - chance)
@@ -200,7 +195,7 @@
         rate_ref[:, at] = rate[i : i + 1]
         errs[:, at] = stacked([lead[i : i + 1], rest[i : i + 1]], 16).astype(BF16)
     for c in range(8):
-        part = jnp.dot(errs[...], pieces.take(c), preferred_element_type=F32)
+        part = jnp.dot(errs[...], events_ref[:, c * 512 : (c + 1) * 512], preferred_element_type=F32)
         line = part[:1] + part[1:2]
         for u in range(4):
             grad_ref[c * 4 + u : c * 4 + u + 1, :] = line[:, u * 128 : (u + 1) * 128]
@@ -248,7 +243,7 @@
 
 
 def scores_kernel(
-    events_ref, w_ref, own, one, two, three, rhs_ref, grad_ref, other_ref, mine_ref, rhs, held=None, sems=None
+    events_ref, w_ref, own, one, two, three, rhs_ref, grad_ref, other_ref, mine_ref, held, rhs, sems
 ):
     x, _, core = place()
     pieces = half_stream(events_ref, held, sems, core)
@@ -280,7 +275,7 @@
     lead = scores.astype(BF16)
     rest = scores[ROWS - 1 :] - lead[ROWS - 1 :].astype(F32)
     out_ref[:ROWS, :] = lead
-    out_ref[ROWS:, :] = stacked([rest, *triple_of(lines[:1]), *triple_of(lines[1:2])], 16).astype(BF16)
+    out_ref[ROWS:, :] = stacked([rest, *triple_of(lines[:1]), *triple_of(lines[1:2])], 8).astype(BF16)
 
 
 def unpacked(own, one, two, three):
@@ -297,27 +292,29 @@
 
 
 def hessian_kernel(
-    events_ref, mine_ref, theirs_ref, rate_ref, own_ref, curv_ref, one_ref, two_ref, three_ref, q, held=None, sems=None
+    events_ref, mine_ref, theirs_ref, rate_ref, own_ref, curv_ref, one_ref, two_ref, three_ref, q
 ):
     x, _, core = place()
     outs = ((2, two_ref), (1, one_ref), (3, three_ref), (0, own_ref))
-    starts = [lax.rem(x + k, XN) * QUARTER * 128 + part * 512 for k, _ in outs for part in range(2)]
-    pieces = Columns(events_ref, held, sems, starts)
     curv = jnp.zeros((ROWS, 128), F32)
-    for half in range(2):
-        scores = jnp.where(core == half, mine_ref[...], theirs_ref[...])
+    first, second = rate_ref[:, :HALF], rate_ref[:, HALF:]
+    mine = core == 0
+    halves = ((theirs_ref, jnp.where(mine, second, first)), (mine_ref, jnp.where(mine, first, second)))
+    for half, (scores_ref, rate) in enumerate(halves):
+        scores = scores_ref[...]
         at = slice(half * HALF, (half + 1) * HALF)
-        weighted = rate_ref[:, at] * scores
+        weighted = rate * scores
         curv = curv + tile_sums(weighted * scores)
         lead = weighted.astype(BF16)
         q[:ROWS, at] = lead
         q[ROWS:, at] = stacked([weighted[ROWS - 1 :] - lead[ROWS - 1 :].astype(F32)], 16).astype(BF16)
     triple = [v.astype(F32) for v in triple_of(line_sums(curv, jnp.zeros_like(curv)))]
     curv_ref[...] = stacked(triple, 8)
-    for i, (k, out_ref) in enumerate(outs):
+    for k, out_ref in outs:
         rests = []
         for part in range(2):
-            total = joined(jnp.dot(q[...], pieces.take(2 * i + part), preferred_element_type=F32))
+            start = pl.multiple_of(lax.rem(x + k, XN) * QUARTER * 128 + part * 512, 512)
+            total = joined(jnp.dot(q[...], events_ref[:, pl.ds(start, 512)], preferred_element_type=F32))
             for u in range(4):
                 t = part * 4 + u
                 values = total[:, u * 128 : (u + 1) * 128]
@@ -368,10 +365,10 @@
 
 
 def second_kernel(
-    events_ref, rhs_ref, grad_ref, own, one, two, three, other_ref, mine_ref, first_ref, res, held=None, sems=None
+    events_ref, rhs_ref, grad_ref, own, one, two, three, other_ref, mine_ref, first_ref, res
 ):
-    x, _, core = place()
-    pieces = half_stream(events_ref, held, sems, core)
+    x, _, _ = place()
+    pieces = Rows(events_ref, None, None, [i * 128 for i in range(COUNT // 128)])
     norm = jnp.zeros((ROWS, 128), F32)
     cross = jnp.zeros((ROWS, 128), F32)
     for k, part in enumerate((own, one, two, three)):
@@ -424,29 +421,42 @@
     features = TILES * 128
     tiled = weights.reshape(TILES, 128)
 
-    rows = [pltpu.VMEM((COUNT, features), BF16), pltpu.SemaphoreType.DMA((10,))]
-    columns = [pltpu.VMEM((8, COUNT, 512), BF16), pltpu.SemaphoreType.DMA((8,))]
-
-    margin, picked = kernel_call(
-        first_kernel,
-        [SMEM, HBM, HBM],
-        [shaped(COUNT // 128, 128), shaped(TILES, ROWS, 128, dtype=BF16)],
-        (contexts, weights.reshape(1, features), events),
-        [pltpu.VMEM((1, features), F32), pltpu.VMEM((ROWS, features), F32), *rows, pltpu.SemaphoreType.DMA],
-        micros=6,
+    whole = shaped(COUNT, features, dtype=BF16)
+    sems = pltpu.SemaphoreType.DMA((10,))
+
+    (picked,) = kernel_call(
+        pick_kernel,
+        [SMEM, HBM],
+        [shaped(TILES, ROWS, 128, dtype=BF16)],
+        (contexts, events),
+        [
+            pltpu.VMEM((ROWS - 1, 16, features), BF16),
+            pltpu.VMEM((ROWS, features), F32),
+            pltpu.SemaphoreType.DMA((ROWS - 1,)),
+        ],
+        micros=2,
         room=ROOM,
     )
     chunks = lax.all_to_all(picked, "event", 0, 0)
+    margin, held = kernel_call(
+        margin_kernel,
+        [VMEM, HBM, HBM],
+        [shaped(COUNT // 128, 128), whole],
+        (weights.reshape(1, features), events, picked),
+        [pltpu.VMEM((1, features), F32), sems],
+        micros=4,
+        room=40,
+    )
 
     margin = margin + core_move(margin)
     rate, grad = kernel_call(
         gradient_kernel,
-        [HBM] + [VMEM] * 5,
+        [VMEM] * 6,
         [shaped(1, COUNT), shaped(TILES, 128)],
-        (events, margin, *y_moves(margin), labels.reshape(COUNT // 128, 128)),
-        [pltpu.VMEM((16, COUNT), BF16), *columns],
+        (held, margin, *y_moves(margin), labels.reshape(COUNT // 128, 128)),
+        [pltpu.VMEM((16, COUNT), BF16)],
         micros=4,
-        room=ROOM,
+        room=8,
     )
     (message,) = kernel_call(
         spread_kernel, [VMEM] * 2, [shaped(ZN, ROWS + 2 * TILES, 128, dtype=BF16)], (chunks, grad)
@@ -457,16 +467,16 @@
     )
 
     half = [shaped(ROWS + 8, HALF), shaped(ROWS + 8, HALF)]
-    rhs, grad, other, mine = kernel_call(
+    rhs, grad, other, mine, held = kernel_call(
         scores_kernel,
         [HBM] + [VMEM] * 5,
-        [shaped(ROWS, features, dtype=BF16), shaped(TILES, 128)] + half,
+        [shaped(ROWS, features, dtype=BF16), shaped(TILES, 128)] + half + [whole],
         (events, tiled, message, *x_moves(message)),
-        [pltpu.VMEM((features, 128), BF16), *rows],
+        [pltpu.VMEM((features, 128), BF16), sems],
         micros=4,
-        room=ROOM,
-    )
-    packed = [shaped(ROWS + 16, HALF, dtype=BF16)]
+        room=40,
+    )
+    packed = [shaped(ROWS + 8, HALF, dtype=BF16)]
     (message,) = kernel_call(pack_kernel, [VMEM] * 2, packed, (mine, core_move(other)))
     scores, norm = kernel_call(
         unpack_kernel, [VMEM] * 4, [shaped(ROWS, HALF), shaped(8, 128)], (message, *y_moves(message))
@@ -475,12 +485,12 @@
     part = shaped(QUARTER * ROWS + 16, 128, dtype=BF16)
     own, curv, one, two, three = kernel_call(
         hessian_kernel,
-        [HBM] + [VMEM] * 3,
+        [VMEM] * 4,
         [shaped(QUARTER * ROWS, 128), shaped(8, 128), part, part, part],
-        (events, scores, core_move(scores), rate),
-        [pltpu.VMEM((ROWS + 16, COUNT), BF16), *columns],
+        (held, scores, core_move(scores), rate),
+        [pltpu.VMEM((ROWS + 16, COUNT), BF16)],
         micros=4,
-        room=ROOM,
+        room=8,
     )
     moved = [
         lax.ppermute(v, "event", [(i, (i + k * ZN) % EN) for i in range(EN)])
@@ -498,9 +508,9 @@
 
     other, mine, first = kernel_call(
         second_kernel,
-        [VMEM] + [VMEM] * 6,
+        [VMEM] * 7,
         half + [shaped(TILES, 128)],
-        (events, rhs, grad, message, *x_moves(message)),
+        (held, rhs, grad, message, *x_moves(message)),
         [pltpu.VMEM((features, 128), BF16)],
         micros=4,
         room=8,

time: 165 us -> 156 us (0.945)
  Pallas kernels: 30.4 us -> 24.4 us
  waiting for transfers between devices: 41.6 us -> 38.8 us
    pallas_call x14 -> x15, Pallas kernels: 30.4 us -> 24.4 us  [kernel_call(): pl.pallas_call(body, out_shape=outs, in_specs=ins, out_specs=[VMEM] * len...]
    ppermute x9, waiting for transfers between devices: 18 us -> 15.3 us  [y_moves(): lax.ppermute(v, 'feat', [(i, (i + k * CN) % n) for i in range(n)])]
  transfers between devices with their start and end apart: 24 -> 24, of which waited for: 22 -> 21; matrix products, arithmetic and copies ran while one was open for 0% -> 0% of each run, Pallas kernels for 3% -> 4%
where the time goes in v5:
time: 156 us
  blocking collectives  48.5 us (31%)
  starting transfers between devices  42.7 us (27%)
  waiting for transfers between devices  38.8 us (25%)
  Pallas kernels  24.4 us (16%)
    all_to_all x3, blocking collectives, z_exchange(): return lax.all_to_all(v, 'event', 0, 0, axis_index_groups=groups)  36.9 us
    pallas_call x15, Pallas kernels, kernel_call(): pl.pallas_call(body, out_shape=outs, in_specs=ins, out_specs=[VMEM] * len...  24.4 us
    ppermute x9, waiting for transfers between devices, y_moves(): lax.ppermute(v, 'feat', [(i, (i + k * CN) % n) for i in range(n)])  15.3 us
    ppermute x5, starting transfers between devices, core_move(): return lax.ppermute(v, 'feat', [(i, i ^ 1) for i in range(YN * CN)])  12.7 us
    ppermute x6, waiting for transfers between devices, x_moves(): lax.ppermute(v, 'event', [(i, (i + k * ZN) % n) for i in range(n)])  12.2 us
    all_to_all x1, starting transfers between devices, on_device(): chunks = lax.all_to_all(picked, 'event', 0, 0)  12 us
    all_to_all x1, blocking collectives, on_device(): lax.all_to_all(jnp.broadcast_to(tail[None], (EN, 1, 128)), 'event', 0, 0)  11.6 us
    ppermute x9, starting transfers between devices, y_moves(): lax.ppermute(v, 'feat', [(i, (i + k * CN) % n) for i in range(n)])  8.52 us
  transfers between devices with their start and end apart: 24, of which 21 were waited for; matrix products, arithmetic and copies ran while one was open for 0% of the time, Pallas kernels for 4%

profile of v5, /device:TPU:1, one launch (start us, length us, event | category | flops | bytes accessed | tf_op | source)
XLA Modules:
  0.0 155.8 jit_solution(11248824049288251978)
XLA Ops:
  0.7 0.7 copy-done.2
  1.3 3.7 %shard_map.59._after = bf16[32,64,128]{2,1,0:T(8,128)(2,1)} custom-call(s32[63]{0:T(128)S(1)} %copy-done.2, bf16[1280,4096]{1,0:T(8,128)(2,1)} %events_ref.5), custom_call_target="tpu_custom_call" | custom-call | bytes 7200000 | tf_op jit(solution)/shard_map/pallas_call | solution.py:30
  5.0 12.0 %all-to-all-start = ((bf16[32,64,128]{2,1,0:T(8,128)(2,1)}), bf16[32,64,128]{2,1,0:T(8,128)(2,1)S(1)}, u32[]{:S(2)}, u32[]{:S(2)}) async-start(bf16[32,64,128]{2,1,0:T(8,128)(2,1)} %shard_map.59._after), calls=%async_computation | async-start | bytes 1048576 | tf_op jit(solution)/shard_map/all_to_all | solution.py:440
  17.0 4.9 %shard_map.60 = (f32[10,128]{1,0:T(8,128)S(1)}, bf16[1280,4096]{1,0:T(8,128)(2,1)S(1)}) custom-call(f32[1,4096]{1,0:T(1,128)S(1)} %bitcast.7, bf16[1280,4096]{1,0:T(8,128)(2,1)} %events_ref.5, bf16[32,64,128]{2,1,0:T(8,128)(2,1)} %shard_map.59._after), custom_call_target="tpu_custom_call" | custom-call | bytes 14400000 | tf_op jit(solution)/shard_map/pallas_call | solution.py:30
  21.9 1.0 collective-permute-start
  22.9 0.8 collective-permute-done
  23.8 2.7 %collective-permute-start.3 = (f32[10,128]{1,0:T(8,128)S(1)}, f32[10,128]{1,0:T(8,128)S(1)}, u32[]{:S(2)}, u32[]{:S(2)}) collective-permute-start(f32[10,128]{1,0:T(8,128)S(1)} %add.6.own), channel_id=1, source_target_pairs={{0,6},{1,7},{2,0},{3,1},{4,2},{5,3},{6,4},{7,5},{8,14},{9,15},{10,... | collective-permute-start | bytes 15368 | tf_op jit(solution)/shard_map/ppermute | solution.py:48
  26.5 0.3 collective-permute-start.2
  26.8 0.7 collective-permute-start.1
  27.5 0.0 collective-permute-done.3.three
  27.5 3.3 %collective-permute-done.2.two = f32[10,128]{1,0:T(8,128)S(1)} collective-permute-done((f32[10,128]{1,0:T(8,128)S(1)}, f32[10,128]{1,0:T(8,128)S(1)}, u32[]{:S(2)}, u32[]{:S(2)}) %collective-permute-start.2) | collective-permute-done | bytes 5152 | tf_op jit(solution)/shard_map/ppermute | solution.py:48
  30.8 0.1 collective-permute-done.1.one
  30.9 1.5 shard_map.61
  32.4 0.1 shard_map.62
  32.5 15.7 %all_to_all.25.in_ref = bf16[8,128,128]{2,1,0:T(8,128)(2,1)S(1)} all-to-all(bf16[8,128,128]{2,1,0:T(8,128)(2,1)S(1)} %shard_map.62), channel_id=1, replica_groups={{0,8,16,24,32,40,48,56},{64,72,80,88,96,104,112,120},{128,136,144,152,1..., dimensions={0} | all-to-all | bytes 524288 | tf_op jit(solution)/shard_map/all_to_all | solution.py:57
  48.2 2.5 %collective-permute-start.6 = (bf16[576,128]{1,0:T(8,128)(2,1)S(1)}, bf16[576,128]{1,0:T(8,128)(2,1)S(1)}, u32[]{:S(2)}, u32[]{:S(2)}) collective-permute-start(bf16[576,128]{1,0:T(8,128)(2,1)S(1)} %shard_map.63.own), channel_id=1, source_target_pairs={{0,192},{8,200},{16,208},{24,216},{32,224},{40,232},{48,240},{56,2... | collective-permute-start | bytes 442376 | tf_op jit(solution)/shard_map/ppermute | solution.py:43
  50.7 0.5 collective-permute-start.5
  51.2 0.6 collective-permute-start.4
  51.8 2.6 %collective-permute-done.6.three = bf16[576,128]{1,0:T(8,128)(2,1)S(1)} collective-permute-done((bf16[576,128]{1,0:T(8,128)(2,1)S(1)}, bf16[576,128]{1,0:T(8,128)(2,1)S(1)}, u32[]{:S(2)}, u32[]{:S(2)}) %collective-permute-start.6) | collective-permute-done | bytes 147488 | tf_op jit(solution)/shard_map/ppermute | solution.py:43
  54.4 1.9 %collective-permute-done.5.two = bf16[576,128]{1,0:T(8,128)(2,1)S(1)} collective-permute-done((bf16[576,128]{1,0:T(8,128)(2,1)S(1)}, bf16[576,128]{1,0:T(8,128)(2,1)S(1)}, u32[]{:S(2)}, u32[]{:S(2)}) %collective-permute-start.5) | collective-permute-done | bytes 147488 | tf_op jit(solution)/shard_map/ppermute | solution.py:43
  56.3 1.5 collective-permute-done.4.one
  57.8 7.6 %shard_map.64 = (bf16[64,4096]{1,0:T(8,128)(2,1)S(1)}, f32[32,128]{1,0:T(8,128)S(1)}, f32[72,640]{1,0:T(8,128)S(1)}, f32[72,640]{1,0:T(8,128)S(1)}, bf16[1280,4096]{1,0:T(8,128)(2,1)S(1)}) custom-call(bf16[1280,4096]{1,0:T(8,128)(2,1)} %events_ref.5, f32[32,128]{1,0:T(8,128)S(1)} %bitcast.8, bf16[576,128]{1,0:T(8,128)(2,1)S(1)} %shard_map.63.own, ...), custom_call_target="tpu_custom_call" | custom-call | bytes 14400000 | tf_op jit(solution)/shard_map/pallas_call | solution.py:30
  65.4 4.9 %collective-permute-start.7 = (f32[72,640]{1,0:T(8,128)S(1)}, f32[72,640]{1,0:T(8,128)S(1)}, u32[]{:S(2)}, u32[]{:S(2)}) collective-permute-start(f32[72,640]{1,0:T(8,128)S(1)} %get-tuple-element.34), channel_id=1, source_target_pairs={{0,1},{1,0},{2,3},{3,2},{4,5},{5,4},{6,7},{7,6},{8,9},{9,8},{10,11... | collective-permute-start | bytes 552968 | tf_op jit(solution)/shard_map/ppermute | solution.py:52
  70.3 1.1 collective-permute-done.7.other
  71.4 0.8 collective-permute-start.10
  72.1 1.2 collective-permute-start.9
  73.3 0.8 collective-permute-start.8
  74.0 1.3 collective-permute-done.10.three
  75.3 1.7 %collective-permute-done.9.two = bf16[72,640]{1,0:T(8,128)(2,1)S(1)} collective-permute-done((bf16[72,640]{1,0:T(8,128)(2,1)S(1)}, bf16[72,640]{1,0:T(8,128)(2,1)S(1)}, u32[]{:S(2)}, u32[]{:S(2)}) %collective-permute-start.9) | collective-permute-done | bytes 92192 | tf_op jit(solution)/shard_map/ppermute | solution.py:48
  77.0 2.8 %collective-permute-done.8.one = bf16[72,640]{1,0:T(8,128)(2,1)S(1)} collective-permute-done((bf16[72,640]{1,0:T(8,128)(2,1)S(1)}, bf16[72,640]{1,0:T(8,128)(2,1)S(1)}, u32[]{:S(2)}, u32[]{:S(2)}) %collective-permute-start.8) | collective-permute-done | bytes 92192 | tf_op jit(solution)/shard_map/ppermute | solution.py:48
  79.8 0.1 shard_map.66
  79.9 0.9 collective-permute-start.11
  80.8 1.0 collective-permute-done.11.theirs_ref
  81.8 2.0 %shard_map.67 = (f32[512,128]{1,0:T(8,128)S(1)}, f32[8,128]{1,0:T(8,128)S(1)}, bf16[528,128]{1,0:T(8,128)(2,1)S(1)}, bf16[528,128]{1,0:T(8,128)(2,1)S(1)}, bf16[528,128]{1,0:T(8,128)(2,1)S(1)}) custom-call(bf16[1280,4096]{1,0:T(8,128)(2,1)S(1)} %get-tuple-element.30.events_ref, f32[64,640]{1,0:T(8,128)S(1)} %get-tuple-element.35.mine_ref.scores_ref, ...), custom_call_target="tpu_custom_call" | custom-call | bytes 14400000 | tf_op jit(solution)/shard_map/pallas_call | solution.py:30
  83.8 0.1 collective-permute-start.12
  83.9 1.5 collective-permute-start.13
  85.4 1.2 collective-permute-start.14
  86.6 6.2 %collective-permute-done.12.one = bf16[528,128]{1,0:T(8,128)(2,1)S(1)} collective-permute-done((bf16[528,128]{1,0:T(8,128)(2,1)S(1)}, bf16[528,128]{1,0:T(8,128)(2,1)S(1)}, u32[]{:S(2)}, u32[]{:S(2)}) %collective-permute-start.12) | collective-permute-done | bytes 135200 | tf_op jit(solution)/shard_map/ppermute | solution.py:496
  92.8 0.3 collective-permute-done.14.three
  93.2 0.1 shard_map.68
  93.2 10.6 %all_to_all.26.in_ref = bf16[8,72,128]{2,1,0:T(8,128)(2,1)S(1)} all-to-all(bf16[8,72,128]{2,1,0:T(8,128)(2,1)S(1)} %shard_map.68), channel_id=1, replica_groups={{0,8,16,24,32,40,48,56},{64,72,80,88,96,104,112,120},{128,136,144,152,1..., dimensions={0} | all-to-all | bytes 294912 | tf_op jit(solution)/shard_map/all_to_all | solution.py:57
  103.8 0.1 shard_map.69
  103.9 10.6 %all_to_all.27.own = bf16[8,72,128]{2,1,0:T(8,128)(2,1)S(1)} all-to-all(bf16[8,72,128]{2,1,0:T(8,128)(2,1)S(1)} %get-tuple-element.43), channel_id=1, replica_groups={{0,8,16,24,32,40,48,56},{64,72,80,88,96,104,112,120},{128,136,144,152,1..., dimensions={0} | all-to-all | bytes 294912 | tf_op jit(solution)/shard_map/all_to_all | solution.py:57
  114.5 2.5 %collective-permute-start.17 = (bf16[8,72,128]{2,1,0:T(8,128)(2,1)S(1)}, bf16[8,72,128]{2,1,0:T(8,128)(2,1)S(1)}, u32[]{:S(2)}, u32[]{:S(2)}) collective-permute-start(bf16[8,72,128]{2,1,0:T(8,128)(2,1)S(1)} %all_to_all.27.own), channel_id=1, source_target_pairs={{0,192},{8,200},{16,208},{24,216},{32,224},{40,232},{48,240},{56,2... | collective-permute-start | bytes 442376 | tf_op jit(solution)/shard_map/ppermute | solution.py:43
  117.0 0.0 collective-permute-start.16
  117.1 0.6 collective-permute-start.15
  117.6 3.1 %collective-permute-done.17.three = bf16[8,72,128]{2,1,0:T(8,128)(2,1)S(1)} collective-permute-done((bf16[8,72,128]{2,1,0:T(8,128)(2,1)S(1)}, bf16[8,72,128]{2,1,0:T(8,128)(2,1)S(1)}, u32[]{:S(2)}, u32[]{:S(2)}) %collective-permute-start.17) | collective-permute-done | bytes 147488 | tf_op jit(solution)/shard_map/ppermute | solution.py:43
  120.7 1.9 %collective-permute-done.16.two = bf16[8,72,128]{2,1,0:T(8,128)(2,1)S(1)} collective-permute-done((bf16[8,72,128]{2,1,0:T(8,128)(2,1)S(1)}, bf16[8,72,128]{2,1,0:T(8,128)(2,1)S(1)}, u32[]{:S(2)}, u32[]{:S(2)}) %collective-permute-start.16) | collective-permute-done | bytes 147488 | tf_op jit(solution)/shard_map/ppermute | solution.py:43
  122.7 1.2 collective-permute-done.15.one
  123.8 3.4 %shard_map.70 = (f32[72,640]{1,0:T(8,128)S(1)}, f32[72,640]{1,0:T(8,128)S(1)}, f32[32,128]{1,0:T(8,128)S(1)}) custom-call(bf16[1280,4096]{1,0:T(8,128)(2,1)S(1)} %get-tuple-element.30.events_ref, bf16[64,4096]{1,0:T(8,128)(2,1)S(1)} %get-tuple-element.31.rhs_ref, f32[32,128]{1,0:T(8,128)S(1)} %get-tuple-element.32.grad_ref, ...), custom_call_target="tpu_custom_call" | custom-call | bytes 14400000 | tf_op jit(solution)/shard_map/pallas_call | solution.py:30
  127.2 4.9 %collective-permute-start.18 = (f32[72,640]{1,0:T(8,128)S(1)}, f32[72,640]{1,0:T(8,128)S(1)}, u32[]{:S(2)}, u32[]{:S(2)}) collective-permute-start(f32[72,640]{1,0:T(8,128)S(1)} %get-tuple-element.45), channel_id=1, source_target_pairs={{0,1},{1,0},{2,3},{3,2},{4,5},{5,4},{6,7},{7,6},{8,9},{9,8},{10,11... | collective-permute-start | bytes 552968 | tf_op jit(solution)/shard_map/ppermute | solution.py:52
  132.2 1.1 collective-permute-done.18.other
  133.2 0.1 shard_map.71.own
  133.3 0.5 collective-permute-start.21
  133.7 1.0 collective-permute-start.20
  134.8 0.6 collective-permute-start.19
  135.3 1.9 %collective-permute-done.21.three = bf16[72,640]{1,0:T(8,128)(2,1)S(1)} collective-permute-done((bf16[72,640]{1,0:T(8,128)(2,1)S(1)}, bf16[72,640]{1,0:T(8,128)(2,1)S(1)}, u32[]{:S(2)}, u32[]{:S(2)}) %collective-permute-start.21) | collective-permute-done | bytes 92192 | tf_op jit(solution)/shard_map/ppermute | solution.py:48
  137.2 1.5 collective-permute-done.20.two
  138.7 2.8 %collective-permute-done.19.one = bf16[72,640]{1,0:T(8,128)(2,1)S(1)} collective-permute-done((bf16[72,640]{1,0:T(8,128)(2,1)S(1)}, bf16[72,640]{1,0:T(8,128)(2,1)S(1)}, u32[]{:S(2)}, u32[]{:S(2)}) %collective-permute-start.19) | collective-permute-done | bytes 92192 | tf_op jit(solution)/shard_map/ppermute | solution.py:48
  141.5 0.2 shard_map.72
  141.6 0.9 collective-permute-start.22
  142.5 0.8 collective-permute-done.22
  143.4 11.6 %all_to_all.28.tails_ref = f32[32,1,128]{2,1,0:T(1,128)S(1)} all-to-all(f32[32,1,128]{2,1,0:T(1,128)S(1)} %broadcast_in_dim.9), channel_id=1, replica_groups=mesh['event'=32,'feat'=8] {'event'}, dimensions={0} | all-to-all | bytes 32768 | tf_op jit(solution)/shard_map/all_to_all | solution.py:526
  155.0 0.8 shard_map.73
  (12 shorter events, 0.1 us)
Async XLA Ops:
  0.6 16.4 %copy-start = (f32[4096]{0:T(1024)S(1)}, f32[4096]{0:T(1024)}, u32[]{:S(2)}) copy-start(f32[4096]{0:T(1024)} %param.6) | copy-start | bytes 49156
  0.6 0.7 copy-start.2
  1.3 29.6 %copy-start.1 = (s32[1280]{0:T(1024)S(1)}, s32[1280]{0:T(1024)}, u32[]{:S(2)}) copy-start(s32[1280]{0:T(1024)} %param.5) | copy-start | bytes 15364
  5.0 27.4 %all-to-all-start = ((bf16[32,64,128]{2,1,0:T(8,128)(2,1)}), bf16[32,64,128]{2,1,0:T(8,128)(2,1)S(1)}, u32[]{:S(2)}, u32[]{:S(2)}) async-start(bf16[32,64,128]{2,1,0:T(8,128)(2,1)} %shard_map.59._after), calls=%async_computation | async-start | bytes 1048576 | tf_op jit(solution)/shard_map/all_to_all | solution.py:440
  21.9 1.9 %collective-permute-start = (f32[10,128]{1,0:T(8,128)S(1)}, f32[10,128]{1,0:T(8,128)S(1)}, u32[]{:S(2)}, u32[]{:S(2)}) collective-permute-start(f32[10,128]{1,0:T(8,128)S(1)} %get-tuple-element.28), channel_id=1, source_target_pairs={{0,1},{1,0},{2,3},{3,2},{4,5},{5,4},{6,7},{7,6},{8,9},{9,8},{10,11... | collective-permute-start | bytes 15368 | tf_op jit(solution)/shard_map/ppermute | solution.py:52
  23.8 3.8 %collective-permute-start.3 = (f32[10,128]{1,0:T(8,128)S(1)}, f32[10,128]{1,0:T(8,128)S(1)}, u32[]{:S(2)}, u32[]{:S(2)}) collective-permute-start(f32[10,128]{1,0:T(8,128)S(1)} %add.6.own), channel_id=1, source_target_pairs={{0,6},{1,7},{2,0},{3,1},{4,2},{5,3},{6,4},{7,5},{8,14},{9,15},{10,... | collective-permute-start | bytes 15368 | tf_op jit(solution)/shard_map/ppermute | solution.py:48
  26.5 4.3 %collective-permute-start.2 = (f32[10,128]{1,0:T(8,128)S(1)}, f32[10,128]{1,0:T(8,128)S(1)}, u32[]{:S(2)}, u32[]{:S(2)}) collective-permute-start(f32[10,128]{1,0:T(8,128)S(1)} %add.6.own), channel_id=1, source_target_pairs={{0,4},{1,5},{2,6},{3,7},{4,0},{5,1},{6,2},{7,3},{8,12},{9,13},{10,... | collective-permute-start | bytes 15368 | tf_op jit(solution)/shard_map/ppermute | solution.py:48
  26.8 4.0 %collective-permute-start.1 = (f32[10,128]{1,0:T(8,128)S(1)}, f32[10,128]{1,0:T(8,128)S(1)}, u32[]{:S(2)}, u32[]{:S(2)}) collective-permute-start(f32[10,128]{1,0:T(8,128)S(1)} %add.6.own), channel_id=1, source_target_pairs={{0,2},{1,3},{2,4},{3,5},{4,6},{5,7},{6,0},{7,1},{8,10},{9,11},{10,... | collective-permute-start | bytes 15368 | tf_op jit(solution)/shard_map/ppermute | solution.py:48
  48.2 6.2 %collective-permute-start.6 = (bf16[576,128]{1,0:T(8,128)(2,1)S(1)}, bf16[576,128]{1,0:T(8,128)(2,1)S(1)}, u32[]{:S(2)}, u32[]{:S(2)}) collective-permute-start(bf16[576,128]{1,0:T(8,128)(2,1)S(1)} %shard_map.63.own), channel_id=1, source_target_pairs={{0,192},{8,200},{16,208},{24,216},{32,224},{40,232},{48,240},{56,2... | collective-permute-start | bytes 442376 | tf_op jit(solution)/shard_map/ppermute | solution.py:43
  50.7 5.6 %collective-permute-start.5 = (bf16[576,128]{1,0:T(8,128)(2,1)S(1)}, bf16[576,128]{1,0:T(8,128)(2,1)S(1)}, u32[]{:S(2)}, u32[]{:S(2)}) collective-permute-start(bf16[576,128]{1,0:T(8,128)(2,1)S(1)} %shard_map.63.own), channel_id=1, source_target_pairs={{0,128},{8,136},{16,144},{24,152},{32,160},{40,168},{48,176},{56,1... | collective-permute-start | bytes 442376 | tf_op jit(solution)/shard_map/ppermute | solution.py:43
  51.2 6.6 %collective-permute-start.4 = (bf16[576,128]{1,0:T(8,128)(2,1)S(1)}, bf16[576,128]{1,0:T(8,128)(2,1)S(1)}, u32[]{:S(2)}, u32[]{:S(2)}) collective-permute-start(bf16[576,128]{1,0:T(8,128)(2,1)S(1)} %shard_map.63.own), channel_id=1, source_target_pairs={{0,64},{8,72},{16,80},{24,88},{32,96},{40,104},{48,112},{56,120},{... | collective-permute-start | bytes 442376 | tf_op jit(solution)/shard_map/ppermute | solution.py:43
  65.4 5.9 %collective-permute-start.7 = (f32[72,640]{1,0:T(8,128)S(1)}, f32[72,640]{1,0:T(8,128)S(1)}, u32[]{:S(2)}, u32[]{:S(2)}) collective-permute-start(f32[72,640]{1,0:T(8,128)S(1)} %get-tuple-element.34), channel_id=1, source_target_pairs={{0,1},{1,0},{2,3},{3,2},{4,5},{5,4},{6,7},{7,6},{8,9},{9,8},{10,11... | collective-permute-start | bytes 552968 | tf_op jit(solution)/shard_map/ppermute | solution.py:52
  71.4 4.0 %collective-permute-start.10 = (bf16[72,640]{1,0:T(8,128)(2,1)S(1)}, bf16[72,640]{1,0:T(8,128)(2,1)S(1)}, u32[]{:S(2)}, u32[]{:S(2)}) collective-permute-start(bf16[72,640]{1,0:T(8,128)(2,1)S(1)} %shard_map.65.own), channel_id=1, source_target_pairs={{0,6},{1,7},{2,0},{3,1},{4,2},{5,3},{6,4},{7,5},{8,14},{9,15},{10,... | collective-permute-start | bytes 276488 | tf_op jit(solution)/shard_map/ppermute | solution.py:48
  72.1 4.9 %collective-permute-start.9 = (bf16[72,640]{1,0:T(8,128)(2,1)S(1)}, bf16[72,640]{1,0:T(8,128)(2,1)S(1)}, u32[]{:S(2)}, u32[]{:S(2)}) collective-permute-start(bf16[72,640]{1,0:T(8,128)(2,1)S(1)} %shard_map.65.own), channel_id=1, source_target_pairs={{0,4},{1,5},{2,6},{3,7},{4,0},{5,1},{6,2},{7,3},{8,12},{9,13},{10,... | collective-permute-start | bytes 276488 | tf_op jit(solution)/shard_map/ppermute | solution.py:48
  73.3 6.6 %collective-permute-start.8 = (bf16[72,640]{1,0:T(8,128)(2,1)S(1)}, bf16[72,640]{1,0:T(8,128)(2,1)S(1)}, u32[]{:S(2)}, u32[]{:S(2)}) collective-permute-start(bf16[72,640]{1,0:T(8,128)(2,1)S(1)} %shard_map.65.own), channel_id=1, source_target_pairs={{0,2},{1,3},{2,4},{3,5},{4,6},{5,7},{6,0},{7,1},{8,10},{9,11},{10,... | collective-permute-start | bytes 276488 | tf_op jit(solution)/shard_map/ppermute | solution.py:48
  79.9 1.9 %collective-permute-start.11 = (f32[64,640]{1,0:T(8,128)S(1)}, f32[64,640]{1,0:T(8,128)S(1)}, u32[]{:S(2)}, u32[]{:S(2)}) collective-permute-start(f32[64,640]{1,0:T(8,128)S(1)} %get-tuple-element.35.mine_ref.scores_ref), channel_id=1, source_target_pairs={{0,1},{1,0},{2,3},{3,2},{4,5},{5,4},{6,7},{7,6},{8,9},{9,8},{10,11... | collective-permute-start | bytes 491528 | tf_op jit(solution)/shard_map/ppermute | solution.py:52
  83.8 9.0 %collective-permute-start.12 = (bf16[528,128]{1,0:T(8,128)(2,1)S(1)}, bf16[528,128]{1,0:T(8,128)(2,1)S(1)}, u32[]{:S(2)}, u32[]{:S(2)}) collective-permute-start(bf16[528,128]{1,0:T(8,128)(2,1)S(1)} %get-tuple-element.39), channel_id=1, source_target_pairs={{0,64},{8,72},{16,80},{24,88},{32,96},{40,104},{48,112},{56,120},{... | collective-permute-start | bytes 405512 | tf_op jit(solution)/shard_map/ppermute | solution.py:496
  83.9 8.9 %collective-permute-start.13 = (bf16[528,128]{1,0:T(8,128)(2,1)S(1)}, bf16[528,128]{1,0:T(8,128)(2,1)S(1)}, u32[]{:S(2)}, u32[]{:S(2)}) collective-permute-start(bf16[528,128]{1,0:T(8,128)(2,1)S(1)} %get-tuple-element.40), channel_id=1, source_target_pairs={{0,128},{8,136},{16,144},{24,152},{32,160},{40,168},{48,176},{56,1... | collective-permute-start | bytes 405512 | tf_op jit(solution)/shard_map/ppermute | solution.py:496
  85.4 7.8 %collective-permute-start.14 = (bf16[528,128]{1,0:T(8,128)(2,1)S(1)}, bf16[528,128]{1,0:T(8,128)(2,1)S(1)}, u32[]{:S(2)}, u32[]{:S(2)}) collective-permute-start(bf16[528,128]{1,0:T(8,128)(2,1)S(1)} %get-tuple-element.41), channel_id=1, source_target_pairs={{0,192},{8,200},{16,208},{24,216},{32,224},{40,232},{48,240},{56,2... | collective-permute-start | bytes 405512 | tf_op jit(solution)/shard_map/ppermute | solution.py:496
  114.5 6.2 %collective-permute-start.17 = (bf16[8,72,128]{2,1,0:T(8,128)(2,1)S(1)}, bf16[8,72,128]{2,1,0:T(8,128)(2,1)S(1)}, u32[]{:S(2)}, u32[]{:S(2)}) collective-permute-start(bf16[8,72,128]{2,1,0:T(8,128)(2,1)S(1)} %all_to_all.27.own), channel_id=1, source_target_pairs={{0,192},{8,200},{16,208},{24,216},{32,224},{40,232},{48,240},{56,2... | collective-permute-start | bytes 442376 | tf_op jit(solution)/shard_map/ppermute | solution.py:43
  117.0 5.6 %collective-permute-start.16 = (bf16[8,72,128]{2,1,0:T(8,128)(2,1)S(1)}, bf16[8,72,128]{2,1,0:T(8,128)(2,1)S(1)}, u32[]{:S(2)}, u32[]{:S(2)}) collective-permute-start(bf16[8,72,128]{2,1,0:T(8,128)(2,1)S(1)} %all_to_all.27.own), channel_id=1, source_target_pairs={{0,128},{8,136},{16,144},{24,152},{32,160},{40,168},{48,176},{56,1... | collective-permute-start | bytes 442376 | tf_op jit(solution)/shard_map/ppermute | solution.py:43
  117.1 6.8 %collective-permute-start.15 = (bf16[8,72,128]{2,1,0:T(8,128)(2,1)S(1)}, bf16[8,72,128]{2,1,0:T(8,128)(2,1)S(1)}, u32[]{:S(2)}, u32[]{:S(2)}) collective-permute-start(bf16[8,72,128]{2,1,0:T(8,128)(2,1)S(1)} %all_to_all.27.own), channel_id=1, source_target_pairs={{0,64},{8,72},{16,80},{24,88},{32,96},{40,104},{48,112},{56,120},{... | collective-permute-start | bytes 442376 | tf_op jit(solution)/shard_map/ppermute | solution.py:43
  127.2 6.0 %collective-permute-start.18 = (f32[72,640]{1,0:T(8,128)S(1)}, f32[72,640]{1,0:T(8,128)S(1)}, u32[]{:S(2)}, u32[]{:S(2)}) collective-permute-start(f32[72,640]{1,0:T(8,128)S(1)} %get-tuple-element.45), channel_id=1, source_target_pairs={{0,1},{1,0},{2,3},{3,2},{4,5},{5,4},{6,7},{7,6},{8,9},{9,8},{10,11... | collective-permute-start | bytes 552968 | tf_op jit(solution)/shard_map/ppermute | solution.py:52
  133.3 4.0 %collective-permute-start.21 = (bf16[72,640]{1,0:T(8,128)(2,1)S(1)}, bf16[72,640]{1,0:T(8,128)(2,1)S(1)}, u32[]{:S(2)}, u32[]{:S(2)}) collective-permute-start(bf16[72,640]{1,0:T(8,128)(2,1)S(1)} %shard_map.71.own), channel_id=1, source_target_pairs={{0,6},{1,7},{2,0},{3,1},{4,2},{5,3},{6,4},{7,5},{8,14},{9,15},{10,... | collective-permute-start | bytes 276488 | tf_op jit(solution)/shard_map/ppermute | solution.py:48
  133.7 4.9 %collective-permute-start.20 = (bf16[72,640]{1,0:T(8,128)(2,1)S(1)}, bf16[72,640]{1,0:T(8,128)(2,1)S(1)}, u32[]{:S(2)}, u32[]{:S(2)}) collective-permute-start(bf16[72,640]{1,0:T(8,128)(2,1)S(1)} %shard_map.71.own), channel_id=1, source_target_pairs={{0,4},{1,5},{2,6},{3,7},{4,0},{5,1},{6,2},{7,3},{8,12},{9,13},{10,... | collective-permute-start | bytes 276488 | tf_op jit(solution)/shard_map/ppermute | solution.py:48
  134.8 6.7 %collective-permute-start.19 = (bf16[72,640]{1,0:T(8,128)(2,1)S(1)}, bf16[72,640]{1,0:T(8,128)(2,1)S(1)}, u32[]{:S(2)}, u32[]{:S(2)}) collective-permute-start(bf16[72,640]{1,0:T(8,128)(2,1)S(1)} %shard_map.71.own), channel_id=1, source_target_pairs={{0,2},{1,3},{2,4},{3,5},{4,6},{5,7},{6,0},{7,1},{8,10},{9,11},{10,... | collective-permute-start | bytes 276488 | tf_op jit(solution)/shard_map/ppermute | solution.py:48
  141.6 1.7 %collective-permute-start.22 = (f32[1,128]{1,0:T(1,128)S(1)}, f32[1,128]{1,0:T(1,128)S(1)}, u32[]{:S(2)}, u32[]{:S(2)}) collective-permute-start(f32[1,128]{1,0:T(1,128)S(1)} %get-tuple-element.46), channel_id=1, source_target_pairs={{0,1},{1,0},{2,3},{3,2},{4,5},{5,4},{6,7},{7,6},{8,9},{9,8},{10,11... | collective-permute-start | bytes 1544 | tf_op jit(solution)/shard_map/ppermute | solution.py:52

commit v6 on v5

--- a/solution.py
+++ b/solution.py
@@ -13,7 +13,7 @@
 QUARTER = TILES // XN
 COUNT = 1280
 HALF = COUNT // 2
-WINDOW = 4
+WINDOW = 10
 ROOM = 48
 F32, BF16 = jnp.float32, jnp.bfloat16
 VMEM = pl.BlockSpec(memory_space=pltpu.VMEM)
@@ -181,6 +181,12 @@
             sums.append(total)
         turned = jnp.transpose(jnp.concatenate(sums, axis=0))
         margin_ref[c : c + 1, :] = jnp.sum(turned, axis=0, keepdims=True)
+
+
+def load_kernel(events_ref, _after, held, sems):
+    pieces = Rows(events_ref, held, sems, [i * 128 for i in range(COUNT // 128)])
+    for i in range(COUNT // 128):
+        pieces.stream.take(i)
 
 
 def gradient_kernel(events_ref, own, one, two, three, labels_ref, rate_ref, grad_ref, errs):
@@ -222,9 +228,9 @@
     out_ref[QUARTER * ROWS + TILES :, :] = rest
 
 
-def half_stream(events_ref, held, sems, core):
+def halves(events_ref, core):
     starts = [half * HALF + i * 128 for half in (1 - core, core) for i in range(HALF // 128)]
-    return Rows(events_ref, held, sems, starts)
+    return Rows(events_ref, None, None, starts)
 
 
 def put_scores(pieces, rhs, other_ref, own_ref, lines):
@@ -243,10 +249,10 @@
 
 
 def scores_kernel(
-    events_ref, w_ref, own, one, two, three, rhs_ref, grad_ref, other_ref, mine_ref, held, rhs, sems
+    events_ref, w_ref, own, one, two, three, rhs_ref, grad_ref, other_ref, mine_ref, rhs
 ):
     x, _, core = place()
-    pieces = half_stream(events_ref, held, sems, core)
+    pieces = halves(events_ref, core)
     tail = QUARTER * ROWS
     grads = [p[tail : tail + TILES, :].astype(F32) + p[tail + TILES :, :].astype(F32) for p in (own, one, two, three)]
     grad_ref[...] = four(*grads) + LAMBDA * w_ref[...]
@@ -297,12 +303,9 @@
     x, _, core = place()
     outs = ((2, two_ref), (1, one_ref), (3, three_ref), (0, own_ref))
     curv = jnp.zeros((ROWS, 128), F32)
-    first, second = rate_ref[:, :HALF], rate_ref[:, HALF:]
-    mine = core == 0
-    halves = ((theirs_ref, jnp.where(mine, second, first)), (mine_ref, jnp.where(mine, first, second)))
-    for half, (scores_ref, rate) in enumerate(halves):
-        scores = scores_ref[...]
+    for half in range(2):
         at = slice(half * HALF, (half + 1) * HALF)
+        scores, rate = jnp.where(core == half, mine_ref[...], theirs_ref[...]), rate_ref[:, at]
         weighted = rate * scores
         curv = curv + tile_sums(weighted * scores)
         lead = weighted.astype(BF16)
@@ -367,8 +370,8 @@
 def second_kernel(
     events_ref, rhs_ref, grad_ref, own, one, two, three, other_ref, mine_ref, first_ref, res
 ):
-    x, _, _ = place()
-    pieces = Rows(events_ref, None, None, [i * 128 for i in range(COUNT // 128)])
+    x, _, core = place()
+    pieces = halves(events_ref, core)
     norm = jnp.zeros((ROWS, 128), F32)
     cross = jnp.zeros((ROWS, 128), F32)
     for k, part in enumerate((own, one, two, three)):
@@ -466,15 +469,18 @@
         collect_kernel, [VMEM], [shaped(QUARTER * ROWS + 2 * TILES, 128, dtype=BF16)], (message,)
     )
 
+    moved = x_moves(message)
+    (held,) = kernel_call(load_kernel, [HBM, HBM], [whole], (events, message), [sems], micros=5, room=40)
+
     half = [shaped(ROWS + 8, HALF), shaped(ROWS + 8, HALF)]
-    rhs, grad, other, mine, held = kernel_call(
+    rhs, grad, other, mine = kernel_call(
         scores_kernel,
-        [HBM] + [VMEM] * 5,
-        [shaped(ROWS, features, dtype=BF16), shaped(TILES, 128)] + half + [whole],
-        (events, tiled, message, *x_moves(message)),
-        [pltpu.VMEM((features, 128), BF16), sems],
-        micros=4,
-        room=40,
+        [VMEM] * 6,
+        [shaped(ROWS, features, dtype=BF16), shaped(TILES, 128)] + half,
+        (held, tiled, message, *moved),
+        [pltpu.VMEM((features, 128), BF16)],
+        micros=3,
+        room=8,
     )
     packed = [shaped(ROWS + 8, HALF, dtype=BF16)]
     (message,) = kernel_call(pack_kernel, [VMEM] * 2, packed, (mine, core_move(other)))

time: 156 us -> 151 us (0.968)
  waiting for transfers between devices: 38.8 us -> 35.1 us
    ppermute x6, waiting for transfers between devices: 12.2 us -> 8.08 us  [x_moves(): lax.ppermute(v, 'event', [(i, (i + k * ZN) % n) for i in range(n)])]
    pallas_call x15 -> x16, Pallas kernels: 24.4 us -> 23.7 us  [kernel_call(): pl.pallas_call(body, out_shape=outs, in_specs=ins, out_specs=[VMEM] * len...]
  transfers between devices with their start and end apart: 24 -> 24, of which waited for: 21 -> 20; matrix products, arithmetic and copies ran while one was open for 0% -> 0% of each run, Pallas kernels for 4% -> 7%
where the time goes in v6:
time: 151 us
  blocking collectives  48.5 us (32%)
  starting transfers between devices  42.1 us (28%)
  waiting for transfers between devices  35.1 us (23%)
  Pallas kernels  23.7 us (16%)
    all_to_all x3, blocking collectives, z_exchange(): return lax.all_to_all(v, 'event', 0, 0, axis_index_groups=groups)  36.9 us
    pallas_call x16, Pallas kernels, kernel_call(): pl.pallas_call(body, out_shape=outs, in_specs=ins, out_specs=[VMEM] * len...  23.7 us
    ppermute x9, waiting for transfers between devices, y_moves(): lax.ppermute(v, 'feat', [(i, (i + k * CN) % n) for i in range(n)])  15.8 us
    ppermute x5, starting transfers between devices, core_move(): return lax.ppermute(v, 'feat', [(i, i ^ 1) for i in range(YN * CN)])  12.1 us
    all_to_all x1, blocking collectives, on_device(): lax.all_to_all(jnp.broadcast_to(tail[None], (EN, 1, 128)), 'event', 0, 0)  11.6 us
    all_to_all x1, starting transfers between devices, on_device(): chunks = lax.all_to_all(picked, 'event', 0, 0)  11.5 us
    ppermute x9, starting transfers between devices, y_moves(): lax.ppermute(v, 'feat', [(i, (i + k * CN) % n) for i in range(n)])  8.19 us
    ppermute x6, waiting for transfers between devices, x_moves(): lax.ppermute(v, 'event', [(i, (i + k * ZN) % n) for i in range(n)])  8.08 us
  transfers between devices with their start and end apart: 24, of which 20 were waited for; matrix products, arithmetic and copies ran while one was open for 0% of the time, Pallas kernels for 7%

profile of v6, /device:TPU:1, one launch (start us, length us, event | category | flops | bytes accessed | tf_op | source)
XLA Modules:
  0.0 150.8 jit_solution(6158123765012597701)
XLA Ops:
  0.7 0.7 copy-done.2
  1.3 3.7 %shard_map.59._after = bf16[32,64,128]{2,1,0:T(8,128)(2,1)} custom-call(s32[63]{0:T(128)S(1)} %copy-done.2, bf16[1280,4096]{1,0:T(8,128)(2,1)} %events_ref.5), custom_call_target="tpu_custom_call" | custom-call | bytes 7200000 | tf_op jit(solution)/shard_map/pallas_call | solution.py:30
  5.0 11.5 %all-to-all-start = ((bf16[32,64,128]{2,1,0:T(8,128)(2,1)}), bf16[32,64,128]{2,1,0:T(8,128)(2,1)S(1)}, u32[]{:S(2)}, u32[]{:S(2)}) async-start(bf16[32,64,128]{2,1,0:T(8,128)(2,1)} %shard_map.59._after), calls=%async_computation | async-start | bytes 1048576 | tf_op jit(solution)/shard_map/all_to_all | solution.py:443
  16.5 4.4 %shard_map.60 = (f32[10,128]{1,0:T(8,128)S(1)}, bf16[1280,4096]{1,0:T(8,128)(2,1)S(1)}) custom-call(f32[1,4096]{1,0:T(1,128)S(1)} %bitcast.7, bf16[1280,4096]{1,0:T(8,128)(2,1)} %events_ref.5, bf16[32,64,128]{2,1,0:T(8,128)(2,1)} %shard_map.59._after), custom_call_target="tpu_custom_call" | custom-call | bytes 14400000 | tf_op jit(solution)/shard_map/pallas_call | solution.py:30
  20.9 1.0 collective-permute-start
  22.0 0.8 collective-permute-done
  22.8 2.7 %collective-permute-start.3 = (f32[10,128]{1,0:T(8,128)S(1)}, f32[10,128]{1,0:T(8,128)S(1)}, u32[]{:S(2)}, u32[]{:S(2)}) collective-permute-start(f32[10,128]{1,0:T(8,128)S(1)} %add.6.own), channel_id=1, source_target_pairs={{0,6},{1,7},{2,0},{3,1},{4,2},{5,3},{6,4},{7,5},{8,14},{9,15},{10,... | collective-permute-start | bytes 15368 | tf_op jit(solution)/shard_map/ppermute | solution.py:48
  25.5 0.3 collective-permute-start.2
  25.9 0.7 collective-permute-start.1
  26.6 3.3 %collective-permute-done.2.two = f32[10,128]{1,0:T(8,128)S(1)} collective-permute-done((f32[10,128]{1,0:T(8,128)S(1)}, f32[10,128]{1,0:T(8,128)S(1)}, u32[]{:S(2)}, u32[]{:S(2)}) %collective-permute-start.2) | collective-permute-done | bytes 5152 | tf_op jit(solution)/shard_map/ppermute | solution.py:48
  29.8 0.1 collective-permute-done.1.one
  29.9 1.5 shard_map.61
  31.4 0.0 all-to-all-done.chunks_ref
  31.4 0.1 shard_map.62
  31.5 15.7 %all_to_all.25.in_ref = bf16[8,128,128]{2,1,0:T(8,128)(2,1)S(1)} all-to-all(bf16[8,128,128]{2,1,0:T(8,128)(2,1)S(1)} %shard_map.62), channel_id=1, replica_groups={{0,8,16,24,32,40,48,56},{64,72,80,88,96,104,112,120},{128,136,144,152,1..., dimensions={0} | all-to-all | bytes 524288 | tf_op jit(solution)/shard_map/all_to_all | solution.py:57
  47.2 2.5 %collective-permute-start.6 = (bf16[576,128]{1,0:T(8,128)(2,1)S(1)}, bf16[576,128]{1,0:T(8,128)(2,1)S(1)}, u32[]{:S(2)}, u32[]{:S(2)}) collective-permute-start(bf16[576,128]{1,0:T(8,128)(2,1)S(1)} %shard_map.63._after.own), channel_id=1, source_target_pairs={{0,192},{8,200},{16,208},{24,216},{32,224},{40,232},{48,240},{56,2... | collective-permute-start | bytes 442376 | tf_op jit(solution)/shard_map/ppermute | solution.py:43
  49.8 0.5 collective-permute-start.5
  50.3 0.6 collective-permute-start.4
  50.9 4.1 %shard_map.64.events_ref = bf16[1280,4096]{1,0:T(8,128)(2,1)S(1)} custom-call(bf16[1280,4096]{1,0:T(8,128)(2,1)} %events_ref.5, bf16[576,128]{1,0:T(8,128)(2,1)S(1)} %shard_map.63._after.own), custom_call_target="tpu_custom_call" | custom-call | bytes 18000000 | tf_op jit(solution)/shard_map/pallas_call | solution.py:30
  55.0 0.4 collective-permute-done.5.two
  55.4 1.5 collective-permute-done.4.one
  56.8 3.3 %shard_map.65 = (bf16[64,4096]{1,0:T(8,128)(2,1)S(1)}, f32[32,128]{1,0:T(8,128)S(1)}, f32[72,640]{1,0:T(8,128)S(1)}, f32[72,640]{1,0:T(8,128)S(1)}) custom-call(bf16[1280,4096]{1,0:T(8,128)(2,1)S(1)} %shard_map.64.events_ref, f32[32,128]{1,0:T(8,128)S(1)} %bitcast.8, bf16[576,128]{1,0:T(8,128)(2,1)S(1)} %shard_map.63._after.own, ...), custom_call_target="tpu_custom_call" | custom-call | bytes 10800000 | tf_op jit(solution)/shard_map/pallas_call | solution.py:30
  60.2 4.9 %collective-permute-start.7 = (f32[72,640]{1,0:T(8,128)S(1)}, f32[72,640]{1,0:T(8,128)S(1)}, u32[]{:S(2)}, u32[]{:S(2)}) collective-permute-start(f32[72,640]{1,0:T(8,128)S(1)} %get-tuple-element.32), channel_id=1, source_target_pairs={{0,1},{1,0},{2,3},{3,2},{4,5},{5,4},{6,7},{7,6},{8,9},{9,8},{10,11... | collective-permute-start | bytes 552968 | tf_op jit(solution)/shard_map/ppermute | solution.py:52
  65.0 1.1 collective-permute-done.7.other
  66.1 0.1 shard_map.66.own
  66.1 0.8 collective-permute-start.10
  66.9 1.2 collective-permute-start.9
  68.0 0.8 collective-permute-start.8
  68.8 1.3 collective-permute-done.10.three
  70.1 1.7 %collective-permute-done.9.two = bf16[72,640]{1,0:T(8,128)(2,1)S(1)} collective-permute-done((bf16[72,640]{1,0:T(8,128)(2,1)S(1)}, bf16[72,640]{1,0:T(8,128)(2,1)S(1)}, u32[]{:S(2)}, u32[]{:S(2)}) %collective-permute-start.9) | collective-permute-done | bytes 92192 | tf_op jit(solution)/shard_map/ppermute | solution.py:48
  71.8 2.8 %collective-permute-done.8.one = bf16[72,640]{1,0:T(8,128)(2,1)S(1)} collective-permute-done((bf16[72,640]{1,0:T(8,128)(2,1)S(1)}, bf16[72,640]{1,0:T(8,128)(2,1)S(1)}, u32[]{:S(2)}, u32[]{:S(2)}) %collective-permute-start.8) | collective-permute-done | bytes 92192 | tf_op jit(solution)/shard_map/ppermute | solution.py:48
  74.6 0.1 shard_map.67
  74.7 0.9 collective-permute-start.11
  75.6 1.0 collective-permute-done.11.theirs_ref
  76.6 2.0 %shard_map.68 = (f32[512,128]{1,0:T(8,128)S(1)}, f32[8,128]{1,0:T(8,128)S(1)}, bf16[528,128]{1,0:T(8,128)(2,1)S(1)}, bf16[528,128]{1,0:T(8,128)(2,1)S(1)}, bf16[528,128]{1,0:T(8,128)(2,1)S(1)}) custom-call(bf16[1280,4096]{1,0:T(8,128)(2,1)S(1)} %shard_map.64.events_ref, f32[64,640]{1,0:T(8,128)S(1)} %get-tuple-element.33.mine_ref.scores_ref, ...), custom_call_target="tpu_custom_call" | custom-call | bytes 14400000 | tf_op jit(solution)/shard_map/pallas_call | solution.py:30
  78.6 0.1 collective-permute-start.12
  78.7 1.5 collective-permute-start.13
  80.2 1.3 collective-permute-start.14
  81.5 6.1 %collective-permute-done.12.one = bf16[528,128]{1,0:T(8,128)(2,1)S(1)} collective-permute-done((bf16[528,128]{1,0:T(8,128)(2,1)S(1)}, bf16[528,128]{1,0:T(8,128)(2,1)S(1)}, u32[]{:S(2)}, u32[]{:S(2)}) %collective-permute-start.12) | collective-permute-done | bytes 135200 | tf_op jit(solution)/shard_map/ppermute | solution.py:502
  87.6 0.0 collective-permute-done.13.two
  87.6 0.3 collective-permute-done.14.three
  87.9 0.1 shard_map.69
  88.0 10.6 %all_to_all.26.in_ref = bf16[8,72,128]{2,1,0:T(8,128)(2,1)S(1)} all-to-all(bf16[8,72,128]{2,1,0:T(8,128)(2,1)S(1)} %shard_map.69), channel_id=1, replica_groups={{0,8,16,24,32,40,48,56},{64,72,80,88,96,104,112,120},{128,136,144,152,1..., dimensions={0} | all-to-all | bytes 294912 | tf_op jit(solution)/shard_map/all_to_all | solution.py:57
  98.6 0.1 shard_map.70
  98.7 10.6 %all_to_all.27.own = bf16[8,72,128]{2,1,0:T(8,128)(2,1)S(1)} all-to-all(bf16[8,72,128]{2,1,0:T(8,128)(2,1)S(1)} %get-tuple-element.41), channel_id=1, replica_groups={{0,8,16,24,32,40,48,56},{64,72,80,88,96,104,112,120},{128,136,144,152,1..., dimensions={0} | all-to-all | bytes 294912 | tf_op jit(solution)/shard_map/all_to_all | solution.py:57
  109.3 3.2 %collective-permute-start.17 = (bf16[8,72,128]{2,1,0:T(8,128)(2,1)S(1)}, bf16[8,72,128]{2,1,0:T(8,128)(2,1)S(1)}, u32[]{:S(2)}, u32[]{:S(2)}) collective-permute-start(bf16[8,72,128]{2,1,0:T(8,128)(2,1)S(1)} %all_to_all.27.own), channel_id=1, source_target_pairs={{0,192},{8,200},{16,208},{24,216},{32,224},{40,232},{48,240},{56,2... | collective-permute-start | bytes 442376 | tf_op jit(solution)/shard_map/ppermute | solution.py:43
  112.5 0.6 collective-permute-start.15
  113.1 3.1 %collective-permute-done.17.three = bf16[8,72,128]{2,1,0:T(8,128)(2,1)S(1)} collective-permute-done((bf16[8,72,128]{2,1,0:T(8,128)(2,1)S(1)}, bf16[8,72,128]{2,1,0:T(8,128)(2,1)S(1)}, u32[]{:S(2)}, u32[]{:S(2)}) %collective-permute-start.17) | collective-permute-done | bytes 147488 | tf_op jit(solution)/shard_map/ppermute | solution.py:43
  116.1 1.9 %collective-permute-done.16.two = bf16[8,72,128]{2,1,0:T(8,128)(2,1)S(1)} collective-permute-done((bf16[8,72,128]{2,1,0:T(8,128)(2,1)S(1)}, bf16[8,72,128]{2,1,0:T(8,128)(2,1)S(1)}, u32[]{:S(2)}, u32[]{:S(2)}) %collective-permute-start.16) | collective-permute-done | bytes 147488 | tf_op jit(solution)/shard_map/ppermute | solution.py:43
  118.1 1.2 collective-permute-done.15.one
  119.3 3.3 %shard_map.71 = (f32[72,640]{1,0:T(8,128)S(1)}, f32[72,640]{1,0:T(8,128)S(1)}, f32[32,128]{1,0:T(8,128)S(1)}) custom-call(bf16[1280,4096]{1,0:T(8,128)(2,1)S(1)} %shard_map.64.events_ref, bf16[64,4096]{1,0:T(8,128)(2,1)S(1)} %get-tuple-element.29.rhs_ref, f32[32,128]{1,0:T(8,128)S(1)} %get-tuple-element.30.grad_ref, bf16[8,72,128]{2,1,0:T(8,128)(2,1)S(1)} %all_to_all.27.own, ...), custom_call_target="tpu_custom_call" | custom-call | bytes 14400000 | tf_op jit(solution)/shard_map/pallas_call | solution.py:30
  122.6 4.6 %collective-permute-start.18 = (f32[72,640]{1,0:T(8,128)S(1)}, f32[72,640]{1,0:T(8,128)S(1)}, u32[]{:S(2)}, u32[]{:S(2)}) collective-permute-start(f32[72,640]{1,0:T(8,128)S(1)} %get-tuple-element.43), channel_id=1, source_target_pairs={{0,1},{1,0},{2,3},{3,2},{4,5},{5,4},{6,7},{7,6},{8,9},{9,8},{10,11... | collective-permute-start | bytes 552968 | tf_op jit(solution)/shard_map/ppermute | solution.py:52
  127.2 1.1 collective-permute-done.18.other
  128.3 0.5 collective-permute-start.21
  128.8 0.7 collective-permute-start.20
  129.5 0.6 collective-permute-start.19
  130.0 2.2 %collective-permute-done.21.three = bf16[72,640]{1,0:T(8,128)(2,1)S(1)} collective-permute-done((bf16[72,640]{1,0:T(8,128)(2,1)S(1)}, bf16[72,640]{1,0:T(8,128)(2,1)S(1)}, u32[]{:S(2)}, u32[]{:S(2)}) %collective-permute-start.21) | collective-permute-done | bytes 92192 | tf_op jit(solution)/shard_map/ppermute | solution.py:48
  132.2 1.5 collective-permute-done.20.two
  133.7 3.0 %collective-permute-done.19.one = bf16[72,640]{1,0:T(8,128)(2,1)S(1)} collective-permute-done((bf16[72,640]{1,0:T(8,128)(2,1)S(1)}, bf16[72,640]{1,0:T(8,128)(2,1)S(1)}, u32[]{:S(2)}, u32[]{:S(2)}) %collective-permute-start.19) | collective-permute-done | bytes 92192 | tf_op jit(solution)/shard_map/ppermute | solution.py:48
  136.7 0.2 shard_map.73
  136.9 0.7 collective-permute-start.22
  137.6 0.8 collective-permute-done.22
  138.4 11.6 %all_to_all.28.tails_ref = f32[32,1,128]{2,1,0:T(1,128)S(1)} all-to-all(f32[32,1,128]{2,1,0:T(1,128)S(1)} %broadcast_in_dim.9), channel_id=1, replica_groups=mesh['event'=32,'feat'=8] {'event'}, dimensions={0} | all-to-all | bytes 32768 | tf_op jit(solution)/shard_map/all_to_all | solution.py:532
  150.0 0.8 shard_map.74
  (13 shorter events, 0.1 us)
Async XLA Ops:
  0.6 15.9 %copy-start = (f32[4096]{0:T(1024)S(1)}, f32[4096]{0:T(1024)}, u32[]{:S(2)}) copy-start(f32[4096]{0:T(1024)} %param.6) | copy-start | bytes 49156
  0.6 0.7 copy-start.2
  1.3 28.6 %copy-start.1 = (s32[1280]{0:T(1024)S(1)}, s32[1280]{0:T(1024)}, u32[]{:S(2)}) copy-start(s32[1280]{0:T(1024)} %param.5) | copy-start | bytes 15364
  5.0 26.4 %all-to-all-start = ((bf16[32,64,128]{2,1,0:T(8,128)(2,1)}), bf16[32,64,128]{2,1,0:T(8,128)(2,1)S(1)}, u32[]{:S(2)}, u32[]{:S(2)}) async-start(bf16[32,64,128]{2,1,0:T(8,128)(2,1)} %shard_map.59._after), calls=%async_computation | async-start | bytes 1048576 | tf_op jit(solution)/shard_map/all_to_all | solution.py:443
  20.9 1.9 %collective-permute-start = (f32[10,128]{1,0:T(8,128)S(1)}, f32[10,128]{1,0:T(8,128)S(1)}, u32[]{:S(2)}, u32[]{:S(2)}) collective-permute-start(f32[10,128]{1,0:T(8,128)S(1)} %get-tuple-element.27), channel_id=1, source_target_pairs={{0,1},{1,0},{2,3},{3,2},{4,5},{5,4},{6,7},{7,6},{8,9},{9,8},{10,11... | collective-permute-start | bytes 15368 | tf_op jit(solution)/shard_map/ppermute | solution.py:52
  22.8 3.8 %collective-permute-start.3 = (f32[10,128]{1,0:T(8,128)S(1)}, f32[10,128]{1,0:T(8,128)S(1)}, u32[]{:S(2)}, u32[]{:S(2)}) collective-permute-start(f32[10,128]{1,0:T(8,128)S(1)} %add.6.own), channel_id=1, source_target_pairs={{0,6},{1,7},{2,0},{3,1},{4,2},{5,3},{6,4},{7,5},{8,14},{9,15},{10,... | collective-permute-start | bytes 15368 | tf_op jit(solution)/shard_map/ppermute | solution.py:48
  25.5 4.3 %collective-permute-start.2 = (f32[10,128]{1,0:T(8,128)S(1)}, f32[10,128]{1,0:T(8,128)S(1)}, u32[]{:S(2)}, u32[]{:S(2)}) collective-permute-start(f32[10,128]{1,0:T(8,128)S(1)} %add.6.own), channel_id=1, source_target_pairs={{0,4},{1,5},{2,6},{3,7},{4,0},{5,1},{6,2},{7,3},{8,12},{9,13},{10,... | collective-permute-start | bytes 15368 | tf_op jit(solution)/shard_map/ppermute | solution.py:48
  25.9 4.0 %collective-permute-start.1 = (f32[10,128]{1,0:T(8,128)S(1)}, f32[10,128]{1,0:T(8,128)S(1)}, u32[]{:S(2)}, u32[]{:S(2)}) collective-permute-start(f32[10,128]{1,0:T(8,128)S(1)} %add.6.own), channel_id=1, source_target_pairs={{0,2},{1,3},{2,4},{3,5},{4,6},{5,7},{6,0},{7,1},{8,10},{9,11},{10,... | collective-permute-start | bytes 15368 | tf_op jit(solution)/shard_map/ppermute | solution.py:48
  47.2 7.7 %collective-permute-start.6 = (bf16[576,128]{1,0:T(8,128)(2,1)S(1)}, bf16[576,128]{1,0:T(8,128)(2,1)S(1)}, u32[]{:S(2)}, u32[]{:S(2)}) collective-permute-start(bf16[576,128]{1,0:T(8,128)(2,1)S(1)} %shard_map.63._after.own), channel_id=1, source_target_pairs={{0,192},{8,200},{16,208},{24,216},{32,224},{40,232},{48,240},{56,2... | collective-permute-start | bytes 442376 | tf_op jit(solution)/shard_map/ppermute | solution.py:43
  49.8 5.6 %collective-permute-start.5 = (bf16[576,128]{1,0:T(8,128)(2,1)S(1)}, bf16[576,128]{1,0:T(8,128)(2,1)S(1)}, u32[]{:S(2)}, u32[]{:S(2)}) collective-permute-start(bf16[576,128]{1,0:T(8,128)(2,1)S(1)} %shard_map.63._after.own), channel_id=1, source_target_pairs={{0,128},{8,136},{16,144},{24,152},{32,160},{40,168},{48,176},{56,1... | collective-permute-start | bytes 442376 | tf_op jit(solution)/shard_map/ppermute | solution.py:43
  50.3 6.6 %collective-permute-start.4 = (bf16[576,128]{1,0:T(8,128)(2,1)S(1)}, bf16[576,128]{1,0:T(8,128)(2,1)S(1)}, u32[]{:S(2)}, u32[]{:S(2)}) collective-permute-start(bf16[576,128]{1,0:T(8,128)(2,1)S(1)} %shard_map.63._after.own), channel_id=1, source_target_pairs={{0,64},{8,72},{16,80},{24,88},{32,96},{40,104},{48,112},{56,120},{... | collective-permute-start | bytes 442376 | tf_op jit(solution)/shard_map/ppermute | solution.py:43
  60.2 5.9 %collective-permute-start.7 = (f32[72,640]{1,0:T(8,128)S(1)}, f32[72,640]{1,0:T(8,128)S(1)}, u32[]{:S(2)}, u32[]{:S(2)}) collective-permute-start(f32[72,640]{1,0:T(8,128)S(1)} %get-tuple-element.32), channel_id=1, source_target_pairs={{0,1},{1,0},{2,3},{3,2},{4,5},{5,4},{6,7},{7,6},{8,9},{9,8},{10,11... | collective-permute-start | bytes 552968 | tf_op jit(solution)/shard_map/ppermute | solution.py:52
  66.1 4.0 %collective-permute-start.10 = (bf16[72,640]{1,0:T(8,128)(2,1)S(1)}, bf16[72,640]{1,0:T(8,128)(2,1)S(1)}, u32[]{:S(2)}, u32[]{:S(2)}) collective-permute-start(bf16[72,640]{1,0:T(8,128)(2,1)S(1)} %shard_map.66.own), channel_id=1, source_target_pairs={{0,6},{1,7},{2,0},{3,1},{4,2},{5,3},{6,4},{7,5},{8,14},{9,15},{10,... | collective-permute-start | bytes 276488 | tf_op jit(solution)/shard_map/ppermute | solution.py:48
  66.9 4.9 %collective-permute-start.9 = (bf16[72,640]{1,0:T(8,128)(2,1)S(1)}, bf16[72,640]{1,0:T(8,128)(2,1)S(1)}, u32[]{:S(2)}, u32[]{:S(2)}) collective-permute-start(bf16[72,640]{1,0:T(8,128)(2,1)S(1)} %shard_map.66.own), channel_id=1, source_target_pairs={{0,4},{1,5},{2,6},{3,7},{4,0},{5,1},{6,2},{7,3},{8,12},{9,13},{10,... | collective-permute-start | bytes 276488 | tf_op jit(solution)/shard_map/ppermute | solution.py:48
  68.0 6.6 %collective-permute-start.8 = (bf16[72,640]{1,0:T(8,128)(2,1)S(1)}, bf16[72,640]{1,0:T(8,128)(2,1)S(1)}, u32[]{:S(2)}, u32[]{:S(2)}) collective-permute-start(bf16[72,640]{1,0:T(8,128)(2,1)S(1)} %shard_map.66.own), channel_id=1, source_target_pairs={{0,2},{1,3},{2,4},{3,5},{4,6},{5,7},{6,0},{7,1},{8,10},{9,11},{10,... | collective-permute-start | bytes 276488 | tf_op jit(solution)/shard_map/ppermute | solution.py:48
  74.7 1.9 %collective-permute-start.11 = (f32[64,640]{1,0:T(8,128)S(1)}, f32[64,640]{1,0:T(8,128)S(1)}, u32[]{:S(2)}, u32[]{:S(2)}) collective-permute-start(f32[64,640]{1,0:T(8,128)S(1)} %get-tuple-element.33.mine_ref.scores_ref), channel_id=1, source_target_pairs={{0,1},{1,0},{2,3},{3,2},{4,5},{5,4},{6,7},{7,6},{8,9},{9,8},{10,11... | collective-permute-start | bytes 491528 | tf_op jit(solution)/shard_map/ppermute | solution.py:52
  78.6 9.0 %collective-permute-start.12 = (bf16[528,128]{1,0:T(8,128)(2,1)S(1)}, bf16[528,128]{1,0:T(8,128)(2,1)S(1)}, u32[]{:S(2)}, u32[]{:S(2)}) collective-permute-start(bf16[528,128]{1,0:T(8,128)(2,1)S(1)} %get-tuple-element.37), channel_id=1, source_target_pairs={{0,64},{8,72},{16,80},{24,88},{32,96},{40,104},{48,112},{56,120},{... | collective-permute-start | bytes 405512 | tf_op jit(solution)/shard_map/ppermute | solution.py:502
  78.7 8.9 %collective-permute-start.13 = (bf16[528,128]{1,0:T(8,128)(2,1)S(1)}, bf16[528,128]{1,0:T(8,128)(2,1)S(1)}, u32[]{:S(2)}, u32[]{:S(2)}) collective-permute-start(bf16[528,128]{1,0:T(8,128)(2,1)S(1)} %get-tuple-element.38), channel_id=1, source_target_pairs={{0,128},{8,136},{16,144},{24,152},{32,160},{40,168},{48,176},{56,1... | collective-permute-start | bytes 405512 | tf_op jit(solution)/shard_map/ppermute | solution.py:502
  80.2 7.8 %collective-permute-start.14 = (bf16[528,128]{1,0:T(8,128)(2,1)S(1)}, bf16[528,128]{1,0:T(8,128)(2,1)S(1)}, u32[]{:S(2)}, u32[]{:S(2)}) collective-permute-start(bf16[528,128]{1,0:T(8,128)(2,1)S(1)} %get-tuple-element.39), channel_id=1, source_target_pairs={{0,192},{8,200},{16,208},{24,216},{32,224},{40,232},{48,240},{56,2... | collective-permute-start | bytes 405512 | tf_op jit(solution)/shard_map/ppermute | solution.py:502
  109.3 6.8 %collective-permute-start.17 = (bf16[8,72,128]{2,1,0:T(8,128)(2,1)S(1)}, bf16[8,72,128]{2,1,0:T(8,128)(2,1)S(1)}, u32[]{:S(2)}, u32[]{:S(2)}) collective-permute-start(bf16[8,72,128]{2,1,0:T(8,128)(2,1)S(1)} %all_to_all.27.own), channel_id=1, source_target_pairs={{0,192},{8,200},{16,208},{24,216},{32,224},{40,232},{48,240},{56,2... | collective-permute-start | bytes 442376 | tf_op jit(solution)/shard_map/ppermute | solution.py:43
  112.5 5.6 %collective-permute-start.16 = (bf16[8,72,128]{2,1,0:T(8,128)(2,1)S(1)}, bf16[8,72,128]{2,1,0:T(8,128)(2,1)S(1)}, u32[]{:S(2)}, u32[]{:S(2)}) collective-permute-start(bf16[8,72,128]{2,1,0:T(8,128)(2,1)S(1)} %all_to_all.27.own), channel_id=1, source_target_pairs={{0,128},{8,136},{16,144},{24,152},{32,160},{40,168},{48,176},{56,1... | collective-permute-start | bytes 442376 | tf_op jit(solution)/shard_map/ppermute | solution.py:43
  112.5 6.8 %collective-permute-start.15 = (bf16[8,72,128]{2,1,0:T(8,128)(2,1)S(1)}, bf16[8,72,128]{2,1,0:T(8,128)(2,1)S(1)}, u32[]{:S(2)}, u32[]{:S(2)}) collective-permute-start(bf16[8,72,128]{2,1,0:T(8,128)(2,1)S(1)} %all_to_all.27.own), channel_id=1, source_target_pairs={{0,64},{8,72},{16,80},{24,88},{32,96},{40,104},{48,112},{56,120},{... | collective-permute-start | bytes 442376 | tf_op jit(solution)/shard_map/ppermute | solution.py:43
  122.6 5.7 %collective-permute-start.18 = (f32[72,640]{1,0:T(8,128)S(1)}, f32[72,640]{1,0:T(8,128)S(1)}, u32[]{:S(2)}, u32[]{:S(2)}) collective-permute-start(f32[72,640]{1,0:T(8,128)S(1)} %get-tuple-element.43), channel_id=1, source_target_pairs={{0,1},{1,0},{2,3},{3,2},{4,5},{5,4},{6,7},{7,6},{8,9},{9,8},{10,11... | collective-permute-start | bytes 552968 | tf_op jit(solution)/shard_map/ppermute | solution.py:52
  128.3 4.0 %collective-permute-start.21 = (bf16[72,640]{1,0:T(8,128)(2,1)S(1)}, bf16[72,640]{1,0:T(8,128)(2,1)S(1)}, u32[]{:S(2)}, u32[]{:S(2)}) collective-permute-start(bf16[72,640]{1,0:T(8,128)(2,1)S(1)} %shard_map.72.own), channel_id=1, source_target_pairs={{0,6},{1,7},{2,0},{3,1},{4,2},{5,3},{6,4},{7,5},{8,14},{9,15},{10,... | collective-permute-start | bytes 276488 | tf_op jit(solution)/shard_map/ppermute | solution.py:48
  128.8 5.0 %collective-permute-start.20 = (bf16[72,640]{1,0:T(8,128)(2,1)S(1)}, bf16[72,640]{1,0:T(8,128)(2,1)S(1)}, u32[]{:S(2)}, u32[]{:S(2)}) collective-permute-start(bf16[72,640]{1,0:T(8,128)(2,1)S(1)} %shard_map.72.own), channel_id=1, source_target_pairs={{0,4},{1,5},{2,6},{3,7},{4,0},{5,1},{6,2},{7,3},{8,12},{9,13},{10,... | collective-permute-start | bytes 276488 | tf_op jit(solution)/shard_map/ppermute | solution.py:48
  129.5 7.2 %collective-permute-start.19 = (bf16[72,640]{1,0:T(8,128)(2,1)S(1)}, bf16[72,640]{1,0:T(8,128)(2,1)S(1)}, u32[]{:S(2)}, u32[]{:S(2)}) collective-permute-start(bf16[72,640]{1,0:T(8,128)(2,1)S(1)} %shard_map.72.own), channel_id=1, source_target_pairs={{0,2},{1,3},{2,4},{3,5},{4,6},{5,7},{6,0},{7,1},{8,10},{9,11},{10,... | collective-permute-start | bytes 276488 | tf_op jit(solution)/shard_map/ppermute | solution.py:48
  136.9 1.5 %collective-permute-start.22 = (f32[1,128]{1,0:T(1,128)S(1)}, f32[1,128]{1,0:T(1,128)S(1)}, u32[]{:S(2)}, u32[]{:S(2)}) collective-permute-start(f32[1,128]{1,0:T(1,128)S(1)} %get-tuple-element.44), channel_id=1, source_target_pairs={{0,1},{1,0},{2,3},{3,2},{4,5},{5,4},{6,7},{7,6},{8,9},{9,8},{10,11... | collective-permute-start | bytes 1544 | tf_op jit(solution)/shard_map/ppermute | solution.py:52

commit v7 on v6

--- a/solution.py
+++ b/solution.py
@@ -1,3 +1,5 @@
+import functools
+
 import jax
 import jax.numpy as jnp
 from jax import lax
@@ -256,9 +258,10 @@
     tail = QUARTER * ROWS
     grads = [p[tail : tail + TILES, :].astype(F32) + p[tail + TILES :, :].astype(F32) for p in (own, one, two, three)]
     grad_ref[...] = four(*grads) + LAMBDA * w_ref[...]
-    norm = jnp.zeros((ROWS, 128), F32)
+    norms = []
     for k, part in enumerate((own, one, two, three)):
         quarter = lax.rem(x + XN - k, XN)
+        norm = jnp.zeros((ROWS, 128), F32)
         for t in range(QUARTER):
             tile = quarter * QUARTER + t
             grad = grad_ref[pl.ds(tile, 1), :]
@@ -271,7 +274,8 @@
             top = jnp.where(last, lead.astype(F32), values)
             rhs_ref[:, at] = top.astype(BF16)
             rhs[at, :] = turned(top, rest)
-    line = line_sums(norm, jnp.zeros_like(norm))
+        norms.append(norm)
+    line = line_sums(four(*norms), jnp.zeros_like(norm))
     put_scores(pieces, rhs, other_ref, mine_ref, stacked([line], 8))
 
 
@@ -367,30 +371,61 @@
     scalars_ref[...] = stacked([step, curv, norm], 8)
 
 
-def second_kernel(
-    events_ref, rhs_ref, grad_ref, own, one, two, three, other_ref, mine_ref, first_ref, res
-):
-    x, _, core = place()
-    pieces = halves(events_ref, core)
+def repack_kernel(in_ref, out_ref):
+    rests = []
+    for t in range(QUARTER):
+        rows = in_ref[t]
+        out_ref[t * ROWS : (t + 1) * ROWS, :] = rows[:ROWS]
+        rests.append(rows[ROWS:].astype(F32)[:1])
+    out_ref[QUARTER * ROWS :, :] = stacked(rests, 16).astype(BF16)
+
+
+def quarter_work(k, events_ref, rhs_ref, grad_ref, part, first_ref, res):
+    x, _, _ = place()
+    quarter = lax.rem(x + XN - k, XN)
     norm = jnp.zeros((ROWS, 128), F32)
     cross = jnp.zeros((ROWS, 128), F32)
-    for k, part in enumerate((own, one, two, three)):
-        quarter = lax.rem(x + XN - k, XN)
-        for t in range(QUARTER):
-            tile = quarter * QUARTER + t
-            at = pl.ds(pl.multiple_of(tile * 128, 128), 128)
-            rows = part[t]
-            values = joined(rows.astype(F32))
-            right = rhs_ref[:, at].astype(F32)
-            right = jnp.where(row_is(right.shape, ROWS - 1), grad_ref[pl.ds(tile, 1), :], right)
-            norm = norm + values * values
-            cross = cross + values * right
-            first_ref[pl.ds(tile, 1), :] = values[ROWS - 1 :]
-            exact = rows.astype(F32)
-            res[at, :] = turned(exact[:ROWS], exact[ROWS : ROWS + 1])
-    line = line_sums(norm, cross)
+    rests = part[QUARTER * ROWS :, :].astype(F32)
+    for t in range(QUARTER):
+        tile = quarter * QUARTER + t
+        at = pl.ds(pl.multiple_of(tile * 128, 128), 128)
+        top, rest = part[t * ROWS : (t + 1) * ROWS, :].astype(F32), rests[t : t + 1]
+        last = row_is(top.shape, ROWS - 1)
+        values = top + jnp.where(last, rest, 0.0)
+        right = jnp.where(last, grad_ref[pl.ds(tile, 1), :], rhs_ref[:, at].astype(F32))
+        norm = norm + values * values
+        cross = cross + values * right
+        first_ref[t : t + 1, :] = values[ROWS - 1 :]
+        res[t * 128 : (t + 1) * 128, :] = turned(top, rest)
+    columns = pl.ds(pl.multiple_of(quarter * QUARTER * 128, 1024), QUARTER * 128)
+    scores = jnp.dot(events_ref[:, columns], res[...], preferred_element_type=F32)
+    return scores, jnp.concatenate([norm, cross], axis=0)
+
+
+def open_kernel(events_ref, rhs_ref, grad_ref, part, total_ref, sums_ref, first_ref, res):
+    total_ref[...], sums_ref[...] = quarter_work(0, events_ref, rhs_ref, grad_ref, part, first_ref, res)
+
+
+def add_kernel(k, events_ref, rhs_ref, grad_ref, part, total, total_ref, sums_ref, first_ref, res):
+    scores, sums_ref[...] = quarter_work(k, events_ref, rhs_ref, grad_ref, part, first_ref, res)
+    total_ref[...] = total[...] + scores
+
+
+def close_kernel(
+    events_ref, rhs_ref, grad_ref, part, total, own, two, three, other_ref, mine_ref, first_ref, res, scores_ref
+):
+    scores, one = quarter_work(1, events_ref, rhs_ref, grad_ref, part, first_ref, res)
+    scores_ref[...] = total[...] + scores
+    sums = four(own[...], one, two[...], three[...])
+    line = line_sums(sums[:ROWS], sums[ROWS:])
     lines = stacked([line, pltpu.roll(line, ROWS, 1)], 8)
-    put_scores(pieces, res, other_ref, mine_ref, lines)
+    core = place()[2]
+    for half, out_ref in ((1 - core, other_ref), (core, mine_ref)):
+        for t in range(HALF // 128):
+            rows = scores_ref[pl.ds(pl.multiple_of(half * HALF + t * 128, 128), 128), :]
+            columns = slice(t * 128, (t + 1) * 128)
+            out_ref[:ROWS, columns] = joined(jnp.transpose(rows))
+            out_ref[ROWS:, columns] = lines if t == 0 else jnp.zeros_like(lines)
 
 
 def tail_kernel(own, one, two, three, scores_ref, rate_ref, tail_ref, lines_ref):
@@ -401,7 +436,9 @@
     lines_ref[...] = stacked([norm, cross], 8)
 
 
-def end_kernel(tails_ref, scalars_ref, lines_ref, w_ref, grad_ref, first_ref, weights_ref, widths_ref):
+def end_kernel(
+    tails_ref, scalars_ref, lines_ref, w_ref, grad_ref, own, one, two, three, weights_ref, widths_ref
+):
     tail = tails_ref[0]
     for e in range(1, EN):
         tail = tail + tails_ref[e]
@@ -415,9 +452,12 @@
     widths = step_one * norm + step_two * (cross + ratio * norm)
     widths_ref[...] = widths[:, : ROWS - 1]
     at = slice(ROWS - 1, ROWS)
-    grad = grad_ref[...]
-    step = step_one[:, at] * grad + step_two[:, at] * (first_ref[...] + ratio[:, at] * grad)
-    weights_ref[...] = w_ref[...] - step
+    x, _, _ = place()
+    for k, first in enumerate((own, one, two, three)):
+        rows = pl.ds(pl.multiple_of(lax.rem(x + XN - k, XN) * QUARTER, QUARTER), QUARTER)
+        grad = grad_ref[rows, :]
+        step = step_one[:, at] * grad + step_two[:, at] * (first[...] + ratio[:, at] * grad)
+        weights_ref[rows, :] = w_ref[rows, :] - step
 
 
 def on_device(events, labels, weights, contexts):
@@ -512,13 +552,39 @@
     )
     message = z_exchange(message)
 
-    other, mine, first = kernel_call(
-        second_kernel,
-        [VMEM] * 7,
-        half + [shaped(TILES, 128)],
-        (held, rhs, grad, message, *x_moves(message)),
-        [pltpu.VMEM((features, 128), BF16)],
-        micros=4,
+    (message,) = kernel_call(repack_kernel, [VMEM], [part], (message,))
+    one, two, three = x_moves(message)
+    sums = [shaped(COUNT, 128), shaped(128, 128)]
+    first = [shaped(QUARTER, 128)]
+    scratch = [pltpu.VMEM((QUARTER * 128, 128), BF16)]
+    total, sum_own, first_own = kernel_call(
+        open_kernel, [VMEM] * 4, sums + first, (held, rhs, grad, message), scratch, micros=1, room=8
+    )
+    total, sum_three, first_three = kernel_call(
+        functools.partial(add_kernel, 3),
+        [VMEM] * 5,
+        sums + first,
+        (held, rhs, grad, three, total),
+        scratch,
+        micros=1,
+        room=8,
+    )
+    total, sum_two, first_two = kernel_call(
+        functools.partial(add_kernel, 2),
+        [VMEM] * 5,
+        sums + first,
+        (held, rhs, grad, two, total),
+        scratch,
+        micros=1,
+        room=8,
+    )
+    other, mine, first_one = kernel_call(
+        close_kernel,
+        [VMEM] * 8,
+        half + first,
+        (held, rhs, grad, one, total, sum_own, sum_two, sum_three),
+        scratch + [pltpu.VMEM((COUNT, 128), F32)],
+        micros=1,
         room=8,
     )
     (message,) = kernel_call(pack_kernel, [VMEM] * 2, packed, (mine, core_move(other)))
@@ -531,7 +597,7 @@
     tail = tail + core_move(tail)
     tails = lax.all_to_all(jnp.broadcast_to(tail[None], (EN, 1, 128)), "event", 0, 0)
     updated, widths = kernel_call(
-        end_kernel, [VMEM] * 6, [shaped(TILES, 128), shaped(1, ROWS - 1)], (tails, scalars, lines, tiled, grad, first)
+        end_kernel, [VMEM] * 9, [shaped(TILES, 128), shaped(1, ROWS - 1)], (tails, scalars, lines, tiled, grad, first_own, first_one, first_two, first_three)
     )
     return updated.reshape(features), widths.reshape(ROWS - 1)
 

time: 151 us -> 149 us (0.987)
  waiting for transfers between devices: 35.1 us -> 25.8 us
  starting transfers between devices: 42.1 us -> 49.2 us
    ppermute x6, waiting for transfers between devices: 8.08 us -> 3.02 us  [x_moves(): lax.ppermute(v, 'event', [(i, (i + k * ZN) % n) for i in range(n)])]
    ppermute x9, waiting for transfers between devices: 15.8 us -> 12.4 us  [y_moves(): lax.ppermute(v, 'feat', [(i, (i + k * CN) % n) for i in range(n)])]
    ppermute x9, starting transfers between devices: 8.19 us -> 11.4 us  [y_moves(): lax.ppermute(v, 'feat', [(i, (i + k * CN) % n) for i in range(n)])]
    ppermute x6, starting transfers between devices: 7.38 us -> 9.1 us  [x_moves(): lax.ppermute(v, 'event', [(i, (i + k * ZN) % n) for i in range(n)])]
    pallas_call x16 -> x20, Pallas kernels: 23.7 us -> 24.4 us  [kernel_call(): pl.pallas_call(body, out_shape=outs, in_specs=ins, out_specs=[VMEM] * len...]
  transfers between devices with their start and end apart: 24 -> 24, of which waited for: 20 -> 17; matrix products, arithmetic and copies ran while one was open for 0% -> 0% of each run, Pallas kernels for 7% -> 9%
where the time goes in v7:
time: 149 us
  starting transfers between devices  49.2 us (33%)
  blocking collectives  48.3 us (32%)
  waiting for transfers between devices  25.8 us (17%)
  Pallas kernels  24.4 us (16%)
    all_to_all x3, blocking collectives, z_exchange(): return lax.all_to_all(v, 'event', 0, 0, axis_index_groups=groups)  36.7 us
    pallas_call x20, Pallas kernels, kernel_call(): pl.pallas_call(body, out_shape=outs, in_specs=ins, out_specs=[VMEM] * len...  24.4 us
    ppermute x5, starting transfers between devices, core_move(): return lax.ppermute(v, 'feat', [(i, i ^ 1) for i in range(YN * CN)])  12.9 us
    ppermute x9, waiting for transfers between devices, y_moves(): lax.ppermute(v, 'feat', [(i, (i + k * CN) % n) for i in range(n)])  12.4 us
    all_to_all x1, starting transfers between devices, on_device(): chunks = lax.all_to_all(picked, 'event', 0, 0)  11.8 us
    all_to_all x1, blocking collectives, on_device(): lax.all_to_all(jnp.broadcast_to(tail[None], (EN, 1, 128)), 'event', 0, 0)  11.6 us
    ppermute x9, starting transfers between devices, y_moves(): lax.ppermute(v, 'feat', [(i, (i + k * CN) % n) for i in range(n)])  11.4 us
    ppermute x6, starting transfers between devices, x_moves(): lax.ppermute(v, 'event', [(i, (i + k * ZN) % n) for i in range(n)])  9.1 us
  transfers between devices with their start and end apart: 24, of which 17 were waited for; matrix products, arithmetic and copies ran while one was open for 0% of the time, Pallas kernels for 9%

profile of v7, /device:TPU:1, one launch (start us, length us, event | category | flops | bytes accessed | tf_op | source)
XLA Modules:
  0.0 149.1 jit_solution(17929819731508536785)
XLA Ops:
  0.7 0.7 copy-done.2
  1.3 3.6 %shard_map.59._after = bf16[32,64,128]{2,1,0:T(8,128)(2,1)} custom-call(s32[63]{0:T(128)S(1)} %copy-done.2, bf16[1280,4096]{1,0:T(8,128)(2,1)} %events_ref.5), custom_call_target="tpu_custom_call" | custom-call | bytes 7200000 | tf_op jit(solution)/shard_map/pallas_call | solution.py:32
  4.9 11.8 %all-to-all-start = ((bf16[32,64,128]{2,1,0:T(8,128)(2,1)}), bf16[32,64,128]{2,1,0:T(8,128)(2,1)S(1)}, u32[]{:S(2)}, u32[]{:S(2)}) async-start(bf16[32,64,128]{2,1,0:T(8,128)(2,1)} %shard_map.59._after), calls=%async_computation | async-start | bytes 1048576 | tf_op jit(solution)/shard_map/all_to_all | solution.py:483
  16.8 4.4 %shard_map.60 = (f32[10,128]{1,0:T(8,128)S(1)}, bf16[1280,4096]{1,0:T(8,128)(2,1)S(1)}) custom-call(f32[1,4096]{1,0:T(1,128)S(1)} %bitcast.7, bf16[1280,4096]{1,0:T(8,128)(2,1)} %events_ref.5, bf16[32,64,128]{2,1,0:T(8,128)(2,1)} %shard_map.59._after), custom_call_target="tpu_custom_call" | custom-call | bytes 14400000 | tf_op jit(solution)/shard_map/pallas_call | solution.py:32
  21.2 1.0 collective-permute-start
  22.2 0.8 collective-permute-done
  23.0 1.3 collective-permute-start.1
  24.3 2.6 %collective-permute-start.2 = (f32[10,128]{1,0:T(8,128)S(1)}, f32[10,128]{1,0:T(8,128)S(1)}, u32[]{:S(2)}, u32[]{:S(2)}) collective-permute-start(f32[10,128]{1,0:T(8,128)S(1)} %add.6.own), channel_id=1, source_target_pairs={{0,4},{1,5},{2,6},{3,7},{4,0},{5,1},{6,2},{7,3},{8,12},{9,13},{10,... | collective-permute-start | bytes 15368 | tf_op jit(solution)/shard_map/ppermute | solution.py:50
  27.0 1.1 collective-permute-start.3
  28.0 0.5 collective-permute-done.2.two
  28.5 1.2 collective-permute-done.3.three
  29.8 1.5 shard_map.61
  31.2 0.1 shard_map.62
  31.3 15.7 %all_to_all.25.in_ref = bf16[8,128,128]{2,1,0:T(8,128)(2,1)S(1)} all-to-all(bf16[8,128,128]{2,1,0:T(8,128)(2,1)S(1)} %shard_map.62), channel_id=1, replica_groups={{0,8,16,24,32,40,48,56},{64,72,80,88,96,104,112,120},{128,136,144,152,1..., dimensions={0} | all-to-all | bytes 524288 | tf_op jit(solution)/shard_map/all_to_all | solution.py:59
  47.1 1.3 collective-permute-start.4
  48.3 2.4 %collective-permute-start.5 = (bf16[576,128]{1,0:T(8,128)(2,1)S(1)}, bf16[576,128]{1,0:T(8,128)(2,1)S(1)}, u32[]{:S(2)}, u32[]{:S(2)}) collective-permute-start(bf16[576,128]{1,0:T(8,128)(2,1)S(1)} %shard_map.63._after.own), channel_id=1, source_target_pairs={{0,128},{8,136},{16,144},{24,152},{32,160},{40,168},{48,176},{56,1... | collective-permute-start | bytes 442376 | tf_op jit(solution)/shard_map/ppermute | solution.py:45
  50.7 1.2 collective-permute-start.6
  51.9 4.1 %shard_map.64.events_ref = bf16[1280,4096]{1,0:T(8,128)(2,1)S(1)} custom-call(bf16[1280,4096]{1,0:T(8,128)(2,1)} %events_ref.5, bf16[576,128]{1,0:T(8,128)(2,1)S(1)} %shard_map.63._after.own), custom_call_target="tpu_custom_call" | custom-call | bytes 18000000 | tf_op jit(solution)/shard_map/pallas_call | solution.py:32
  56.0 0.0 collective-permute-done.5.two
  56.0 3.3 %shard_map.65 = (bf16[64,4096]{1,0:T(8,128)(2,1)S(1)}, f32[32,128]{1,0:T(8,128)S(1)}, f32[72,640]{1,0:T(8,128)S(1)}, f32[72,640]{1,0:T(8,128)S(1)}) custom-call(bf16[1280,4096]{1,0:T(8,128)(2,1)S(1)} %shard_map.64.events_ref, f32[32,128]{1,0:T(8,128)S(1)} %bitcast.8, bf16[576,128]{1,0:T(8,128)(2,1)S(1)} %shard_map.63._after.own, ...), custom_call_target="tpu_custom_call" | custom-call | bytes 10800000 | tf_op jit(solution)/shard_map/pallas_call | solution.py:32
  59.4 4.6 %collective-permute-start.7 = (f32[72,640]{1,0:T(8,128)S(1)}, f32[72,640]{1,0:T(8,128)S(1)}, u32[]{:S(2)}, u32[]{:S(2)}) collective-permute-start(f32[72,640]{1,0:T(8,128)S(1)} %get-tuple-element.41), channel_id=1, source_target_pairs={{0,1},{1,0},{2,3},{3,2},{4,5},{5,4},{6,7},{7,6},{8,9},{9,8},{10,11... | collective-permute-start | bytes 552968 | tf_op jit(solution)/shard_map/ppermute | solution.py:54
  64.0 1.1 collective-permute-done.7.other
  65.0 0.1 shard_map.66.own
  65.1 2.4 %collective-permute-start.10 = (bf16[72,640]{1,0:T(8,128)(2,1)S(1)}, bf16[72,640]{1,0:T(8,128)(2,1)S(1)}, u32[]{:S(2)}, u32[]{:S(2)}) collective-permute-start(bf16[72,640]{1,0:T(8,128)(2,1)S(1)} %shard_map.66.own), channel_id=1, source_target_pairs={{0,6},{1,7},{2,0},{3,1},{4,2},{5,3},{6,4},{7,5},{8,14},{9,15},{10,... | collective-permute-start | bytes 276488 | tf_op jit(solution)/shard_map/ppermute | solution.py:50
  67.4 1.3 collective-permute-start.9
  68.7 0.3 collective-permute-done.10.three
  69.0 5.7 %collective-permute-done.8.one = bf16[72,640]{1,0:T(8,128)(2,1)S(1)} collective-permute-done((bf16[72,640]{1,0:T(8,128)(2,1)S(1)}, bf16[72,640]{1,0:T(8,128)(2,1)S(1)}, u32[]{:S(2)}, u32[]{:S(2)}) %collective-permute-start.8) | collective-permute-done | bytes 92192 | tf_op jit(solution)/shard_map/ppermute | solution.py:50
  74.7 0.1 shard_map.67
  74.7 1.1 collective-permute-start.11
  75.8 1.0 collective-permute-done.11.theirs_ref
  76.9 2.0 %shard_map.68 = (f32[512,128]{1,0:T(8,128)S(1)}, f32[8,128]{1,0:T(8,128)S(1)}, bf16[528,128]{1,0:T(8,128)(2,1)S(1)}, bf16[528,128]{1,0:T(8,128)(2,1)S(1)}, bf16[528,128]{1,0:T(8,128)(2,1)S(1)}) custom-call(bf16[1280,4096]{1,0:T(8,128)(2,1)S(1)} %shard_map.64.events_ref, f32[64,640]{1,0:T(8,128)S(1)} %get-tuple-element.42.mine_ref.scores_ref, ...), custom_call_target="tpu_custom_call" | custom-call | bytes 14400000 | tf_op jit(solution)/shard_map/pallas_call | solution.py:32
  78.9 0.9 collective-permute-start.12
  79.7 2.3 %collective-permute-start.13 = (bf16[528,128]{1,0:T(8,128)(2,1)S(1)}, bf16[528,128]{1,0:T(8,128)(2,1)S(1)}, u32[]{:S(2)}, u32[]{:S(2)}) collective-permute-start(bf16[528,128]{1,0:T(8,128)(2,1)S(1)} %get-tuple-element.47), channel_id=1, source_target_pairs={{0,128},{8,136},{16,144},{24,152},{32,160},{40,168},{48,176},{56,1... | collective-permute-start | bytes 405512 | tf_op jit(solution)/shard_map/ppermute | solution.py:542
  82.1 0.7 collective-permute-start.14
  82.8 2.1 %collective-permute-done.12.one = bf16[528,128]{1,0:T(8,128)(2,1)S(1)} collective-permute-done((bf16[528,128]{1,0:T(8,128)(2,1)S(1)}, bf16[528,128]{1,0:T(8,128)(2,1)S(1)}, u32[]{:S(2)}, u32[]{:S(2)}) %collective-permute-start.12) | collective-permute-done | bytes 135200 | tf_op jit(solution)/shard_map/ppermute | solution.py:542
  84.9 3.4 %collective-permute-done.13.two = bf16[528,128]{1,0:T(8,128)(2,1)S(1)} collective-permute-done((bf16[528,128]{1,0:T(8,128)(2,1)S(1)}, bf16[528,128]{1,0:T(8,128)(2,1)S(1)}, u32[]{:S(2)}, u32[]{:S(2)}) %collective-permute-start.13) | collective-permute-done | bytes 135200 | tf_op jit(solution)/shard_map/ppermute | solution.py:542
  88.3 0.1 shard_map.69
  88.4 10.4 %all_to_all.26.in_ref = bf16[8,72,128]{2,1,0:T(8,128)(2,1)S(1)} all-to-all(bf16[8,72,128]{2,1,0:T(8,128)(2,1)S(1)} %shard_map.69), channel_id=1, replica_groups={{0,8,16,24,32,40,48,56},{64,72,80,88,96,104,112,120},{128,136,144,152,1..., dimensions={0} | all-to-all | bytes 294912 | tf_op jit(solution)/shard_map/all_to_all | solution.py:59
  98.9 0.1 shard_map.70
  99.0 10.6 %all_to_all.27.in_ref = bf16[8,72,128]{2,1,0:T(8,128)(2,1)S(1)} all-to-all(bf16[8,72,128]{2,1,0:T(8,128)(2,1)S(1)} %get-tuple-element.50), channel_id=1, replica_groups={{0,8,16,24,32,40,48,56},{64,72,80,88,96,104,112,120},{128,136,144,152,1..., dimensions={0} | all-to-all | bytes 294912 | tf_op jit(solution)/shard_map/all_to_all | solution.py:59
  109.6 3.4 %collective-permute-start.17 = (bf16[528,128]{1,0:T(8,128)(2,1)S(1)}, bf16[528,128]{1,0:T(8,128)(2,1)S(1)}, u32[]{:S(2)}, u32[]{:S(2)}) collective-permute-start(bf16[528,128]{1,0:T(8,128)(2,1)S(1)} %shard_map.71.part), channel_id=1, source_target_pairs={{0,192},{8,200},{16,208},{24,216},{32,224},{40,232},{48,240},{56,2... | collective-permute-start | bytes 405512 | tf_op jit(solution)/shard_map/ppermute | solution.py:45
  113.0 0.9 collective-permute-start.16
  113.8 0.0 collective-permute-start.15
  113.8 1.0 shard_map.72
  114.8 1.5 %collective-permute-done.17.part = bf16[528,128]{1,0:T(8,128)(2,1)S(1)} collective-permute-done((bf16[528,128]{1,0:T(8,128)(2,1)S(1)}, bf16[528,128]{1,0:T(8,128)(2,1)S(1)}, u32[]{:S(2)}, u32[]{:S(2)}) %collective-permute-start.17) | collective-permute-done | bytes 135200 | tf_op jit(solution)/shard_map/ppermute | solution.py:45
  116.4 1.0 shard_map.73
  117.3 1.1 collective-permute-done.16.part
  118.4 1.0 shard_map.74
  119.4 0.4 collective-permute-done.15.part
  119.8 1.1 shard_map.75
  120.9 4.6 %collective-permute-start.18 = (f32[72,640]{1,0:T(8,128)S(1)}, f32[72,640]{1,0:T(8,128)S(1)}, u32[]{:S(2)}, u32[]{:S(2)}) collective-permute-start(f32[72,640]{1,0:T(8,128)S(1)} %get-tuple-element.58), channel_id=1, source_target_pairs={{0,1},{1,0},{2,3},{3,2},{4,5},{5,4},{6,7},{7,6},{8,9},{9,8},{10,11... | collective-permute-start | bytes 552968 | tf_op jit(solution)/shard_map/ppermute | solution.py:54
  125.5 1.1 collective-permute-done.18.other
  126.6 0.1 shard_map.76.own
  126.6 0.1 collective-permute-start.19
  126.7 2.6 %collective-permute-start.20 = (bf16[72,640]{1,0:T(8,128)(2,1)S(1)}, bf16[72,640]{1,0:T(8,128)(2,1)S(1)}, u32[]{:S(2)}, u32[]{:S(2)}) collective-permute-start(bf16[72,640]{1,0:T(8,128)(2,1)S(1)} %shard_map.76.own), channel_id=1, source_target_pairs={{0,4},{1,5},{2,6},{3,7},{4,0},{5,1},{6,2},{7,3},{8,12},{9,13},{10,... | collective-permute-start | bytes 276488 | tf_op jit(solution)/shard_map/ppermute | solution.py:50
  129.3 0.1 collective-permute-start.21
  129.4 2.5 %collective-permute-done.19.one = bf16[72,640]{1,0:T(8,128)(2,1)S(1)} collective-permute-done((bf16[72,640]{1,0:T(8,128)(2,1)S(1)}, bf16[72,640]{1,0:T(8,128)(2,1)S(1)}, u32[]{:S(2)}, u32[]{:S(2)}) %collective-permute-start.19) | collective-permute-done | bytes 92192 | tf_op jit(solution)/shard_map/ppermute | solution.py:50
  131.9 1.8 %collective-permute-done.20.two = bf16[72,640]{1,0:T(8,128)(2,1)S(1)} collective-permute-done((bf16[72,640]{1,0:T(8,128)(2,1)S(1)}, bf16[72,640]{1,0:T(8,128)(2,1)S(1)}, u32[]{:S(2)}, u32[]{:S(2)}) %collective-permute-start.20) | collective-permute-done | bytes 92192 | tf_op jit(solution)/shard_map/ppermute | solution.py:50
  133.7 0.4 collective-permute-done.21.three
  134.1 0.2 shard_map.77
  134.3 1.6 %collective-permute-start.22 = (f32[1,128]{1,0:T(1,128)S(1)}, f32[1,128]{1,0:T(1,128)S(1)}, u32[]{:S(2)}, u32[]{:S(2)}) collective-permute-start(f32[1,128]{1,0:T(1,128)S(1)} %get-tuple-element.59), channel_id=1, source_target_pairs={{0,1},{1,0},{2,3},{3,2},{4,5},{5,4},{6,7},{7,6},{8,9},{9,8},{10,11... | collective-permute-start | bytes 1544 | tf_op jit(solution)/shard_map/ppermute | solution.py:54
  135.8 0.8 collective-permute-done.22
  136.7 11.6 %all_to_all.28.tails_ref = f32[32,1,128]{2,1,0:T(1,128)S(1)} all-to-all(f32[32,1,128]{2,1,0:T(1,128)S(1)} %broadcast_in_dim.9), channel_id=1, replica_groups=mesh['event'=32,'feat'=8] {'event'}, dimensions={0} | all-to-all | bytes 32768 | tf_op jit(solution)/shard_map/all_to_all | solution.py:598
  148.3 0.8 shard_map.78
  (17 shorter events, 0.1 us)
Async XLA Ops:
  0.6 16.1 %copy-start = (f32[4096]{0:T(1024)S(1)}, f32[4096]{0:T(1024)}, u32[]{:S(2)}) copy-start(f32[4096]{0:T(1024)} %param.6) | copy-start | bytes 49156
  0.6 0.7 copy-start.2
  1.3 28.5 %copy-start.1 = (s32[1280]{0:T(1024)S(1)}, s32[1280]{0:T(1024)}, u32[]{:S(2)}) copy-start(s32[1280]{0:T(1024)} %param.5) | copy-start | bytes 15364
  4.9 26.3 %all-to-all-start = ((bf16[32,64,128]{2,1,0:T(8,128)(2,1)}), bf16[32,64,128]{2,1,0:T(8,128)(2,1)S(1)}, u32[]{:S(2)}, u32[]{:S(2)}) async-start(bf16[32,64,128]{2,1,0:T(8,128)(2,1)} %shard_map.59._after), calls=%async_computation | async-start | bytes 1048576 | tf_op jit(solution)/shard_map/all_to_all | solution.py:483
  21.2 1.9 %collective-permute-start = (f32[10,128]{1,0:T(8,128)S(1)}, f32[10,128]{1,0:T(8,128)S(1)}, u32[]{:S(2)}, u32[]{:S(2)}) collective-permute-start(f32[10,128]{1,0:T(8,128)S(1)} %get-tuple-element.36), channel_id=1, source_target_pairs={{0,1},{1,0},{2,3},{3,2},{4,5},{5,4},{6,7},{7,6},{8,9},{9,8},{10,11... | collective-permute-start | bytes 15368 | tf_op jit(solution)/shard_map/ppermute | solution.py:54
  23.0 5.0 %collective-permute-start.1 = (f32[10,128]{1,0:T(8,128)S(1)}, f32[10,128]{1,0:T(8,128)S(1)}, u32[]{:S(2)}, u32[]{:S(2)}) collective-permute-start(f32[10,128]{1,0:T(8,128)S(1)} %add.6.own), channel_id=1, source_target_pairs={{0,2},{1,3},{2,4},{3,5},{4,6},{5,7},{6,0},{7,1},{8,10},{9,11},{10,... | collective-permute-start | bytes 15368 | tf_op jit(solution)/shard_map/ppermute | solution.py:50
  24.3 4.2 %collective-permute-start.2 = (f32[10,128]{1,0:T(8,128)S(1)}, f32[10,128]{1,0:T(8,128)S(1)}, u32[]{:S(2)}, u32[]{:S(2)}) collective-permute-start(f32[10,128]{1,0:T(8,128)S(1)} %add.6.own), channel_id=1, source_target_pairs={{0,4},{1,5},{2,6},{3,7},{4,0},{5,1},{6,2},{7,3},{8,12},{9,13},{10,... | collective-permute-start | bytes 15368 | tf_op jit(solution)/shard_map/ppermute | solution.py:50
  27.0 2.8 %collective-permute-start.3 = (f32[10,128]{1,0:T(8,128)S(1)}, f32[10,128]{1,0:T(8,128)S(1)}, u32[]{:S(2)}, u32[]{:S(2)}) collective-permute-start(f32[10,128]{1,0:T(8,128)S(1)} %add.6.own), channel_id=1, source_target_pairs={{0,6},{1,7},{2,0},{3,1},{4,2},{5,3},{6,4},{7,5},{8,14},{9,15},{10,... | collective-permute-start | bytes 15368 | tf_op jit(solution)/shard_map/ppermute | solution.py:50
  47.1 8.9 %collective-permute-start.4 = (bf16[576,128]{1,0:T(8,128)(2,1)S(1)}, bf16[576,128]{1,0:T(8,128)(2,1)S(1)}, u32[]{:S(2)}, u32[]{:S(2)}) collective-permute-start(bf16[576,128]{1,0:T(8,128)(2,1)S(1)} %shard_map.63._after.own), channel_id=1, source_target_pairs={{0,64},{8,72},{16,80},{24,88},{32,96},{40,104},{48,112},{56,120},{... | collective-permute-start | bytes 442376 | tf_op jit(solution)/shard_map/ppermute | solution.py:45
  48.3 7.7 %collective-permute-start.5 = (bf16[576,128]{1,0:T(8,128)(2,1)S(1)}, bf16[576,128]{1,0:T(8,128)(2,1)S(1)}, u32[]{:S(2)}, u32[]{:S(2)}) collective-permute-start(bf16[576,128]{1,0:T(8,128)(2,1)S(1)} %shard_map.63._after.own), channel_id=1, source_target_pairs={{0,128},{8,136},{16,144},{24,152},{32,160},{40,168},{48,176},{56,1... | collective-permute-start | bytes 442376 | tf_op jit(solution)/shard_map/ppermute | solution.py:45
  50.7 5.3 %collective-permute-start.6 = (bf16[576,128]{1,0:T(8,128)(2,1)S(1)}, bf16[576,128]{1,0:T(8,128)(2,1)S(1)}, u32[]{:S(2)}, u32[]{:S(2)}) collective-permute-start(bf16[576,128]{1,0:T(8,128)(2,1)S(1)} %shard_map.63._after.own), channel_id=1, source_target_pairs={{0,192},{8,200},{16,208},{24,216},{32,224},{40,232},{48,240},{56,2... | collective-permute-start | bytes 442376 | tf_op jit(solution)/shard_map/ppermute | solution.py:45
  59.4 5.7 %collective-permute-start.7 = (f32[72,640]{1,0:T(8,128)S(1)}, f32[72,640]{1,0:T(8,128)S(1)}, u32[]{:S(2)}, u32[]{:S(2)}) collective-permute-start(f32[72,640]{1,0:T(8,128)S(1)} %get-tuple-element.41), channel_id=1, source_target_pairs={{0,1},{1,0},{2,3},{3,2},{4,5},{5,4},{6,7},{7,6},{8,9},{9,8},{10,11... | collective-permute-start | bytes 552968 | tf_op jit(solution)/shard_map/ppermute | solution.py:54
  65.1 4.0 %collective-permute-start.10 = (bf16[72,640]{1,0:T(8,128)(2,1)S(1)}, bf16[72,640]{1,0:T(8,128)(2,1)S(1)}, u32[]{:S(2)}, u32[]{:S(2)}) collective-permute-start(bf16[72,640]{1,0:T(8,128)(2,1)S(1)} %shard_map.66.own), channel_id=1, source_target_pairs={{0,6},{1,7},{2,0},{3,1},{4,2},{5,3},{6,4},{7,5},{8,14},{9,15},{10,... | collective-permute-start | bytes 276488 | tf_op jit(solution)/shard_map/ppermute | solution.py:50
  67.4 7.3 %collective-permute-start.8 = (bf16[72,640]{1,0:T(8,128)(2,1)S(1)}, bf16[72,640]{1,0:T(8,128)(2,1)S(1)}, u32[]{:S(2)}, u32[]{:S(2)}) collective-permute-start(bf16[72,640]{1,0:T(8,128)(2,1)S(1)} %shard_map.66.own), channel_id=1, source_target_pairs={{0,2},{1,3},{2,4},{3,5},{4,6},{5,7},{6,0},{7,1},{8,10},{9,11},{10,... | collective-permute-start | bytes 276488 | tf_op jit(solution)/shard_map/ppermute | solution.py:50
  67.4 7.3 %collective-permute-start.9 = (bf16[72,640]{1,0:T(8,128)(2,1)S(1)}, bf16[72,640]{1,0:T(8,128)(2,1)S(1)}, u32[]{:S(2)}, u32[]{:S(2)}) collective-permute-start(bf16[72,640]{1,0:T(8,128)(2,1)S(1)} %shard_map.66.own), channel_id=1, source_target_pairs={{0,4},{1,5},{2,6},{3,7},{4,0},{5,1},{6,2},{7,3},{8,12},{9,13},{10,... | collective-permute-start | bytes 276488 | tf_op jit(solution)/shard_map/ppermute | solution.py:50
  74.7 2.1 %collective-permute-start.11 = (f32[64,640]{1,0:T(8,128)S(1)}, f32[64,640]{1,0:T(8,128)S(1)}, u32[]{:S(2)}, u32[]{:S(2)}) collective-permute-start(f32[64,640]{1,0:T(8,128)S(1)} %get-tuple-element.42.mine_ref.scores_ref), channel_id=1, source_target_pairs={{0,1},{1,0},{2,3},{3,2},{4,5},{5,4},{6,7},{7,6},{8,9},{9,8},{10,11... | collective-permute-start | bytes 491528 | tf_op jit(solution)/shard_map/ppermute | solution.py:54
  78.9 6.1 %collective-permute-start.12 = (bf16[528,128]{1,0:T(8,128)(2,1)S(1)}, bf16[528,128]{1,0:T(8,128)(2,1)S(1)}, u32[]{:S(2)}, u32[]{:S(2)}) collective-permute-start(bf16[528,128]{1,0:T(8,128)(2,1)S(1)} %get-tuple-element.46), channel_id=1, source_target_pairs={{0,64},{8,72},{16,80},{24,88},{32,96},{40,104},{48,112},{56,120},{... | collective-permute-start | bytes 405512 | tf_op jit(solution)/shard_map/ppermute | solution.py:542
  79.7 8.6 %collective-permute-start.13 = (bf16[528,128]{1,0:T(8,128)(2,1)S(1)}, bf16[528,128]{1,0:T(8,128)(2,1)S(1)}, u32[]{:S(2)}, u32[]{:S(2)}) collective-permute-start(bf16[528,128]{1,0:T(8,128)(2,1)S(1)} %get-tuple-element.47), channel_id=1, source_target_pairs={{0,128},{8,136},{16,144},{24,152},{32,160},{40,168},{48,176},{56,1... | collective-permute-start | bytes 405512 | tf_op jit(solution)/shard_map/ppermute | solution.py:542
  82.1 6.2 %collective-permute-start.14 = (bf16[528,128]{1,0:T(8,128)(2,1)S(1)}, bf16[528,128]{1,0:T(8,128)(2,1)S(1)}, u32[]{:S(2)}, u32[]{:S(2)}) collective-permute-start(bf16[528,128]{1,0:T(8,128)(2,1)S(1)} %get-tuple-element.48), channel_id=1, source_target_pairs={{0,192},{8,200},{16,208},{24,216},{32,224},{40,232},{48,240},{56,2... | collective-permute-start | bytes 405512 | tf_op jit(solution)/shard_map/ppermute | solution.py:542
  109.6 6.8 %collective-permute-start.17 = (bf16[528,128]{1,0:T(8,128)(2,1)S(1)}, bf16[528,128]{1,0:T(8,128)(2,1)S(1)}, u32[]{:S(2)}, u32[]{:S(2)}) collective-permute-start(bf16[528,128]{1,0:T(8,128)(2,1)S(1)} %shard_map.71.part), channel_id=1, source_target_pairs={{0,192},{8,200},{16,208},{24,216},{32,224},{40,232},{48,240},{56,2... | collective-permute-start | bytes 405512 | tf_op jit(solution)/shard_map/ppermute | solution.py:45
  113.0 5.5 %collective-permute-start.16 = (bf16[528,128]{1,0:T(8,128)(2,1)S(1)}, bf16[528,128]{1,0:T(8,128)(2,1)S(1)}, u32[]{:S(2)}, u32[]{:S(2)}) collective-permute-start(bf16[528,128]{1,0:T(8,128)(2,1)S(1)} %shard_map.71.part), channel_id=1, source_target_pairs={{0,128},{8,136},{16,144},{24,152},{32,160},{40,168},{48,176},{56,1... | collective-permute-start | bytes 405512 | tf_op jit(solution)/shard_map/ppermute | solution.py:45
  113.8 5.9 %collective-permute-start.15 = (bf16[528,128]{1,0:T(8,128)(2,1)S(1)}, bf16[528,128]{1,0:T(8,128)(2,1)S(1)}, u32[]{:S(2)}, u32[]{:S(2)}) collective-permute-start(bf16[528,128]{1,0:T(8,128)(2,1)S(1)} %shard_map.71.part), channel_id=1, source_target_pairs={{0,64},{8,72},{16,80},{24,88},{32,96},{40,104},{48,112},{56,120},{... | collective-permute-start | bytes 405512 | tf_op jit(solution)/shard_map/ppermute | solution.py:45
  120.9 5.7 %collective-permute-start.18 = (f32[72,640]{1,0:T(8,128)S(1)}, f32[72,640]{1,0:T(8,128)S(1)}, u32[]{:S(2)}, u32[]{:S(2)}) collective-permute-start(f32[72,640]{1,0:T(8,128)S(1)} %get-tuple-element.58), channel_id=1, source_target_pairs={{0,1},{1,0},{2,3},{3,2},{4,5},{5,4},{6,7},{7,6},{8,9},{9,8},{10,11... | collective-permute-start | bytes 552968 | tf_op jit(solution)/shard_map/ppermute | solution.py:54
  126.6 5.3 %collective-permute-start.19 = (bf16[72,640]{1,0:T(8,128)(2,1)S(1)}, bf16[72,640]{1,0:T(8,128)(2,1)S(1)}, u32[]{:S(2)}, u32[]{:S(2)}) collective-permute-start(bf16[72,640]{1,0:T(8,128)(2,1)S(1)} %shard_map.76.own), channel_id=1, source_target_pairs={{0,2},{1,3},{2,4},{3,5},{4,6},{5,7},{6,0},{7,1},{8,10},{9,11},{10,... | collective-permute-start | bytes 276488 | tf_op jit(solution)/shard_map/ppermute | solution.py:50
  126.7 6.9 %collective-permute-start.20 = (bf16[72,640]{1,0:T(8,128)(2,1)S(1)}, bf16[72,640]{1,0:T(8,128)(2,1)S(1)}, u32[]{:S(2)}, u32[]{:S(2)}) collective-permute-start(bf16[72,640]{1,0:T(8,128)(2,1)S(1)} %shard_map.76.own), channel_id=1, source_target_pairs={{0,4},{1,5},{2,6},{3,7},{4,0},{5,1},{6,2},{7,3},{8,12},{9,13},{10,... | collective-permute-start | bytes 276488 | tf_op jit(solution)/shard_map/ppermute | solution.py:50
  129.3 4.8 %collective-permute-start.21 = (bf16[72,640]{1,0:T(8,128)(2,1)S(1)}, bf16[72,640]{1,0:T(8,128)(2,1)S(1)}, u32[]{:S(2)}, u32[]{:S(2)}) collective-permute-start(bf16[72,640]{1,0:T(8,128)(2,1)S(1)} %shard_map.76.own), channel_id=1, source_target_pairs={{0,6},{1,7},{2,0},{3,1},{4,2},{5,3},{6,4},{7,5},{8,14},{9,15},{10,... | collective-permute-start | bytes 276488 | tf_op jit(solution)/shard_map/ppermute | solution.py:50
  134.3 2.4 %collective-permute-start.22 = (f32[1,128]{1,0:T(1,128)S(1)}, f32[1,128]{1,0:T(1,128)S(1)}, u32[]{:S(2)}, u32[]{:S(2)}) collective-permute-start(f32[1,128]{1,0:T(1,128)S(1)} %get-tuple-element.59), channel_id=1, source_target_pairs={{0,1},{1,0},{2,3},{3,2},{4,5},{5,4},{6,7},{7,6},{8,9},{9,8},{10,11... | collective-permute-start | bytes 1544 | tf_op jit(solution)/shard_map/ppermute | solution.py:54

commit v8 on v7

--- a/solution.py
+++ b/solution.py
@@ -45,6 +45,14 @@
     return [lax.ppermute(v, "event", [(i, (i + k * ZN) % n) for i in range(n)]) for k in (1, 2, 3)]
 
 
+def x_scatter(one, two, three):
+    n = XN * ZN
+    return [
+        lax.ppermute(v, "event", [(i, (i + k * ZN) % n) for i in range(n)])
+        for k, v in ((1, one), (2, two), (3, three))
+    ]
+
+
 def y_moves(v):
     n = YN * CN
     return [lax.ppermute(v, "feat", [(i, (i + k * CN) % n) for i in range(n)]) for k in (1, 2, 3)]
@@ -138,7 +146,7 @@
     return lax.div(event, ZN), lax.rem(event, ZN), lax.rem(lax.axis_index("feat"), CN)
 
 
-def pick_kernel(contexts_ref, events_ref, out_ref, blocks, rows, sems):
+def pick_kernel(contexts_ref, events_ref, own_ref, one_ref, two_ref, three_ref, blocks, rows, sems):
     base = lax.axis_index("event") * COUNT
 
     def owned(j):
@@ -165,11 +173,21 @@
             found = jnp.where(row_is(block.shape, lax.rem(contexts_ref[j] - base, 16)), block, 0.0)
             rows[pl.ds(j, 1), :] = jnp.sum(found, axis=0, keepdims=True)
 
-    for t in range(TILES):
-        out_ref[t] = rows[:, t * 128 : (t + 1) * 128].astype(BF16)
-
-
-def margin_kernel(w_ref, events_ref, _after, margin_ref, held, w, sems):
+    x, _, _ = place()
+    for k, out_ref in enumerate((own_ref, one_ref, two_ref, three_ref)):
+        quarter = lax.rem(x + k, XN)
+        for t in range(QUARTER):
+            at = pl.ds(pl.multiple_of((quarter * QUARTER + t) * 128, 128), 128)
+            out_ref[t * ROWS : (t + 1) * ROWS, :] = rows[:, at].astype(BF16)
+
+
+def join_kernel(own, one, two, three, _after, out_ref):
+    for t in range(QUARTER):
+        at = slice(t * ROWS, (t + 1) * ROWS)
+        out_ref[t] = four(*(p[at, :].astype(F32) for p in (own, one, two, three))).astype(BF16)
+
+
+def margin_kernel(w_ref, events_ref, _after, margin_ref, w, held, sems):
     pieces = Rows(events_ref, held, sems, [i * 128 for i in range(COUNT // 128)])
     w[...] = w_ref[...].astype(BF16).astype(F32)
     for c in range(COUNT // 128):
@@ -211,8 +229,8 @@
 
 def spread_kernel(chunks_ref, grad_ref, out_ref):
     total = chunks_ref[0].astype(F32)
-    for e in range(1, EN):
-        total = total + chunks_ref[e].astype(F32)
+    for z in range(1, ZN):
+        total = total + chunks_ref[z].astype(F32)
     lead, rest = pair_of(grad_ref[...])
     for z in range(ZN):
         out_ref[z, :ROWS, :] = total.astype(BF16)
@@ -467,10 +485,10 @@
     whole = shaped(COUNT, features, dtype=BF16)
     sems = pltpu.SemaphoreType.DMA((10,))
 
-    (picked,) = kernel_call(
+    own, *picked = kernel_call(
         pick_kernel,
         [SMEM, HBM],
-        [shaped(TILES, ROWS, 128, dtype=BF16)],
+        [shaped(QUARTER * ROWS, 128, dtype=BF16)] * 4,
         (contexts, events),
         [
             pltpu.VMEM((ROWS - 1, 16, features), BF16),
@@ -480,18 +498,23 @@
         micros=2,
         room=ROOM,
     )
-    chunks = lax.all_to_all(picked, "event", 0, 0)
-    margin, held = kernel_call(
+    picked = x_scatter(*picked)
+    (margin,) = kernel_call(
         margin_kernel,
         [VMEM, HBM, HBM],
-        [shaped(COUNT // 128, 128), whole],
-        (weights.reshape(1, features), events, picked),
-        [pltpu.VMEM((1, features), F32), sems],
+        [shaped(COUNT // 128, 128)],
+        (weights.reshape(1, features), events, own),
+        [pltpu.VMEM((1, features), F32), pltpu.VMEM((COUNT, features), BF16), sems],
         micros=4,
-        room=40,
+        room=ROOM,
     )
 
     margin = margin + core_move(margin)
+    (chunks,) = kernel_call(
+        join_kernel, [VMEM] * 4 + [HBM], [shaped(ZN, ROWS, 128, dtype=BF16)], (own, *picked, margin)
+    )
+    (held,) = kernel_call(load_kernel, [HBM, HBM], [whole], (events, chunks), [sems], micros=5, room=40)
+    chunks = z_exchange(chunks)
     rate, grad = kernel_call(
         gradient_kernel,
         [VMEM] * 6,
@@ -538,10 +561,7 @@
         micros=4,
         room=8,
     )
-    moved = [
-        lax.ppermute(v, "event", [(i, (i + k * ZN) % EN) for i in range(EN)])
-        for k, v in ((1, one), (2, two), (3, three))
-    ]
+    moved = x_scatter(one, two, three)
     shard = [shaped(ZN, ROWS + 8, 128, dtype=BF16)]
     (message,) = kernel_call(cut_kernel, [VMEM] * 5, shard, (own, curv, *moved))
     message, scalars = kernel_call(

time: 149 us -> 152 us (1.020)
  Pallas kernels: 24.4 us -> 28.4 us
  waiting for transfers between devices: 25.8 us -> 23.1 us
    ppermute x3 -> x6, starting transfers between devices: 3.95 us -> 9.14 us  [x_scatter(): lax.ppermute(v, 'event', [(i, (i + k * ZN) % n) for i in range(n)])]
    pallas_call x20 -> x22, Pallas kernels: 24.4 us -> 28.4 us  [kernel_call(): pl.pallas_call(body, out_shape=outs, in_specs=ins, out_specs=[VMEM] * len...]
    ppermute x9, waiting for transfers between devices: 12.4 us -> 8.92 us  [y_moves(): lax.ppermute(v, 'feat', [(i, (i + k * CN) % n) for i in range(n)])]
    all_to_all x1, starting transfers between devices: 11.8 us -> 8.36 us  [z_exchange(): return lax.all_to_all(v, 'event', 0, 0, axis_index_groups=groups)]
    ppermute x6, starting transfers between devices: 9.1 us -> 7.17 us  [x_moves(): lax.ppermute(v, 'event', [(i, (i + k * ZN) % n) for i in range(n)])]
    ppermute x3 -> x6, waiting for transfers between devices: 5.51 us -> 6.24 us  [x_scatter(): lax.ppermute(v, 'event', [(i, (i + k * ZN) % n) for i in range(n)])]
  transfers between devices with their start and end apart: 24 -> 27, of which waited for: 17 -> 15; matrix products, arithmetic and copies ran while one was open for 0% -> 0% of each run, Pallas kernels for 9% -> 11%
where the time goes in v8:
time: 152 us
  starting transfers between devices  50.5 us (33%)
  blocking collectives  48.1 us (32%)
  Pallas kernels  28.4 us (19%)
  waiting for transfers between devices  23.1 us (15%)
    all_to_all x3, blocking collectives, z_exchange(): return lax.all_to_all(v, 'event', 0, 0, axis_index_groups=groups)  36.4 us
    pallas_call x22, Pallas kernels, kernel_call(): pl.pallas_call(body, out_shape=outs, in_specs=ins, out_specs=[VMEM] * len...  28.4 us
    ppermute x5, starting transfers between devices, core_move(): return lax.ppermute(v, 'feat', [(i, i ^ 1) for i in range(YN * CN)])  14.3 us
    all_to_all x1, blocking collectives, on_device(): lax.all_to_all(jnp.broadcast_to(tail[None], (EN, 1, 128)), 'event', 0, 0)  11.6 us
    ppermute x9, starting transfers between devices, y_moves(): lax.ppermute(v, 'feat', [(i, (i + k * CN) % n) for i in range(n)])  11.6 us
    ppermute x6, starting transfers between devices, x_scatter(): lax.ppermute(v, 'event', [(i, (i + k * ZN) % n) for i in range(n)])  9.14 us
    ppermute x9, waiting for transfers between devices, y_moves(): lax.ppermute(v, 'feat', [(i, (i + k * CN) % n) for i in range(n)])  8.92 us
    all_to_all x1, starting transfers between devices, z_exchange(): return lax.all_to_all(v, 'event', 0, 0, axis_index_groups=groups)  8.36 us
  transfers between devices with their start and end apart: 27, of which 15 were waited for; matrix products, arithmetic and copies ran while one was open for 0% of the time, Pallas kernels for 11%

profile of v8, /device:TPU:1, one launch (start us, length us, event | category | flops | bytes accessed | tf_op | source)
XLA Modules:
  0.0 151.7 jit_solution(6648291199790512538)
XLA Ops:
  0.6 0.7 copy-done.2
  1.3 3.0 %shard_map.59 = (bf16[512,128]{1,0:T(8,128)(2,1)S(1)}, bf16[512,128]{1,0:T(8,128)(2,1)S(1)}, bf16[512,128]{1,0:T(8,128)(2,1)S(1)}, bf16[512,128]{1,0:T(8,128)(2,1)S(1)}) custom-call(s32[63]{0:T(128)S(1)} %copy-done.2, bf16[1280,4096]{1,0:T(8,128)(2,1)} %events_ref.7), custom_call_target="tpu_custom_call" | custom-call | bytes 7200000 | tf_op jit(solution)/shard_map/pallas_call | solution.py:32
  4.3 2.0 %collective-permute-start = (bf16[512,128]{1,0:T(8,128)(2,1)S(1)}, bf16[512,128]{1,0:T(8,128)(2,1)S(1)}, u32[]{:S(2)}, u32[]{:S(2)}) collective-permute-start(bf16[512,128]{1,0:T(8,128)(2,1)S(1)} %get-tuple-element.38), channel_id=1, source_target_pairs={{0,64},{8,72},{16,80},{24,88},{32,96},{40,104},{48,112},{56,120},{... | collective-permute-start | bytes 393224 | tf_op jit(solution)/shard_map/ppermute | solution.py:51
  6.3 2.7 %collective-permute-start.1 = (bf16[512,128]{1,0:T(8,128)(2,1)S(1)}, bf16[512,128]{1,0:T(8,128)(2,1)S(1)}, u32[]{:S(2)}, u32[]{:S(2)}) collective-permute-start(bf16[512,128]{1,0:T(8,128)(2,1)S(1)} %get-tuple-element.39), channel_id=1, source_target_pairs={{0,128},{8,136},{16,144},{24,152},{32,160},{40,168},{48,176},{56,1... | collective-permute-start | bytes 393224 | tf_op jit(solution)/shard_map/ppermute | solution.py:51
  9.0 0.8 collective-permute-start.2
  9.8 4.4 %shard_map.60 = f32[10,128]{1,0:T(8,128)S(1)} custom-call(f32[1,4096]{1,0:T(1,128)S(1)} %bitcast.7, bf16[1280,4096]{1,0:T(8,128)(2,1)} %events_ref.7, bf16[512,128]{1,0:T(8,128)(2,1)S(1)} %get-tuple-element.37._after.own), custom_call_target="tpu_custom_call" | custom-call | bytes 14400000 | tf_op jit(solution)/shard_map/pallas_call | solution.py:32
  14.2 1.6 %collective-permute-start.3 = (f32[10,128]{1,0:T(8,128)S(1)}, f32[10,128]{1,0:T(8,128)S(1)}, u32[]{:S(2)}, u32[]{:S(2)}) collective-permute-start(f32[10,128]{1,0:T(8,128)S(1)} %shard_map.60), channel_id=1, source_target_pairs={{0,1},{1,0},{2,3},{3,2},{4,5},{5,4},{6,7},{7,6},{8,9},{9,8},{10,11... | collective-permute-start | bytes 15368 | tf_op jit(solution)/shard_map/ppermute | solution.py:62
  15.8 0.8 collective-permute-done.3
  16.6 0.0 collective-permute-done.one
  16.6 0.7 shard_map.61._after
  17.3 8.4 %all-to-all-start = ((bf16[8,64,128]{2,1,0:T(8,128)(2,1)}), bf16[8,64,128]{2,1,0:T(8,128)(2,1)S(1)}, u32[]{:S(2)}, u32[]{:S(2)}) async-start(bf16[8,64,128]{2,1,0:T(8,128)(2,1)} %shard_map.61._after), calls=%async_computation | async-start | bytes 262144 | tf_op jit(solution)/shard_map/all_to_all | solution.py:67
  25.7 1.4 collective-permute-start.4
  27.1 2.6 %collective-permute-start.5 = (f32[10,128]{1,0:T(8,128)S(1)}, f32[10,128]{1,0:T(8,128)S(1)}, u32[]{:S(2)}, u32[]{:S(2)}) collective-permute-start(f32[10,128]{1,0:T(8,128)S(1)} %add.6._after.own), channel_id=1, source_target_pairs={{0,4},{1,5},{2,6},{3,7},{4,0},{5,1},{6,2},{7,3},{8,12},{9,13},{10,... | collective-permute-start | bytes 15368 | tf_op jit(solution)/shard_map/ppermute | solution.py:58
  29.7 1.1 collective-permute-start.6
  30.8 4.1 %shard_map.62.events_ref = bf16[1280,4096]{1,0:T(8,128)(2,1)S(1)} custom-call(bf16[1280,4096]{1,0:T(8,128)(2,1)} %events_ref.7, bf16[8,64,128]{2,1,0:T(8,128)(2,1)} %shard_map.61._after), custom_call_target="tpu_custom_call" | custom-call | bytes 18000000 | tf_op jit(solution)/shard_map/pallas_call | solution.py:32
  34.9 1.5 shard_map.63
  36.4 15.6 %all_to_all.25.in_ref = bf16[8,128,128]{2,1,0:T(8,128)(2,1)S(1)} all-to-all(bf16[8,128,128]{2,1,0:T(8,128)(2,1)S(1)} %shard_map.64), channel_id=1, replica_groups={{0,8,16,24,32,40,48,56},{64,72,80,88,96,104,112,120},{128,136,144,152,1..., dimensions={0} | all-to-all | bytes 524288 | tf_op jit(solution)/shard_map/all_to_all | solution.py:67
  52.0 0.6 collective-permute-start.7
  52.6 1.0 collective-permute-start.8
  53.6 1.5 collective-permute-start.9
  55.1 4.1 %shard_map.66.events_ref = bf16[1280,4096]{1,0:T(8,128)(2,1)S(1)} custom-call(bf16[1280,4096]{1,0:T(8,128)(2,1)} %events_ref.7, bf16[576,128]{1,0:T(8,128)(2,1)S(1)} %shard_map.65._after.own), custom_call_target="tpu_custom_call" | custom-call | bytes 18000000 | tf_op jit(solution)/shard_map/pallas_call | solution.py:32
  59.2 0.2 collective-permute-done.9.three
  59.4 3.3 %shard_map.67 = (bf16[64,4096]{1,0:T(8,128)(2,1)S(1)}, f32[32,128]{1,0:T(8,128)S(1)}, f32[72,640]{1,0:T(8,128)S(1)}, f32[72,640]{1,0:T(8,128)S(1)}) custom-call(bf16[1280,4096]{1,0:T(8,128)(2,1)S(1)} %shard_map.66.events_ref, f32[32,128]{1,0:T(8,128)S(1)} %bitcast.8, bf16[576,128]{1,0:T(8,128)(2,1)S(1)} %shard_map.65._after.own, ...), custom_call_target="tpu_custom_call" | custom-call | bytes 10800000 | tf_op jit(solution)/shard_map/pallas_call | solution.py:32
  62.8 5.2 %collective-permute-start.10 = (f32[72,640]{1,0:T(8,128)S(1)}, f32[72,640]{1,0:T(8,128)S(1)}, u32[]{:S(2)}, u32[]{:S(2)}) collective-permute-start(f32[72,640]{1,0:T(8,128)S(1)} %get-tuple-element.45), channel_id=1, source_target_pairs={{0,1},{1,0},{2,3},{3,2},{4,5},{5,4},{6,7},{7,6},{8,9},{9,8},{10,11... | collective-permute-start | bytes 552968 | tf_op jit(solution)/shard_map/ppermute | solution.py:62
  67.9 1.1 collective-permute-done.10.other
  69.0 0.1 shard_map.68.own
  69.1 0.5 collective-permute-start.11
  69.5 0.9 collective-permute-start.12
  70.4 1.6 %collective-permute-start.13 = (bf16[72,640]{1,0:T(8,128)(2,1)S(1)}, bf16[72,640]{1,0:T(8,128)(2,1)S(1)}, u32[]{:S(2)}, u32[]{:S(2)}) collective-permute-start(bf16[72,640]{1,0:T(8,128)(2,1)S(1)} %shard_map.68.own), channel_id=1, source_target_pairs={{0,6},{1,7},{2,0},{3,1},{4,2},{5,3},{6,4},{7,5},{8,14},{9,15},{10,... | collective-permute-start | bytes 276488 | tf_op jit(solution)/shard_map/ppermute | solution.py:58
  72.0 4.2 %collective-permute-done.11.one = bf16[72,640]{1,0:T(8,128)(2,1)S(1)} collective-permute-done((bf16[72,640]{1,0:T(8,128)(2,1)S(1)}, bf16[72,640]{1,0:T(8,128)(2,1)S(1)}, u32[]{:S(2)}, u32[]{:S(2)}) %collective-permute-start.11) | collective-permute-done | bytes 92192 | tf_op jit(solution)/shard_map/ppermute | solution.py:58
  76.2 0.3 collective-permute-done.13.three
  76.5 0.1 shard_map.69
  76.6 1.6 %collective-permute-start.14 = (f32[64,640]{1,0:T(8,128)S(1)}, f32[64,640]{1,0:T(8,128)S(1)}, u32[]{:S(2)}, u32[]{:S(2)}) collective-permute-start(f32[64,640]{1,0:T(8,128)S(1)} %get-tuple-element.46.mine_ref.scores_ref), channel_id=1, source_target_pairs={{0,1},{1,0},{2,3},{3,2},{4,5},{5,4},{6,7},{7,6},{8,9},{9,8},{10,11... | collective-permute-start | bytes 491528 | tf_op jit(solution)/shard_map/ppermute | solution.py:62
  78.2 1.0 collective-permute-done.14.theirs_ref
  79.2 2.0 %shard_map.70 = (f32[512,128]{1,0:T(8,128)S(1)}, f32[8,128]{1,0:T(8,128)S(1)}, bf16[528,128]{1,0:T(8,128)(2,1)S(1)}, bf16[528,128]{1,0:T(8,128)(2,1)S(1)}, bf16[528,128]{1,0:T(8,128)(2,1)S(1)}) custom-call(bf16[1280,4096]{1,0:T(8,128)(2,1)S(1)} %shard_map.66.events_ref, f32[64,640]{1,0:T(8,128)S(1)} %get-tuple-element.46.mine_ref.scores_ref, ...), custom_call_target="tpu_custom_call" | custom-call | bytes 14400000 | tf_op jit(solution)/shard_map/pallas_call | solution.py:32
  81.2 0.4 collective-permute-start.15
  81.6 3.2 %collective-permute-start.16 = (bf16[528,128]{1,0:T(8,128)(2,1)S(1)}, bf16[528,128]{1,0:T(8,128)(2,1)S(1)}, u32[]{:S(2)}, u32[]{:S(2)}) collective-permute-start(bf16[528,128]{1,0:T(8,128)(2,1)S(1)} %get-tuple-element.51), channel_id=1, source_target_pairs={{0,128},{8,136},{16,144},{24,152},{32,160},{40,168},{48,176},{56,1... | collective-permute-start | bytes 405512 | tf_op jit(solution)/shard_map/ppermute | solution.py:51
  84.8 2.4 %collective-permute-done.15.one = bf16[528,128]{1,0:T(8,128)(2,1)S(1)} collective-permute-done((bf16[528,128]{1,0:T(8,128)(2,1)S(1)}, bf16[528,128]{1,0:T(8,128)(2,1)S(1)}, u32[]{:S(2)}, u32[]{:S(2)}) %collective-permute-start.15) | collective-permute-done | bytes 135200 | tf_op jit(solution)/shard_map/ppermute | solution.py:51
  87.3 3.8 %collective-permute-done.16.two = bf16[528,128]{1,0:T(8,128)(2,1)S(1)} collective-permute-done((bf16[528,128]{1,0:T(8,128)(2,1)S(1)}, bf16[528,128]{1,0:T(8,128)(2,1)S(1)}, u32[]{:S(2)}, u32[]{:S(2)}) %collective-permute-start.16) | collective-permute-done | bytes 135200 | tf_op jit(solution)/shard_map/ppermute | solution.py:51
  91.1 0.1 shard_map.71
  91.2 10.3 %all_to_all.26.in_ref = bf16[8,72,128]{2,1,0:T(8,128)(2,1)S(1)} all-to-all(bf16[8,72,128]{2,1,0:T(8,128)(2,1)S(1)} %shard_map.71), channel_id=1, replica_groups={{0,8,16,24,32,40,48,56},{64,72,80,88,96,104,112,120},{128,136,144,152,1..., dimensions={0} | all-to-all | bytes 294912 | tf_op jit(solution)/shard_map/all_to_all | solution.py:67
  101.5 0.1 shard_map.72
  101.6 10.6 %all_to_all.27.in_ref = bf16[8,72,128]{2,1,0:T(8,128)(2,1)S(1)} all-to-all(bf16[8,72,128]{2,1,0:T(8,128)(2,1)S(1)} %get-tuple-element.54), channel_id=1, replica_groups={{0,8,16,24,32,40,48,56},{64,72,80,88,96,104,112,120},{128,136,144,152,1..., dimensions={0} | all-to-all | bytes 294912 | tf_op jit(solution)/shard_map/all_to_all | solution.py:67
  112.2 3.4 %collective-permute-start.20 = (bf16[528,128]{1,0:T(8,128)(2,1)S(1)}, bf16[528,128]{1,0:T(8,128)(2,1)S(1)}, u32[]{:S(2)}, u32[]{:S(2)}) collective-permute-start(bf16[528,128]{1,0:T(8,128)(2,1)S(1)} %shard_map.73.part), channel_id=1, source_target_pairs={{0,192},{8,200},{16,208},{24,216},{32,224},{40,232},{48,240},{56,2... | collective-permute-start | bytes 405512 | tf_op jit(solution)/shard_map/ppermute | solution.py:45
  115.6 0.7 collective-permute-start.18
  116.3 1.0 shard_map.74
  117.2 1.8 %collective-permute-done.20.part = bf16[528,128]{1,0:T(8,128)(2,1)S(1)} collective-permute-done((bf16[528,128]{1,0:T(8,128)(2,1)S(1)}, bf16[528,128]{1,0:T(8,128)(2,1)S(1)}, u32[]{:S(2)}, u32[]{:S(2)}) %collective-permute-start.20) | collective-permute-done | bytes 135200 | tf_op jit(solution)/shard_map/ppermute | solution.py:45
  119.0 1.0 shard_map.75
  119.9 1.1 collective-permute-done.19.part
  121.0 1.0 shard_map.76
  122.0 0.1 collective-permute-done.18.part
  122.1 1.1 shard_map.77
  123.2 4.7 %collective-permute-start.21 = (f32[72,640]{1,0:T(8,128)S(1)}, f32[72,640]{1,0:T(8,128)S(1)}, u32[]{:S(2)}, u32[]{:S(2)}) collective-permute-start(f32[72,640]{1,0:T(8,128)S(1)} %get-tuple-element.62), channel_id=1, source_target_pairs={{0,1},{1,0},{2,3},{3,2},{4,5},{5,4},{6,7},{7,6},{8,9},{9,8},{10,11... | collective-permute-start | bytes 552968 | tf_op jit(solution)/shard_map/ppermute | solution.py:62
  127.9 1.1 collective-permute-done.21.other
  128.9 0.1 shard_map.78.own
  129.0 0.3 collective-permute-start.22
  129.3 3.3 %collective-permute-start.23 = (bf16[72,640]{1,0:T(8,128)(2,1)S(1)}, bf16[72,640]{1,0:T(8,128)(2,1)S(1)}, u32[]{:S(2)}, u32[]{:S(2)}) collective-permute-start(bf16[72,640]{1,0:T(8,128)(2,1)S(1)} %shard_map.78.own), channel_id=1, source_target_pairs={{0,4},{1,5},{2,6},{3,7},{4,0},{5,1},{6,2},{7,3},{8,12},{9,13},{10,... | collective-permute-start | bytes 276488 | tf_op jit(solution)/shard_map/ppermute | solution.py:58
  132.5 1.6 %collective-permute-done.22.one = bf16[72,640]{1,0:T(8,128)(2,1)S(1)} collective-permute-done((bf16[72,640]{1,0:T(8,128)(2,1)S(1)}, bf16[72,640]{1,0:T(8,128)(2,1)S(1)}, u32[]{:S(2)}, u32[]{:S(2)}) %collective-permute-start.22) | collective-permute-done | bytes 92192 | tf_op jit(solution)/shard_map/ppermute | solution.py:58
  134.2 2.8 %collective-permute-done.23.two = bf16[72,640]{1,0:T(8,128)(2,1)S(1)} collective-permute-done((bf16[72,640]{1,0:T(8,128)(2,1)S(1)}, bf16[72,640]{1,0:T(8,128)(2,1)S(1)}, u32[]{:S(2)}, u32[]{:S(2)}) %collective-permute-start.23) | collective-permute-done | bytes 92192 | tf_op jit(solution)/shard_map/ppermute | solution.py:58
  136.9 0.2 shard_map.79
  137.1 1.3 collective-permute-start.25
  138.4 0.8 collective-permute-done.25
  139.2 11.6 %all_to_all.28.tails_ref = f32[32,1,128]{2,1,0:T(1,128)S(1)} all-to-all(f32[32,1,128]{2,1,0:T(1,128)S(1)} %broadcast_in_dim.9), channel_id=1, replica_groups=mesh['event'=32,'feat'=8] {'event'}, dimensions={0} | all-to-all | bytes 32768 | tf_op jit(solution)/shard_map/all_to_all | solution.py:618
  150.8 0.8 shard_map.80
  (25 shorter events, 0.2 us)
Async XLA Ops:
  0.6 9.1 %copy-start = (f32[4096]{0:T(1024)S(1)}, f32[4096]{0:T(1024)}, u32[]{:S(2)}) copy-start(f32[4096]{0:T(1024)} %param.6) | copy-start | bytes 49156
  0.6 0.7 copy-start.2
  4.3 12.3 %collective-permute-start = (bf16[512,128]{1,0:T(8,128)(2,1)S(1)}, bf16[512,128]{1,0:T(8,128)(2,1)S(1)}, u32[]{:S(2)}, u32[]{:S(2)}) collective-permute-start(bf16[512,128]{1,0:T(8,128)(2,1)S(1)} %get-tuple-element.38), channel_id=1, source_target_pairs={{0,64},{8,72},{16,80},{24,88},{32,96},{40,104},{48,112},{56,120},{... | collective-permute-start | bytes 393224 | tf_op jit(solution)/shard_map/ppermute | solution.py:51
  6.3 10.3 %collective-permute-start.1 = (bf16[512,128]{1,0:T(8,128)(2,1)S(1)}, bf16[512,128]{1,0:T(8,128)(2,1)S(1)}, u32[]{:S(2)}, u32[]{:S(2)}) collective-permute-start(bf16[512,128]{1,0:T(8,128)(2,1)S(1)} %get-tuple-element.39), channel_id=1, source_target_pairs={{0,128},{8,136},{16,144},{24,152},{32,160},{40,168},{48,176},{56,1... | collective-permute-start | bytes 393224 | tf_op jit(solution)/shard_map/ppermute | solution.py:51
  9.0 7.6 %collective-permute-start.2 = (bf16[512,128]{1,0:T(8,128)(2,1)S(1)}, bf16[512,128]{1,0:T(8,128)(2,1)S(1)}, u32[]{:S(2)}, u32[]{:S(2)}) collective-permute-start(bf16[512,128]{1,0:T(8,128)(2,1)S(1)} %get-tuple-element.40), channel_id=1, source_target_pairs={{0,192},{8,200},{16,208},{24,216},{32,224},{40,232},{48,240},{56,2... | collective-permute-start | bytes 393224 | tf_op jit(solution)/shard_map/ppermute | solution.py:51
  14.2 2.4 %collective-permute-start.3 = (f32[10,128]{1,0:T(8,128)S(1)}, f32[10,128]{1,0:T(8,128)S(1)}, u32[]{:S(2)}, u32[]{:S(2)}) collective-permute-start(f32[10,128]{1,0:T(8,128)S(1)} %shard_map.60), channel_id=1, source_target_pairs={{0,1},{1,0},{2,3},{3,2},{4,5},{5,4},{6,7},{7,6},{8,9},{9,8},{10,11... | collective-permute-start | bytes 15368 | tf_op jit(solution)/shard_map/ppermute | solution.py:62
  17.3 19.0 %all-to-all-start = ((bf16[8,64,128]{2,1,0:T(8,128)(2,1)}), bf16[8,64,128]{2,1,0:T(8,128)(2,1)S(1)}, u32[]{:S(2)}, u32[]{:S(2)}) async-start(bf16[8,64,128]{2,1,0:T(8,128)(2,1)} %shard_map.61._after), calls=%async_computation | async-start | bytes 262144 | tf_op jit(solution)/shard_map/all_to_all | solution.py:67
  25.7 9.2 %copy-start.1 = (s32[1280]{0:T(1024)S(1)}, s32[1280]{0:T(1024)}, u32[]{:S(2)}) copy-start(s32[1280]{0:T(1024)} %param.5) | copy-start | bytes 15364
  25.7 9.2 %collective-permute-start.4 = (f32[10,128]{1,0:T(8,128)S(1)}, f32[10,128]{1,0:T(8,128)S(1)}, u32[]{:S(2)}, u32[]{:S(2)}) collective-permute-start(f32[10,128]{1,0:T(8,128)S(1)} %add.6._after.own), channel_id=1, source_target_pairs={{0,2},{1,3},{2,4},{3,5},{4,6},{5,7},{6,0},{7,1},{8,10},{9,11},{10,... | collective-permute-start | bytes 15368 | tf_op jit(solution)/shard_map/ppermute | solution.py:58
  27.1 7.8 %collective-permute-start.5 = (f32[10,128]{1,0:T(8,128)S(1)}, f32[10,128]{1,0:T(8,128)S(1)}, u32[]{:S(2)}, u32[]{:S(2)}) collective-permute-start(f32[10,128]{1,0:T(8,128)S(1)} %add.6._after.own), channel_id=1, source_target_pairs={{0,4},{1,5},{2,6},{3,7},{4,0},{5,1},{6,2},{7,3},{8,12},{9,13},{10,... | collective-permute-start | bytes 15368 | tf_op jit(solution)/shard_map/ppermute | solution.py:58
  29.7 5.2 %collective-permute-start.6 = (f32[10,128]{1,0:T(8,128)S(1)}, f32[10,128]{1,0:T(8,128)S(1)}, u32[]{:S(2)}, u32[]{:S(2)}) collective-permute-start(f32[10,128]{1,0:T(8,128)S(1)} %add.6._after.own), channel_id=1, source_target_pairs={{0,6},{1,7},{2,0},{3,1},{4,2},{5,3},{6,4},{7,5},{8,14},{9,15},{10,... | collective-permute-start | bytes 15368 | tf_op jit(solution)/shard_map/ppermute | solution.py:58
  52.0 7.2 %collective-permute-start.7 = (bf16[576,128]{1,0:T(8,128)(2,1)S(1)}, bf16[576,128]{1,0:T(8,128)(2,1)S(1)}, u32[]{:S(2)}, u32[]{:S(2)}) collective-permute-start(bf16[576,128]{1,0:T(8,128)(2,1)S(1)} %shard_map.65._after.own), channel_id=1, source_target_pairs={{0,64},{8,72},{16,80},{24,88},{32,96},{40,104},{48,112},{56,120},{... | collective-permute-start | bytes 442376 | tf_op jit(solution)/shard_map/ppermute | solution.py:45
  52.6 6.6 %collective-permute-start.8 = (bf16[576,128]{1,0:T(8,128)(2,1)S(1)}, bf16[576,128]{1,0:T(8,128)(2,1)S(1)}, u32[]{:S(2)}, u32[]{:S(2)}) collective-permute-start(bf16[576,128]{1,0:T(8,128)(2,1)S(1)} %shard_map.65._after.own), channel_id=1, source_target_pairs={{0,128},{8,136},{16,144},{24,152},{32,160},{40,168},{48,176},{56,1... | collective-permute-start | bytes 442376 | tf_op jit(solution)/shard_map/ppermute | solution.py:45
  53.6 5.8 %collective-permute-start.9 = (bf16[576,128]{1,0:T(8,128)(2,1)S(1)}, bf16[576,128]{1,0:T(8,128)(2,1)S(1)}, u32[]{:S(2)}, u32[]{:S(2)}) collective-permute-start(bf16[576,128]{1,0:T(8,128)(2,1)S(1)} %shard_map.65._after.own), channel_id=1, source_target_pairs={{0,192},{8,200},{16,208},{24,216},{32,224},{40,232},{48,240},{56,2... | collective-permute-start | bytes 442376 | tf_op jit(solution)/shard_map/ppermute | solution.py:45
  62.8 6.2 %collective-permute-start.10 = (f32[72,640]{1,0:T(8,128)S(1)}, f32[72,640]{1,0:T(8,128)S(1)}, u32[]{:S(2)}, u32[]{:S(2)}) collective-permute-start(f32[72,640]{1,0:T(8,128)S(1)} %get-tuple-element.45), channel_id=1, source_target_pairs={{0,1},{1,0},{2,3},{3,2},{4,5},{5,4},{6,7},{7,6},{8,9},{9,8},{10,11... | collective-permute-start | bytes 552968 | tf_op jit(solution)/shard_map/ppermute | solution.py:62
  69.1 7.2 %collective-permute-start.11 = (bf16[72,640]{1,0:T(8,128)(2,1)S(1)}, bf16[72,640]{1,0:T(8,128)(2,1)S(1)}, u32[]{:S(2)}, u32[]{:S(2)}) collective-permute-start(bf16[72,640]{1,0:T(8,128)(2,1)S(1)} %shard_map.68.own), channel_id=1, source_target_pairs={{0,2},{1,3},{2,4},{3,5},{4,6},{5,7},{6,0},{7,1},{8,10},{9,11},{10,... | collective-permute-start | bytes 276488 | tf_op jit(solution)/shard_map/ppermute | solution.py:58
  69.5 6.7 %collective-permute-start.12 = (bf16[72,640]{1,0:T(8,128)(2,1)S(1)}, bf16[72,640]{1,0:T(8,128)(2,1)S(1)}, u32[]{:S(2)}, u32[]{:S(2)}) collective-permute-start(bf16[72,640]{1,0:T(8,128)(2,1)S(1)} %shard_map.68.own), channel_id=1, source_target_pairs={{0,4},{1,5},{2,6},{3,7},{4,0},{5,1},{6,2},{7,3},{8,12},{9,13},{10,... | collective-permute-start | bytes 276488 | tf_op jit(solution)/shard_map/ppermute | solution.py:58
  70.4 6.1 %collective-permute-start.13 = (bf16[72,640]{1,0:T(8,128)(2,1)S(1)}, bf16[72,640]{1,0:T(8,128)(2,1)S(1)}, u32[]{:S(2)}, u32[]{:S(2)}) collective-permute-start(bf16[72,640]{1,0:T(8,128)(2,1)S(1)} %shard_map.68.own), channel_id=1, source_target_pairs={{0,6},{1,7},{2,0},{3,1},{4,2},{5,3},{6,4},{7,5},{8,14},{9,15},{10,... | collective-permute-start | bytes 276488 | tf_op jit(solution)/shard_map/ppermute | solution.py:58
  76.6 2.6 %collective-permute-start.14 = (f32[64,640]{1,0:T(8,128)S(1)}, f32[64,640]{1,0:T(8,128)S(1)}, u32[]{:S(2)}, u32[]{:S(2)}) collective-permute-start(f32[64,640]{1,0:T(8,128)S(1)} %get-tuple-element.46.mine_ref.scores_ref), channel_id=1, source_target_pairs={{0,1},{1,0},{2,3},{3,2},{4,5},{5,4},{6,7},{7,6},{8,9},{9,8},{10,11... | collective-permute-start | bytes 491528 | tf_op jit(solution)/shard_map/ppermute | solution.py:62
  81.2 6.1 %collective-permute-start.15 = (bf16[528,128]{1,0:T(8,128)(2,1)S(1)}, bf16[528,128]{1,0:T(8,128)(2,1)S(1)}, u32[]{:S(2)}, u32[]{:S(2)}) collective-permute-start(bf16[528,128]{1,0:T(8,128)(2,1)S(1)} %get-tuple-element.50), channel_id=1, source_target_pairs={{0,64},{8,72},{16,80},{24,88},{32,96},{40,104},{48,112},{56,120},{... | collective-permute-start | bytes 405512 | tf_op jit(solution)/shard_map/ppermute | solution.py:51
  81.6 9.5 %collective-permute-start.16 = (bf16[528,128]{1,0:T(8,128)(2,1)S(1)}, bf16[528,128]{1,0:T(8,128)(2,1)S(1)}, u32[]{:S(2)}, u32[]{:S(2)}) collective-permute-start(bf16[528,128]{1,0:T(8,128)(2,1)S(1)} %get-tuple-element.51), channel_id=1, source_target_pairs={{0,128},{8,136},{16,144},{24,152},{32,160},{40,168},{48,176},{56,1... | collective-permute-start | bytes 405512 | tf_op jit(solution)/shard_map/ppermute | solution.py:51
  84.8 6.2 %collective-permute-start.17 = (bf16[528,128]{1,0:T(8,128)(2,1)S(1)}, bf16[528,128]{1,0:T(8,128)(2,1)S(1)}, u32[]{:S(2)}, u32[]{:S(2)}) collective-permute-start(bf16[528,128]{1,0:T(8,128)(2,1)S(1)} %get-tuple-element.52), channel_id=1, source_target_pairs={{0,192},{8,200},{16,208},{24,216},{32,224},{40,232},{48,240},{56,2... | collective-permute-start | bytes 405512 | tf_op jit(solution)/shard_map/ppermute | solution.py:51
  112.2 6.8 %collective-permute-start.20 = (bf16[528,128]{1,0:T(8,128)(2,1)S(1)}, bf16[528,128]{1,0:T(8,128)(2,1)S(1)}, u32[]{:S(2)}, u32[]{:S(2)}) collective-permute-start(bf16[528,128]{1,0:T(8,128)(2,1)S(1)} %shard_map.73.part), channel_id=1, source_target_pairs={{0,192},{8,200},{16,208},{24,216},{32,224},{40,232},{48,240},{56,2... | collective-permute-start | bytes 405512 | tf_op jit(solution)/shard_map/ppermute | solution.py:45
  115.6 5.5 %collective-permute-start.19 = (bf16[528,128]{1,0:T(8,128)(2,1)S(1)}, bf16[528,128]{1,0:T(8,128)(2,1)S(1)}, u32[]{:S(2)}, u32[]{:S(2)}) collective-permute-start(bf16[528,128]{1,0:T(8,128)(2,1)S(1)} %shard_map.73.part), channel_id=1, source_target_pairs={{0,128},{8,136},{16,144},{24,152},{32,160},{40,168},{48,176},{56,1... | collective-permute-start | bytes 405512 | tf_op jit(solution)/shard_map/ppermute | solution.py:45
  115.6 6.5 %collective-permute-start.18 = (bf16[528,128]{1,0:T(8,128)(2,1)S(1)}, bf16[528,128]{1,0:T(8,128)(2,1)S(1)}, u32[]{:S(2)}, u32[]{:S(2)}) collective-permute-start(bf16[528,128]{1,0:T(8,128)(2,1)S(1)} %shard_map.73.part), channel_id=1, source_target_pairs={{0,64},{8,72},{16,80},{24,88},{32,96},{40,104},{48,112},{56,120},{... | collective-permute-start | bytes 405512 | tf_op jit(solution)/shard_map/ppermute | solution.py:45
  123.2 5.7 %collective-permute-start.21 = (f32[72,640]{1,0:T(8,128)S(1)}, f32[72,640]{1,0:T(8,128)S(1)}, u32[]{:S(2)}, u32[]{:S(2)}) collective-permute-start(f32[72,640]{1,0:T(8,128)S(1)} %get-tuple-element.62), channel_id=1, source_target_pairs={{0,1},{1,0},{2,3},{3,2},{4,5},{5,4},{6,7},{7,6},{8,9},{9,8},{10,11... | collective-permute-start | bytes 552968 | tf_op jit(solution)/shard_map/ppermute | solution.py:62
  129.0 5.2 %collective-permute-start.22 = (bf16[72,640]{1,0:T(8,128)(2,1)S(1)}, bf16[72,640]{1,0:T(8,128)(2,1)S(1)}, u32[]{:S(2)}, u32[]{:S(2)}) collective-permute-start(bf16[72,640]{1,0:T(8,128)(2,1)S(1)} %shard_map.78.own), channel_id=1, source_target_pairs={{0,2},{1,3},{2,4},{3,5},{4,6},{5,7},{6,0},{7,1},{8,10},{9,11},{10,... | collective-permute-start | bytes 276488 | tf_op jit(solution)/shard_map/ppermute | solution.py:58
  129.3 7.6 %collective-permute-start.23 = (bf16[72,640]{1,0:T(8,128)(2,1)S(1)}, bf16[72,640]{1,0:T(8,128)(2,1)S(1)}, u32[]{:S(2)}, u32[]{:S(2)}) collective-permute-start(bf16[72,640]{1,0:T(8,128)(2,1)S(1)} %shard_map.78.own), channel_id=1, source_target_pairs={{0,4},{1,5},{2,6},{3,7},{4,0},{5,1},{6,2},{7,3},{8,12},{9,13},{10,... | collective-permute-start | bytes 276488 | tf_op jit(solution)/shard_map/ppermute | solution.py:58
  132.5 4.4 %collective-permute-start.24 = (bf16[72,640]{1,0:T(8,128)(2,1)S(1)}, bf16[72,640]{1,0:T(8,128)(2,1)S(1)}, u32[]{:S(2)}, u32[]{:S(2)}) collective-permute-start(bf16[72,640]{1,0:T(8,128)(2,1)S(1)} %shard_map.78.own), channel_id=1, source_target_pairs={{0,6},{1,7},{2,0},{3,1},{4,2},{5,3},{6,4},{7,5},{8,14},{9,15},{10,... | collective-permute-start | bytes 276488 | tf_op jit(solution)/shard_map/ppermute | solution.py:58
  137.1 2.1 %collective-permute-start.25 = (f32[1,128]{1,0:T(1,128)S(1)}, f32[1,128]{1,0:T(1,128)S(1)}, u32[]{:S(2)}, u32[]{:S(2)}) collective-permute-start(f32[1,128]{1,0:T(1,128)S(1)} %get-tuple-element.63), channel_id=1, source_target_pairs={{0,1},{1,0},{2,3},{3,2},{4,5},{5,4},{6,7},{7,6},{8,9},{9,8},{10,11... | collective-permute-start | bytes 1544 | tf_op jit(solution)/shard_map/ppermute | solution.py:62

commit v9 on v7

--- a/solution.py
+++ b/solution.py
@@ -1,5 +1,3 @@
-import functools
-
 import jax
 import jax.numpy as jnp
 from jax import lax
@@ -406,17 +404,16 @@
     total_ref[...], sums_ref[...] = quarter_work(0, events_ref, rhs_ref, grad_ref, part, first_ref, res)
 
 
-def add_kernel(k, events_ref, rhs_ref, grad_ref, part, total, total_ref, sums_ref, first_ref, res):
-    scores, sums_ref[...] = quarter_work(k, events_ref, rhs_ref, grad_ref, part, first_ref, res)
-    total_ref[...] = total[...] + scores
-
-
 def close_kernel(
-    events_ref, rhs_ref, grad_ref, part, total, own, two, three, other_ref, mine_ref, first_ref, res, scores_ref
+    events_ref, rhs_ref, grad_ref, one, two, three, total, own, other_ref, mine_ref, f1, f2, f3, res, scores_ref
 ):
-    scores, one = quarter_work(1, events_ref, rhs_ref, grad_ref, part, first_ref, res)
-    scores_ref[...] = total[...] + scores
-    sums = four(own[...], one, two[...], three[...])
+    scores, sums = total[...], [own[...]]
+    for k, part, first_ref in ((1, one, f1), (2, two, f2), (3, three, f3)):
+        more, sum_k = quarter_work(k, events_ref, rhs_ref, grad_ref, part, first_ref, res.at[k - 1])
+        scores = scores + more
+        sums.append(sum_k)
+    scores_ref[...] = scores
+    sums = four(*sums)
     line = line_sums(sums[:ROWS], sums[ROWS:])
     lines = stacked([line, pltpu.roll(line, ROWS, 1)], 8)
     core = place()[2]
@@ -560,31 +557,13 @@
     total, sum_own, first_own = kernel_call(
         open_kernel, [VMEM] * 4, sums + first, (held, rhs, grad, message), scratch, micros=1, room=8
     )
-    total, sum_three, first_three = kernel_call(
-        functools.partial(add_kernel, 3),
-        [VMEM] * 5,
-        sums + first,
-        (held, rhs, grad, three, total),
-        scratch,
-        micros=1,
-        room=8,
-    )
-    total, sum_two, first_two = kernel_call(
-        functools.partial(add_kernel, 2),
-        [VMEM] * 5,
-        sums + first,
-        (held, rhs, grad, two, total),
-        scratch,
-        micros=1,
-        room=8,
-    )
-    other, mine, first_one = kernel_call(
+    other, mine, first_one, first_two, first_three = kernel_call(
         close_kernel,
         [VMEM] * 8,
-        half + first,
-        (held, rhs, grad, one, total, sum_own, sum_two, sum_three),
-        scratch + [pltpu.VMEM((COUNT, 128), F32)],
-        micros=1,
+        half + first * 3,
+        (held, rhs, grad, one, two, three, total, sum_own),
+        [pltpu.VMEM((3, QUARTER * 128, 128), BF16), pltpu.VMEM((COUNT, 128), F32)],
+        micros=2,
         room=8,
     )
     (message,) = kernel_call(pack_kernel, [VMEM] * 2, packed, (mine, core_move(other)))

time: 149 us -> 150 us (level)
  waiting for transfers between devices: 25.8 us -> 33.8 us
  starting transfers between devices: 49.2 us -> 42.4 us
    ppermute x6, waiting for transfers between devices: 3.02 us -> 6.75 us  [x_moves(): lax.ppermute(v, 'event', [(i, (i + k * ZN) % n) for i in range(n)])]
    ppermute x9, waiting for transfers between devices: 12.4 us -> 15.8 us  [y_moves(): lax.ppermute(v, 'feat', [(i, (i + k * CN) % n) for i in range(n)])]
    ppermute x9, starting transfers between devices: 11.4 us -> 8.19 us  [y_moves(): lax.ppermute(v, 'feat', [(i, (i + k * CN) % n) for i in range(n)])]
    ppermute x6, starting transfers between devices: 9.1 us -> 7.55 us  [x_moves(): lax.ppermute(v, 'event', [(i, (i + k * ZN) % n) for i in range(n)])]
    pallas_call x20 -> x18, Pallas kernels: 24.4 us -> 23.9 us  [kernel_call(): pl.pallas_call(body, out_shape=outs, in_specs=ins, out_specs=[VMEM] * len...]
  transfers between devices with their start and end apart: 24 -> 24, of which waited for: 17 -> 20; matrix products, arithmetic and copies ran while one was open for 0% -> 0% of each run, Pallas kernels for 9% -> 7%
where the time goes in v9:
time: 150 us
  blocking collectives  48.5 us (32%)
  starting transfers between devices  42.4 us (28%)
  waiting for transfers between devices  33.8 us (23%)
  Pallas kernels  23.9 us (16%)
    all_to_all x3, blocking collectives, z_exchange(): return lax.all_to_all(v, 'event', 0, 0, axis_index_groups=groups)  36.9 us
    pallas_call x18, Pallas kernels, kernel_call(): pl.pallas_call(body, out_shape=outs, in_specs=ins, out_specs=[VMEM] * len...  23.9 us
    ppermute x9, waiting for transfers between devices, y_moves(): lax.ppermute(v, 'feat', [(i, (i + k * CN) % n) for i in range(n)])  15.8 us
    ppermute x5, starting transfers between devices, core_move(): return lax.ppermute(v, 'feat', [(i, i ^ 1) for i in range(YN * CN)])  12.2 us
    all_to_all x1, blocking collectives, on_device(): lax.all_to_all(jnp.broadcast_to(tail[None], (EN, 1, 128)), 'event', 0, 0)  11.6 us
    all_to_all x1, starting transfers between devices, on_device(): chunks = lax.all_to_all(picked, 'event', 0, 0)  11.6 us
    ppermute x9, starting transfers between devices, y_moves(): lax.ppermute(v, 'feat', [(i, (i + k * CN) % n) for i in range(n)])  8.19 us
    ppermute x6, starting transfers between devices, x_moves(): lax.ppermute(v, 'event', [(i, (i + k * ZN) % n) for i in range(n)])  7.55 us
  transfers between devices with their start and end apart: 24, of which 20 were waited for; matrix products, arithmetic and copies ran while one was open for 0% of the time, Pallas kernels for 7%

profile of v9, /device:TPU:1, one launch (start us, length us, event | category | flops | bytes accessed | tf_op | source)
XLA Modules:
  0.0 150.0 jit_solution(14414768165328354733)
XLA Ops:
  0.7 0.7 copy-done.2
  1.3 3.6 %shard_map.59._after = bf16[32,64,128]{2,1,0:T(8,128)(2,1)} custom-call(s32[63]{0:T(128)S(1)} %copy-done.2, bf16[1280,4096]{1,0:T(8,128)(2,1)} %events_ref.5), custom_call_target="tpu_custom_call" | custom-call | bytes 7200000 | tf_op jit(solution)/shard_map/pallas_call | solution.py:30
  4.9 11.6 %all-to-all-start = ((bf16[32,64,128]{2,1,0:T(8,128)(2,1)}), bf16[32,64,128]{2,1,0:T(8,128)(2,1)S(1)}, u32[]{:S(2)}, u32[]{:S(2)}) async-start(bf16[32,64,128]{2,1,0:T(8,128)(2,1)} %shard_map.59._after), calls=%async_computation | async-start | bytes 1048576 | tf_op jit(solution)/shard_map/all_to_all | solution.py:480
  16.4 4.4 %shard_map.60 = (f32[10,128]{1,0:T(8,128)S(1)}, bf16[1280,4096]{1,0:T(8,128)(2,1)S(1)}) custom-call(f32[1,4096]{1,0:T(1,128)S(1)} %bitcast.7, bf16[1280,4096]{1,0:T(8,128)(2,1)} %events_ref.5, bf16[32,64,128]{2,1,0:T(8,128)(2,1)} %shard_map.59._after), custom_call_target="tpu_custom_call" | custom-call | bytes 14400000 | tf_op jit(solution)/shard_map/pallas_call | solution.py:30
  20.9 1.0 collective-permute-start
  21.9 0.8 collective-permute-done
  22.7 2.7 %collective-permute-start.3 = (f32[10,128]{1,0:T(8,128)S(1)}, f32[10,128]{1,0:T(8,128)S(1)}, u32[]{:S(2)}, u32[]{:S(2)}) collective-permute-start(f32[10,128]{1,0:T(8,128)S(1)} %add.6.own), channel_id=1, source_target_pairs={{0,6},{1,7},{2,0},{3,1},{4,2},{5,3},{6,4},{7,5},{8,14},{9,15},{10,... | collective-permute-start | bytes 15368 | tf_op jit(solution)/shard_map/ppermute | solution.py:48
  25.5 0.3 collective-permute-start.2
  25.8 0.7 collective-permute-start.1
  26.5 3.3 %collective-permute-done.2.two = f32[10,128]{1,0:T(8,128)S(1)} collective-permute-done((f32[10,128]{1,0:T(8,128)S(1)}, f32[10,128]{1,0:T(8,128)S(1)}, u32[]{:S(2)}, u32[]{:S(2)}) %collective-permute-start.2) | collective-permute-done | bytes 5152 | tf_op jit(solution)/shard_map/ppermute | solution.py:48
  29.8 0.1 collective-permute-done.1.one
  29.9 1.5 shard_map.61
  31.3 0.0 all-to-all-done.chunks_ref
  31.3 0.1 shard_map.62
  31.4 15.7 %all_to_all.25.in_ref = bf16[8,128,128]{2,1,0:T(8,128)(2,1)S(1)} all-to-all(bf16[8,128,128]{2,1,0:T(8,128)(2,1)S(1)} %shard_map.62), channel_id=1, replica_groups={{0,8,16,24,32,40,48,56},{64,72,80,88,96,104,112,120},{128,136,144,152,1..., dimensions={0} | all-to-all | bytes 524288 | tf_op jit(solution)/shard_map/all_to_all | solution.py:57
  47.2 2.5 %collective-permute-start.6 = (bf16[576,128]{1,0:T(8,128)(2,1)S(1)}, bf16[576,128]{1,0:T(8,128)(2,1)S(1)}, u32[]{:S(2)}, u32[]{:S(2)}) collective-permute-start(bf16[576,128]{1,0:T(8,128)(2,1)S(1)} %shard_map.63._after.own), channel_id=1, source_target_pairs={{0,192},{8,200},{16,208},{24,216},{32,224},{40,232},{48,240},{56,2... | collective-permute-start | bytes 442376 | tf_op jit(solution)/shard_map/ppermute | solution.py:43
  49.7 0.5 collective-permute-start.5
  50.2 0.6 collective-permute-start.4
  50.8 4.1 %shard_map.64.events_ref = bf16[1280,4096]{1,0:T(8,128)(2,1)S(1)} custom-call(bf16[1280,4096]{1,0:T(8,128)(2,1)} %events_ref.5, bf16[576,128]{1,0:T(8,128)(2,1)S(1)} %shard_map.63._after.own), custom_call_target="tpu_custom_call" | custom-call | bytes 18000000 | tf_op jit(solution)/shard_map/pallas_call | solution.py:30
  54.9 0.4 collective-permute-done.5.two
  55.3 1.5 collective-permute-done.4.one
  56.8 3.3 %shard_map.65 = (bf16[64,4096]{1,0:T(8,128)(2,1)S(1)}, f32[32,128]{1,0:T(8,128)S(1)}, f32[72,640]{1,0:T(8,128)S(1)}, f32[72,640]{1,0:T(8,128)S(1)}) custom-call(bf16[1280,4096]{1,0:T(8,128)(2,1)S(1)} %shard_map.64.events_ref, f32[32,128]{1,0:T(8,128)S(1)} %bitcast.8, bf16[576,128]{1,0:T(8,128)(2,1)S(1)} %shard_map.63._after.own, ...), custom_call_target="tpu_custom_call" | custom-call | bytes 10800000 | tf_op jit(solution)/shard_map/pallas_call | solution.py:30
  60.1 4.9 %collective-permute-start.7 = (f32[72,640]{1,0:T(8,128)S(1)}, f32[72,640]{1,0:T(8,128)S(1)}, u32[]{:S(2)}, u32[]{:S(2)}) collective-permute-start(f32[72,640]{1,0:T(8,128)S(1)} %get-tuple-element.37), channel_id=1, source_target_pairs={{0,1},{1,0},{2,3},{3,2},{4,5},{5,4},{6,7},{7,6},{8,9},{9,8},{10,11... | collective-permute-start | bytes 552968 | tf_op jit(solution)/shard_map/ppermute | solution.py:52
  65.0 1.1 collective-permute-done.7.other
  66.0 0.1 shard_map.66.own
  66.1 0.8 collective-permute-start.10
  66.8 1.2 collective-permute-start.9
  68.0 0.8 collective-permute-start.8
  68.7 1.3 collective-permute-done.10.three
  70.0 1.7 %collective-permute-done.9.two = bf16[72,640]{1,0:T(8,128)(2,1)S(1)} collective-permute-done((bf16[72,640]{1,0:T(8,128)(2,1)S(1)}, bf16[72,640]{1,0:T(8,128)(2,1)S(1)}, u32[]{:S(2)}, u32[]{:S(2)}) %collective-permute-start.9) | collective-permute-done | bytes 92192 | tf_op jit(solution)/shard_map/ppermute | solution.py:48
  71.7 2.8 %collective-permute-done.8.one = bf16[72,640]{1,0:T(8,128)(2,1)S(1)} collective-permute-done((bf16[72,640]{1,0:T(8,128)(2,1)S(1)}, bf16[72,640]{1,0:T(8,128)(2,1)S(1)}, u32[]{:S(2)}, u32[]{:S(2)}) %collective-permute-start.8) | collective-permute-done | bytes 92192 | tf_op jit(solution)/shard_map/ppermute | solution.py:48
  74.6 0.1 shard_map.67
  74.6 0.9 collective-permute-start.11
  75.5 1.0 collective-permute-done.11.theirs_ref
  76.6 2.0 %shard_map.68 = (f32[512,128]{1,0:T(8,128)S(1)}, f32[8,128]{1,0:T(8,128)S(1)}, bf16[528,128]{1,0:T(8,128)(2,1)S(1)}, bf16[528,128]{1,0:T(8,128)(2,1)S(1)}, bf16[528,128]{1,0:T(8,128)(2,1)S(1)}) custom-call(bf16[1280,4096]{1,0:T(8,128)(2,1)S(1)} %shard_map.64.events_ref, f32[64,640]{1,0:T(8,128)S(1)} %get-tuple-element.38.mine_ref.scores_ref, ...), custom_call_target="tpu_custom_call" | custom-call | bytes 14400000 | tf_op jit(solution)/shard_map/pallas_call | solution.py:30
  78.5 0.1 collective-permute-start.12
  78.6 1.5 collective-permute-start.13
  80.1 1.4 collective-permute-start.14
  81.5 6.1 %collective-permute-done.12.one = bf16[528,128]{1,0:T(8,128)(2,1)S(1)} collective-permute-done((bf16[528,128]{1,0:T(8,128)(2,1)S(1)}, bf16[528,128]{1,0:T(8,128)(2,1)S(1)}, u32[]{:S(2)}, u32[]{:S(2)}) %collective-permute-start.12) | collective-permute-done | bytes 135200 | tf_op jit(solution)/shard_map/ppermute | solution.py:539
  87.5 0.4 collective-permute-done.14.three
  87.9 0.1 shard_map.69
  88.0 10.6 %all_to_all.26.in_ref = bf16[8,72,128]{2,1,0:T(8,128)(2,1)S(1)} all-to-all(bf16[8,72,128]{2,1,0:T(8,128)(2,1)S(1)} %shard_map.69), channel_id=1, replica_groups={{0,8,16,24,32,40,48,56},{64,72,80,88,96,104,112,120},{128,136,144,152,1..., dimensions={0} | all-to-all | bytes 294912 | tf_op jit(solution)/shard_map/all_to_all | solution.py:57
  98.6 0.1 shard_map.70
  98.7 10.6 %all_to_all.27.in_ref = bf16[8,72,128]{2,1,0:T(8,128)(2,1)S(1)} all-to-all(bf16[8,72,128]{2,1,0:T(8,128)(2,1)S(1)} %get-tuple-element.46), channel_id=1, replica_groups={{0,8,16,24,32,40,48,56},{64,72,80,88,96,104,112,120},{128,136,144,152,1..., dimensions={0} | all-to-all | bytes 294912 | tf_op jit(solution)/shard_map/all_to_all | solution.py:57
  109.3 3.2 %collective-permute-start.17 = (bf16[528,128]{1,0:T(8,128)(2,1)S(1)}, bf16[528,128]{1,0:T(8,128)(2,1)S(1)}, u32[]{:S(2)}, u32[]{:S(2)}) collective-permute-start(bf16[528,128]{1,0:T(8,128)(2,1)S(1)} %shard_map.71.part), channel_id=1, source_target_pairs={{0,192},{8,200},{16,208},{24,216},{32,224},{40,232},{48,240},{56,2... | collective-permute-start | bytes 405512 | tf_op jit(solution)/shard_map/ppermute | solution.py:43
  112.5 0.7 collective-permute-start.15
  113.2 1.0 shard_map.72
  114.2 1.8 %collective-permute-done.17.three = bf16[528,128]{1,0:T(8,128)(2,1)S(1)} collective-permute-done((bf16[528,128]{1,0:T(8,128)(2,1)S(1)}, bf16[528,128]{1,0:T(8,128)(2,1)S(1)}, u32[]{:S(2)}, u32[]{:S(2)}) %collective-permute-start.17) | collective-permute-done | bytes 135200 | tf_op jit(solution)/shard_map/ppermute | solution.py:43
  115.9 2.1 %collective-permute-done.16.two = bf16[528,128]{1,0:T(8,128)(2,1)S(1)} collective-permute-done((bf16[528,128]{1,0:T(8,128)(2,1)S(1)}, bf16[528,128]{1,0:T(8,128)(2,1)S(1)}, u32[]{:S(2)}, u32[]{:S(2)}) %collective-permute-start.16) | collective-permute-done | bytes 135200 | tf_op jit(solution)/shard_map/ppermute | solution.py:43
  118.0 1.1 collective-permute-done.15.one
  119.0 2.6 %shard_map.73 = (f32[72,640]{1,0:T(8,128)S(1)}, f32[72,640]{1,0:T(8,128)S(1)}, f32[8,128]{1,0:T(8,128)S(1)}, f32[8,128]{1,0:T(8,128)S(1)}, f32[8,128]{1,0:T(8,128)S(1)}) custom-call(bf16[1280,4096]{1,0:T(8,128)(2,1)S(1)} %shard_map.64.events_ref, bf16[64,4096]{1,0:T(8,128)(2,1)S(1)} %get-tuple-element.34.rhs_ref, f32[32,128]{1,0:T(8,128)S(1)} %get-tuple-element.35.grad_ref, ...), custom_call_target="tpu_custom_call" | custom-call | bytes 7200000 | tf_op jit(solution)/shard_map/pallas_call | solution.py:30
  121.7 4.6 %collective-permute-start.18 = (f32[72,640]{1,0:T(8,128)S(1)}, f32[72,640]{1,0:T(8,128)S(1)}, u32[]{:S(2)}, u32[]{:S(2)}) collective-permute-start(f32[72,640]{1,0:T(8,128)S(1)} %get-tuple-element.50), channel_id=1, source_target_pairs={{0,1},{1,0},{2,3},{3,2},{4,5},{5,4},{6,7},{7,6},{8,9},{9,8},{10,11... | collective-permute-start | bytes 552968 | tf_op jit(solution)/shard_map/ppermute | solution.py:52
  126.3 1.1 collective-permute-done.18.other
  127.4 0.5 collective-permute-start.21
  127.9 0.7 collective-permute-start.20
  128.6 0.6 collective-permute-start.19
  129.2 2.2 %collective-permute-done.21.three = bf16[72,640]{1,0:T(8,128)(2,1)S(1)} collective-permute-done((bf16[72,640]{1,0:T(8,128)(2,1)S(1)}, bf16[72,640]{1,0:T(8,128)(2,1)S(1)}, u32[]{:S(2)}, u32[]{:S(2)}) %collective-permute-start.21) | collective-permute-done | bytes 92192 | tf_op jit(solution)/shard_map/ppermute | solution.py:48
  131.4 1.5 collective-permute-done.20.two
  132.8 3.0 %collective-permute-done.19.one = bf16[72,640]{1,0:T(8,128)(2,1)S(1)} collective-permute-done((bf16[72,640]{1,0:T(8,128)(2,1)S(1)}, bf16[72,640]{1,0:T(8,128)(2,1)S(1)}, u32[]{:S(2)}, u32[]{:S(2)}) %collective-permute-start.19) | collective-permute-done | bytes 92192 | tf_op jit(solution)/shard_map/ppermute | solution.py:48
  135.8 0.2 shard_map.75
  136.0 0.7 collective-permute-start.22
  136.7 0.8 collective-permute-done.22
  137.5 11.6 %all_to_all.28.tails_ref = f32[32,1,128]{2,1,0:T(1,128)S(1)} all-to-all(f32[32,1,128]{2,1,0:T(1,128)S(1)} %broadcast_in_dim.9), channel_id=1, replica_groups=mesh['event'=32,'feat'=8] {'event'}, dimensions={0} | all-to-all | bytes 32768 | tf_op jit(solution)/shard_map/all_to_all | solution.py:577
  149.1 0.8 shard_map.76
  (15 shorter events, 0.1 us)
Async XLA Ops:
  0.6 15.8 %copy-start = (f32[4096]{0:T(1024)S(1)}, f32[4096]{0:T(1024)}, u32[]{:S(2)}) copy-start(f32[4096]{0:T(1024)} %param.6) | copy-start | bytes 49156
  0.6 0.7 copy-start.2
  1.3 28.6 %copy-start.1 = (s32[1280]{0:T(1024)S(1)}, s32[1280]{0:T(1024)}, u32[]{:S(2)}) copy-start(s32[1280]{0:T(1024)} %param.5) | copy-start | bytes 15364
  4.9 26.5 %all-to-all-start = ((bf16[32,64,128]{2,1,0:T(8,128)(2,1)}), bf16[32,64,128]{2,1,0:T(8,128)(2,1)S(1)}, u32[]{:S(2)}, u32[]{:S(2)}) async-start(bf16[32,64,128]{2,1,0:T(8,128)(2,1)} %shard_map.59._after), calls=%async_computation | async-start | bytes 1048576 | tf_op jit(solution)/shard_map/all_to_all | solution.py:480
  20.9 1.9 %collective-permute-start = (f32[10,128]{1,0:T(8,128)S(1)}, f32[10,128]{1,0:T(8,128)S(1)}, u32[]{:S(2)}, u32[]{:S(2)}) collective-permute-start(f32[10,128]{1,0:T(8,128)S(1)} %get-tuple-element.32), channel_id=1, source_target_pairs={{0,1},{1,0},{2,3},{3,2},{4,5},{5,4},{6,7},{7,6},{8,9},{9,8},{10,11... | collective-permute-start | bytes 15368 | tf_op jit(solution)/shard_map/ppermute | solution.py:52
  22.7 3.8 %collective-permute-start.3 = (f32[10,128]{1,0:T(8,128)S(1)}, f32[10,128]{1,0:T(8,128)S(1)}, u32[]{:S(2)}, u32[]{:S(2)}) collective-permute-start(f32[10,128]{1,0:T(8,128)S(1)} %add.6.own), channel_id=1, source_target_pairs={{0,6},{1,7},{2,0},{3,1},{4,2},{5,3},{6,4},{7,5},{8,14},{9,15},{10,... | collective-permute-start | bytes 15368 | tf_op jit(solution)/shard_map/ppermute | solution.py:48
  25.5 4.3 %collective-permute-start.2 = (f32[10,128]{1,0:T(8,128)S(1)}, f32[10,128]{1,0:T(8,128)S(1)}, u32[]{:S(2)}, u32[]{:S(2)}) collective-permute-start(f32[10,128]{1,0:T(8,128)S(1)} %add.6.own), channel_id=1, source_target_pairs={{0,4},{1,5},{2,6},{3,7},{4,0},{5,1},{6,2},{7,3},{8,12},{9,13},{10,... | collective-permute-start | bytes 15368 | tf_op jit(solution)/shard_map/ppermute | solution.py:48
  25.8 4.0 %collective-permute-start.1 = (f32[10,128]{1,0:T(8,128)S(1)}, f32[10,128]{1,0:T(8,128)S(1)}, u32[]{:S(2)}, u32[]{:S(2)}) collective-permute-start(f32[10,128]{1,0:T(8,128)S(1)} %add.6.own), channel_id=1, source_target_pairs={{0,2},{1,3},{2,4},{3,5},{4,6},{5,7},{6,0},{7,1},{8,10},{9,11},{10,... | collective-permute-start | bytes 15368 | tf_op jit(solution)/shard_map/ppermute | solution.py:48
  47.2 7.7 %collective-permute-start.6 = (bf16[576,128]{1,0:T(8,128)(2,1)S(1)}, bf16[576,128]{1,0:T(8,128)(2,1)S(1)}, u32[]{:S(2)}, u32[]{:S(2)}) collective-permute-start(bf16[576,128]{1,0:T(8,128)(2,1)S(1)} %shard_map.63._after.own), channel_id=1, source_target_pairs={{0,192},{8,200},{16,208},{24,216},{32,224},{40,232},{48,240},{56,2... | collective-permute-start | bytes 442376 | tf_op jit(solution)/shard_map/ppermute | solution.py:43
  49.7 5.6 %collective-permute-start.5 = (bf16[576,128]{1,0:T(8,128)(2,1)S(1)}, bf16[576,128]{1,0:T(8,128)(2,1)S(1)}, u32[]{:S(2)}, u32[]{:S(2)}) collective-permute-start(bf16[576,128]{1,0:T(8,128)(2,1)S(1)} %shard_map.63._after.own), channel_id=1, source_target_pairs={{0,128},{8,136},{16,144},{24,152},{32,160},{40,168},{48,176},{56,1... | collective-permute-start | bytes 442376 | tf_op jit(solution)/shard_map/ppermute | solution.py:43
  50.2 6.6 %collective-permute-start.4 = (bf16[576,128]{1,0:T(8,128)(2,1)S(1)}, bf16[576,128]{1,0:T(8,128)(2,1)S(1)}, u32[]{:S(2)}, u32[]{:S(2)}) collective-permute-start(bf16[576,128]{1,0:T(8,128)(2,1)S(1)} %shard_map.63._after.own), channel_id=1, source_target_pairs={{0,64},{8,72},{16,80},{24,88},{32,96},{40,104},{48,112},{56,120},{... | collective-permute-start | bytes 442376 | tf_op jit(solution)/shard_map/ppermute | solution.py:43
  60.1 5.9 %collective-permute-start.7 = (f32[72,640]{1,0:T(8,128)S(1)}, f32[72,640]{1,0:T(8,128)S(1)}, u32[]{:S(2)}, u32[]{:S(2)}) collective-permute-start(f32[72,640]{1,0:T(8,128)S(1)} %get-tuple-element.37), channel_id=1, source_target_pairs={{0,1},{1,0},{2,3},{3,2},{4,5},{5,4},{6,7},{7,6},{8,9},{9,8},{10,11... | collective-permute-start | bytes 552968 | tf_op jit(solution)/shard_map/ppermute | solution.py:52
  66.1 4.0 %collective-permute-start.10 = (bf16[72,640]{1,0:T(8,128)(2,1)S(1)}, bf16[72,640]{1,0:T(8,128)(2,1)S(1)}, u32[]{:S(2)}, u32[]{:S(2)}) collective-permute-start(bf16[72,640]{1,0:T(8,128)(2,1)S(1)} %shard_map.66.own), channel_id=1, source_target_pairs={{0,6},{1,7},{2,0},{3,1},{4,2},{5,3},{6,4},{7,5},{8,14},{9,15},{10,... | collective-permute-start | bytes 276488 | tf_op jit(solution)/shard_map/ppermute | solution.py:48
  66.8 4.9 %collective-permute-start.9 = (bf16[72,640]{1,0:T(8,128)(2,1)S(1)}, bf16[72,640]{1,0:T(8,128)(2,1)S(1)}, u32[]{:S(2)}, u32[]{:S(2)}) collective-permute-start(bf16[72,640]{1,0:T(8,128)(2,1)S(1)} %shard_map.66.own), channel_id=1, source_target_pairs={{0,4},{1,5},{2,6},{3,7},{4,0},{5,1},{6,2},{7,3},{8,12},{9,13},{10,... | collective-permute-start | bytes 276488 | tf_op jit(solution)/shard_map/ppermute | solution.py:48
  68.0 6.6 %collective-permute-start.8 = (bf16[72,640]{1,0:T(8,128)(2,1)S(1)}, bf16[72,640]{1,0:T(8,128)(2,1)S(1)}, u32[]{:S(2)}, u32[]{:S(2)}) collective-permute-start(bf16[72,640]{1,0:T(8,128)(2,1)S(1)} %shard_map.66.own), channel_id=1, source_target_pairs={{0,2},{1,3},{2,4},{3,5},{4,6},{5,7},{6,0},{7,1},{8,10},{9,11},{10,... | collective-permute-start | bytes 276488 | tf_op jit(solution)/shard_map/ppermute | solution.py:48
  74.6 1.9 %collective-permute-start.11 = (f32[64,640]{1,0:T(8,128)S(1)}, f32[64,640]{1,0:T(8,128)S(1)}, u32[]{:S(2)}, u32[]{:S(2)}) collective-permute-start(f32[64,640]{1,0:T(8,128)S(1)} %get-tuple-element.38.mine_ref.scores_ref), channel_id=1, source_target_pairs={{0,1},{1,0},{2,3},{3,2},{4,5},{5,4},{6,7},{7,6},{8,9},{9,8},{10,11... | collective-permute-start | bytes 491528 | tf_op jit(solution)/shard_map/ppermute | solution.py:52
  78.5 9.0 %collective-permute-start.12 = (bf16[528,128]{1,0:T(8,128)(2,1)S(1)}, bf16[528,128]{1,0:T(8,128)(2,1)S(1)}, u32[]{:S(2)}, u32[]{:S(2)}) collective-permute-start(bf16[528,128]{1,0:T(8,128)(2,1)S(1)} %get-tuple-element.42), channel_id=1, source_target_pairs={{0,64},{8,72},{16,80},{24,88},{32,96},{40,104},{48,112},{56,120},{... | collective-permute-start | bytes 405512 | tf_op jit(solution)/shard_map/ppermute | solution.py:539
  78.6 8.9 %collective-permute-start.13 = (bf16[528,128]{1,0:T(8,128)(2,1)S(1)}, bf16[528,128]{1,0:T(8,128)(2,1)S(1)}, u32[]{:S(2)}, u32[]{:S(2)}) collective-permute-start(bf16[528,128]{1,0:T(8,128)(2,1)S(1)} %get-tuple-element.43), channel_id=1, source_target_pairs={{0,128},{8,136},{16,144},{24,152},{32,160},{40,168},{48,176},{56,1... | collective-permute-start | bytes 405512 | tf_op jit(solution)/shard_map/ppermute | solution.py:539
  80.1 7.8 %collective-permute-start.14 = (bf16[528,128]{1,0:T(8,128)(2,1)S(1)}, bf16[528,128]{1,0:T(8,128)(2,1)S(1)}, u32[]{:S(2)}, u32[]{:S(2)}) collective-permute-start(bf16[528,128]{1,0:T(8,128)(2,1)S(1)} %get-tuple-element.44), channel_id=1, source_target_pairs={{0,192},{8,200},{16,208},{24,216},{32,224},{40,232},{48,240},{56,2... | collective-permute-start | bytes 405512 | tf_op jit(solution)/shard_map/ppermute | solution.py:539
  109.3 6.6 %collective-permute-start.17 = (bf16[528,128]{1,0:T(8,128)(2,1)S(1)}, bf16[528,128]{1,0:T(8,128)(2,1)S(1)}, u32[]{:S(2)}, u32[]{:S(2)}) collective-permute-start(bf16[528,128]{1,0:T(8,128)(2,1)S(1)} %shard_map.71.part), channel_id=1, source_target_pairs={{0,192},{8,200},{16,208},{24,216},{32,224},{40,232},{48,240},{56,2... | collective-permute-start | bytes 405512 | tf_op jit(solution)/shard_map/ppermute | solution.py:43
  112.5 5.5 %collective-permute-start.16 = (bf16[528,128]{1,0:T(8,128)(2,1)S(1)}, bf16[528,128]{1,0:T(8,128)(2,1)S(1)}, u32[]{:S(2)}, u32[]{:S(2)}) collective-permute-start(bf16[528,128]{1,0:T(8,128)(2,1)S(1)} %shard_map.71.part), channel_id=1, source_target_pairs={{0,128},{8,136},{16,144},{24,152},{32,160},{40,168},{48,176},{56,1... | collective-permute-start | bytes 405512 | tf_op jit(solution)/shard_map/ppermute | solution.py:43
  112.5 6.5 %collective-permute-start.15 = (bf16[528,128]{1,0:T(8,128)(2,1)S(1)}, bf16[528,128]{1,0:T(8,128)(2,1)S(1)}, u32[]{:S(2)}, u32[]{:S(2)}) collective-permute-start(bf16[528,128]{1,0:T(8,128)(2,1)S(1)} %shard_map.71.part), channel_id=1, source_target_pairs={{0,64},{8,72},{16,80},{24,88},{32,96},{40,104},{48,112},{56,120},{... | collective-permute-start | bytes 405512 | tf_op jit(solution)/shard_map/ppermute | solution.py:43
  121.7 5.7 %collective-permute-start.18 = (f32[72,640]{1,0:T(8,128)S(1)}, f32[72,640]{1,0:T(8,128)S(1)}, u32[]{:S(2)}, u32[]{:S(2)}) collective-permute-start(f32[72,640]{1,0:T(8,128)S(1)} %get-tuple-element.50), channel_id=1, source_target_pairs={{0,1},{1,0},{2,3},{3,2},{4,5},{5,4},{6,7},{7,6},{8,9},{9,8},{10,11... | collective-permute-start | bytes 552968 | tf_op jit(solution)/shard_map/ppermute | solution.py:52
  127.4 4.0 %collective-permute-start.21 = (bf16[72,640]{1,0:T(8,128)(2,1)S(1)}, bf16[72,640]{1,0:T(8,128)(2,1)S(1)}, u32[]{:S(2)}, u32[]{:S(2)}) collective-permute-start(bf16[72,640]{1,0:T(8,128)(2,1)S(1)} %shard_map.74.own), channel_id=1, source_target_pairs={{0,6},{1,7},{2,0},{3,1},{4,2},{5,3},{6,4},{7,5},{8,14},{9,15},{10,... | collective-permute-start | bytes 276488 | tf_op jit(solution)/shard_map/ppermute | solution.py:48
  127.9 5.0 %collective-permute-start.20 = (bf16[72,640]{1,0:T(8,128)(2,1)S(1)}, bf16[72,640]{1,0:T(8,128)(2,1)S(1)}, u32[]{:S(2)}, u32[]{:S(2)}) collective-permute-start(bf16[72,640]{1,0:T(8,128)(2,1)S(1)} %shard_map.74.own), channel_id=1, source_target_pairs={{0,4},{1,5},{2,6},{3,7},{4,0},{5,1},{6,2},{7,3},{8,12},{9,13},{10,... | collective-permute-start | bytes 276488 | tf_op jit(solution)/shard_map/ppermute | solution.py:48
  128.6 7.2 %collective-permute-start.19 = (bf16[72,640]{1,0:T(8,128)(2,1)S(1)}, bf16[72,640]{1,0:T(8,128)(2,1)S(1)}, u32[]{:S(2)}, u32[]{:S(2)}) collective-permute-start(bf16[72,640]{1,0:T(8,128)(2,1)S(1)} %shard_map.74.own), channel_id=1, source_target_pairs={{0,2},{1,3},{2,4},{3,5},{4,6},{5,7},{6,0},{7,1},{8,10},{9,11},{10,... | collective-permute-start | bytes 276488 | tf_op jit(solution)/shard_map/ppermute | solution.py:48
  136.0 1.5 %collective-permute-start.22 = (f32[1,128]{1,0:T(1,128)S(1)}, f32[1,128]{1,0:T(1,128)S(1)}, u32[]{:S(2)}, u32[]{:S(2)}) collective-permute-start(f32[1,128]{1,0:T(1,128)S(1)} %get-tuple-element.51), channel_id=1, source_target_pairs={{0,1},{1,0},{2,3},{3,2},{4,5},{5,4},{6,7},{7,6},{8,9},{9,8},{10,11... | collective-permute-start | bytes 1544 | tf_op jit(solution)/shard_map/ppermute | solution.py:52
